TPU v7x, 32 devices: a whole 2x2x4 slice. The times are simulated.
32 devices in a mesh: rows: 2 (over x), frames: 16 (over z, y, core).
Axes of the slice: x: 2, y: 2, z: 4, core: 2. Of those that a mesh axis runs over, the one named last changes fastest.
Arguments:
- features: bfloat16 [4, 4096, 512], P('rows', 'frames'), may hold values from -16 to 16
- lengths: int32 [4, 17], replicated, may hold values from 0 to 4096, as said below
- windows: int32 [4], P('rows'), may hold values from 64 to 128, as said below
- feed_in: bfloat16 [2, 512, 2048], replicated, may hold values from -0.25 to 0.25
- feed_in_bias: float32 [2, 2048], replicated, may hold values from -1.75 to 1.75
- feed_out: bfloat16 [2, 2048, 512], replicated, may hold values from -0.125 to 0.125
- attend_in: bfloat16 [512, 1536], replicated, may hold values from -0.25 to 0.25
- attend_out: bfloat16 [512, 512], replicated, may hold values from -1 to 1
- position_proj: bfloat16 [512, 512], replicated, may hold values from -0.375 to 0.375
- convolve_in: bfloat16 [512, 1024], replicated, may hold values from -0.25 to 0.25
- convolve_out: bfloat16 [512, 512], replicated, may hold values from -0.25 to 0.25
- depthwise: float32 [9, 512], replicated, may hold values from -2 to 2
- norm_gain: float32 [6, 512], replicated, may hold values from 0.25 to 1.75
- norm_shift: float32 [6, 512], replicated, may hold values from -1.25 to 1.25
- biases: float32 [10, 512], replicated, may hold values from -1.75 to 1.75
- cotangent: bfloat16 [4, 4096, 512], P('rows', 'frames'), may hold values from -6 to 6
Outputs:
- out: bfloat16 [4, 4096, 512], P('rows', 'frames')
- grad_features: float32 [4, 4096, 512], P('rows', 'frames')
- grad_feed_in: float32 [2, 512, 2048], P(None, None, 'frames')
- grad_feed_in_bias: float32 [2, 2048], P(None, 'frames')
- grad_feed_out: float32 [2, 2048, 512], P(None, 'frames')
- grad_attend_in: float32 [512, 1536], P('frames')
- grad_attend_out: float32 [512, 512], P('frames')
- grad_position_proj: float32 [512, 512], P('frames')
- grad_convolve_in: float32 [512, 1024], P('frames')
- grad_convolve_out: float32 [512, 512], P('frames')
- grad_depthwise: float32 [9, 512], P(None, 'frames')
- grad_norm_gain: float32 [6, 512], P(None, 'frames')
- grad_norm_shift: float32 [6, 512], P(None, 'frames')
- grad_biases: float32 [10, 512], P(None, 'frames')
Inputs may be any that keep to these rules, and one draw needn't show every extreme that they name: Row r holds utterances of lengths[r, 0], lengths[r, 1], ... frames one after the other from frame 0, then zeros; the frames after their sum are padding. In each aligned block of 2 rows one row holds a single utterance of 4096 frames; in the other rows every utterance but the last has 256 to 1024 frames, and fewer than 256 frames are padding. `windows`: some row's reach is 128.
All inputs are finite; a program needn't handle non-finite values.
Results may differ from a plain program's by a relative error of at most 0.035.
Values may be sent and summed in bfloat16 or wider, within the bound.
No kernel may reach another device: no remote copies, remote signals or barrier semaphores. Data moves between devices by JAX's collectives and lax.ppermute only.
A program may use at most 192 MiB of HBM per device.

v0:
```python
import math

import jax
import jax.numpy as jnp
from jax import lax
from jax.sharding import PartitionSpec as P

H = 8
DH = 64
KERNEL = 9
WIN = 128


eps_norm = 1e-05
negative = -1e30
rows_first = (((0,), (0,)), ((), ()))
columns_last = (((1,), (1,)), ((), ()))


def padded_2(x, sides, width):
    for axis, dim in sides:
        devices, length = (lax.axis_size(axis), x.shape[dim])
        up = [(i, (i + 1) % devices) for i in range(devices - 1)]
        down = [(j, i) for i, j in up]
        last = lax.slice_in_dim(x, length - width, length, axis=dim)
        first = lax.slice_in_dim(x, 0, width, axis=dim)
        before = lax.ppermute(last, axis, up)
        after = lax.ppermute(first, axis, down)
        x = jnp.concatenate([before, x, after], axis=dim)
    return x


def product(left, right):
    return jnp.dot(left, right, preferred_element_type=jnp.float32)


def left_product(left, right):
    return lax.dot_general(left, right, rows_first, preferred_element_type=jnp.float32)


def right_product(left, right):
    return lax.dot_general(left, right, columns_last, preferred_element_type=jnp.float32)


def position_table(width, model):
    offsets = (jnp.arange(2 * width + 1, dtype=jnp.int32) - width).astype(jnp.float32)
    rates = jnp.exp(
        jnp.arange(model // 2, dtype=jnp.int32).astype(jnp.float32)
        * (-2.0 * math.log(10000.0) / model)
    )
    angles = offsets[:, None] * rates[None, :]
    return jnp.stack([jnp.sin(angles), jnp.cos(angles)], axis=2).reshape(2 * width + 1, model)


def into_band(table):
    heads, queries, band = table.shape
    width = queries + band - 1
    padded = jnp.pad(table, ((0, 0), (0, 0), (0, width + 1 - band)))
    flat = padded.reshape(heads, queries * (width + 1))[:, : queries * width]
    return flat.reshape(heads, queries, width)


def from_band(grid, band):
    heads, queries, width = grid.shape
    flat = jnp.pad(grid.reshape(heads, queries * width), ((0, 0), (0, queries)))
    return flat.reshape(heads, queries, width + 1)[:, :, :band]


def documents(positions, ends):
    return jnp.sum((ends[None, :] <= positions[:, None]).astype(jnp.int32), axis=1, dtype=jnp.int32)


def pair_mask(query_pos, key_pos, ends, limit, row_len):
    same = documents(query_pos, ends)[:, None] == documents(key_pos, ends)[None, :]
    near = jnp.abs(key_pos[None, :] - query_pos[:, None]) <= limit
    inside = (key_pos >= 0) & (key_pos < row_len)
    return same & near & inside[None, :]


def layer_norm_keep(values, gain, shift):
    centered = values - jnp.mean(values, axis=-1, keepdims=True)
    inverse = lax.rsqrt(jnp.mean(centered * centered, axis=-1, keepdims=True) + eps_norm)
    normal = centered * inverse
    return (normal * gain + shift, normal, inverse)


def layer_norm_back(grad_out, normal, inverse, gain):
    scaled = grad_out * gain
    centred = scaled - jnp.mean(scaled, axis=-1, keepdims=True)
    grad_in = inverse * (centred - normal * jnp.mean(scaled * normal, axis=-1, keepdims=True))
    return (grad_in, jnp.sum(grad_out * normal, axis=0), jnp.sum(grad_out, axis=0))


def feed_forward(hidden, gain, shift, weight_in, bias_in, weight_out, bias_out):
    normed, normal, inverse = layer_norm_keep(hidden, gain, shift)
    normed = normed.astype(jnp.bfloat16)
    inner = product(normed, weight_in) + bias_in
    sigma = jax.nn.sigmoid(inner)
    active = (inner * sigma).astype(jnp.bfloat16)
    return (product(active, weight_out) + bias_out, (normal, inverse, normed, inner, sigma, active))


def feed_back(grad_branch, kept, gain, weight_in, weight_out):
    normal, inverse, normed, inner, sigma, active = kept
    grad_low = grad_branch.astype(jnp.bfloat16)
    grad_active = right_product(grad_low, weight_out)
    grad_inner = (grad_active * sigma * (1.0 + inner * (1.0 - sigma))).astype(jnp.bfloat16)
    grad_normed = right_product(grad_inner, weight_in)
    grad_hidden, grad_gain, grad_shift = layer_norm_back(grad_normed, normal, inverse, gain)
    grads = (
        left_product(normed, grad_inner),
        jnp.sum(grad_inner.astype(jnp.float32), axis=0),
        left_product(active, grad_low),
        jnp.sum(grad_low.astype(jnp.float32), axis=0),
        grad_gain,
        grad_shift,
    )
    return (grad_hidden, grads)


def per_device(
    features,
    lengths,
    windows,
    feed_in,
    feed_in_bias,
    feed_out,
    attend_in,
    attend_out,
    position_proj,
    convolve_in,
    convolve_out,
    depthwise,
    norm_gain,
    norm_shift,
    biases,
    cotangent,
):
    rows_here, frames_here, model = features.shape
    tokens = rows_here * frames_here
    half = KERNEL // 2
    band = 2 * WIN + 1
    factor = 1.0 / math.sqrt(DH)
    row_len = frames_here * lax.axis_size("frames")
    start = lax.axis_index("frames") * frames_here
    ends_every = jnp.cumsum(lengths, axis=1, dtype=jnp.int32)
    count = jnp.sum(ends_every[:, -1].astype(jnp.float32))
    ends_all = lax.dynamic_slice_in_dim(
        ends_every, lax.axis_index("rows") * rows_here, rows_here, 0
    )
    local_pos = start + jnp.arange(frames_here, dtype=jnp.int32)
    valid = (local_pos[None, :] < ends_all[:, -1:]).astype(jnp.float32).reshape(tokens, 1)
    stream_in = features.reshape(tokens, model).astype(jnp.float32)
    first_branch, first_kept = feed_forward(
        stream_in, norm_gain[0], norm_shift[0], feed_in[0], feed_in_bias[0], feed_out[0], biases[6]
    )
    after_first = stream_in + 0.5 * first_branch
    normed_a, normal_a, inverse_a = layer_norm_keep(after_first, norm_gain[1], norm_shift[1])
    normed_a = normed_a.astype(jnp.bfloat16)
    joined = product(normed_a, attend_in)
    query = joined[:, :model] + biases[0]
    query_u = (query + biases[8]).astype(jnp.bfloat16).reshape(rows_here, frames_here, H, DH)
    query_v = (query + biases[9]).astype(jnp.bfloat16).reshape(rows_here, frames_here, H, DH)
    pair = jnp.concatenate(
        [joined[:, model : 2 * model], joined[:, 2 * model :] + biases[1]], axis=1
    )
    pair = pair.astype(jnp.bfloat16).reshape(rows_here, frames_here, 2 * model)
    window = padded_2(pair, (("frames", 1),), WIN)
    key_rows = window[..., :model].reshape(rows_here, frames_here + 2 * WIN, H, DH)
    value_rows = window[..., model:].reshape(rows_here, frames_here + 2 * WIN, H, DH)
    sinusoid = position_table(WIN, model).astype(jnp.bfloat16)
    table = product(sinusoid, position_proj).astype(jnp.bfloat16).reshape(band, H, DH)
    key_pos = start - WIN + jnp.arange(frames_here + 2 * WIN, dtype=jnp.int32)

    def scores_of(row_index):
        allowed = pair_mask(local_pos, key_pos, ends_all[row_index], windows[row_index], row_len)
        content = jnp.einsum(
            "qhd,khd->hqk",
            query_u[row_index],
            key_rows[row_index],
            preferred_element_type=jnp.float32,
        )
        spread = jnp.einsum(
            "qhd,bhd->hqb", query_v[row_index], table, preferred_element_type=jnp.float32
        )
        return jnp.where(allowed[None], (content + into_band(spread)) * factor, negative)

    mixed_rows = []
    logsum_rows = []
    for row_index in range(rows_here):
        scores = scores_of(row_index)
        top = jnp.max(scores, axis=2, keepdims=True)
        powers = jnp.exp(scores - top)
        total = jnp.sum(powers, axis=2, keepdims=True)
        weights = (powers / total).astype(jnp.bfloat16)
        mixed = jnp.einsum(
            "hqk,khd->qhd", weights, value_rows[row_index], preferred_element_type=jnp.float32
        )
        mixed_rows.append(mixed.astype(jnp.bfloat16).reshape(frames_here, model))
        logsum_rows.append(top + jnp.log(total))
    mixed_low = jnp.concatenate(mixed_rows, axis=0)
    after_attend = after_first + product(mixed_low, attend_out) + biases[2]
    normed_c, normal_c, inverse_c = layer_norm_keep(after_attend, norm_gain[2], norm_shift[2])
    normed_c = normed_c.astype(jnp.bfloat16)
    paired = product(normed_c, convolve_in) + jnp.concatenate([biases[3], biases[4]])
    gate_sigma = jax.nn.sigmoid(paired[:, model:])
    gated = (
        (paired[:, :model] * gate_sigma).astype(jnp.bfloat16).reshape(rows_here, frames_here, model)
    )
    rim = padded_2(gated, (("frames", 1),), half)
    rim_positions = start - half + jnp.arange(frames_here + 2 * half, dtype=jnp.int32)
    rim_documents = jax.vmap(lambda ends: documents(rim_positions, ends))(ends_all)
    rim_inside = (rim_positions >= 0) & (rim_positions < row_len)
    centre = rim_documents[:, half : half + frames_here]
    keeps = []
    for tap in range(KERNEL):
        keep = (rim_documents[:, tap : tap + frames_here] == centre) & rim_inside[
            None, tap : tap + frames_here
        ]
        keeps.append(keep.astype(jnp.float32)[..., None])
    depth = jnp.zeros((rows_here, frames_here, model), jnp.float32)
    for tap in range(KERNEL):
        depth = depth + depthwise[tap] * rim[:, tap : tap + frames_here] * keeps[tap]
    depth = depth.reshape(tokens, model)
    first_sum = lax.psum(jnp.sum(depth * valid, axis=0), ("rows", "frames"))
    mean = first_sum / count
    centered = depth - mean
    spread_sum = lax.psum(jnp.sum(centered * centered * valid, axis=0), ("rows", "frames"))
    variance = spread_sum / count
    batch_inverse = lax.rsqrt(variance + eps_norm)
    batch_normal = centered * batch_inverse
    batch = batch_normal * norm_gain[5] + norm_shift[5]
    batch_sigma = jax.nn.sigmoid(batch)
    swished = (batch * batch_sigma).astype(jnp.bfloat16)
    after_conv = after_attend + product(swished, convolve_out) + biases[5]
    second_branch, second_kept = feed_forward(
        after_conv, norm_gain[3], norm_shift[3], feed_in[1], feed_in_bias[1], feed_out[1], biases[7]
    )
    after_second = after_conv + 0.5 * second_branch
    final, normal_o, inverse_o = layer_norm_keep(after_second, norm_gain[4], norm_shift[4])
    out = (valid * final).astype(jnp.bfloat16).reshape(rows_here, frames_here, model)
    grad_final = valid * cotangent.reshape(tokens, model).astype(jnp.float32)
    grad_second, gain_out, shift_out = layer_norm_back(
        grad_final, normal_o, inverse_o, norm_gain[4]
    )
    grad_from_second, second_grads = feed_back(
        0.5 * grad_second, second_kept, norm_gain[3], feed_in[1], feed_out[1]
    )
    grad_conv_stream = grad_second + grad_from_second
    grad_conv_low = grad_conv_stream.astype(jnp.bfloat16)
    grad_convolve_out = left_product(swished, grad_conv_low)
    conv_out_bias = jnp.sum(grad_conv_low.astype(jnp.float32), axis=0)
    grad_swished = right_product(grad_conv_low, convolve_out)
    grad_batch = grad_swished * batch_sigma * (1.0 + batch * (1.0 - batch_sigma))
    total_a, total_b = lax.psum(
        (jnp.sum(grad_batch, axis=0), jnp.sum(grad_batch * batch_normal, axis=0)),
        ("rows", "frames"),
    )
    batch_gain = norm_gain[5]
    grad_depth = batch_inverse * (
        grad_batch * batch_gain - valid * batch_gain * (total_a + batch_normal * total_b) / count
    )
    grad_depth = grad_depth.astype(jnp.bfloat16).reshape(rows_here, frames_here, model)
    grad_rim = padded_2(grad_depth, (("frames", 1),), half)
    grad_depth_wide = grad_depth.astype(jnp.float32)
    depth_grads = []
    grad_gated = jnp.zeros((rows_here, frames_here, model), jnp.float32)
    for tap in range(KERNEL):
        depth_grads.append(
            jnp.sum(grad_depth_wide * rim[:, tap : tap + frames_here] * keeps[tap], axis=(0, 1))
        )
        mirror = 2 * half - tap
        grad_gated = (
            grad_gated + depthwise[tap] * grad_rim[:, mirror : mirror + frames_here] * keeps[mirror]
        )
    grad_gated = grad_gated.reshape(tokens, model)
    value_half = paired[:, :model]
    grad_paired = jnp.concatenate(
        [grad_gated * gate_sigma, grad_gated * value_half * gate_sigma * (1.0 - gate_sigma)], axis=1
    ).astype(jnp.bfloat16)
    grad_convolve_in = left_product(normed_c, grad_paired)
    conv_in_bias = jnp.sum(grad_paired.astype(jnp.float32), axis=0)
    grad_normed_c = right_product(grad_paired, convolve_in)
    grad_from_conv, gain_c, shift_c = layer_norm_back(
        grad_normed_c, normal_c, inverse_c, norm_gain[2]
    )
    grad_attend_stream = grad_conv_stream + grad_from_conv
    grad_attend_low = grad_attend_stream.astype(jnp.bfloat16)
    grad_attend_out = left_product(mixed_low, grad_attend_low)
    attend_out_bias = jnp.sum(grad_attend_low.astype(jnp.float32), axis=0)
    grad_mixed = (
        right_product(grad_attend_low, attend_out)
        .astype(jnp.bfloat16)
        .reshape(rows_here, frames_here, H, DH)
    )
    grad_table = jnp.zeros((band, H, DH), jnp.float32)
    key_grads = []
    value_grads = []
    content_grads = []
    spread_grads = []
    for row_index in range(rows_here):
        scores = scores_of(row_index)
        probability = jnp.exp(scores - logsum_rows[row_index])
        grad_probability = jnp.einsum(
            "qhd,khd->hqk",
            grad_mixed[row_index],
            value_rows[row_index],
            preferred_element_type=jnp.float32,
        )
        delta = jnp.sum(probability * grad_probability, axis=2, keepdims=True)
        grad_raw = (probability * (grad_probability - delta) * factor).astype(jnp.bfloat16)
        value_grads.append(
            jnp.einsum(
                "hqk,qhd->khd",
                probability.astype(jnp.bfloat16),
                grad_mixed[row_index],
                preferred_element_type=jnp.float32,
            )
        )
        key_grads.append(
            jnp.einsum(
                "hqk,qhd->khd", grad_raw, query_u[row_index], preferred_element_type=jnp.float32
            )
        )
        content_grads.append(
            jnp.einsum(
                "hqk,khd->qhd", grad_raw, key_rows[row_index], preferred_element_type=jnp.float32
            )
        )
        band_grad = from_band(grad_raw, band)
        spread_grads.append(
            jnp.einsum("hqb,bhd->qhd", band_grad, table, preferred_element_type=jnp.float32)
        )
        grad_table = grad_table + jnp.einsum(
            "hqb,qhd->bhd", band_grad, query_v[row_index], preferred_element_type=jnp.float32
        )
    window_span = frames_here + 2 * WIN
    grad_window = jnp.concatenate(
        [
            jnp.stack(key_grads).reshape(rows_here, window_span, model),
            jnp.stack(value_grads).reshape(rows_here, window_span, model),
        ],
        axis=2,
    )
    edges = jnp.concatenate([grad_window[:, :WIN], grad_window[:, frames_here + WIN :]], axis=1)
    returned = padded_2(edges.astype(jnp.bfloat16), (("frames", 1),), WIN).astype(edges.dtype)
    from_left = jnp.pad(returned[:, :WIN], ((0, 0), (0, frames_here - WIN), (0, 0)))
    from_right = jnp.pad(returned[:, 3 * WIN :], ((0, 0), (frames_here - WIN, 0), (0, 0)))
    grad_pair = (grad_window[:, WIN : WIN + frames_here] + from_left + from_right).reshape(
        tokens, 2 * model
    )
    grad_pair_low = grad_pair.astype(jnp.bfloat16)
    grad_query_u = jnp.stack(content_grads).reshape(tokens, model)
    grad_query_v = jnp.stack(spread_grads).reshape(tokens, model)
    grad_query = (grad_query_u + grad_query_v).astype(jnp.bfloat16)
    grad_joined = jnp.concatenate([grad_query, grad_pair_low], axis=1)
    grad_attend_in = left_product(normed_a, grad_joined)
    grad_normed_a = right_product(grad_joined, attend_in)
    grad_from_attend, gain_a, shift_a = layer_norm_back(
        grad_normed_a, normal_a, inverse_a, norm_gain[1]
    )
    grad_first_stream = grad_attend_stream + grad_from_attend
    grad_position_proj = lax.dot_general(
        sinusoid.astype(jnp.float32),
        grad_table.reshape(band, model),
        rows_first,
        precision=lax.Precision.HIGHEST,
        preferred_element_type=jnp.float32,
    )
    grad_from_first, first_grads = feed_back(
        0.5 * grad_first_stream, first_kept, norm_gain[0], feed_in[0], feed_out[0]
    )
    grad_features = (grad_first_stream + grad_from_first).reshape(rows_here, frames_here, model)
    bias_rows = jnp.stack(
        [
            jnp.sum(grad_query.astype(jnp.float32), axis=0),
            jnp.sum(grad_pair_low[:, model:].astype(jnp.float32), axis=0),
            attend_out_bias,
            conv_in_bias[:model],
            conv_in_bias[model:],
            conv_out_bias,
            first_grads[3],
            second_grads[3],
            jnp.sum(grad_query_u, axis=0),
            jnp.sum(grad_query_v, axis=0),
        ]
    )
    depth_rows = jnp.stack(depth_grads)
    gain_rows = jnp.stack([first_grads[4], gain_a, gain_c, second_grads[4], gain_out])
    shift_rows = jnp.stack([first_grads[5], shift_a, shift_c, second_grads[5], shift_out])
    summed = (
        lax.psum_scatter(
            jnp.stack([first_grads[0], second_grads[0]]), "frames", scatter_dimension=2, tiled=True
        ),
        lax.psum_scatter(
            jnp.stack([first_grads[1], second_grads[1]]), "frames", scatter_dimension=1, tiled=True
        ),
        lax.psum_scatter(
            jnp.stack([first_grads[2], second_grads[2]]), "frames", scatter_dimension=1, tiled=True
        ),
        lax.psum_scatter(grad_attend_in, "frames", scatter_dimension=0, tiled=True),
        lax.psum_scatter(grad_attend_out, "frames", scatter_dimension=0, tiled=True),
        lax.psum_scatter(grad_position_proj, "frames", scatter_dimension=0, tiled=True),
        lax.psum_scatter(grad_convolve_in, "frames", scatter_dimension=0, tiled=True),
        lax.psum_scatter(grad_convolve_out, "frames", scatter_dimension=0, tiled=True),
        lax.psum_scatter(depth_rows, "frames", scatter_dimension=1, tiled=True),
        lax.psum_scatter(gain_rows, "frames", scatter_dimension=1, tiled=True),
        lax.psum_scatter(shift_rows, "frames", scatter_dimension=1, tiled=True),
        lax.psum_scatter(bias_rows, "frames", scatter_dimension=1, tiled=True),
    )
    summed = (
        lax.psum(summed[0].astype(jnp.bfloat16), "rows").astype(jnp.float32),
        lax.psum(summed[1].astype(jnp.bfloat16), "rows").astype(jnp.float32),
        lax.psum(summed[2].astype(jnp.bfloat16), "rows").astype(jnp.float32),
        lax.psum(summed[3].astype(jnp.bfloat16), "rows").astype(jnp.float32),
        lax.psum(summed[4].astype(jnp.bfloat16), "rows").astype(jnp.float32),
        lax.psum(summed[5].astype(jnp.bfloat16), "rows").astype(jnp.float32),
        lax.psum(summed[6].astype(jnp.bfloat16), "rows").astype(jnp.float32),
        lax.psum(summed[7].astype(jnp.bfloat16), "rows").astype(jnp.float32),
        lax.psum(summed[8].astype(jnp.bfloat16), "rows").astype(jnp.float32),
        lax.psum(summed[9].astype(jnp.bfloat16), "rows").astype(jnp.float32),
        lax.psum(summed[10].astype(jnp.bfloat16), "rows").astype(jnp.float32),
        lax.psum(summed[11].astype(jnp.bfloat16), "rows").astype(jnp.float32),
    )
    feed_parts = (summed[0], summed[1], summed[2])
    rest = summed[3:]
    slice_width = model // lax.axis_size("frames")
    slice_start = lax.axis_index("frames") * slice_width
    total_b_part = lax.dynamic_slice_in_dim(total_b, slice_start, slice_width, 0)
    total_a_part = lax.dynamic_slice_in_dim(total_a, slice_start, slice_width, 0)
    grad_norm_gain = jnp.concatenate([rest[6], total_b_part[None, :]], axis=0)
    grad_norm_shift = jnp.concatenate([rest[7], total_a_part[None, :]], axis=0)
    return (
        out,
        grad_features,
        feed_parts[0],
        feed_parts[1],
        feed_parts[2],
        rest[0],
        rest[1],
        rest[2],
        rest[3],
        rest[4],
        rest[5],
        grad_norm_gain,
        grad_norm_shift,
        rest[8],
    )


def solution(mesh):
    placed = (
        P("rows", "frames", None),
        P(),
        P("rows"),
        P(),
        P(),
        P(),
        P(),
        P(),
        P(),
        P(),
        P(),
        P(),
        P(),
        P(),
        P(),
        P("rows", "frames", None),
    )
    return jax.shard_map(
        per_device,
        mesh=mesh,
        in_specs=placed,
        out_specs=(
            P("rows", "frames", None),
            P("rows", "frames", None),
            P(None, None, "frames"),
            P(None, "frames"),
            P(None, "frames", None),
            P("frames", None),
            P("frames", None),
            P("frames", None),
            P("frames", None),
            P("frames", None),
            P(None, "frames"),
            P(None, "frames"),
            P(None, "frames"),
            P(None, "frames"),
        ),
        check_vma=False,
    )
```

profile of v0, /device:TPU:0, one launch (start us, length us, event | category | flops | bytes accessed | tf_op | source)
XLA Modules:
  0.0 1284.7 jit_solution(93465366723532468)
XLA Ops:
  26.4 3.1 collective-permute-start
  39.0 12.9 %multiply_sine_fusion = (bf16[257,256,1]{0,2,1:T(2,128)(2,1)S(1)}, bf16[257,256,1]{0,2,1:T(2,128)(2,1)S(1)}) fusion(f32[257]{0:T(512)} %add_convert_fusion.7, f32[256]{0:T(256)} %multiply_exponential_fusion), kind=kLoop, calls=%fused_computation.291 | loop fusion | flops 197376 | bytes 265220 | tf_op jit(solution)/shard_map/sin | solution.py:52
  72.5 7.0 reshape.704
  79.5 4.4 slice.538
  87.3 7.0 reshape.707
  109.9 6.1 fusion.201
  120.3 3.5 fusion.200
  130.6 4.4 collective-permute-start.2
  139.5 3.4 fusion.137
  143.5 43.4 %psum.112 = f32[512]{0:T(512)S(1)} all-reduce(f32[512]{0:T(512)} %get-tuple-element.44), channel_id=1, replica_groups=mesh['rows'=2,'frames'=16] {'rows','frames'}, use_global_device_ids=true, to_apply=%region_17.18 | all-reduce | flops 512 | bytes 4096 | tf_op jit(solution)/shard_map/psum | solution.py:225
  188.4 40.0 %psum.113 = f32[512]{0:T(512)} all-reduce(f32[512]{0:T(512)S(1)} %multiply_reduce_fusion.17), channel_id=1, replica_groups=mesh['rows'=2,'frames'=16] {'rows','frames'}, use_global_device_ids=true, to_apply=%region_20.21 | all-reduce | flops 512 | bytes 4096 | tf_op jit(solution)/shard_map/psum | solution.py:228
  239.8 3.0 convert_reduce_fusion
  248.8 40.2 %all-reduce.5 = (f32[512]{0:T(512)}, f32[512]{0:T(512)}) all-reduce(f32[512]{0:T(512)S(1)} %get-tuple-element.41, f32[512]{0:T(512)S(1)} %get-tuple-element.40), channel_id=1, replica_groups=mesh['rows'=2,'frames'=16] {'rows','frames'}, use_global_device_ids=true, to_apply=%region_32.33 | all-reduce | flops 1024 | bytes 8192 | tf_op jit(solution)/shard_map/psum | solution.py:255
  289.0 5.2 fusion.122
  296.1 3.6 collective-permute-start.5
  299.7 3.6 fusion.114
  309.4 4.1 fusion.106
  323.9 10.0 multiply_convert_fusion.1
  333.9 3.9 bitcast_reduce_fusion.2
  337.8 3.2 fusion.208
  342.9 9.9 multiply_convert_fusion.2
  352.8 3.9 bitcast_reduce_fusion.3
  373.0 4.3 collective-permute-start.6
  381.2 6.1 reshape.738
  387.4 6.6 reshape.716
  394.0 3.4 bitcast_reduce_fusion.1
  401.6 6.0 reshape.736
  407.7 6.9 reshape.718
  449.7 3.1 fusion.173
  461.6 3.8 fusion.162
  465.6 4.1 fusion.134
  469.8 4.1 convolution_bitcast_fusion
  475.4 4.2 pad_maximum_fusion.1
  480.9 3.2 convolution_bitcast_fusion.2
  485.4 3.8 pad_maximum_fusion
  492.2 9.0 reduce-scatter.43.cloned.1.call-done
  502.5 56.6 %reduce-scatter.41.cloned.1.call-done = f32[32,5]{1,0:T(8,128)} async-done(((f32[512,5]{1,0:T(8,128)}), f32[32,5]{1,0:T(8,128)}) %reduce-scatter.41.cloned.1.call-update) | async-done | bytes 656
  560.5 58.6 %reduce-scatter.37.cloned.1.call-done = f32[128,2]{1,0:T(8,128)} async-done(((f32[2048,2]{1,0:T(8,128)}), f32[128,2]{1,0:T(8,128)}) %reduce-scatter.37.cloned.1.call-update) | async-done | bytes 1040
  620.5 56.7 %reduce-scatter.45.cloned.1.call-done = f32[32,10]{1,0:T(8,128)} async-done(((f32[512,10]{1,0:T(8,128)}), f32[32,10]{1,0:T(8,128)}) %reduce-scatter.45.cloned.1.call-update) | async-done | bytes 1296
  678.6 58.9 %reduce-scatter.35.cloned.1.call-done = f32[32,512]{1,0:T(8,128)} async-done(((f32[512,512]{1,0:T(8,128)}), f32[32,512]{1,0:T(8,128)}) %reduce-scatter.35.cloned.1.call-update) | async-done | bytes 65552 | tf_op jit(solution)/shard_map/reduce_scatter | solution.py:405
  739.0 58.6 %reduce-scatter.29.cloned.1.call-done = f32[32,512]{1,0:T(8,128)} async-done(((f32[512,512]{1,0:T(8,128)}), f32[32,512]{1,0:T(8,128)}) %reduce-scatter.29.cloned.1.call-update) | async-done | bytes 65552 | tf_op jit(solution)/shard_map/reduce_scatter | solution.py:402
  799.0 59.0 %reduce-scatter.31.cloned.1.call-done = f32[32,512]{1,0:T(8,128)} async-done(((f32[512,512]{1,0:T(8,128)}), f32[32,512]{1,0:T(8,128)}) %reduce-scatter.31.cloned.1.call-update) | async-done | bytes 65552 | tf_op jit(solution)/shard_map/reduce_scatter | solution.py:403
  859.6 62.8 %reduce-scatter.33.cloned.1.call-done = f32[32,1024]{1,0:T(8,128)} async-done(((f32[512,1024]{1,0:T(8,128)}), f32[32,1024]{1,0:T(8,128)}) %reduce-scatter.33.cloned.1.call-update) | async-done | bytes 131088 | tf_op jit(solution)/shard_map/reduce_scatter | solution.py:404
  924.0 67.8 %reduce-scatter.27.cloned.1.call-done = f32[32,1536]{1,0:T(8,128)} async-done(((f32[512,1536]{1,0:T(8,128)}), f32[32,1536]{1,0:T(8,128)}) %reduce-scatter.27.cloned.1.call-update) | async-done | bytes 196624 | tf_op jit(solution)/shard_map/reduce_scatter | solution.py:401
  993.4 106.5 %reduce-scatter.25.cloned.1.call-done = f32[2,128,512]{2,1,0:T(8,128)} async-done(((f32[2,2048,512]{2,1,0:T(8,128)}), f32[2,128,512]{2,1,0:T(8,128)}) %reduce-scatter.25.cloned.1.call-update) | async-done | bytes 524304 | tf_op jit(solution)/shard_map/reduce_scatter | solution.py:398
  1101.7 107.3 %reduce-scatter.23.cloned.1.call-done = f32[2,512,128]{2,1,0:T(8,128)} async-done(((f32[2,512,2048]{2,1,0:T(8,128)}), f32[2,512,128]{2,1,0:T(8,128)}) %reduce-scatter.23.cloned.1.call-update) | async-done | bytes 524304 | tf_op jit(solution)/shard_map/reduce_scatter | solution.py:392
  1213.4 21.5 %all-reduce.11.cloned.1.call-done = (bf16[2,128]{1,0:T(2,128)(2,1)}, bf16[32,512]{1,0:T(8,128)(2,1)}, bf16[32,512]{1,0:T(8,128)(2,1)}, bf16[32,512]{1,0:T(8,128)...) async-done(((bf16[2,128]{1,0:T(2,128)(2,1)}, bf16[32,512]{1,0:T(8,128)(2,1)}, bf16[32,512]{1,0:T(8,128)(2,1)}, ...) | async-done | bytes 100688 | tf_op jit(solution)/shard_map/psum | solution.py:413
  1245.4 25.9 %all-reduce.13.cloned.1.call-done = (bf16[2,512,128]{2,1,0:T(8,128)(2,1)}, bf16[2,128,512]{2,1,0:T(8,128)(2,1)}, bf16[32,1536]{1,0:T(8,128)(2,1)}, bf16[32,1024]{1,0:T(8,128)(2,1)}) async-done(((bf16[2,512,128]{2,1,0:T(8,128)(2,1)}, bf16[2,128,512]{2,1,0:T(8,128)(2,1)}, bf16[32,1536]{1,0:T(8,128)(2,1)}, bf16[32,1024]{1,0:T(8,128)(2,1)}), (bf16[2,512,128]{2,1,0:T(8,128)(2,1)}, ...) | async-done | bytes 688144 | tf_op jit(solution)/shard_map/psum | solution.py:412
  (577 shorter events, 233.3 us)
Async XLA Ops:
  7.2 15.6 %copy-start = (bf16[512,1536]{1,0:T(8,128)(2,1)S(1)}, bf16[512,1536]{1,0:T(8,128)(2,1)}, u32[]{:S(2)}) copy-start(bf16[512,1536]{1,0:T(8,128)(2,1)} %param.22) | copy-start | bytes 4718596
  7.2 483.6 %reduce-scatter.39.cloned.1.call-start = ((), (), s32[]{:S(2)}) async-start(), calls=%async_computation.20 | async-start | bytes 278528
  11.6 127.7 %copy-start.65 = (f32[1,512]{1,0:T(1,128)}, f32[1,512]{1,0:T(1,128)S(1)}, u32[]{:S(2)}) copy-start(f32[1,512]{1,0:T(1,128)S(1)} %get-tuple-element.132) | copy-start | bytes 6148
  22.5 104.3 %copy-start.9 = (f32[512,512]{1,0:T(8,128)}, f32[512,512]{1,0:T(8,128)S(1)}, u32[]{:S(2)}) copy-start(f32[512,512]{1,0:T(8,128)S(1)} %get-tuple-element.167) | copy-start | bytes 3145732
  26.4 73.1 %collective-permute-start = (bf16[2,128,1024]{2,1,0:T(8,128)(2,1)}, bf16[2,128,1024]{2,1,0:T(8,128)(2,1)}, u32[]{:S(2)}, u32[]{:S(2)}) collective-permute-start(bf16[2,128,1024]{2,1,0:T(8,128)(2,1)} %get-tuple-element.87), channel_id=1, source_target_pairs={{0,1},{1,2},{2,3},{3,4},{4,5},{5,6},{6,7},{7,8},{8,9},{9,10},{10,1... | collective-permute-start | bytes 1572872 | tf_op jit(solution)/shard_map/ppermute | solution.py:27
  29.5 69.9 %collective-permute-start.1 = (bf16[2,128,1024]{2,1,0:T(8,128)(2,1)}, bf16[2,128,1024]{2,1,0:T(8,128)(2,1)}, u32[]{:S(2)}, u32[]{:S(2)}) collective-permute-start(bf16[2,128,1024]{2,1,0:T(8,128)(2,1)} %get-tuple-element.88), channel_id=1, source_target_pairs={{1,0},{2,1},{3,2},{4,3},{5,4},{6,5},{7,6},{8,7},{9,8},{10,9},{11,1... | collective-permute-start | bytes 1572872 | tf_op jit(solution)/shard_map/ppermute | solution.py:28
  103.5 12.4 copy-start.23
  127.4 11.9 copy-start.20
  127.4 11.9 copy-start.67
  127.4 11.9 copy-start.69
  127.4 11.9 copy-start.70
  127.5 11.9 copy-start.71
  127.5 11.9 copy-start.72
  127.5 11.9 copy-start.74
  127.5 11.9 copy-start.75
  127.5 11.9 copy-start.76
  127.5 11.9 copy-start.86
  127.5 11.9 copy-start.87
  127.5 11.9 copy-start.88
  127.5 11.9 copy-start.89
  127.5 11.9 copy-start.90
  127.6 11.9 copy-start.91
  127.9 15.0 %copy-start.115 = (f32[512]{0:T(512)}, f32[512]{0:T(512)S(1)}, u32[]{:S(2)}) copy-start(f32[512]{0:T(512)S(1)} %add_rsqrt_fusion.3) | copy-start | bytes 6148
  130.6 6.3 collective-permute-start.2
  135.0 4.3 collective-permute-start.3
  187.6 44.7 %copy-start.73 = (f32[512]{0:T(512)}, f32[512]{0:T(512)S(1)}, u32[]{:S(2)}) copy-start(f32[512]{0:T(512)S(1)} %broadcast_divide_fusion) | copy-start | bytes 6148
  229.9 16.1 %copy-start.53 = (f32[512,512]{1,0:T(8,128)}, f32[512,512]{1,0:T(8,128)S(1)}, u32[]{:S(2)}) copy-start(f32[512,512]{1,0:T(8,128)S(1)} %fusion.132) | copy-start | bytes 3145732
  232.3 12.7 copy-start.15
  289.0 14.3 %copy-start.6 = (f32[512,1024]{1,0:T(8,128)S(1)}, f32[512,1024]{1,0:T(8,128)}, u32[]{:S(2)}) copy-start(f32[512,1024]{1,0:T(8,128)} %copy-done.5) | copy-start | bytes 6291460
  294.8 14.6 %collective-permute-start.4 = (bf16[2,4,512]{2,1,0:T(4,128)(2,1)}, bf16[2,4,512]{2,1,0:T(4,128)(2,1)}, u32[]{:S(2)}, u32[]{:S(2)}) collective-permute-start(bf16[2,4,512]{2,1,0:T(4,128)(2,1)} %get-tuple-element.92), channel_id=1, source_target_pairs={{1,0},{2,1},{3,2},{4,3},{5,4},{6,5},{7,6},{8,7},{9,8},{10,9},{11,1... | collective-permute-start | bytes 24584 | tf_op jit(solution)/shard_map/ppermute | solution.py:28
  296.1 13.3 %collective-permute-start.5 = (bf16[2,4,512]{2,1,0:T(4,128)(2,1)}, bf16[2,4,512]{2,1,0:T(4,128)(2,1)}, u32[]{:S(2)}, u32[]{:S(2)}) collective-permute-start(bf16[2,4,512]{2,1,0:T(4,128)(2,1)} %get-tuple-element.93), channel_id=1, source_target_pairs={{0,1},{1,2},{2,3},{3,4},{4,5},{5,6},{6,7},{7,8},{8,9},{9,10},{10,1... | collective-permute-start | bytes 24584 | tf_op jit(solution)/shard_map/ppermute | solution.py:27
  303.3 13.3 %copy-start.13 = (f32[512,512]{1,0:T(8,128)S(1)}, f32[512,512]{1,0:T(8,128)}, u32[]{:S(2)}) copy-start(f32[512,512]{1,0:T(8,128)} %copy-done.12) | copy-start | bytes 3145732
  309.3 191.9 %reduce-scatter.43.cloned.1.call-start = ((), (), s32[]{:S(2)}) async-start(), calls=%async_computation.22 | async-start | bytes 278528
  373.0 56.8 %collective-permute-start.6 = (bf16[2,128,1024]{2,1,0:T(8,128)(2,1)S(1)}, bf16[2,128,1024]{2,1,0:T(8,128)(2,1)}, u32[]{:S(2)}, u32[]{:S(2)}) collective-permute-start(bf16[2,128,1024]{2,1,0:T(8,128)(2,1)S(1)} %get-tuple-element.80), channel_id=1, source_target_pairs={{0,1},{1,2},{2,3},{3,4},{4,5},{5,6},{6,7},{7,8},{8,9},{9,10},{10,1... | collective-permute-start | bytes 1572872 | tf_op jit(solution)/shard_map/ppermute | solution.py:27
  377.3 52.5 %collective-permute-start.7 = (bf16[2,128,1024]{2,1,0:T(8,128)(2,1)}, bf16[2,128,1024]{2,1,0:T(8,128)(2,1)}, u32[]{:S(2)}, u32[]{:S(2)}) collective-permute-start(bf16[2,128,1024]{2,1,0:T(8,128)(2,1)} %get-tuple-element.81), channel_id=1, source_target_pairs={{1,0},{2,1},{3,2},{4,3},{5,4},{6,5},{7,6},{8,7},{9,8},{10,9},{11,1... | collective-permute-start | bytes 1572872 | tf_op jit(solution)/shard_map/ppermute | solution.py:28
  444.7 114.4 %reduce-scatter.41.cloned.1.call-start = ((), (), s32[]{:S(2)}) async-start(), calls=%async_computation.21 | async-start | bytes 278528
  446.0 173.0 %reduce-scatter.37.cloned.1.call-start = ((), (), s32[]{:S(2)}) async-start(), calls=%async_computation.19 | async-start | bytes 1114112
  447.5 229.7 %reduce-scatter.45.cloned.1.call-start = ((), (), s32[]{:S(2)}) async-start(), calls=%async_computation.23 | async-start | bytes 278528
  449.7 287.8 %reduce-scatter.35.cloned.1.call-start = ((), (), s32[]{:S(2)}) async-start(), calls=%async_computation.18 | async-start | bytes 1114112 | tf_op jit(solution)/shard_map/reduce_scatter | solution.py:405
  452.8 344.8 %reduce-scatter.29.cloned.1.call-start = ((), (), s32[]{:S(2)}) async-start(), calls=%async_computation.15 | async-start | bytes 1114112 | tf_op jit(solution)/shard_map/reduce_scatter | solution.py:402
  455.4 402.7 %reduce-scatter.31.cloned.1.call-start = ((), (), s32[]{:S(2)}) async-start(), calls=%async_computation.16 | async-start | bytes 1114112 | tf_op jit(solution)/shard_map/reduce_scatter | solution.py:403
  461.6 460.9 %reduce-scatter.33.cloned.1.call-start = ((), (), s32[]{:S(2)}) async-start(), calls=%async_computation.17 | async-start | bytes 2228224 | tf_op jit(solution)/shard_map/reduce_scatter | solution.py:404
  465.5 526.3 %reduce-scatter.27.cloned.1.call-start = ((), (), s32[]{:S(2)}) async-start(), calls=%async_computation.14 | async-start | bytes 3342336 | tf_op jit(solution)/shard_map/reduce_scatter | solution.py:401
  469.8 630.2 %reduce-scatter.25.cloned.1.call-start = ((), (), s32[]{:S(2)}) async-start(), calls=%async_computation.13 | async-start | bytes 8912896 | tf_op jit(solution)/shard_map/reduce_scatter | solution.py:398
  479.7 729.3 %reduce-scatter.23.cloned.1.call-start = ((), (), s32[]{:S(2)}) async-start(), calls=%async_computation.12 | async-start | bytes 8912896 | tf_op jit(solution)/shard_map/reduce_scatter | solution.py:392
  489.2 721.6 %copy-start.30 = (f32[512,512]{1,0:T(8,128)S(1)}, f32[512,512]{1,0:T(8,128)}, u32[]{:S(2)}) copy-start(f32[512,512]{1,0:T(8,128)} %copy-done.28) | copy-start | bytes 3145732
  489.2 745.7 %all-reduce.11.cloned.1.call-start = ((), (), s32[]{:S(2)}) async-start(), calls=%async_computation.24 | async-start | bytes 222208 | tf_op jit(solution)/shard_map/psum | solution.py:413
  859.6 411.8 %all-reduce.13.cloned.1.call-start = ((), (), s32[]{:S(2)}) async-start(), calls=%async_computation.25 | async-start | bytes 1376256 | tf_op jit(solution)/shard_map/psum | solution.py:412
  (146 other events, 591.9 us)
Sparse Core Ops, SparseCore 0:
  309.4 56.2 reduce-scatter.38
  444.8 56.2 reduce-scatter.42
  504.7 54.3 reduce-scatter.40
  562.6 56.4 reduce-scatter.36
  622.8 54.2 reduce-scatter.44
  681.1 56.3 reduce-scatter.34
  741.1 56.4 reduce-scatter.28
  801.6 56.3 reduce-scatter.30
  861.8 60.5 reduce-scatter.32
  926.6 65.1 reduce-scatter.26
  996.4 103.4 reduce-scatter.24
  1104.4 104.5 reduce-scatter.22
  1213.0 21.8 all-reduce.10
  1238.5 32.7 all-reduce.12
where the time goes:
time: 1290 us; the launch traced here: 1280 us
  waiting for transfers between devices  752 us (58%)
  local copies, waits for them, and re-layouts  136 us (11%)
  blocking collectives  124 us (10%)
  other arithmetic  118 us (9%)
  matrix products  117 us (9%)
  starting transfers between devices  21.6 us (2%)
  between operations  16.3 us (1%)
    unnamed x19, waiting for transfers between devices  181 us
    reduce_scatter x1, waiting for transfers between devices, per_device(): lax.psum_scatter(jnp.stack([first_grads[0], second_grads[0]]), 'frames',...  107 us
    reduce_scatter x1, waiting for transfers between devices, per_device(): lax.psum_scatter(jnp.stack([first_grads[2], second_grads[2]]), 'frames',...  107 us
    reduce_scatter x1, waiting for transfers between devices, per_device(): lax.psum_scatter(grad_attend_in, 'frames', scatter_dimension=0, tiled=True)  67.8 us
    reduce_scatter x1, waiting for transfers between devices, per_device(): lax.psum_scatter(grad_convolve_in, 'frames', scatter_dimension=0, tiled=T...  62.8 us
    reduce_scatter x1, waiting for transfers between devices, per_device(): lax.psum_scatter(grad_position_proj, 'frames', scatter_dimension=0, tiled...  59 us
    reduce_scatter x1, waiting for transfers between devices, per_device(): lax.psum_scatter(grad_convolve_out, 'frames', scatter_dimension=0, tiled=...  58.9 us
    reduce_scatter x1, waiting for transfers between devices, per_device(): lax.psum_scatter(grad_attend_out, 'frames', scatter_dimension=0, tiled=True)  58.6 us
  transfers between devices with their start and end apart: 22, of which 14 were waited for; matrix products, arithmetic and copies ran while one was open for 21% of the time, Pallas kernels for 0%

commit v1 on v0

--- a/solution.py
+++ b/solution.py
@@ -2,6 +2,8 @@
 
 import jax
 import jax.numpy as jnp
+import ml_dtypes
+import numpy as np
 from jax import lax
 from jax.sharding import PartitionSpec as P
 
@@ -43,13 +45,20 @@
 
 
 def position_table(width, model):
-    offsets = (jnp.arange(2 * width + 1, dtype=jnp.int32) - width).astype(jnp.float32)
-    rates = jnp.exp(
-        jnp.arange(model // 2, dtype=jnp.int32).astype(jnp.float32)
-        * (-2.0 * math.log(10000.0) / model)
-    )
-    angles = offsets[:, None] * rates[None, :]
-    return jnp.stack([jnp.sin(angles), jnp.cos(angles)], axis=2).reshape(2 * width + 1, model)
+    offsets = (np.arange(2 * width + 1) - width).astype(np.float32)
+    rates = np.exp(
+        np.arange(model // 2).astype(np.float32) * np.float32(-2.0 * math.log(10000.0) / model)
+    )
+    angles = (offsets[:, None] * rates[None, :]).astype(np.float32)
+    both = np.stack([np.sin(angles), np.cos(angles)], axis=2)
+    return both.reshape(2 * width + 1, model).astype(ml_dtypes.bfloat16)
+
+
+def gather_all(block):
+    axes = ("rows", "frames")
+    devices = lax.axis_size("rows") * lax.axis_size("frames")
+    copies = jnp.broadcast_to(block[None], (devices,) + block.shape)
+    return lax.all_to_all(copies, axes, 0, 0, tiled=True)
 
 
 def into_band(table):
@@ -168,7 +177,7 @@
     window = padded_2(pair, (("frames", 1),), WIN)
     key_rows = window[..., :model].reshape(rows_here, frames_here + 2 * WIN, H, DH)
     value_rows = window[..., model:].reshape(rows_here, frames_here + 2 * WIN, H, DH)
-    sinusoid = position_table(WIN, model).astype(jnp.bfloat16)
+    sinusoid = jnp.asarray(position_table(WIN, model))
     table = product(sinusoid, position_proj).astype(jnp.bfloat16).reshape(band, H, DH)
     key_pos = start - WIN + jnp.arange(frames_here + 2 * WIN, dtype=jnp.int32)
 
@@ -222,11 +231,19 @@
     for tap in range(KERNEL):
         depth = depth + depthwise[tap] * rim[:, tap : tap + frames_here] * keeps[tap]
     depth = depth.reshape(tokens, model)
-    first_sum = lax.psum(jnp.sum(depth * valid, axis=0), ("rows", "frames"))
-    mean = first_sum / count
+    frames_axis = lax.axis_size("frames")
+    devices = lax.axis_size("rows") * frames_axis
+    here_count = jnp.maximum(jnp.sum(valid), 1.0)
+    here_sum = jnp.sum(depth * valid, axis=0)
+    here_mean = here_sum / here_count
+    off = depth - here_mean
+    here_spread = jnp.sum(off * off * valid, axis=0)
+    counts = jnp.full((model,), jnp.sum(valid))
+    stats = gather_all(jnp.stack([here_sum, here_spread, counts]))
+    mean = jnp.sum(stats[:, 0], axis=0) / count
+    off_means = stats[:, 0] / jnp.maximum(stats[:, 2], 1.0) - mean
+    variance = jnp.sum(stats[:, 1] + stats[:, 2] * off_means * off_means, axis=0) / count
     centered = depth - mean
-    spread_sum = lax.psum(jnp.sum(centered * centered * valid, axis=0), ("rows", "frames"))
-    variance = spread_sum / count
     batch_inverse = lax.rsqrt(variance + eps_norm)
     batch_normal = centered * batch_inverse
     batch = batch_normal * norm_gain[5] + norm_shift[5]
@@ -252,10 +269,13 @@
     conv_out_bias = jnp.sum(grad_conv_low.astype(jnp.float32), axis=0)
     grad_swished = right_product(grad_conv_low, convolve_out)
     grad_batch = grad_swished * batch_sigma * (1.0 + batch * (1.0 - batch_sigma))
-    total_a, total_b = lax.psum(
-        (jnp.sum(grad_batch, axis=0), jnp.sum(grad_batch * batch_normal, axis=0)),
-        ("rows", "frames"),
-    )
+    totals = jnp.sum(
+        gather_all(
+            jnp.stack([jnp.sum(grad_batch, axis=0), jnp.sum(grad_batch * batch_normal, axis=0)])
+        ),
+        axis=0,
+    )
+    total_a, total_b = totals[0], totals[1]
     batch_gain = norm_gain[5]
     grad_depth = batch_inverse * (
         grad_batch * batch_gain - valid * batch_gain * (total_a + batch_normal * total_b) / count
@@ -388,42 +408,61 @@
     depth_rows = jnp.stack(depth_grads)
     gain_rows = jnp.stack([first_grads[4], gain_a, gain_c, second_grads[4], gain_out])
     shift_rows = jnp.stack([first_grads[5], shift_a, shift_c, second_grads[5], shift_out])
-    summed = (
-        lax.psum_scatter(
-            jnp.stack([first_grads[0], second_grads[0]]), "frames", scatter_dimension=2, tiled=True
-        ),
-        lax.psum_scatter(
-            jnp.stack([first_grads[1], second_grads[1]]), "frames", scatter_dimension=1, tiled=True
-        ),
-        lax.psum_scatter(
-            jnp.stack([first_grads[2], second_grads[2]]), "frames", scatter_dimension=1, tiled=True
-        ),
-        lax.psum_scatter(grad_attend_in, "frames", scatter_dimension=0, tiled=True),
-        lax.psum_scatter(grad_attend_out, "frames", scatter_dimension=0, tiled=True),
-        lax.psum_scatter(grad_position_proj, "frames", scatter_dimension=0, tiled=True),
-        lax.psum_scatter(grad_convolve_in, "frames", scatter_dimension=0, tiled=True),
-        lax.psum_scatter(grad_convolve_out, "frames", scatter_dimension=0, tiled=True),
-        lax.psum_scatter(depth_rows, "frames", scatter_dimension=1, tiled=True),
-        lax.psum_scatter(gain_rows, "frames", scatter_dimension=1, tiled=True),
-        lax.psum_scatter(shift_rows, "frames", scatter_dimension=1, tiled=True),
-        lax.psum_scatter(bias_rows, "frames", scatter_dimension=1, tiled=True),
-    )
-    summed = (
-        lax.psum(summed[0].astype(jnp.bfloat16), "rows").astype(jnp.float32),
-        lax.psum(summed[1].astype(jnp.bfloat16), "rows").astype(jnp.float32),
-        lax.psum(summed[2].astype(jnp.bfloat16), "rows").astype(jnp.float32),
-        lax.psum(summed[3].astype(jnp.bfloat16), "rows").astype(jnp.float32),
-        lax.psum(summed[4].astype(jnp.bfloat16), "rows").astype(jnp.float32),
-        lax.psum(summed[5].astype(jnp.bfloat16), "rows").astype(jnp.float32),
-        lax.psum(summed[6].astype(jnp.bfloat16), "rows").astype(jnp.float32),
-        lax.psum(summed[7].astype(jnp.bfloat16), "rows").astype(jnp.float32),
-        lax.psum(summed[8].astype(jnp.bfloat16), "rows").astype(jnp.float32),
-        lax.psum(summed[9].astype(jnp.bfloat16), "rows").astype(jnp.float32),
-        lax.psum(summed[10].astype(jnp.bfloat16), "rows").astype(jnp.float32),
-        lax.psum(summed[11].astype(jnp.bfloat16), "rows").astype(jnp.float32),
-    )
-    feed_parts = (summed[0], summed[1], summed[2])
-    rest = summed[3:]
+    width = feed_in.shape[2] // frames_axis
+    slim = model // frames_axis
+
+    def chunks(grad):
+        return grad.astype(jnp.bfloat16).reshape(frames_axis, -1, model)
+
+    bulk = jnp.concatenate(
+        [
+            chunks(first_grads[0].T),
+            chunks(second_grads[0].T),
+            chunks(first_grads[2]),
+            chunks(second_grads[2]),
+            chunks(grad_attend_in),
+            chunks(grad_attend_out),
+            chunks(grad_position_proj),
+            chunks(grad_convolve_in),
+            chunks(grad_convolve_out),
+        ],
+        axis=1,
+    )
+    bulk = lax.psum_scatter(bulk, "frames", scatter_dimension=0, tiled=True)[0]
+    both = [(0, 1), (1, 0)]
+    bulk = bulk.astype(jnp.float32) + lax.ppermute(bulk, "rows", both).astype(jnp.float32)
+    cuts = [width] * 4 + [3 * slim, slim, slim, 2 * slim, slim]
+    parts = []
+    at = 0
+    for cut in cuts:
+        parts.append(bulk[at : at + cut])
+        at += cut
+    vectors = jnp.concatenate([depth_rows, gain_rows, shift_rows, bias_rows], axis=0)
+    vectors = vectors.reshape(-1, frames_axis, slim).transpose(1, 0, 2).reshape(frames_axis, -1)
+    feed_vectors = jnp.stack([first_grads[1], second_grads[1]])
+    feed_vectors = feed_vectors.reshape(2, frames_axis, width).transpose(1, 0, 2)
+    small = jnp.concatenate([vectors, feed_vectors.reshape(frames_axis, -1)], axis=1)
+    small = jnp.concatenate([small] * lax.axis_size("rows"), axis=0)
+    small = jnp.sum(lax.all_to_all(small, ("rows", "frames"), 0, 0, tiled=True), axis=0)
+    n_vectors = KERNEL + 5 + 5 + 10
+    thin = small[: n_vectors * slim].reshape(n_vectors, slim)
+    feed_bias_part = small[n_vectors * slim :].reshape(2, width)
+    feed_parts = (
+        jnp.stack([parts[0].T, parts[1].T]),
+        feed_bias_part,
+        jnp.stack([parts[2], parts[3]]),
+    )
+    rest = (
+        parts[4].reshape(slim, 3 * model),
+        parts[5],
+        parts[6],
+        parts[7].reshape(slim, 2 * model),
+        parts[8],
+        thin[:KERNEL],
+        thin[KERNEL : KERNEL + 5],
+        thin[KERNEL + 5 : KERNEL + 10],
+        thin[KERNEL + 10 :],
+    )
     slice_width = model // lax.axis_size("frames")
     slice_start = lax.axis_index("frames") * slice_width
     total_b_part = lax.dynamic_slice_in_dim(total_b, slice_start, slice_width, 0)

time: 1290 us -> 543 us (0.42)
  waiting for transfers between devices: 752 us -> 143 us
  blocking collectives: 124 us -> 0 us
  other arithmetic: 118 us -> 69.7 us
  starting transfers between devices: 21.6 us -> 38 us
  local copies, waits for them, and re-layouts: 136 us -> 149 us
    reduce_scatter x7 -> x1, waiting for transfers between devices: 521 us -> 119 us  [per_device(): bulk = lax.psum_scatter(bulk, 'frames', scatter_dimension=0, tiled=True)[0]]
    unnamed x19 -> x1, waiting for transfers between devices: 181 us -> 0.02 us
    psum x3 -> x0, blocking collectives: 124 us -> none  [the longest x1 43.4 us: per_device(): first_sum = lax.psum(jnp.sum(depth * valid, axis=0), ('rows', 'frames'))]
    psum x2 -> x0, waiting for transfers between devices: 47.4 us -> none  [the longest x1 25.9 us: per_device(): lax.psum(summed[0].astype(jnp.bfloat16), 'rows').astype(jnp.float32)]
    convert_element_type x21 -> x0, other arithmetic: 29.3 us -> none  [the longest x1 1.8 us: per_device(): lax.psum(summed[2].astype(jnp.bfloat16), 'rows').astype(jnp.float32)]
    all_to_all x0 -> x3, starting transfers between devices: none -> 16 us  [the longest x2 12.2 us: gather_all(): return lax.all_to_all(copies, axes, 0, 0, tiled=True)]
    unnamed x362 -> x384, local copies, waits for them, and re-layouts: 44.4 us -> 40.9 us
  transfers between devices with their start and end apart: 22 -> 13, of which waited for: 14 -> 5; matrix products, arithmetic and copies ran while one was open for 21% -> 22% of each run, Pallas kernels for 0% -> 0%
where the time goes in v1:
time: 543 us; the launch traced here: 536 us
  local copies, waits for them, and re-layouts  149 us (27%)
  waiting for transfers between devices  143 us (26%)
  matrix products  119 us (22%)
  other arithmetic  69.7 us (13%)
  starting transfers between devices  38 us (7%)
  between operations  17.5 us (3%)
    reduce_scatter x1, waiting for transfers between devices, per_device(): bulk = lax.psum_scatter(bulk, 'frames', scatter_dimension=0, tiled=True)[0]  119 us
    unnamed x384, local copies, waits for them, and re-layouts  40.9 us
    sub x2, matrix products, per_device(): grad_probability - delta  19.8 us
    dot_general x8, matrix products, left_product(): lax.dot_general(left, right, rows_first, preferred_element_type=jnp.float32)  19.2 us
    dot_general x9, matrix products, product(): return jnp.dot(left, right, preferred_element_type=jnp.float32)  16.8 us
    dot_general x8, matrix products, right_product(): lax.dot_general(left, right, columns_last, preferred_element_type=jnp.flo...  15.9 us
    ppermute x4, starting transfers between devices, padded_2(): before = lax.ppermute(last, axis, up)  14.8 us
    reshape x2, local copies, waits for them, and re-layouts, into_band(): flat = padded.reshape(heads, queries * (width + 1))[:, :queries * width]  14 us
  transfers between devices with their start and end apart: 13, of which 5 were waited for; matrix products, arithmetic and copies ran while one was open for 22% of the time, Pallas kernels for 0%

profile of v1, /device:TPU:0, one launch (start us, length us, event | category | flops | bytes accessed | tf_op | source)
XLA Modules:
  0.0 536.0 jit_solution(2121890759603021986)
XLA Ops:
  17.2 5.4 %multiply_convert_fusion.5 = (bf16[512,2048]{1,0:T(8,128)(2,1)S(1)}, f32[512,2048]{1,0:T(8,128)}) fusion(f32[2048]{0:T(1024)S(1)} %bitcast.468, bf16[512,512]{1,0:T(8,128)(2,1)S(1)} %bitcast.407, bf16[2,512,2048]{2,1,0:T(8,128)(2,1)} %param.20), kind=kOutput, calls=%fused_computation.27 | convolution fusion | flops 1080033280 | bytes 8921088 | tf_op jit(solution)/shard_map/dot_general | solution.py:36
  28.7 3.2 collective-permute-start
  54.7 2.8 pad.24.clone
  57.5 7.0 %reshape.770 = f32[8,131328]{1,0:T(8,128)} reshape(f32[8,256,513]{2,1,0:T(8,128)} %pad.24.clone) | data formatting | bytes 8404992 | tf_op jit(solution)/shard_map/reshape | solution.py:68
  64.5 4.5 slice.685
  69.6 2.8 pad.25.clone
  72.3 7.0 %reshape.773 = f32[8,131328]{1,0:T(8,128)} reshape(f32[8,256,513]{2,1,0:T(8,128)} %pad.25.clone) | data formatting | bytes 8404992 | tf_op jit(solution)/shard_map/reshape | solution.py:68
  85.7 3.0 fusion.155
  99.3 6.0 %fusion.205 = (f32[8,256]{1,0:T(8,128)S(1)}, f32[8,256,512]{2,1,0:T(8,128)S(1)}) fusion(f32[1,8,256,512]{3,1,2,0:T(8,128)} %bitcast.343, bf16[256,8,64]{0,2,1:T(8,128)(2,1)} %bitcast.377, bf16[512,8,64]{0,2,1:T(8,128)(2,1)S(1)} %bitcast.361, pred[256,512]{1,0:T(8,128)(4,1)} %get-tuple-element.207), kind=kOutput, calls=%fused_computation.418 | convolution fusion | flops 138409984 | bytes 9314304 | tf_op jit(solution)/shard_map/qhd,khd->hqk/dot_general | solution.py:186
  109.4 3.5 fusion.204
  119.8 4.4 collective-permute-start.2
  133.0 9.0 %all-to-all-start = ((f32[32,3,512]{2,1,0:T(4,128)}), f32[32,3,512]{2,1,0:T(4,128)}, u32[]{:S(2)}, u32[]{:S(2)}) async-start(f32[32,3,512]{2,1,0:T(4,128)} %broadcast_in_dim.33), calls=%async_computation | async-start | bytes 524288 | tf_op jit(solution)/shard_map/all_to_all | solution.py:61
  144.5 7.7 %all-to-all-done = f32[32,3,512]{2,1,0:T(4,128)} async-done(((f32[32,3,512]{2,1,0:T(4,128)}), f32[32,3,512]{2,1,0:T(4,128)}, u32[]{:S(2)}, u32[]{:S(2)}) %all-to-all-start) | async-done | bytes 196640 | tf_op jit(solution)/shard_map/all_to_all | solution.py:61
  165.1 3.0 convert_reduce_fusion
  170.1 2.8 convolution_convert_fusion.3
  177.5 3.3 all-to-all-start.1
  180.8 4.5 convolution_convert_fusion.1
  185.3 3.6 all-to-all-done.1
  191.5 3.8 fusion.122
  196.9 3.0 collective-permute-start.5
  199.9 2.8 convolution_convert_fusion.6
  203.0 2.8 fusion.106
  214.7 10.0 %multiply_convert_fusion.1 = bf16[8,256,512]{2,1,0:T(8,128)(2,1)} fusion(f32[8,256,512]{2,1,0:T(8,128)} %copy-done.3, f32[8,256]{1,0:T(8,128)S(1)} %copy-done.77, bf16[256,8,64]{0,2,1:T(8,128)(2,1)} %bitcast.400, bf16[512,8,64]{0,2,1:T(8,128)(2,1)} %bitcast.404), kind=kOutput, calls=%fused_computation.12 | convolution fusion | flops 275778048 | bytes 7086080 | tf_op jit(solution)/shard_map/sub | solution.py:331
  224.6 4.0 bitcast_reduce_fusion.2
  228.7 3.2 fusion.212
  233.7 9.9 %multiply_convert_fusion.2 = bf16[8,256,512]{2,1,0:T(8,128)(2,1)} fusion(f32[8,256,512]{2,1,0:T(8,128)} %copy-done.1, f32[8,256]{1,0:T(8,128)S(1)} %copy-done.76, bf16[256,8,64]{0,2,1:T(8,128)(2,1)} %bitcast.397, bf16[512,8,64]{0,2,1:T(8,128)(2,1)} %bitcast.402), kind=kOutput, calls=%fused_computation.16 | convolution fusion | flops 275778048 | bytes 7086080 | tf_op jit(solution)/shard_map/sub | solution.py:331
  243.6 4.2 bitcast_reduce_fusion.3
  250.2 2.5 copy.138
  252.7 2.5 copy.136
  255.2 2.5 copy.137
  260.3 3.9 fusion.181
  269.3 6.1 %reshape.807 = bf16[1050624]{0:T(1024)(128)(2,1)} reshape(bf16[8,131328]{1,0:T(8,128)(2,1)} %pad.27) | data formatting | bytes 4202496
  275.4 6.7 %reshape.784 = bf16[8,256,513]{2,1,0:T(8,128)(2,1)} reshape(bf16[1050624]{0:T(1024)(128)(2,1)} %reshape.807) | data formatting | bytes 4202496 | tf_op jit(solution)/shard_map/reshape | solution.py:75
  282.1 3.4 bitcast_reduce_fusion
  285.5 2.7 fusion.53
  292.7 4.2 collective-permute-start.6
  298.2 2.8 copy.159
  302.6 6.1 %reshape.809 = bf16[1050624]{0:T(1024)(128)(2,1)} reshape(bf16[8,131328]{1,0:T(8,128)(2,1)} %pad.26) | data formatting | bytes 4202496
  308.7 6.7 %reshape.782 = bf16[8,256,513]{2,1,0:T(8,128)(2,1)} reshape(bf16[1050624]{0:T(1024)(128)(2,1)} %reshape.809) | data formatting | bytes 4202496 | tf_op jit(solution)/shard_map/reshape | solution.py:75
  315.4 2.8 bitcast_reduce_fusion.1
  318.2 2.9 fusion.80
  324.6 2.5 reshape.804
  329.5 3.0 convolution_convert_fusion.7
  342.0 3.9 reshape.790
  381.9 3.8 all-to-all-start.2
  385.7 118.7 %reduce-scatter.2.cloned.1.call-done = bf16[1,768,512]{2,1,0:T(8,128)(2,1)} async-done(((bf16[16,768,512]{2,1,0:T(8,128)(2,1)}), bf16[1,768,512]{2,1,0:T(8,128)(2,1)}) %reduce-scatter.2.cloned.1.call-update) | async-done | bytes 786448 | tf_op jit(solution)/shard_map/reduce_scatter | solution.py:431
  505.9 2.9 multiply_add_fusion
  512.4 10.8 %collective-permute-done.8 = bf16[768,512]{1,0:T(8,128)(2,1)} collective-permute-done((bf16[768,512]{1,0:T(8,128)(2,1)}, bf16[768,512]{1,0:T(8,128)(2,1)}, u32[]{:S(2)}, u32[]{:S(2)}) %collective-permute-start.8) | collective-permute-done | bytes 786464 | tf_op jit(solution)/shard_map/ppermute | solution.py:433
  (598 shorter events, 189.8 us)
Async XLA Ops:
  7.2 17.9 %copy-start = (bf16[512,1536]{1,0:T(8,128)(2,1)S(1)}, bf16[512,1536]{1,0:T(8,128)(2,1)}, u32[]{:S(2)}) copy-start(bf16[512,1536]{1,0:T(8,128)(2,1)} %param.23) | copy-start | bytes 4718596
  11.4 13.0 %copy-start.122 = (f32[1,512]{1,0:T(1,128)}, f32[1,512]{1,0:T(1,128)S(1)}, u32[]{:S(2)}) copy-start(f32[1,512]{1,0:T(1,128)S(1)} %get-tuple-element.198) | copy-start | bytes 6148
  11.4 105.6 %copy-start.124 = (f32[1,512]{1,0:T(1,128)}, f32[1,512]{1,0:T(1,128)S(1)}, u32[]{:S(2)}) copy-start(f32[1,512]{1,0:T(1,128)S(1)} %get-tuple-element.197) | copy-start | bytes 6148
  24.1 91.8 %copy-start.10 = (f32[512,512]{1,0:T(8,128)}, f32[512,512]{1,0:T(8,128)S(1)}, u32[]{:S(2)}) copy-start(f32[512,512]{1,0:T(8,128)S(1)} %get-tuple-element.239) | copy-start | bytes 3145732
  26.2 14.4 %copy-start.47 = (bf16[257,512]{1,0:T(8,128)(2,1)S(1)}, bf16[257,512]{1,0:T(8,128)(2,1)}, u32[]{:S(2)}) copy-start(bf16[257,512]{1,0:T(8,128)(2,1)} %constant.84.clone) | copy-start | bytes 789508
  28.7 60.0 %collective-permute-start = (bf16[2,128,1024]{2,1,0:T(8,128)(2,1)}, bf16[2,128,1024]{2,1,0:T(8,128)(2,1)}, u32[]{:S(2)}, u32[]{:S(2)}) collective-permute-start(bf16[2,128,1024]{2,1,0:T(8,128)(2,1)} %get-tuple-element.151), channel_id=1, source_target_pairs={{0,1},{1,2},{2,3},{3,4},{4,5},{5,6},{6,7},{7,8},{8,9},{9,10},{10,1... | collective-permute-start | bytes 1572872 | tf_op jit(solution)/shard_map/ppermute | solution.py:29
  31.9 56.9 %collective-permute-start.1 = (bf16[2,128,1024]{2,1,0:T(8,128)(2,1)}, bf16[2,128,1024]{2,1,0:T(8,128)(2,1)}, u32[]{:S(2)}, u32[]{:S(2)}) collective-permute-start(bf16[2,128,1024]{2,1,0:T(8,128)(2,1)} %get-tuple-element.152), channel_id=1, source_target_pairs={{1,0},{2,1},{3,2},{4,3},{5,4},{6,5},{7,6},{8,7},{9,8},{10,9},{11,1... | collective-permute-start | bytes 1572872 | tf_op jit(solution)/shard_map/ppermute | solution.py:30
  92.9 12.4 %copy-start.26 = (bf16[1,512,512]{1,2,0:T(8,128)(2,1)}, bf16[1,512,512]{1,2,0:T(8,128)(2,1)S(1)}, u32[]{:S(2)}) copy-start(bf16[1,512,512]{1,2,0:T(8,128)(2,1)S(1)} %copy.119) | copy-start | bytes 1572868
  116.5 11.9 %copy-start.62 = (f32[2,256]{1,0:T(2,128)S(1)}, f32[2,256]{1,0:T(2,128)}, u32[]{:S(2)}) copy-start(f32[2,256]{1,0:T(2,128)} %get-tuple-element.215) | copy-start | bytes 6148
  116.5 11.9 %copy-start.67 = (f32[2,256]{1,0:T(2,128)S(1)}, f32[2,256]{1,0:T(2,128)}, u32[]{:S(2)}) copy-start(f32[2,256]{1,0:T(2,128)} %get-tuple-element.209) | copy-start | bytes 6148
  116.5 11.9 %copy-start.70 = (f32[2,256]{1,0:T(2,128)S(1)}, f32[2,256]{1,0:T(2,128)}, u32[]{:S(2)}) copy-start(f32[2,256]{1,0:T(2,128)} %get-tuple-element.213) | copy-start | bytes 6148
  116.5 11.9 %copy-start.73 = (f32[2,256]{1,0:T(2,128)S(1)}, f32[2,256]{1,0:T(2,128)}, u32[]{:S(2)}) copy-start(f32[2,256]{1,0:T(2,128)} %get-tuple-element.214) | copy-start | bytes 6148
  116.5 11.9 %copy-start.79 = (f32[2,256]{1,0:T(2,128)S(1)}, f32[2,256]{1,0:T(2,128)}, u32[]{:S(2)}) copy-start(f32[2,256]{1,0:T(2,128)} %get-tuple-element.216) | copy-start | bytes 6148
  116.6 11.9 %copy-start.82 = (f32[2,256]{1,0:T(2,128)S(1)}, f32[2,256]{1,0:T(2,128)}, u32[]{:S(2)}) copy-start(f32[2,256]{1,0:T(2,128)} %get-tuple-element.210) | copy-start | bytes 6148
  116.6 11.9 %copy-start.84 = (f32[2,256]{1,0:T(2,128)S(1)}, f32[2,256]{1,0:T(2,128)}, u32[]{:S(2)}) copy-start(f32[2,256]{1,0:T(2,128)} %get-tuple-element.211) | copy-start | bytes 6148
  116.6 11.9 %copy-start.86 = (f32[2,256]{1,0:T(2,128)S(1)}, f32[2,256]{1,0:T(2,128)}, u32[]{:S(2)}) copy-start(f32[2,256]{1,0:T(2,128)} %get-tuple-element.212) | copy-start | bytes 6148
  116.6 11.9 %copy-start.95 = (f32[1,512]{1,0:T(1,128)S(1)}, f32[1,512]{1,0:T(1,128)}, u32[]{:S(2)}) copy-start(f32[1,512]{1,0:T(1,128)} %get-tuple-element.178) | copy-start | bytes 6148
  116.6 11.9 %copy-start.97 = (f32[1,512]{1,0:T(1,128)S(1)}, f32[1,512]{1,0:T(1,128)}, u32[]{:S(2)}) copy-start(f32[1,512]{1,0:T(1,128)} %get-tuple-element.179) | copy-start | bytes 6148
  116.6 11.9 %copy-start.99 = (f32[1,512]{1,0:T(1,128)S(1)}, f32[1,512]{1,0:T(1,128)}, u32[]{:S(2)}) copy-start(f32[1,512]{1,0:T(1,128)} %get-tuple-element.180) | copy-start | bytes 6148
  116.6 11.9 %copy-start.101 = (f32[1,512]{1,0:T(1,128)S(1)}, f32[1,512]{1,0:T(1,128)}, u32[]{:S(2)}) copy-start(f32[1,512]{1,0:T(1,128)} %get-tuple-element.181) | copy-start | bytes 6148
  116.6 11.9 %copy-start.103 = (f32[1,512]{1,0:T(1,128)S(1)}, f32[1,512]{1,0:T(1,128)}, u32[]{:S(2)}) copy-start(f32[1,512]{1,0:T(1,128)} %get-tuple-element.182) | copy-start | bytes 6148
  116.6 11.9 %copy-start.105 = (f32[1,512]{1,0:T(1,128)S(1)}, f32[1,512]{1,0:T(1,128)}, u32[]{:S(2)}) copy-start(f32[1,512]{1,0:T(1,128)} %get-tuple-element.183) | copy-start | bytes 6148
  116.6 11.9 %copy-start.107 = (f32[1,512]{1,0:T(1,128)S(1)}, f32[1,512]{1,0:T(1,128)}, u32[]{:S(2)}) copy-start(f32[1,512]{1,0:T(1,128)} %get-tuple-element.184) | copy-start | bytes 6148
  116.7 11.9 %copy-start.109 = (f32[1,512]{1,0:T(1,128)S(1)}, f32[1,512]{1,0:T(1,128)}, u32[]{:S(2)}) copy-start(f32[1,512]{1,0:T(1,128)} %get-tuple-element.185) | copy-start | bytes 6148
  116.7 11.9 %copy-start.111 = (f32[1,512]{1,0:T(1,128)S(1)}, f32[1,512]{1,0:T(1,128)}, u32[]{:S(2)}) copy-start(f32[1,512]{1,0:T(1,128)} %get-tuple-element.186) | copy-start | bytes 6148
  116.7 11.9 %copy-start.113 = (f32[2,256]{1,0:T(2,128)S(1)}, f32[2,256]{1,0:T(2,128)}, u32[]{:S(2)}) copy-start(f32[2,256]{1,0:T(2,128)} %get-tuple-element.271) | copy-start | bytes 6148
  116.7 11.9 %copy-start.119 = (f32[256]{0:T(256)S(1)}, f32[256]{0:T(256)}, u32[]{:S(2)}) copy-start(f32[256]{0:T(256)} %get-tuple-element.230) | copy-start | bytes 3076
  117.3 13.8 %copy-start.23 = (bf16[2,256,512]{2,1,0:T(8,128)(2,1)S(1)}, bf16[2,256,512]{2,1,0:T(8,128)(2,1)}, u32[]{:S(2)}) copy-start(bf16[2,256,512]{2,1,0:T(8,128)(2,1)} %param.32) | copy-start | bytes 1572868
  117.3 13.8 %copy-start.65 = (f32[1,512]{1,0:T(1,128)S(1)}, f32[1,512]{1,0:T(1,128)}, u32[]{:S(2)}) copy-start(f32[1,512]{1,0:T(1,128)} %get-tuple-element.200) | copy-start | bytes 6148
  119.5 12.7 %copy-start.169 = (f32[3]{0:T(128)S(1)}, f32[3]{0:T(128)}, u32[]{:S(2)}) copy-start(f32[3]{0:T(128)} %pad.68.clone) | copy-start | bytes 40
  119.8 6.3 %collective-permute-start.2 = (bf16[2,4,512]{2,1,0:T(4,128)(2,1)S(1)}, bf16[2,4,512]{2,1,0:T(4,128)(2,1)S(1)}, u32[]{:S(2)}, u32[]{:S(2)}) collective-permute-start(bf16[2,4,512]{2,1,0:T(4,128)(2,1)S(1)} %get-tuple-element.158), channel_id=1, source_target_pairs={{0,1},{1,2},{2,3},{3,4},{4,5},{5,6},{6,7},{7,8},{8,9},{9,10},{10,1... | collective-permute-start | bytes 24584 | tf_op jit(solution)/shard_map/ppermute | solution.py:29
  124.2 4.3 collective-permute-start.3
  133.0 19.2 %all-to-all-start = ((f32[32,3,512]{2,1,0:T(4,128)}), f32[32,3,512]{2,1,0:T(4,128)}, u32[]{:S(2)}, u32[]{:S(2)}) async-start(f32[32,3,512]{2,1,0:T(4,128)} %broadcast_in_dim.33), calls=%async_computation | async-start | bytes 524288 | tf_op jit(solution)/shard_map/all_to_all | solution.py:61
  155.1 18.8 %copy-start.49 = (f32[512,512]{1,0:T(8,128)}, f32[512,512]{1,0:T(8,128)S(1)}, u32[]{:S(2)}) copy-start(f32[512,512]{1,0:T(8,128)S(1)} %fusion.132) | copy-start | bytes 3145732
  177.5 11.5 %all-to-all-start.1 = ((f32[32,2,512]{2,1,0:T(2,128)}), f32[32,2,512]{2,1,0:T(2,128)}, u32[]{:S(2)}, u32[]{:S(2)}) async-start(f32[32,2,512]{2,1,0:T(2,128)} %broadcast_in_dim.34), calls=%async_computation.1 | async-start | bytes 262144 | tf_op jit(solution)/shard_map/all_to_all | solution.py:61
  180.8 323.7 %reduce-scatter.2.cloned.1.call-start = ((), (), s32[]{:S(2)}) async-start(), calls=%async_computation.4 | async-start | bytes 13369344 | tf_op jit(solution)/shard_map/reduce_scatter | solution.py:431
  191.3 11.5 %copy-start.63 = (f32[2,256]{1,0:T(2,128)S(1)}, f32[2,256]{1,0:T(2,128)}, u32[]{:S(2)}) copy-start(f32[2,256]{1,0:T(2,128)} %get-tuple-element.215) | copy-start | bytes 6148
  191.3 11.5 %copy-start.68 = (f32[2,256]{1,0:T(2,128)S(1)}, f32[2,256]{1,0:T(2,128)}, u32[]{:S(2)}) copy-start(f32[2,256]{1,0:T(2,128)} %get-tuple-element.209) | copy-start | bytes 6148
  191.3 11.5 %copy-start.71 = (f32[2,256]{1,0:T(2,128)S(1)}, f32[2,256]{1,0:T(2,128)}, u32[]{:S(2)}) copy-start(f32[2,256]{1,0:T(2,128)} %get-tuple-element.213) | copy-start | bytes 6148
  191.3 11.5 %copy-start.74 = (f32[2,256]{1,0:T(2,128)S(1)}, f32[2,256]{1,0:T(2,128)}, u32[]{:S(2)}) copy-start(f32[2,256]{1,0:T(2,128)} %get-tuple-element.214) | copy-start | bytes 6148
  191.3 11.5 %copy-start.80 = (f32[2,256]{1,0:T(2,128)S(1)}, f32[2,256]{1,0:T(2,128)}, u32[]{:S(2)}) copy-start(f32[2,256]{1,0:T(2,128)} %get-tuple-element.216) | copy-start | bytes 6148
  195.3 7.5 %collective-permute-start.4 = (bf16[2,4,512]{2,1,0:T(4,128)(2,1)S(1)}, bf16[2,4,512]{2,1,0:T(4,128)(2,1)S(1)}, u32[]{:S(2)}, u32[]{:S(2)}) collective-permute-start(bf16[2,4,512]{2,1,0:T(4,128)(2,1)S(1)} %get-tuple-element.156), channel_id=1, source_target_pairs={{1,0},{2,1},{3,2},{4,3},{5,4},{6,5},{7,6},{8,7},{9,8},{10,9},{11,1... | collective-permute-start | bytes 24584 | tf_op jit(solution)/shard_map/ppermute | solution.py:30
  196.9 5.9 %collective-permute-start.5 = (bf16[2,4,512]{2,1,0:T(4,128)(2,1)S(1)}, bf16[2,4,512]{2,1,0:T(4,128)(2,1)S(1)}, u32[]{:S(2)}, u32[]{:S(2)}) collective-permute-start(bf16[2,4,512]{2,1,0:T(4,128)(2,1)S(1)} %get-tuple-element.157), channel_id=1, source_target_pairs={{0,1},{1,2},{2,3},{3,4},{4,5},{5,6},{6,7},{7,8},{8,9},{9,10},{10,1... | collective-permute-start | bytes 24584 | tf_op jit(solution)/shard_map/ppermute | solution.py:29
  292.7 39.8 %collective-permute-start.6 = (bf16[2,128,1024]{2,1,0:T(8,128)(2,1)}, bf16[2,128,1024]{2,1,0:T(8,128)(2,1)}, u32[]{:S(2)}, u32[]{:S(2)}) collective-permute-start(bf16[2,128,1024]{2,1,0:T(8,128)(2,1)} %get-tuple-element.137), channel_id=1, source_target_pairs={{0,1},{1,2},{2,3},{3,4},{4,5},{5,6},{6,7},{7,8},{8,9},{9,10},{10,1... | collective-permute-start | bytes 1572872 | tf_op jit(solution)/shard_map/ppermute | solution.py:29
  296.9 35.6 %collective-permute-start.7 = (bf16[2,128,1024]{2,1,0:T(8,128)(2,1)}, bf16[2,128,1024]{2,1,0:T(8,128)(2,1)}, u32[]{:S(2)}, u32[]{:S(2)}) collective-permute-start(bf16[2,128,1024]{2,1,0:T(8,128)(2,1)} %get-tuple-element.138), channel_id=1, source_target_pairs={{1,0},{2,1},{3,2},{4,3},{5,4},{6,5},{7,6},{8,7},{9,8},{10,9},{11,1... | collective-permute-start | bytes 1572872 | tf_op jit(solution)/shard_map/ppermute | solution.py:30
  381.9 126.9 %all-to-all-start.2 = ((f32[32,1,1184]{2,1,0:T(1,128)}), f32[32,1,1184]{2,1,0:T(1,128)S(1)}, u32[]{:S(2)}, u32[]{:S(2)}) async-start(f32[32,1,1184]{2,1,0:T(1,128)} %copy.140), calls=%async_computation.3 | async-start | bytes 327680 | tf_op jit(solution)/shard_map/all_to_all | solution.py:446
  504.4 18.8 %copy-start.54 = (bf16[1,768,512]{2,1,0:T(8,128)(2,1)S(1)}, bf16[1,768,512]{2,1,0:T(8,128)(2,1)}, u32[]{:S(2)}) copy-start(bf16[1,768,512]{2,1,0:T(8,128)(2,1)} %reduce-scatter.2.cloned.1.call-done) | copy-start | bytes 2359300
  504.5 18.8 %collective-permute-start.8 = (bf16[768,512]{1,0:T(8,128)(2,1)}, bf16[768,512]{1,0:T(8,128)(2,1)}, u32[]{:S(2)}, u32[]{:S(2)}) collective-permute-start(bf16[768,512]{1,0:T(8,128)(2,1)} %bitcast.401), channel_id=1, source_target_pairs={{0,16},{16,0},{1,17},{17,1},{2,18},{18,2},{3,19},{19,3},{4,20},{20... | collective-permute-start | bytes 2359304 | tf_op jit(solution)/shard_map/ppermute | solution.py:433
  (148 other events, 653.6 us)
Sparse Core Ops, SparseCore 0:
  370.4 134.0 reduce-scatter.1

commit v2 on v0

v2 whole, which is shorter than its diff:
```python
import functools
import math

import jax
import jax.numpy as jnp
import ml_dtypes
import numpy as np
from jax import lax
from jax.experimental import pallas as pl
from jax.experimental.pallas import tpu as pltpu
from jax.sharding import PartitionSpec as P

H = 8
DH = 64
KERNEL = 9
WIN = 128

HALF = KERNEL // 2
SPAN = 3 * WIN
MANY = 4
GROUPS = H // MANY
WIDE = MANY * DH
RIM = 16
RIM_GRAD = 8
eps_norm = 1e-05
negative = -1e30
f32 = jnp.float32
bf16 = jnp.bfloat16
DEVICES = ("rows", "frames")
VMEM_LIMIT = 60 * 1024 * 1024
FOLD_LIMIT = 14 * 1024 * 1024


def dot(left, right):
    return jnp.dot(left, right, preferred_element_type=f32)


def dot_last(left, right):
    return lax.dot_general(left, right, (((1,), (1,)), ((), ())), preferred_element_type=f32)


def dot_first(left, right):
    return lax.dot_general(left, right, (((0,), (0,)), ((), ())), preferred_element_type=f32)


def sigmoid(x):
    return 0.5 * jnp.tanh(0.5 * x) + 0.5


def total(x):
    return jnp.sum(x, axis=0, keepdims=True)


def normalize(values):
    centered = values - jnp.mean(values, axis=-1, keepdims=True)
    inverse = lax.rsqrt(jnp.mean(centered * centered, axis=-1, keepdims=True) + eps_norm)
    return centered * inverse, inverse


def norm_back(grad_out, normal, inverse, gain):
    scaled = grad_out * gain
    centred = scaled - jnp.mean(scaled, axis=-1, keepdims=True)
    grad_in = inverse * (centred - normal * jnp.mean(scaled * normal, axis=-1, keepdims=True))
    return grad_in, total(grad_out * normal), total(grad_out)


def position_table(width, model):
    offsets = (np.arange(2 * width + 1) - width).astype(np.float32)
    rates = np.exp(
        np.arange(model // 2).astype(np.float32) * np.float32(-2.0 * math.log(10000.0) / model)
    )
    angles = (offsets[:, None] * rates[None, :]).astype(np.float32)
    both = np.stack([np.sin(angles), np.cos(angles)], axis=2).reshape(2 * width + 1, model)
    padded = np.zeros((3 * width, model), np.float32)
    padded[: 2 * width + 1] = both
    return padded.astype(ml_dtypes.bfloat16)


def bounds(ends, at, row_len):
    low = jnp.max(jnp.where(ends <= at, ends, 0.0), axis=1, keepdims=True)
    high = jnp.min(jnp.where(ends > at, ends, row_len), axis=1, keepdims=True)
    return low, high


def column(count, offset):
    return lax.broadcasted_iota(jnp.int32, (count, 1), 0).astype(f32) + offset


def head_lanes(rows):
    return lax.broadcasted_iota(jnp.int32, (rows, WIDE), 1) // DH


def heads_apart(group):
    at = head_lanes(group.shape[0])
    zero = jnp.zeros_like(group)
    return jnp.concatenate([jnp.where(at == k, group, zero) for k in range(MANY)], axis=0)


def heads_joined(stacked):
    rows = stacked.shape[0] // MANY
    at = head_lanes(rows)
    joined = stacked[:rows]
    for k in range(1, MANY):
        joined = jnp.where(at == k, stacked[k * rows : (k + 1) * rows], joined)
    return joined


def beside(stacked):
    rows = stacked.shape[0] // MANY
    return jnp.concatenate([stacked[k * rows : (k + 1) * rows] for k in range(MANY)], axis=1)


def below(joined):
    width = joined.shape[1] // MANY
    return jnp.concatenate([joined[:, k * width : (k + 1) * width] for k in range(MANY)], axis=0)


def flip(rows):
    i = lax.broadcasted_iota(jnp.int32, (rows, rows), 0)
    j = lax.broadcasted_iota(jnp.int32, (rows, rows), 1)
    return (i + j == rows - 1).astype(f32).astype(bf16)


class Stage:
    def __init__(self, loads, stores, sems):
        self.loads, self.stores, self.sems = loads, stores, sems
        self.copies, self.waited, self.sent, self.pending = {}, set(), set(), []
        self.used = 0
        for key, (source, buffer) in loads.items():
            self.copies[key] = pltpu.make_async_copy(source, buffer, self.sem())
            self.copies[key].start()

    def sem(self):
        self.used += 1
        return self.sems.at[self.used - 1]

    def __getitem__(self, key):
        if key in self.stores:
            return self.stores[key][1]
        if key not in self.waited:
            self.copies[key].wait()
            self.waited.add(key)
        return self.loads[key][1]

    def send(self, key, at=None):
        target, buffer = self.stores[key]
        if at is not None:
            target, buffer = target.at[at], buffer.at[at]
        copy = pltpu.make_async_copy(buffer, target, self.sem())
        copy.start()
        self.pending.append(copy)
        self.sent.add(key)

    def finish(self):
        for key in self.stores:
            if key not in self.sent:
                self.send(key)
        for key in self.loads:
            self[key]
        for copy in self.pending:
            copy.wait()


def staged(
    name, body, ins, outs, smem=(), scratch=(), flops=0, moved=0, sends=0, filled=None,
    limit=VMEM_LIMIT,
):
    operands, loads = [], []
    for key, item in ins.items():
        array, view, shape = item if isinstance(item, tuple) else (item, None, item.shape)
        at = next((i for i, other in enumerate(operands) if other is array), None)
        if at is None:
            at = len(operands)
            operands.append(array)
        loads.append((key, at, view, shape, array.dtype))
    outs = {
        key: item if isinstance(item, tuple) else (item, None, item.shape)
        for key, item in outs.items()
    }
    aliases = {}
    if filled is not None:
        aliases = {len(smem) + len(operands): 0}
        operands.append(filled)
    n_smem, n_ops, n_outs, n_loads = len(smem), len(operands), len(outs), len(loads)

    def run(*refs):
        cuts = [n_smem, n_ops, n_outs, n_loads, n_outs, 1]
        groups, at = [], 0
        for cut in cuts:
            groups.append(refs[at : at + cut])
            at += cut
        scalars, given, targets, buffers, results, sems = groups
        stage = Stage(
            {
                key: (given[at] if view is None else view(given[at]), buffer)
                for (key, at, view, _, _), buffer in zip(loads, buffers)
            },
            {
                key: (target if view is None else view(target), result)
                for (key, (_, view, _)), target, result in zip(outs.items(), targets, results)
            },
            sems[0],
        )
        body(stage, *scalars, *refs[at:])
        stage.finish()

    hbm = pl.BlockSpec(memory_space=pl.ANY)
    got = pl.pallas_call(
        run,
        in_specs=[pl.BlockSpec(memory_space=pltpu.SMEM)] * n_smem + [hbm] * n_ops,
        out_specs=[hbm] * n_outs,
        out_shape=[whole for whole, _, _ in outs.values()],
        scratch_shapes=[pltpu.VMEM(shape, dtype) for _, _, _, shape, dtype in loads]
        + [pltpu.VMEM(shape, whole.dtype) for whole, _, shape in outs.values()]
        + [pltpu.SemaphoreType.DMA((n_loads + n_outs + sends,))]
        + list(scratch),
        input_output_aliases=aliases,
        compiler_params=pltpu.CompilerParams(vmem_limit_bytes=limit),
        cost_estimate=pl.CostEstimate(flops=flops, bytes_accessed=moved, transcendentals=0),
        name=name,
    )(*smem, *operands)
    return dict(zip(outs, got))


def sds(shape, dtype):
    return jax.ShapeDtypeStruct(shape, dtype)


def slab(array, *at):
    shape = tuple(a[1] for a in at if isinstance(a, tuple))
    index = tuple(pl.ds(*a) if isinstance(a, tuple) else a for a in at)
    return (array, lambda ref: ref.at[index], shape)


PART = 1024


def activate(inner):
    half = 0.5 * inner
    turn = jnp.tanh(half)
    up = 1.0 + turn
    active = half * up
    return active, 0.5 * (up + active * (1.0 - turn))


def feed_slabs(feed_in, feed_out, module):
    _, model, hidden = feed_in.shape
    slabs = {}
    for k in range(hidden // PART):
        slabs[f"w_in{k}"] = slab(feed_in, module, (0, model), (k * PART, PART))
        slabs[f"w_out{k}"] = slab(feed_out, module, (k * PART, PART), (0, model))
    return slabs


def front(row, features, feed_in, feed_in_bias, feed_out, attend_in, gain, shift, bias):
    _, frames, model = features.shape
    hidden = feed_in.shape[2]
    parts = hidden // PART
    low = sds((frames, model), bf16)

    def body(k):
        gain, shift = k["gain"], k["shift"]
        x = k["x"][...].astype(f32)
        normal, _ = normalize(x)
        k["n0"][...] = (normal * gain[0:1] + shift[0:1]).astype(bf16)
        k.send("n0")
        for part in range(parts):
            cut = slice(part * PART, (part + 1) * PART)
            inner = dot(k["n0"][...], k[f"w_in{part}"][...]) + k["b_in"][0:1, cut]
            active, slope = activate(inner)
            k["act"][:, cut] = active.astype(bf16)
            k["slope"][:, cut] = slope.astype(bf16)
        k.send("slope")
        k.send("act")
        branch = k["bias"][6:7]
        for part in range(parts):
            cut = slice(part * PART, (part + 1) * PART)
            branch = branch + dot(k["act"][:, cut], k[f"w_out{part}"][...])
        after = x + 0.5 * branch
        k["after"][...] = after
        k.send("after")
        normal, _ = normalize(after)
        normed = (normal * gain[1:2] + shift[1:2]).astype(bf16)
        k["na"][...] = normed
        k.send("na")
        attend_in, bias = k["attend_in"], k["bias"]
        keys = dot(normed, attend_in[:, model : 2 * model]).astype(bf16)
        values = (dot(normed, attend_in[:, 2 * model :]) + bias[1:2]).astype(bf16)
        k["lo"][:, :model] = keys[:WIN]
        k["lo"][:, model:] = values[:WIN]
        k["hi"][:, :model] = keys[WIN:]
        k["hi"][:, model:] = values[WIN:]
        k.send("lo")
        k.send("hi")
        query = dot(normed, attend_in[:, :model]) + bias[0:1]
        factor = 1.0 / math.sqrt(DH)
        k["qu"][...] = ((query + bias[8:9]) * factor).astype(bf16)
        k["qv"][...] = ((query + bias[9:10]) * factor).astype(bf16)

    ins = {"x": slab(features, row, (0, frames), (0, model)), "gain": gain, "shift": shift}
    ins["b_in"] = feed_in_bias
    weights = feed_slabs(feed_in, feed_out, 0)
    ins |= {key: weights[key] for key in weights if "in" in key}
    ins["bias"] = bias
    ins |= {key: weights[key] for key in weights if "out" in key}
    ins["attend_in"] = attend_in
    return staged(
        "front",
        body,
        ins,
        {
            "after": sds((frames, model), f32), "n0": low, "na": low, "qu": low, "qv": low,
            "lo": sds((WIN, 2 * model), bf16), "hi": sds((WIN, 2 * model), bf16),
            "act": sds((frames, hidden), bf16), "slope": sds((frames, hidden), bf16),
        },
        flops=2 * frames * model * (2 * hidden + 3 * model),
        moved=10 << 20,
    )


def attend(
    row_len, row, rows, info, ends, got, before, after, sinusoid, proj, table, attend_out,
    convolve_in, gain, shift, bias, edges,
):
    frames, model = got["after"].shape
    low = sds((frames, model), bf16)
    final = row == rows - 1

    def body(k, info):
        if table is None:
            k["table"][...] = dot(k["sinusoid"][...], k["proj"][...]).astype(bf16)
            k.send("table")
        bands = k["table"]
        start = info[0].astype(f32)
        reach = info[1 + row].astype(f32)
        row_ends = k["ends"][row : row + 1, :]
        turn = flip(WIN)
        key_at = lax.broadcasted_iota(jnp.int32, (WIN, SPAN), 1).astype(f32)
        blocks = (k["before"], k["lo"], k["hi"], k["next"])
        qu, qv = k["qu"], k["qv"]
        for block in range(2):
            at = column(WIN, start + WIN * block)
            lower, upper = bounds(row_ends, at, row_len)
            base = start + (WIN * (block - 1))
            lower = jnp.maximum(lower, at - reach) - base
            upper = jnp.minimum(upper - 1.0, at + reach) - base
            allowed = ((key_at >= lower) & (key_at <= upper))[None]
            here = slice(WIN * block, WIN * (block + 1))
            some = blocks[block : block + 3]

            for group in range(GROUPS):
                cut = slice(WIDE * group, WIDE * (group + 1))
                cut_v = slice(model + WIDE * group, model + WIDE * (group + 1))
                keys = jnp.concatenate([b[:, cut] for b in some], axis=0)
                values = jnp.concatenate([b[:, cut_v] for b in some], axis=0)
                spread = dot_last(heads_apart(qv[here, cut]), bands[:, cut])
                content = dot_last(heads_apart(qu[here, cut]), keys)
                spread = pltpu.roll(
                    spread.reshape(MANY, WIN, SPAN), 0, 2, stride=1, stride_axis=1
                )
                scores = jnp.where(allowed, content.reshape(MANY, WIN, SPAN) + spread, negative)
                powers = jnp.exp(scores - jnp.max(scores, axis=2, keepdims=True))
                weights = powers * (1.0 / jnp.sum(powers, axis=2, keepdims=True))
                weights = weights.astype(bf16).reshape(MANY * WIN, SPAN)
                k["mixed"][here, cut] = heads_joined(dot(weights, values)).astype(bf16)
                k["prob"][block, group] = dot(turn, beside(weights)).astype(bf16)
            k.send("prob", block)
        k.send("mixed")
        after_attend = k["after"][...] + dot(k["mixed"][...], k["attend_out"][...])
        after_attend = after_attend + k["bias"][2:3]
        k["out"][...] = after_attend
        k.send("out")
        normal, _ = normalize(after_attend)
        normed = (normal * k["gain"][2:3] + k["shift"][2:3]).astype(bf16)
        k["nc"][...] = normed
        k.send("nc")
        value = dot(normed, k["convolve_in"][:, :model]) + k["bias"][3:4]
        k["paired"][:, :model] = value
        gate = dot(normed, k["convolve_in"][:, model:]) + k["bias"][4:5]
        k["paired"][:, model:] = gate
        k.send("paired")
        gated = (value * sigmoid(gate)).astype(bf16)
        k["gated"][...] = gated
        if final:
            for other in range(row):
                k["first"][other] = k[f"first{other}"][...]
                k["last"][other] = k[f"last{other}"][...]
            k["first"][row] = gated[:RIM]
            k["last"][row] = gated[frames - RIM :]
        else:
            k["first"][...] = gated[:RIM]
            k["last"][...] = gated[frames - RIM :]

    ins = {"ends": ends}
    if table is None:
        ins |= {"sinusoid": sinusoid, "proj": proj}
    else:
        ins["table"] = table
    ins |= {
        "qu": got["qu"], "qv": got["qv"], "before": before, "lo": got["lo"], "hi": got["hi"],
        "next": after, "after": got["after"], "attend_out": attend_out, "bias": bias,
        "gain": gain, "shift": shift, "convolve_in": convolve_in,
    }
    for other, (first, last) in enumerate(edges):
        ins |= {f"first{other}": first, f"last{other}": last}
    rim = sds((rows, RIM, model) if final else (RIM, model), bf16)
    outs = {
        "prob": sds((2, GROUPS, WIN, MANY * SPAN), bf16), "mixed": low,
        "out": sds((frames, model), f32), "nc": low, "paired": sds((frames, 2 * model), f32),
        "gated": low, "first": rim, "last": rim,
    }
    if table is None:
        outs["table"] = sds((SPAN, model), bf16)
    return staged(
        "attend",
        body,
        ins,
        outs,
        smem=[info],
        flops=8 * 8 * 256 * 384 * 128,
        moved=8 << 20,
        sends=1,
    )


def valid_column(info, row, rows, frames):
    at = column(frames, info[0].astype(f32))
    return (at < info[1 + rows + row].astype(f32)).astype(f32)


def pack(ref, vectors):
    at = 0
    for vector in vectors:
        for k in range(0, vector.shape[1], 128):
            ref[at : at + 1, :] = vector[:, k : k + 128]
            at += 1


def by_rows(count, size, step, init=None):
    def one(i, carry):
        return step(pl.ds(pl.multiple_of(i * size, size), size), carry)

    return lax.fori_loop(0, count // size, one, init)


def by_lanes(width, step):
    def one(i, carry):
        step(pl.ds(pl.multiple_of(i * 128, 128), 128))
        return carry

    lax.fori_loop(0, width // 128, one, 0)


def spread(column):
    return jnp.broadcast_to(column, (column.shape[0], 128))


def tap_masks(keep_s, at, low, high):
    for tap in range(KERNEL):
        off = tap - HALF
        keep_s[tap] = spread(((at + off >= low) & (at + off < high)).astype(f32))


def depth_conv(row_len, devices, info, ends, gated, before, after, taps):
    frames, model = gated[0].shape
    rows = len(gated)

    def body(k, info, rim, keep_s, valid_s, sums, tile):
        start = info[0].astype(f32)
        counts = 0.0
        taps = k["taps"]
        for row in range(rows):
            here = slice(row * frames, (row + 1) * frames)
            at = column(frames, start)
            low, high = bounds(k["ends"][row : row + 1, :], at, row_len)
            tap_masks(keep_s, at, low, high)
            valid = valid_column(info, row, rows, frames)
            valid_s[here] = spread(valid)
            counts += total(valid)
            rim[0:RIM] = k["before"][row].astype(f32)
            rim[RIM : RIM + frames] = k[f"gated{row}"][...].astype(f32)
            rim[RIM + frames :] = k["after"][row].astype(f32)

            def one(lanes):
                depth = jnp.zeros((frames, 128), f32)
                for tap in range(KERNEL):
                    off = tap - HALF
                    part = rim[RIM + off : RIM + off + frames, lanes] * keep_s[tap]
                    depth += taps[tap : tap + 1, lanes] * part
                k["depth"][here, lanes] = depth
                sums[row : row + 1, lanes] = total(depth * valid_s[here])

            by_lanes(model, one)
            k.send("depth", pl.ds(row * frames, frames))
        first = total(sums[0:rows, :])
        mean = first / jnp.maximum(counts, 1.0)
        sums[rows : rows + 1, :] = mean

        def two(lanes):
            centered = k["depth"][:, lanes] - sums[rows : rows + 1, lanes]
            sums[rows + 1 : rows + 2, lanes] = total(centered * centered * valid_s[...])

        by_lanes(model, two)
        pack(tile, [first, sums[rows + 1 : rows + 2, :]])
        k["stats"][...] = jnp.broadcast_to(tile[...][None], k["stats"].shape)

    ins = {"ends": ends, "before": before, "taps": taps}
    ins |= {f"gated{row}": gated[row] for row in range(rows)}
    ins["after"] = after
    return staged(
        "depth_conv",
        body,
        ins,
        {"depth": sds((rows * frames, model), f32), "stats": sds((devices, 8, 128), f32)},
        smem=[info],
        scratch=[
            pltpu.VMEM((frames + 2 * RIM, model), f32),
            pltpu.VMEM((KERNEL, frames, 128), f32),
            pltpu.VMEM((rows * frames, 128), f32),
            pltpu.VMEM((8, model), f32),
            pltpu.VMEM((8, 128), f32),
        ],
        flops=rows * frames * model * 30,
        moved=2 << 20,
        sends=rows - 1,
    )


def middle(
    devices, rows, info, stats, counts, depth, stream, feed_in, feed_in_bias, feed_out,
    convolve_out, gain, shift, bias, cotangent,
):
    tokens, model = depth.shape
    frames = tokens // rows
    hidden = feed_in.shape[2]
    parts = hidden // PART

    def body(k, info, conv_s, slope_s, tile):
        stats, each = k["stats"], k["counts"][:, 0:1]
        gain, shift, bias = k["gain"], k["shift"], k["bias"]
        count = total(each)
        means, inverses = [], []
        for at in range(model // 128):
            sums = stats[:, at, :]
            mean = total(sums) / count
            off = sums / jnp.maximum(each, 1.0) - mean
            spread = total(stats[:, model // 128 + at, :]) + total(each * off * off)
            means.append(mean)
            inverses.append(lax.rsqrt(spread / count + eps_norm))
        mean = jnp.concatenate(means, axis=1)
        inverse = jnp.concatenate(inverses, axis=1)
        k["inv"][0:1] = inverse
        k["inv"][1:2] = jnp.broadcast_to(1.0 / count, (1, model))
        normal = (k["depth"][...] - mean) * inverse
        k["bn"][...] = normal
        k.send("bn")
        batch = normal * gain[5:6] + shift[5:6]
        swished = (batch * sigmoid(batch)).astype(bf16)
        k["sw"][...] = swished
        k.send("sw")
        streams = jnp.concatenate([k[f"stream{row}"][...] for row in range(rows)], axis=0)
        after_conv = streams + dot(swished, k["convolve_out"][...]) + bias[5:6]
        conv_s[...] = after_conv
        normal, _ = normalize(after_conv)
        k["nf"][...] = (normal * gain[3:4] + shift[3:4]).astype(bf16)
        k.send("nf")
        for part in range(parts):
            cut = slice(part * PART, (part + 1) * PART)
            inner = dot(k["nf"][...], k[f"w_in{part}"][...]) + k["b_in"][1:2, cut]
            active, slope = activate(inner)
            k["act"][:, cut] = active.astype(bf16)
            slope_s[:, cut] = slope
        k.send("act")
        branch = bias[7:8]
        for part in range(parts):
            cut = slice(part * PART, (part + 1) * PART)
            branch = branch + dot(k["act"][:, cut], k[f"w_out{part}"][...])
        normal, inverse = normalize(conv_s[...] + 0.5 * branch)
        valid = jnp.concatenate(
            [valid_column(info, row, rows, frames) for row in range(rows)], axis=0
        )
        k["out"][...] = (valid * (normal * gain[4:5] + shift[4:5])).astype(bf16)
        k.send("out")
        grad = valid * k["cotangent"][...].astype(f32)
        grad, gain_grad, shift_grad = norm_back(grad, normal, inverse, gain[4:5])
        k["gcs"][...] = grad
        low = (0.5 * grad).astype(bf16)
        k["gl"][...] = low
        k.send("gl")
        vec = k["vec"]
        vec[2:3] = gain_grad
        vec[3:4] = shift_grad
        vec[5:6] = total(low.astype(f32))
        back = 0.0
        for part in range(parts):
            cut = slice(part * PART, (part + 1) * PART)
            grad = (dot_last(k["gl"][...], k[f"w_out{part}"][...]) * slope_s[:, cut]).astype(bf16)
            k["gi"][:, cut] = grad
            k["fb"][:, cut] = total(grad.astype(f32))
            back = back + dot_last(grad, k[f"w_in{part}"][...])
        k.send("gi")
        normal, inverse = normalize(conv_s[...])
        grad, gain_grad, shift_grad = norm_back(back, normal, inverse, gain[3:4])
        vec[0:1] = gain_grad
        vec[1:2] = shift_grad
        grad = k["gcs"][...] + grad
        k["gcs"][...] = grad
        k.send("gcs")
        low = grad.astype(bf16)
        k["gcl"][...] = low
        k.send("gcl")
        vec[4:5] = total(low.astype(f32))
        bn = k["bn"][...]
        batch = bn * gain[5:6] + shift[5:6]
        _, slope = activate(batch)
        grad = dot_last(low, k["convolve_out"][...]) * slope
        k["gb"][...] = grad
        k.send("gb")
        pack(tile, [total(grad), total(grad * bn)])
        k["totals"][...] = jnp.broadcast_to(tile[...][None], k["totals"].shape)
        k.send("totals")
        for row in range(rows):
            at, end = row * frames, (row + 1) * frames
            k["first"][row, :, :model] = k["gb"][at : at + RIM_GRAD]
            k["first"][row, :, model:] = k["bn"][at : at + RIM_GRAD]
            k["last"][row, :, :model] = k["gb"][end - RIM_GRAD : end]
            k["last"][row, :, model:] = k["bn"][end - RIM_GRAD : end]

    ins = {"stats": stats, "counts": counts, "gain": gain, "shift": shift, "depth": depth}
    ins |= {"bias": bias, "convolve_out": convolve_out}
    ins |= {f"stream{row}": stream[row] for row in range(rows)}
    weights = feed_slabs(feed_in, feed_out, 1)
    ins["b_in"] = feed_in_bias
    ins |= {key: weights[key] for key in weights if "in" in key}
    ins |= {key: weights[key] for key in weights if "out" in key}
    ins["cotangent"] = cotangent
    low = sds((tokens, model), bf16)
    wide = sds((tokens, model), f32)
    rim = sds((rows, RIM_GRAD, 2 * model), f32)
    return staged(
        "middle",
        body,
        ins,
        {
            "out": low, "act": sds((tokens, hidden), bf16), "gi": sds((tokens, hidden), bf16),
            "nf": low, "gl": low, "sw": low, "gcl": low, "gcs": wide, "gb": wide, "bn": wide,
            "inv": sds((8, model), f32), "totals": sds((devices, 8, 128), f32), "first": rim,
            "last": rim, "vec": sds((8, model), f32), "fb": sds((1, hidden), f32),
        },
        smem=[info],
        scratch=[
            pltpu.VMEM((tokens, model), f32),
            pltpu.VMEM((tokens, hidden), f32),
            pltpu.VMEM((8, 128), f32),
        ],
        flops=2 * tokens * model * (4 * hidden + 2 * model),
        moved=24 << 20,
    )


def conv_back(
    row_len, info, ends, taps, convolve_in, attend_out, gain, totals, mid, edge_before,
    edge_after, rim_before, rim_after, gated, paired, after_attend,
):
    tokens, model = mid["gb"].shape
    rows = len(gated)
    frames = tokens // rows

    def body(k, info, grads, rim, keep_s):
        start = info[0].astype(f32)
        parts = model // 128
        sums = [total(k["totals"][:, at, :]) for at in range(2 * parts)]
        total_a = jnp.concatenate(sums[:parts], axis=1)
        total_b = jnp.concatenate(sums[parts:], axis=1)
        inverse, per_count = k["inv"][0:1], k["inv"][1:2]
        gain, taps, vec = k["gain"], k["taps"], k["vec"]
        own_scale = inverse * gain[5:6]
        share_a = own_scale * total_a * per_count
        share_b = own_scale * total_b * per_count
        vec[14:15] = total_a
        vec[15:16] = total_b
        vec[0:9] = jnp.zeros((9, model), f32)
        vec[9:14] = jnp.zeros((5, model), f32)

        def grad_of(grad, normal, valid):
            grad = grad * own_scale - valid * (share_a + normal * share_b)
            return grad.astype(bf16).astype(f32)

        for row in range(rows):
            first = row * frames
            last = info[1 + rows + row].astype(f32)
            at = column(frames, start)
            low, high = bounds(k["ends"][row : row + 1, :], at, row_len)
            tap_masks(keep_s, at, low, high)
            before, after = k["edge_before"], k["edge_after"]
            edge_at = column(RIM_GRAD, start - RIM_GRAD)
            grads[0:RIM_GRAD] = grad_of(
                before[row, :, :model], before[row, :, model:], (edge_at < last).astype(f32)
            )
            for step in range(0, frames, 32):
                here = slice(step, step + 32)
                at = column(32, start + step)
                grads[RIM_GRAD + step : RIM_GRAD + step + 32] = grad_of(
                    k[f"gb{row}"][here], k[f"bn{row}"][here], (at < last).astype(f32)
                )
            edge_at = column(RIM_GRAD, start + frames)
            grads[RIM_GRAD + frames :] = grad_of(
                after[row, :, :model], after[row, :, model:], (edge_at < last).astype(f32)
            )
            rim[0:RIM] = k["rim_before"][row].astype(f32)
            rim[RIM : RIM + frames] = k[f"gated{row}"][...].astype(f32)
            rim[RIM + frames :] = k["rim_after"][row].astype(f32)
            paired = k[f"paired{row}"]
            half = frames // 2

            def one(i, carry):
                lane = pl.multiple_of(i * 128, 128)
                lanes, gates = pl.ds(lane, 128), pl.ds(model + lane, 128)
                for base in range(0, frames, half):
                    own = grads[RIM_GRAD + base : RIM_GRAD + base + half, lanes]
                    grad = jnp.zeros((half, 128), f32)
                    for tap in range(KERNEL):
                        off = base + tap - HALF
                        keep = keep_s[tap, base : base + half]
                        part = own * (rim[RIM + off : RIM + off + half, lanes] * keep)
                        vec[tap : tap + 1, lanes] += total(part)
                        mirror = KERNEL - 1 - tap
                        part = grads[RIM_GRAD + off : RIM_GRAD + off + half, lanes] * keep
                        grad += taps[mirror : mirror + 1, lanes] * part
                    sigma = sigmoid(paired[base : base + half, gates])
                    one = (grad * sigma).astype(bf16)
                    value = paired[base : base + half, lanes]
                    two = (grad * sigma * value * (1.0 - sigma)).astype(bf16)
                    here = slice(first + base, first + base + half)
                    k["gp"][here, lanes] = one
                    k["gp"][here, gates] = two
                    vec[11:12, lanes] += total(one.astype(f32))
                    vec[12:13, lanes] += total(two.astype(f32))
                return carry

            lax.fori_loop(0, model // 128, one, 0)
            k.send("gp", pl.ds(first, frames))
        grad = dot_last(k["gp"][...], k["convolve_in"][...])
        streams = jnp.concatenate([k[f"after{row}"][...] for row in range(rows)], axis=0)
        normal, inverse = normalize(streams)
        grad, gain_grad, shift_grad = norm_back(grad, normal, inverse, gain[2:3])
        vec[9:10] = gain_grad
        vec[10:11] = shift_grad
        grad = k["gcs"][...] + grad
        k["gas"][...] = grad
        k.send("gas")
        low = grad.astype(bf16)
        k["gal"][...] = low
        k.send("gal")
        vec[13:14] = total(low.astype(f32))
        k["gm"][...] = dot_last(k["gal"][...], k["attend_out"][...]).astype(bf16)

    ins = {"totals": totals, "inv": mid["inv"], "gain": gain, "ends": ends, "taps": taps}
    ins |= {"edge_before": edge_before, "edge_after": edge_after}
    ins |= {"rim_before": rim_before, "rim_after": rim_after}
    for row in range(rows):
        span = (row * frames, frames)
        ins |= {
            f"gb{row}": slab(mid["gb"], span, (0, model)),
            f"bn{row}": slab(mid["bn"], span, (0, model)),
            f"gated{row}": gated[row], f"paired{row}": paired[row],
        }
    ins["convolve_in"] = convolve_in
    ins |= {f"after{row}": after_attend[row] for row in range(rows)}
    ins |= {"gcs": mid["gcs"], "attend_out": attend_out}
    low = sds((tokens, model), bf16)
    return staged(
        "conv_back",
        body,
        ins,
        {
            "gp": sds((tokens, 2 * model), bf16), "gas": sds((tokens, model), f32), "gal": low,
            "gm": low, "vec": sds((16, model), f32),
        },
        smem=[info],
        scratch=[
            pltpu.VMEM((frames + 2 * RIM_GRAD, model), f32),
            pltpu.VMEM((frames + 2 * RIM, model), f32),
            pltpu.VMEM((KERNEL, frames, 128), f32),
        ],
        flops=2 * tokens * model * 3 * model,
        moved=12 << 20,
        sends=rows - 1,
    )


def attend_back(row, got, before, after, prob, table, gm, sofar):
    frames, model = got["qu"].shape
    factor = 1.0 / math.sqrt(DH)

    def body(k, acc, turned):
        g_table, vec = k["g_table"], k["vec"]
        if sofar:
            g_table[...] = k["g_table_in"][...]
            vec[...] = k["vec_in"][...]
        else:
            g_table[...] = jnp.zeros_like(g_table)
            vec[...] = jnp.zeros_like(vec)
        acc[...] = jnp.zeros_like(acc)
        turn = flip(WIN)
        table = k["table"]
        for block in range(2):
            here = slice(WIN * block, WIN * (block + 1))
            span = slice(WIN * block, WIN * block + SPAN)
            blocks = ("before", "lo", "hi", "next")[block : block + 3]
            blocks = [k[name] for name in blocks]
            turned[0] = dot(turn, k["gm"][here]).astype(bf16)
            turned[1] = dot(turn, k["qu"][here]).astype(bf16)
            turned[2] = dot(turn, k["qv"][here]).astype(bf16)
            prob = k[f"prob{block}"]

            for group in range(GROUPS):
                cut = slice(WIDE * group, WIDE * (group + 1))
                cut_v = slice(model + WIDE * group, model + WIDE * (group + 1))
                keys = jnp.concatenate([b[:, cut] for b in blocks], axis=0)
                values = jnp.concatenate([b[:, cut_v] for b in blocks], axis=0)
                weights = below(prob[group])
                grad_mixed = heads_apart(turned[0, :, cut])
                grad = dot_last(grad_mixed, values)
                wide = weights.astype(f32)
                delta = jnp.sum(wide * grad, axis=1, keepdims=True)
                raw = (wide * (grad - delta)).astype(bf16)
                acc[span, cut_v] += dot_first(weights, grad_mixed)
                acc[span, cut] += dot_first(raw, heads_apart(turned[1, :, cut]))
                grad_u = heads_joined(dot(raw, keys)) * factor
                band = pltpu.roll(
                    raw.astype(f32).reshape(MANY, WIN, SPAN),
                    SPAN - (WIN - 1),
                    2,
                    stride=1,
                    stride_axis=1,
                )
                band = band.astype(bf16).reshape(MANY * WIN, SPAN)
                grad_v = heads_joined(dot(band, table[:, cut])) * factor
                g_table[:, cut] += dot_first(band, heads_apart(turned[2, :, cut]))
                vec[0:1, cut] += total(grad_u)
                vec[1:2, cut] += total(grad_v)
                k["gq"][here, cut] = dot(turn, (grad_u + grad_v).astype(bf16)).astype(bf16)
            if block == 0:
                k["g_before"][...] = acc[0:WIN].astype(bf16)
                k.send("g_before")
        k["g_after"][...] = acc[3 * WIN :].astype(bf16)
        k.send("g_after")
        k["g_lo"][...] = acc[WIN : 2 * WIN]
        k["g_hi"][...] = acc[2 * WIN : 3 * WIN]

    ins = {"gm": slab(gm, (row * frames, frames), (0, model)), "qu": got["qu"], "qv": got["qv"]}
    ins |= {"before": before, "lo": got["lo"], "hi": got["hi"]}
    ins["prob0"] = slab(prob, 0, (0, GROUPS), (0, WIN), (0, MANY * SPAN))
    ins |= {"table": table, "next": after}
    ins["prob1"] = slab(prob, 1, (0, GROUPS), (0, WIN), (0, MANY * SPAN))
    if sofar:
        ins |= {"g_table_in": sofar[0], "vec_in": sofar[1]}
    kv = (WIN, 2 * model)
    return staged(
        "attend_back",
        body,
        ins,
        {
            "gq": sds((frames, model), bf16), "g_before": sds(kv, bf16), "g_lo": sds(kv, f32),
            "g_hi": sds(kv, f32), "g_after": sds(kv, bf16), "g_table": sds((SPAN, model), f32),
            "vec": sds((8, model), f32),
        },
        scratch=[
            pltpu.VMEM((4 * WIN, 2 * model), f32),
            pltpu.VMEM((3, WIN, model), bf16),
        ],
        flops=8 * 14 * 256 * 384 * 128,
        moved=8 << 20,
    )


def back(row, grads, halo, attend_in, after_first, gas, gain):
    frames, model = after_first.shape

    def body(k):
        joined, vec, gain = k["gj"], k["vec"], k["gain"]
        joined[:, :model] = k["gq"][...]
        joined[:WIN, model:] = (k["g_lo"][...] + k["left"][...].astype(f32)).astype(bf16)
        joined[WIN:, model:] = (k["g_hi"][...] + k["right"][...].astype(f32)).astype(bf16)
        k.send("gj")
        joined = joined[...]
        vec[0:1] = total(joined[:, :model].astype(f32))
        vec[1:2] = total(joined[:, 2 * model :].astype(f32))
        grad = dot_last(joined, k["attend_in"][...])
        normal, inverse = normalize(k["after"][...])
        grad, gain_grad, shift_grad = norm_back(grad, normal, inverse, gain[1:2])
        vec[2:3] = gain_grad
        vec[3:4] = shift_grad
        grad = k["gas"][...] + grad
        k["gfs"][...] = grad
        k.send("gfs")
        low = (0.5 * grad).astype(bf16)
        k["gl"][...] = low
        vec[4:5] = total(low.astype(f32))

    ins = {
        "gain": gain, "gq": grads["gq"], "g_lo": grads["g_lo"], "left": halo[0],
        "g_hi": grads["g_hi"], "right": halo[1], "attend_in": attend_in, "after": after_first,
        "gas": slab(gas, (row * frames, frames), (0, model)),
    }
    return staged(
        "back",
        body,
        ins,
        {
            "gj": sds((frames, 3 * model), bf16), "gfs": sds((frames, model), f32),
            "gl": sds((frames, model), bf16), "vec": sds((8, model), f32),
        },
        flops=2 * frames * model * 3 * model,
        moved=5 << 20,
    )


def keep_half(block, core, mine_ref, other_ref, rows, at=0):
    model = mine_ref.shape[2]
    pairs = rows[1] - rows[0]
    size = block.shape[0] // (2 * pairs)
    shaped = block.reshape(pairs, 2, size, model)
    even, odd = shaped[:, 0], shaped[:, 1]
    here = slice(*rows)
    mine_ref[here, at : at + size] = jnp.where(core == 0, even, odd).astype(bf16)
    other_ref[here, at : at + size] = jnp.where(core == 0, odd, even).astype(bf16)


def sum_first(lefts, rights):
    return sum(dot_first(left, right) for left, right in zip(lefts, rights))


def late_weights(info, place_of_core, n, act, gl, na, gj, sinusoid, g_table):
    rows = len(act)
    frames, hidden = act[0].shape
    model = gl[0].shape[1]
    parts = hidden // PART
    width, slim = hidden // n, model // n
    pairs = (0, n // 2)

    def body(k, info):
        core = info[place_of_core]
        for part in range(2):
            cut = slice(part * model, (part + 1) * model)
            block = sum_first(
                [k[f"na{row}"][...] for row in range(rows)],
                [k[f"gj{row}"][:, cut] for row in range(rows)],
            )
            keep_half(block, core, k["mine"], k["other"], pairs, width + part * slim)
        high = k["g_table"][...].astype(bf16)
        low = (k["g_table"][...] - high.astype(f32)).astype(bf16)
        place = dot_first(k["sinusoid"][...], high) + dot_first(k["sinusoid"][...], low)
        keep_half(place, core, k["mine"], k["other"], pairs, width + 2 * slim)
        step = n // 2 // parts
        for part in range(parts):
            block = sum_first(
                [k[f"act{row}_{part}"][...] for row in range(rows)],
                [k[f"gl{row}"][...] for row in range(rows)],
            )
            some = (part * step, (part + 1) * step)
            keep_half(block, core, k["mine"], k["other"], some)
            k.send("other", pl.ds(part * step, step))
            k.send("mine", pl.ds(part * step, step))

    half = sds((n // 2, width + 3 * slim, model), bf16)
    ins = {f"na{row}": na[row] for row in range(rows)}
    ins |= {f"gj{row}": slab(gj[row], (0, frames), (0, 2 * model)) for row in range(rows)}
    ins |= {"g_table": g_table, "sinusoid": sinusoid}
    ins |= {f"gl{row}": gl[row] for row in range(rows)}
    for part in range(parts):
        for row in range(rows):
            ins[f"act{row}_{part}"] = slab(act[row], (0, frames), (part * PART, PART))
    got = staged(
        "late_weights",
        body,
        ins,
        {"other": half, "mine": half},
        smem=[info],
        flops=2 * rows * frames * model * (hidden + 3 * model),
        moved=9 << 20,
        sends=2 * parts - 2,
    )
    return got["mine"], got["other"]


def first_back(info, place_of_core, n, gl, slope, feed_in, feed_out, n0, na, gj):
    rows = len(slope)
    frames, hidden = slope[0].shape
    model = gl[0].shape[1]
    tokens = rows * frames
    parts = hidden // PART

    def body(k, info):
        core = info[place_of_core]
        low = jnp.concatenate([k[f"gl{row}"][...] for row in range(rows)], axis=0)
        step = n // 2 // parts
        back = 0.0
        block = sum_first(
            [k[f"na{row}"][...] for row in range(rows)],
            [k[f"gj{row}"][...] for row in range(rows)],
        )
        keep_half(block, core, k["mine"], k["other"], (0, n // 2), hidden // n)
        for part in range(parts):
            cut = slice(part * PART, (part + 1) * PART)
            grad = dot_last(low, k[f"w_out{part}"][...])
            scale = jnp.concatenate([k[f"slope{row}_{part}"][...] for row in range(rows)], axis=0)
            grad = (grad * scale.astype(f32)).astype(bf16)
            k["fb"][:, cut] = total(grad.astype(f32))
            block = sum_first(
                [grad[row * frames : (row + 1) * frames] for row in range(rows)],
                [k[f"n0{row}"][...] for row in range(rows)],
            )
            pairs = (part * step, (part + 1) * step)
            keep_half(block, core, k["mine"], k["other"], pairs)
            k.send("other", pl.ds(part * step, step))
            k.send("mine", pl.ds(part * step, step))
            back = back + dot_last(grad, k[f"w_in{part}"][...])
        k["gn"][...] = back

    half = sds((n // 2, hidden // n + model // n, model), bf16)
    ins = {f"na{row}": na[row] for row in range(rows)}
    ins |= {f"gj{row}": slab(gj[row], (0, frames), (2 * model, model)) for row in range(rows)}
    ins |= {f"gl{row}": gl[row] for row in range(rows)}
    weights = feed_slabs(feed_in, feed_out, 0)
    for part in range(parts):
        ins[f"w_out{part}"] = weights[f"w_out{part}"]
        for row in range(rows):
            ins[f"slope{row}_{part}"] = slab(slope[row], (0, frames), (part * PART, PART))
        if part == 0:
            ins |= {f"n0{row}": n0[row] for row in range(rows)}
        ins[f"w_in{part}"] = weights[f"w_in{part}"]
    return staged(
        "first_back",
        body,
        ins,
        {
            "other": half, "mine": half, "fb": sds((1, hidden), f32),
            "gn": sds((tokens, model), f32),
        },
        smem=[info],
        flops=2 * tokens * model * hidden * 3,
        moved=12 << 20,
        sends=2 * parts - 2,
    )


def last(features, gn, gfs, gain):
    rows, frames, model = features.shape

    def body(k):
        gain_grads, shift_grads = 0.0, 0.0
        for row in range(rows):
            here = slice(row * frames, (row + 1) * frames)
            normal, inverse = normalize(k[f"x{row}"][...].astype(f32))
            grad = k[f"gn{row}"][...]
            grad, gain_grad, shift_grad = norm_back(grad, normal, inverse, k["gain"][0:1])
            k["out"][row] = k[f"gfs{row}"][...] + grad
            k.send("out", row)
            gain_grads += gain_grad
            shift_grads += shift_grad
        k["vec"][0:1] = gain_grads
        k["vec"][1:2] = shift_grads

    ins = {"gain": gain}
    for row in range(rows):
        span = (row * frames, frames)
        ins |= {
            f"x{row}": slab(features, row, (0, frames), (0, model)),
            f"gn{row}": slab(gn, span, (0, model)),
            f"gfs{row}": gfs[row],
        }
    return staged(
        "last",
        body,
        ins,
        {"out": sds(features.shape, f32), "vec": sds((8, model), f32)},
        flops=rows * frames * model * 20,
        moved=4 << 20,
        sends=rows - 1,
        limit=FOLD_LIMIT,
    )


def feed_weights(n, gi, nf, act, gl):
    tokens, model = nf.shape
    hidden = gi.shape[1]
    parts = hidden // PART
    size, slim = hidden // n, model // n
    step = n // parts
    room = 2 * slim if slim % 8 == 0 else 0

    def body(k):
        for part in range(parts):
            here = slice(part * step, (part + 1) * step)
            block = dot_first(k[f"gi{part}"][...], k["nf"][...]).astype(bf16)
            k["out"][here, :, :model] = block.reshape(step, size, model)
            block = dot_first(k[f"act{part}"][...], k["gl"][...]).astype(bf16)
            k["out"][here, :, model:] = block.reshape(step, size, model)
            k.send("out", pl.ds(part * step, step))

    ins = {"nf": nf}
    for part in range(parts):
        ins[f"gi{part}"] = slab(gi, (0, tokens), (part * PART, PART))
        if part == 0:
            ins["gl"] = gl
        ins[f"act{part}"] = slab(act, (0, tokens), (part * PART, PART))
    own = (n, size, 2 * model)
    shape = sds((n, size + room, 2 * model), bf16)
    return staged(
        "feed_weights",
        body,
        ins,
        {"out": (shape, lambda ref: ref.at[:, pl.ds(0, size)] if room else ref, own)},
        flops=4 * tokens * model * hidden,
        moved=10 << 20,
        sends=parts - 1,
    )["out"]


def side_weights(n, early, nc, gp, sw, gcl, mixed, gal):
    rows = len(nc)
    tokens, model = sw.shape
    frames = tokens // rows
    slim = model // n
    room = slim % 8 == 0
    own = (n, 2 * slim, 2 * model)

    def body(k):
        out = k["out"]
        spans = [slice(row * frames, (row + 1) * frames) for row in range(rows)]
        for part in range(2):
            cut = slice(part * model, (part + 1) * model)
            block = sum_first(
                [k[f"nc{row}"][...] for row in range(rows)], [k["gp"][at, cut] for at in spans]
            )
            out[:, :slim, cut] = block.astype(bf16).reshape(n, slim, model)
        block = dot_first(k["sw"][...], k["gcl"][...]).astype(bf16)
        out[:, slim:, :model] = block.reshape(n, slim, model)
        block = sum_first(
            [k[f"mixed{row}"][...] for row in range(rows)], [k["gal"][at] for at in spans]
        )
        out[:, slim:, model:] = block.astype(bf16).reshape(n, slim, model)

    ins = {f"nc{row}": nc[row] for row in range(rows)}
    ins |= {"gp": gp, "sw": sw, "gcl": gcl}
    ins |= {f"mixed{row}": mixed[row] for row in range(rows)}
    ins["gal"] = gal
    size = early.shape[1] - 2 * slim
    if room:
        out = (sds(early.shape, bf16), lambda ref: ref.at[:, pl.ds(size, 2 * slim)], own)
    else:
        out = sds(own, bf16)
    got = staged(
        "side_weights",
        body,
        ins,
        {"out": out},
        flops=2 * tokens * model * model * 4,
        moved=6 << 20,
        filled=early if room else None,
    )["out"]
    return got if room else jnp.concatenate([early, got], axis=1)


def neighbours(last_block, first_block):
    devices = lax.axis_size("frames")
    up = [(i, i + 1) for i in range(devices - 1)]
    down = [(i + 1, i) for i in range(devices - 1)]
    return lax.ppermute(last_block, "frames", up), lax.ppermute(first_block, "frames", down)


def gather(copies):
    return lax.all_to_all(copies, DEVICES, 0, 0, tiled=True)


def scatter_sum(grads):
    return lax.psum_scatter(grads, "frames", scatter_dimension=0, tiled=True)


ROW_PAIR = [(0, 1), (1, 0)]


def swap(x, k):
    n = lax.axis_size("frames")
    return lax.ppermute(x, "frames", [(i, i ^ k) for i in range(n)])


def swaps(sends, group):
    k, size = group
    return [swap(send, k * one) for one, send in zip(range(1, size), sends)]


def fold(name, info, row_at, states, small=None):
    ins, outs, plans = {}, {}, []
    for at, (mine, got, how) in enumerate(states):
        size, height, model = mine.shape
        if isinstance(how, tuple):
            _, place, range_ = how
            view = (size // (range_ * place), range_, place, height, model)
            half = (view[0], place, height, model)
        else:
            view = mine.shape
            half = (size, height, model // 2) if how == "columns" else mine.shape
        ins[f"mine{at}"] = mine.reshape(view)
        ins |= {f"got{at}_{k}": one.reshape(view) for k, one in enumerate(got)}
        outs[f"keep{at}"] = sds(half, f32 if how == "wide" else bf16)
        sends = how[2] - 1 if isinstance(how, tuple) else int(how == "columns")
        outs |= {f"send{at}_{k}": sds(half, bf16) for k in range(sends)}
        plans.append((len(got), how))
    if small is not None:
        ins |= {f"small{k}": one for k, one in enumerate(small)}
        outs["sum"] = sds(small[0].shape, f32)

    def body(k, info):
        for at, (count, how) in enumerate(plans):
            parts = [k[f"mine{at}"]] + [k[f"got{at}_{one}"] for one in range(count)]

            def added(*index):
                return sum(part[index].astype(f32) for part in parts)

            keep = k[f"keep{at}"]
            if how is None or how == "wide":
                keep[...] = added(...).astype(keep.dtype)
            elif how == "columns":
                half = keep.shape[2]
                both = [
                    added(slice(None), slice(None), slice(one * half, (one + 1) * half))
                    for one in range(2)
                ]
                first = info[row_at] == 0
                k[f"send{at}_0"][...] = jnp.where(first, both[1], both[0]).astype(bf16)
                k.send(f"send{at}_0")
                keep[...] = jnp.where(first, both[0], both[1]).astype(bf16)
            else:
                digit = info[how[0]]
                for one in range(1, how[2]):
                    other = digit
                    for bit in (1, 2):
                        if one & bit:
                            other = other + bit * (1 - 2 * ((digit // bit) % 2))
                    k[f"send{at}_{one - 1}"][...] = added(slice(None), other).astype(bf16)
                    k.send(f"send{at}_{one - 1}")
                keep[...] = added(slice(None), digit).astype(bf16)
        if small is not None:
            k["sum"][...] = sum(k[f"small{one}"][...] for one in range(len(small)))

    got = staged(name, body, ins, outs, smem=[info], flops=1 << 20, moved=2 << 20, limit=FOLD_LIMIT)
    results = []
    for at, (mine, _, how) in enumerate(states):
        size, height, model = mine.shape
        shape = (size // how[2], height, model) if isinstance(how, tuple) else None
        keys = [key for key in got if key.startswith((f"keep{at}", f"send{at}_"))]
        keep, *sends = [got[key].reshape(shape) if shape else got[key] for key in keys]
        results.append((keep, sends))
    if small is not None:
        results.append(got["sum"])
    return results


def per_device(
    features,
    lengths,
    windows,
    feed_in,
    feed_in_bias,
    feed_out,
    attend_in,
    attend_out,
    position_proj,
    convolve_in,
    convolve_out,
    depthwise,
    norm_gain,
    norm_shift,
    biases,
    cotangent,
):
    rows, frames, model = features.shape
    tokens = rows * frames
    n = lax.axis_size("frames")
    devices = lax.axis_size("rows") * n
    row_len = float(frames * n)
    me = lax.axis_index("frames")
    start = me * frames
    hidden = feed_in.shape[2]
    ends_every = jnp.cumsum(lengths, axis=1, dtype=jnp.int32)
    ends_here = lax.dynamic_slice_in_dim(ends_every, lax.axis_index("rows") * rows, rows, 0)
    slots = ends_here.shape[1]
    ends = jnp.pad(
        ends_here.astype(f32), ((0, 8 - rows), (0, -slots % 128)), constant_values=row_len
    )
    groups, k = [(2, 2)], 4
    while k < n:
        groups.append((k, min(4, n // k)))
        k *= groups[-1][1]
    places = [lax.axis_index("rows"), me % 2] + [(me // k) % size for k, size in groups]
    info = jnp.concatenate(
        [start[None].astype(jnp.int32), windows, ends_here[:, -1], jnp.stack(places)]
    )
    row_at = 1 + 2 * rows
    core_at = row_at + 1
    starts = jnp.arange(n, dtype=jnp.int32) * frames
    counts = jnp.clip(ends_every[:, -1][:, None] - starts[None, :], 0, frames)
    counts = jnp.sum(counts.reshape(-1, rows, n), axis=1).astype(f32).reshape(devices, 1)
    counts = jnp.broadcast_to(counts, (devices, 128))
    sinusoid = jnp.asarray(position_table(WIN, model))
    each = range(rows)

    fronts, befores, afters = [], [], []
    for row in each:
        got = front(
            row, features, feed_in, feed_in_bias, feed_out, attend_in, norm_gain, norm_shift,
            biases,
        )
        fronts.append(got)
        left, right = neighbours(got["hi"], got["lo"])
        befores.append(left)
        afters.append(right)
    attends, edges, table = [], [], None
    for row in each:
        got = attend(
            row_len, row, rows, info, ends, fronts[row], befores[row], afters[row], sinusoid,
            position_proj, table, attend_out, convolve_in, norm_gain, norm_shift, biases, edges,
        )
        if row == 0:
            table = got["table"]
        attends.append(got)
        edges.append((got["first"], got["last"]))
    first, final = edges[-1]
    rim_before, rim_after = neighbours(final, first)
    gated = [got["gated"] for got in attends]
    after_attend = [got["out"] for got in attends]
    got = depth_conv(row_len, devices, info, ends, gated, rim_before, rim_after, depthwise)
    mid = middle(
        devices, rows, info, gather(got["stats"]), counts, got["depth"], after_attend, feed_in,
        feed_in_bias, feed_out, convolve_out, norm_gain, norm_shift, biases,
        cotangent.reshape(tokens, model),
    )
    edge_before, edge_after = neighbours(mid["last"], mid["first"])
    totals = gather(mid["totals"])
    early = feed_weights(n, mid["gi"], mid["nf"], mid["act"], mid["gl"])
    totals, early = lax.optimization_barrier((totals, early))
    conv = conv_back(
        row_len, info, ends, depthwise, convolve_in, attend_out, norm_gain, totals, mid,
        edge_before, edge_after, rim_before, rim_after, gated,
        [got["paired"] for got in attends], after_attend,
    )
    early = side_weights(
        n, early, [got["nc"] for got in attends], conv["gp"], mid["sw"], mid["gcl"],
        [got["mixed"] for got in attends], conv["gal"],
    )
    early, gm = lax.optimization_barrier((early, conv["gm"]))
    early = scatter_sum(early)
    grads, halos, sofar = [], [], ()
    for row in each:
        got = attend_back(
            row, fronts[row], befores[row], afters[row], attends[row]["prob"], table, gm, sofar
        )
        sofar = (got["g_table"], got["vec"])
        grads.append(got)
        halos.append(neighbours(got["g_after"], got["g_before"]))
    end = [
        back(
            row, grads[row], halos[row], attend_in, fronts[row]["after"], conv["gas"], norm_gain
        )
        for row in each
    ]
    acts, normeds = [got["act"] for got in fronts], [got["na"] for got in fronts]
    lows, joined = [got["gl"] for got in end], [got["gj"] for got in end]
    b, b_send = late_weights(info, core_at, n, acts, lows, normeds, joined, sinusoid, sofar[0])
    b_got = [swap(b_send, 1)]
    got = first_back(
        info, core_at, n, lows, [got["slope"] for got in fronts], feed_in, feed_out,
        [got["n0"] for got in fronts], normeds, joined,
    )
    a, a_send = got["mine"], got["other"]
    a_got = [swap(a_send, 1)]
    ((b, b_send),) = fold("fold_b", info, row_at, [(b, b_got, "columns")])
    b_got = [lax.ppermute(b_send[0], "rows", ROW_PAIR)]
    ((a, a_send),) = fold("fold_a", info, row_at, [(a, a_got, (core_at + 1, 1, 2))])
    a_got = swaps(a_send, groups[0])
    gn, a = lax.optimization_barrier((got["gn"], a))
    ending = last(features, gn, [one["gfs"] for one in end], norm_gain)

    vec_conv, vec_mid, vec_back, vec_last = conv["vec"], mid["vec"], sum(one["vec"] for one in end), ending["vec"]
    small = jnp.concatenate(
        [
            vec_conv[:KERNEL],
            vec_last[0:1], vec_back[2:3], vec_conv[9:10], vec_mid[0:1], vec_mid[2:3],
            vec_last[1:2], vec_back[3:4], vec_conv[10:11], vec_mid[1:2], vec_mid[3:4],
            vec_back[0:2], vec_conv[13:14], vec_conv[11:13], vec_mid[4:5], vec_back[4:5],
            vec_mid[5:6], sofar[1][0:2],
            got["fb"].reshape(-1, model), mid["fb"].reshape(-1, model),
            jnp.zeros((3, model), f32),
        ],
        axis=0,
    )
    small = [small, swap(small, 1)]
    for at, group in enumerate(groups):
        deeper = at + 1 < len(groups)
        a_how = (core_at + 2 + at, 1, groups[at + 1][1]) if deeper else None
        states = [(a, a_got, a_how), (b, b_got, (core_at + 1 + at, 1, group[1]))]
        if at == 1:
            states.append((early, early_got, "wide"))
        folded = fold(f"fold_{at}", info, row_at, states, small)
        one = folded.pop()
        if at == 1:
            early = folded.pop()[0][0]
        (a, a_send), (b, b_send) = folded
        if at == 0:
            early, a = lax.optimization_barrier((early, a))
            early_got = [lax.ppermute(early, "rows", ROW_PAIR)]
        if deeper:
            a_got = swaps(a_send, groups[at + 1])
        else:
            a_got = [lax.ppermute(a, "rows", ROW_PAIR)]
        b_got = swaps(b_send, group)
        small = [one] + swaps([one] * (group[1] - 1), group)
    (b, _), one = fold("fold_last", info, row_at, [(b, b_got, None)], small)
    b_got = lax.ppermute(b, "rows", ROW_PAIR)
    small = one + lax.ppermute(one, "rows", ROW_PAIR)
    a = a[0].astype(f32) + a_got[0][0].astype(f32)
    first = lax.axis_index("rows") == 0
    b = jnp.concatenate(
        [jnp.where(first, b[0], b_got[0]), jnp.where(first, b_got[0], b[0])], axis=1
    ).astype(f32)
    slim = model // n
    width = hidden // n
    n_vectors = small.shape[0] - 3 - 2 * (hidden // model)
    vectors = jnp.concatenate([small[:n_vectors], vec_conv[14:16]], axis=0)
    thin = lax.dynamic_slice_in_dim(vectors, me * slim, slim, 1)
    feed_bias = small[n_vectors:-3].reshape(2, hidden)
    feed_bias = lax.dynamic_slice_in_dim(feed_bias, me * width, width, 1)
    return (
        mid["out"].reshape(rows, frames, model),
        ending["out"],
        jnp.stack([a[:width].T, early[:width, :model].T]),
        feed_bias,
        jnp.stack([b[:width], early[:width, model:]]),
        jnp.concatenate(
            [b[width : width + slim], b[width + slim : width + 2 * slim], a[width:]], axis=1
        ),
        early[width + slim :, model:],
        b[width + 2 * slim :],
        early[width : width + slim],
        early[width + slim :, :model],
        thin[:KERNEL],
        jnp.concatenate([thin[KERNEL : KERNEL + 5], thin[n_vectors + 1 :]], axis=0),
        jnp.concatenate([thin[KERNEL + 5 : KERNEL + 10], thin[n_vectors : n_vectors + 1]], axis=0),
        thin[KERNEL + 10 : n_vectors],
    )


def solution(mesh):
    placed = (
        P("rows", "frames", None),
        P(),
        P("rows"),
        P(),
        P(),
        P(),
        P(),
        P(),
        P(),
        P(),
        P(),
        P(),
        P(),
        P(),
        P(),
        P("rows", "frames", None),
    )
    return jax.shard_map(
        per_device,
        mesh=mesh,
        in_specs=placed,
        out_specs=(
            P("rows", "frames", None),
            P("rows", "frames", None),
            P(None, None, "frames"),
            P(None, "frames"),
            P(None, "frames", None),
            P("frames", None),
            P("frames", None),
            P("frames", None),
            P("frames", None),
            P("frames", None),
            P(None, "frames"),
            P(None, "frames"),
            P(None, "frames"),
            P(None, "frames"),
        ),
        check_vma=False,
    )
```

time: 1290 us -> 300 us (0.23)
  waiting for transfers between devices: 752 us -> 40.7 us
  Pallas kernels: 0 us -> 132 us
  blocking collectives: 124 us -> 0 us
  local copies, waits for them, and re-layouts: 136 us -> 18.8 us
  matrix products: 117 us -> 0 us
  other arithmetic: 118 us -> 5.25 us
  starting transfers between devices: 21.6 us -> 83 us
    reduce_scatter x7 -> x1, waiting for transfers between devices: 521 us -> 0.01 us  [scatter_sum(): return lax.psum_scatter(grads, 'frames', scatter_dimension=0, tiled=True)]
    unnamed x19 -> x1, waiting for transfers between devices: 181 us -> 0.02 us
    pallas_call x0 -> x21, Pallas kernels: none -> 132 us  [staged(): pl.pallas_call(run, in_specs=[pl.BlockSpec(memory_space=pltpu.SMEM)] * n_...]
    psum x3 -> x0, blocking collectives: 124 us -> none  [the longest x1 43.4 us: per_device(): first_sum = lax.psum(jnp.sum(depth * valid, axis=0), ('rows', 'frames'))]
    dot_general x40 -> x0, matrix products: 94.9 us -> none  [the longest x8 23.5 us: left_product(): lax.dot_general(left, right, rows_first, preferred_element_type=jnp.float32)]
    ppermute x8 -> x32, starting transfers between devices: 20.6 us -> 70.5 us  [the longest x15 33.3 us: swap(): return lax.ppermute(x, 'frames', [(i, i ^ k) for i in range(n)])]
    psum x2 -> x0, waiting for transfers between devices: 47.4 us -> none  [the longest x1 25.9 us: per_device(): lax.psum(summed[0].astype(jnp.bfloat16), 'rows').astype(jnp.float32)]
    convert_element_type x28 -> x3, other arithmetic: 35.7 us -> 0.06 us  [the longest x1 0.04 us: per_device(): b = jnp.concatenate([jnp.where(first, b[0], b_got[0]), jnp.where(first, b...]
  transfers between devices with their start and end apart: 22 -> 35, of which waited for: 14 -> 9; matrix products, arithmetic and copies ran while one was open for 21% -> 4% of each run, Pallas kernels for 0% -> 26%
where the time goes in v2:
time: 300 us; the launch traced here: 295 us
  Pallas kernels  132 us (44%)
  starting transfers between devices  83 us (28%)
  waiting for transfers between devices  40.7 us (14%)
  local copies, waits for them, and re-layouts  18.8 us (6%)
  between operations  15.2 us (5%)
  other arithmetic  5.25 us (2%)
    pallas_call x21, Pallas kernels, staged(): pl.pallas_call(run, in_specs=[pl.BlockSpec(memory_space=pltpu.SMEM)] * n_...  132 us
    ppermute x15, starting transfers between devices, swap(): return lax.ppermute(x, 'frames', [(i, i ^ k) for i in range(n)])  33.3 us
    ppermute x15, waiting for transfers between devices, swap(): return lax.ppermute(x, 'frames', [(i, i ^ k) for i in range(n)])  28.7 us
    ppermute x6, starting transfers between devices, neighbours(): lax.ppermute(last_block, 'frames', up)  22.5 us
    all_to_all x2, starting transfers between devices, gather(): return lax.all_to_all(copies, DEVICES, 0, 0, tiled=True)  12.4 us
    unnamed x79, local copies, waits for them, and re-layouts  11.6 us
    ppermute x6, starting transfers between devices, neighbours(): lax.ppermute(first_block, 'frames', down)  8.33 us
    all_to_all x2, waiting for transfers between devices, gather(): return lax.all_to_all(copies, DEVICES, 0, 0, tiled=True)  7.78 us
  transfers between devices with their start and end apart: 35, of which 9 were waited for; matrix products, arithmetic and copies ran while one was open for 4% of the time, Pallas kernels for 26%

profile of v2, /device:TPU:0, one launch (start us, length us, event | category | flops | bytes accessed | tf_op | source)
XLA Modules:
  0.0 294.5 jit_solution(18218027084512279143)
XLA Ops:
  7.2 5.3 %front.2 = (f32[256,512]{1,0:T(8,128)}, bf16[256,512]{1,0:T(8,128)(2,1)}, bf16[256,512]{1,0:T(8,128)(2,1)}, bf16[256,512]{1,0:T(8,128)(2,1)}, bf16[256,512]{1,0:...) custom-call(bf16[2,256,512]{2,1,0:T(8,128)(2,1)} %refs_1_.5, ...), custom_call_target="tpu_custom_call" | custom-call | flops 1476395008 | bytes 10485760 | tf_op jit(solution)/shard_map/front/pallas_call | solution.py:208
  12.5 2.4 collective-permute-start
  16.2 5.3 %front.3 = (f32[256,512]{1,0:T(8,128)}, bf16[256,512]{1,0:T(8,128)(2,1)}, bf16[256,512]{1,0:T(8,128)(2,1)}, bf16[256,512]{1,0:T(8,128)(2,1)}, bf16[256,512]{1,0:...) custom-call(bf16[2,256,512]{2,1,0:T(8,128)(2,1)} %refs_1_.5, ...), custom_call_target="tpu_custom_call" | custom-call | flops 1476395008 | bytes 10485760 | tf_op jit(solution)/shard_map/front/pallas_call | solution.py:208
  21.5 5.2 %collective-permute-start.2 = (bf16[128,1024]{1,0:T(8,128)(2,1)}, bf16[128,1024]{1,0:T(8,128)(2,1)S(1)}, u32[]{:S(2)}, u32[]{:S(2)}) collective-permute-start(bf16[128,1024]{1,0:T(8,128)(2,1)} %get-tuple-element.138.refs_7_.refs_5_), channel_id=1, source_target_pairs={{0,1},{1,2},{2,3},{3,4},{4,5},{5,6},{6,7},{7,8},{8,9},{9,10},{10,1... | collective-permute-start | bytes 786440 | tf_op jit(solution)/shard_map/ppermute | solution.py:1171
  30.7 10.4 %attend.2 = (bf16[2,2,128,1536]{3,2,1,0:T(8,128)(2,1)}, bf16[256,512]{1,0:T(8,128)(2,1)}, f32[256,512]{1,0:T(8,128)}, bf16[256,512]{1,0:T(8,128)(2,1)}, f32[256,...) custom-call(s32[9]{0:T(128)} %concatenate.21.refs_0_, ...), custom_call_target="tpu_custom_call" | custom-call | flops 805306368 | bytes 8388608 | tf_op jit(solution)/shard_map/attend/pallas_call | solution.py:208
  41.9 10.4 %attend.3 = (bf16[2,2,128,1536]{3,2,1,0:T(8,128)(2,1)}, bf16[256,512]{1,0:T(8,128)(2,1)}, f32[256,512]{1,0:T(8,128)}, bf16[256,512]{1,0:T(8,128)(2,1)}, f32[256,...) custom-call(s32[9]{0:T(128)} %concatenate.21.refs_0_, ...), custom_call_target="tpu_custom_call" | custom-call | flops 805306368 | bytes 8388608 | tf_op jit(solution)/shard_map/attend/pallas_call | solution.py:208
  52.3 4.3 %collective-permute-start.4 = (bf16[2,16,512]{2,1,0:T(8,128)(2,1)}, bf16[2,16,512]{2,1,0:T(8,128)(2,1)S(1)}, u32[]{:S(2)}, u32[]{:S(2)}) collective-permute-start(bf16[2,16,512]{2,1,0:T(8,128)(2,1)} %get-tuple-element.143), channel_id=1, source_target_pairs={{0,1},{1,2},{2,3},{3,4},{4,5},{5,6},{6,7},{7,8},{8,9},{9,10},{10,1... | collective-permute-start | bytes 98312 | tf_op jit(solution)/shard_map/ppermute | solution.py:1171
  56.6 1.7 collective-permute-start.5
  58.3 2.8 collective-permute-done.5.refs_6_.refs_9_
  61.7 5.9 %depth_conv.1 = (f32[512,512]{1,0:T(8,128)}, f32[32,8,128]{2,1,0:T(8,128)}) custom-call(s32[9]{0:T(128)} %concatenate.21.refs_0_, f32[8,128]{1,0:T(8,128)} %pad.4.refs_1_.refs_4_, bf16[2,16,512]{2,1,0:T(8,128)(2,1)} %copy-done.24, f32[9,512]{1,0:T(8,128)} %refs_5_.5, bf16[256,512]{1,0:T(8,128)(2,1)} %get-tuple-element.144.refs_4_.refs_12_, ...), custom_call_target="tpu_custom_call" | custom-call | flops 7864320 | bytes 2097152 | tf_op jit(solution)/shard_map/depth_conv/pallas_call | solution.py:208
  67.6 9.8 %all-to-all-start = ((f32[32,8,128]{2,1,0:T(8,128)}), f32[32,8,128]{2,1,0:T(8,128)S(1)}, u32[]{:S(2)}, u32[]{:S(2)}) async-start(f32[32,8,128]{2,1,0:T(8,128)} %get-tuple-element.147), calls=%async_computation | async-start | bytes 262144 | tf_op jit(solution)/shard_map/all_to_all | solution.py:1175
  77.9 7.8 %all-to-all-done.refs_1_ = f32[32,8,128]{2,1,0:T(8,128)S(1)} async-done(((f32[32,8,128]{2,1,0:T(8,128)}), f32[32,8,128]{2,1,0:T(8,128)S(1)}, u32[]{:S(2)}, u32[]{:S(2)}) %all-to-all-start) | async-done | bytes 131104 | tf_op jit(solution)/shard_map/all_to_all | solution.py:1175
  86.3 12.6 %middle.1 = (bf16[512,512]{1,0:T(8,128)(2,1)}, bf16[512,2048]{1,0:T(8,128)(2,1)}, bf16[512,2048]{1,0:T(8,128)(2,1)}, bf16[512,512]{1,0:T(8,128)(2,1)}, bf16[512,...) custom-call(s32[9]{0:T(128)} %concatenate.21.refs_0_, ...), custom_call_target="tpu_custom_call" | custom-call | flops 4831838208 | bytes 25165824 | tf_op jit(solution)/shard_map/middle/pallas_call | solution.py:208
  98.9 2.6 all-to-all-start.1
  101.5 2.0 collective-permute-start.6
  104.8 5.9 %feed_weights.1.refs_8_ = bf16[16,192,1024]{2,1,0:T(8,128)(2,1)} custom-call(bf16[512,512]{1,0:T(8,128)(2,1)} %get-tuple-element.157.refs_0_, bf16[512,2048]{1,0:T(8,128)(2,1)} %get-tuple-element.158.refs_1_, bf16[512,512]{1,0:T(8,128)(2,1)} %get-tuple-element.159.refs_2_, bf16[512,2048]{1,0:T(8,128)(2,1)} %get-tuple-element.160.refs_3_), custom_call_target="tpu_custom_call" | custom-call | flops 2147483648 | bytes 10485760 | tf_op jit(solution)/shard_map/feed_weights/pallas_call | solution.py:208
  111.5 12.1 %conv_back.1 = (bf16[512,1024]{1,0:T(8,128)(2,1)}, f32[512,512]{1,0:T(8,128)}, bf16[512,512]{1,0:T(8,128)(2,1)}, bf16[512,512]{1,0:T(8,128)(2,1)}, f32[16,512]{1,0:T(8,128)}) custom-call(s32[9]{0:T(128)} %concatenate.21.refs_0_, f32[32,8,128]{2,1,0:T(8,128)} %copy-done.15, f32[8,512]{1,0:T(8,128)} %get-tuple-element.162.refs_2_, f32[6,512]{1,0:T(8,128)} %refs_0_.9, ...), custom_call_target="tpu_custom_call" | custom-call | flops 805306368 | bytes 12582912 | tf_op jit(solution)/shard_map/conv_back/pallas_call | solution.py:208
  123.6 4.6 %side_weights.1 = bf16[16,192,1024]{2,1,0:T(8,128)(2,1)} custom-call(bf16[256,512]{1,0:T(8,128)(2,1)} %get-tuple-element.154.refs_0_, bf16[256,512]{1,0:T(8,128)(2,1)} %get-tuple-element.155.refs_1_, bf16[512,1024]{1,0:T(8,128)(2,1)} %get-tuple-element.170.refs_2_, bf16[512,512]{1,0:T(8,128)(2,1)} %get-tuple-element.171.refs_3_, ...), custom_call_target="tpu_custom_call", output_to_operand_aliasing={{}: (8, {})} | custom-call | flops 1073741824 | bytes 6291456 | tf_op jit(solution)/shard_map/side_weights/pallas_call | solution.py:208
  128.2 8.6 %attend_back.2 = (bf16[256,512]{1,0:T(8,128)(2,1)}, bf16[128,1024]{1,0:T(8,128)(2,1)}, f32[128,1024]{1,0:T(8,128)}, f32[128,1024]{1,0:T(8,128)}, bf16[128,1024]{...) custom-call(bf16[512,512]{1,0:T(8,128)(2,1)} %get-tuple-element.178.refs_0_, ...), custom_call_target="tpu_custom_call" | custom-call | flops 1409286144 | bytes 8388608 | tf_op jit(solution)/shard_map/attend_back/pallas_call | solution.py:208
  136.8 9.6 %attend_back.3 = (bf16[256,512]{1,0:T(8,128)(2,1)}, bf16[128,1024]{1,0:T(8,128)(2,1)}, f32[128,1024]{1,0:T(8,128)}, f32[128,1024]{1,0:T(8,128)}, bf16[128,1024]{...) custom-call(bf16[512,512]{1,0:T(8,128)(2,1)} %get-tuple-element.178.refs_0_, ...), custom_call_target="tpu_custom_call" | custom-call | flops 1409286144 | bytes 8388608 | tf_op jit(solution)/shard_map/attend_back/pallas_call | solution.py:208
  146.5 4.4 %collective-permute-start.10 = (bf16[128,1024]{1,0:T(8,128)(2,1)}, bf16[128,1024]{1,0:T(8,128)(2,1)S(1)}, u32[]{:S(2)}, u32[]{:S(2)}) collective-permute-start(bf16[128,1024]{1,0:T(8,128)(2,1)} %get-tuple-element.192), channel_id=1, source_target_pairs={{0,1},{1,2},{2,3},{3,4},{4,5},{5,6},{6,7},{7,8},{8,9},{9,10},{10,1... | collective-permute-start | bytes 786440 | tf_op jit(solution)/shard_map/ppermute | solution.py:1171
  152.2 4.3 %collective-permute-start.8 = (bf16[128,1024]{1,0:T(8,128)(2,1)S(1)}, bf16[128,1024]{1,0:T(8,128)(2,1)S(1)}, u32[]{:S(2)}, u32[]{:S(2)}) collective-permute-start(bf16[128,1024]{1,0:T(8,128)(2,1)S(1)} %copy-done.38), channel_id=1, source_target_pairs={{0,1},{1,2},{2,3},{3,4},{4,5},{5,6},{6,7},{7,8},{8,9},{9,10},{10,1... | collective-permute-start | bytes 786440 | tf_op jit(solution)/shard_map/ppermute | solution.py:1171
  158.6 4.0 %back.3 = (bf16[256,1536]{1,0:T(8,128)(2,1)}, f32[256,512]{1,0:T(8,128)}, bf16[256,512]{1,0:T(8,128)(2,1)}, f32[8,512]{1,0:T(8,128)}) custom-call(f32[6,512]{1,0:T(8,128)} %refs_0_.9, bf16[256,512]{1,0:T(8,128)(2,1)} %get-tuple-element.190.refs_1_, f32[128,1024]{1,0:T(8,128)} %get-tuple-element.191.refs_2_, bf16[128,1024]{1,0:T(8,128)(2,1)} %copy-done.22, ...), custom_call_target="tpu_custom_call" | custom-call | flops 402653184 | bytes 5242880 | tf_op jit(solution)/shard_map/back/pallas_call | solution.py:208
  163.5 4.0 %back.2 = (bf16[256,1536]{1,0:T(8,128)(2,1)}, f32[256,512]{1,0:T(8,128)}, bf16[256,512]{1,0:T(8,128)(2,1)}, f32[8,512]{1,0:T(8,128)}) custom-call(f32[6,512]{1,0:T(8,128)} %refs_0_.9, bf16[256,512]{1,0:T(8,128)(2,1)} %get-tuple-element.180.refs_1_, f32[128,1024]{1,0:T(8,128)} %get-tuple-element.181.refs_2_, bf16[128,1024]{1,0:T(8,128)(2,1)} %copy-done.20, ...), custom_call_target="tpu_custom_call" | custom-call | flops 402653184 | bytes 5242880 | tf_op jit(solution)/shard_map/back/pallas_call | solution.py:208
  167.5 6.7 %late_weights.1 = (bf16[8,224,512]{2,1,0:T(8,128)(2,1)}, bf16[8,224,512]{2,1,0:T(8,128)(2,1)}) custom-call(s32[9]{0:T(128)} %concatenate.21.refs_0_, bf16[256,512]{1,0:T(8,128)(2,1)} %get-tuple-element.152.refs_1_, bf16[256,512]{1,0:T(8,128)(2,1)} %get-tuple-element.153.refs_2_, bf16[256,1536]{1,0:T(8,128)(2,1)} %get-tuple-element.186.refs_3_, ...), custom_call_target="tpu_custom_call" | custom-call | flops 1879048192 | bytes 9437184 | tf_op jit(solution)/shard_map/late_weights/pallas_call | solution.py:208
  174.2 6.9 %collective-permute-start.14 = (bf16[8,224,512]{2,1,0:T(8,128)(2,1)}, bf16[8,224,512]{2,1,0:T(8,128)(2,1)}, u32[]{:S(2)}, u32[]{:S(2)}) collective-permute-start(bf16[8,224,512]{2,1,0:T(8,128)(2,1)} %get-tuple-element.217), channel_id=1, source_target_pairs={{0,1},{1,0},{2,3},{3,2},{4,5},{5,4},{6,7},{7,6},{8,9},{9,8},{10,11... | collective-permute-start | bytes 5505032 | tf_op jit(solution)/shard_map/ppermute | solution.py:1187
  181.1 8.8 %first_back.1 = (bf16[8,160,512]{2,1,0:T(8,128)(2,1)}, bf16[8,160,512]{2,1,0:T(8,128)(2,1)}, f32[1,2048]{1,0:T(1,128)}, f32[512,512]{1,0:T(8,128)}) custom-call(s32[9]{0:T(128)} %concatenate.21.refs_0_, bf16[256,512]{1,0:T(8,128)(2,1)} %get-tuple-element.152.refs_1_, bf16[256,512]{1,0:T(8,128)(2,1)} %get-tuple-element.153.refs_2_, ...), custom_call_target="tpu_custom_call" | custom-call | flops 3221225472 | bytes 12582912 | tf_op jit(solution)/shard_map/first_back/pallas_call | solution.py:208
  191.3 3.9 %fold_b.1 = (bf16[8,224,256]{2,1,0:T(8,128)(2,1)S(1)}, bf16[8,224,256]{2,1,0:T(8,128)(2,1)}) custom-call(s32[9]{0:T(128)S(1)} %copy-done.12, bf16[8,224,512]{2,1,0:T(8,128)(2,1)S(1)} %copy-done.1, bf16[8,224,512]{2,1,0:T(8,128)(2,1)} %collective-permute-done.14.refs_2_), custom_call_target="tpu_custom_call" | custom-call | flops 1048576 | bytes 2097152 | tf_op jit(solution)/shard_map/fold_b/pallas_call | solution.py:208
  196.2 1.6 collective-permute-start.15
  198.5 1.8 fold_a.1
  201.1 9.1 %collective-permute-start.13 = (bf16[4,160,512]{2,1,0:T(8,128)(2,1)}, bf16[4,160,512]{2,1,0:T(8,128)(2,1)}, u32[]{:S(2)}, u32[]{:S(2)}) collective-permute-start(bf16[4,160,512]{2,1,0:T(8,128)(2,1)} %bitcast.11), channel_id=1, source_target_pairs={{0,2},{1,3},{2,0},{3,1},{4,6},{5,7},{6,4},{7,5},{8,10},{9,11},{10,... | collective-permute-start | bytes 1966088 | tf_op jit(solution)/shard_map/ppermute | solution.py:1187
  213.2 2.2 last.1
  216.9 8.7 %collective-permute-done.13 = bf16[4,160,512]{2,1,0:T(8,128)(2,1)} collective-permute-done((bf16[4,160,512]{2,1,0:T(8,128)(2,1)}, bf16[4,160,512]{2,1,0:T(8,128)(2,1)}, u32[]{:S(2)}, u32[]{:S(2)}) %collective-permute-start.13) | collective-permute-done | bytes 655392 | tf_op jit(solution)/shard_map/ppermute | solution.py:1187
  225.7 3.6 %fold_0.1 = (bf16[1,1,160,512]{3,2,1,0:T(8,128)(2,1)S(1)}, bf16[1,1,160,512]{3,2,1,0:T(8,128)(2,1)S(1)}, bf16[1,1,160,512]{3,2,1,0:T(8,128)(2,1)S(1)}, bf16[1,1,...) custom-call(s32[9]{0:T(128)S(1)} %copy-done.12, ...), custom_call_target="tpu_custom_call" | custom-call | flops 1048576 | bytes 2097152 | tf_op jit(solution)/shard_map/fold_0/pallas_call | solution.py:208
  230.7 2.8 collective-permute-start.20
  235.5 2.4 collective-permute-start.18
  237.9 7.9 %collective-permute-done.22.refs_10_ = f32[40,512]{1,0:T(8,128)S(1)} collective-permute-done((f32[40,512]{1,0:T(8,128)S(1)}, f32[40,512]{1,0:T(8,128)S(1)}, u32[]{:S(2)}, u32[]{:S(2)}) %collective-permute-start.22) | collective-permute-done | bytes 81952 | tf_op jit(solution)/shard_map/ppermute | solution.py:1187
  245.8 2.2 collective-permute-start.19
  248.0 4.9 %collective-permute-done.19.refs_4_ = bf16[1,160,512]{2,1,0:T(8,128)(2,1)S(1)} collective-permute-done((bf16[1,160,512]{2,1,0:T(8,128)(2,1)S(1)}, bf16[1,160,512]{2,1,0:T(8,128)(2,1)S(1)}, u32[]{:S(2)}, u32[]{:S(2)}) %collective-permute-start.19) | collective-permute-done | bytes 163872 | tf_op jit(solution)/shard_map/ppermute | solution.py:1187
  254.0 4.0 %fold_1.1 = (bf16[1,160,512]{2,1,0:T(8,128)(2,1)S(1)}, bf16[1,1,224,256]{3,2,1,0:T(8,128)(2,1)S(1)}, bf16[1,1,224,256]{3,2,1,0:T(8,128)(2,1)S(1)}, bf16[1,1,224,...) custom-call(s32[9]{0:T(128)S(1)} %copy-done.12, ...), custom_call_target="tpu_custom_call" | custom-call | flops 1048576 | bytes 2097152 | tf_op jit(solution)/shard_map/fold_1/pallas_call | solution.py:208
  258.0 2.2 collective-permute-start.27
  260.8 1.8 collective-permute-start.29
  263.7 1.6 collective-permute-start.25
  265.9 1.8 collective-permute-start.26
  267.8 2.8 collective-permute-done.28.refs_7_
  272.4 3.1 %collective-permute-done.25.refs_3_ = bf16[1,224,256]{2,1,0:T(8,128)(2,1)S(1)} collective-permute-done((bf16[1,224,256]{2,1,0:T(8,128)(2,1)S(1)}, bf16[1,224,256]{2,1,0:T(8,128)(2,1)S(1)}, u32[]{:S(2)}, u32[]{:S(2)}) %collective-permute-start.25) | collective-permute-done | bytes 114720 | tf_op jit(solution)/shard_map/ppermute | solution.py:1187
  275.5 2.0 fold_last.1
  277.5 2.0 collective-permute-start.30
  (174 shorter events, 38.6 us)
Async XLA Ops:
  12.5 17.4 %collective-permute-start = (bf16[128,1024]{1,0:T(8,128)(2,1)}, bf16[128,1024]{1,0:T(8,128)(2,1)S(1)}, u32[]{:S(2)}, u32[]{:S(2)}) collective-permute-start(bf16[128,1024]{1,0:T(8,128)(2,1)} %get-tuple-element.132.refs_8_.refs_5_), channel_id=1, source_target_pairs={{0,1},{1,2},{2,3},{3,4},{4,5},{5,6},{6,7},{7,8},{8,9},{9,10},{10,1... | collective-permute-start | bytes 786440 | tf_op jit(solution)/shard_map/ppermute | solution.py:1171
  14.9 13.3 %copy-start.35 = (s32[4,17]{1,0:T(4,128)S(1)}, s32[4,17]{1,0:T(4,128)}, u32[]{:S(2)}) copy-start(s32[4,17]{1,0:T(4,128)} %param.18) | copy-start | bytes 820
  14.9 14.3 %copy-start.36 = (s32[2]{0:T(128)S(1)}, s32[2]{0:T(128)}, u32[]{:S(2)}) copy-start(s32[2]{0:T(128)} %param.19) | copy-start | bytes 28
  14.9 15.0 %collective-permute-start.1 = (bf16[128,1024]{1,0:T(8,128)(2,1)}, bf16[128,1024]{1,0:T(8,128)(2,1)S(1)}, u32[]{:S(2)}, u32[]{:S(2)}) collective-permute-start(bf16[128,1024]{1,0:T(8,128)(2,1)} %get-tuple-element.133.refs_7_.refs_4_), channel_id=1, source_target_pairs={{1,0},{2,1},{3,2},{4,3},{5,4},{6,5},{7,6},{8,7},{9,8},{10,9},{11,1... | collective-permute-start | bytes 786440 | tf_op jit(solution)/shard_map/ppermute | solution.py:1171
  21.5 19.6 %collective-permute-start.2 = (bf16[128,1024]{1,0:T(8,128)(2,1)}, bf16[128,1024]{1,0:T(8,128)(2,1)S(1)}, u32[]{:S(2)}, u32[]{:S(2)}) collective-permute-start(bf16[128,1024]{1,0:T(8,128)(2,1)} %get-tuple-element.138.refs_7_.refs_5_), channel_id=1, source_target_pairs={{0,1},{1,2},{2,3},{3,4},{4,5},{5,6},{6,7},{7,8},{8,9},{9,10},{10,1... | collective-permute-start | bytes 786440 | tf_op jit(solution)/shard_map/ppermute | solution.py:1171
  26.7 14.5 %collective-permute-start.3 = (bf16[128,1024]{1,0:T(8,128)(2,1)}, bf16[128,1024]{1,0:T(8,128)(2,1)S(1)}, u32[]{:S(2)}, u32[]{:S(2)}) collective-permute-start(bf16[128,1024]{1,0:T(8,128)(2,1)} %get-tuple-element.139.refs_6_.refs_4_), channel_id=1, source_target_pairs={{1,0},{2,1},{3,2},{4,3},{5,4},{6,5},{7,6},{8,7},{9,8},{10,9},{11,1... | collective-permute-start | bytes 786440 | tf_op jit(solution)/shard_map/ppermute | solution.py:1171
  52.3 6.0 %collective-permute-start.4 = (bf16[2,16,512]{2,1,0:T(8,128)(2,1)}, bf16[2,16,512]{2,1,0:T(8,128)(2,1)S(1)}, u32[]{:S(2)}, u32[]{:S(2)}) collective-permute-start(bf16[2,16,512]{2,1,0:T(8,128)(2,1)} %get-tuple-element.143), channel_id=1, source_target_pairs={{0,1},{1,2},{2,3},{3,4},{4,5},{5,6},{6,7},{7,8},{8,9},{9,10},{10,1... | collective-permute-start | bytes 98312 | tf_op jit(solution)/shard_map/ppermute | solution.py:1171
  56.6 4.6 %collective-permute-start.5 = (bf16[2,16,512]{2,1,0:T(8,128)(2,1)}, bf16[2,16,512]{2,1,0:T(8,128)(2,1)S(1)}, u32[]{:S(2)}, u32[]{:S(2)}) collective-permute-start(bf16[2,16,512]{2,1,0:T(8,128)(2,1)} %get-tuple-element.146), channel_id=1, source_target_pairs={{1,0},{2,1},{3,2},{4,3},{5,4},{6,5},{7,6},{8,7},{9,8},{10,9},{11,1... | collective-permute-start | bytes 98312 | tf_op jit(solution)/shard_map/ppermute | solution.py:1171
  67.6 18.0 %all-to-all-start = ((f32[32,8,128]{2,1,0:T(8,128)}), f32[32,8,128]{2,1,0:T(8,128)S(1)}, u32[]{:S(2)}, u32[]{:S(2)}) async-start(f32[32,8,128]{2,1,0:T(8,128)} %get-tuple-element.147), calls=%async_computation | async-start | bytes 262144 | tf_op jit(solution)/shard_map/all_to_all | solution.py:1175
  98.9 11.9 %all-to-all-start.1 = ((f32[32,8,128]{2,1,0:T(8,128)}), f32[32,8,128]{2,1,0:T(8,128)S(1)}, u32[]{:S(2)}, u32[]{:S(2)}) async-start(f32[32,8,128]{2,1,0:T(8,128)} %get-tuple-element.156), calls=%async_computation.1 | async-start | bytes 262144 | tf_op jit(solution)/shard_map/all_to_all | solution.py:1175
  101.5 132.0 %reduce-scatter.2.cloned.1.call-start = ((), (), s32[]{:S(2)}) async-start(), calls=%async_computation.3 | async-start | bytes 6684672 | tf_op jit(solution)/shard_map/reduce_scatter | solution.py:1179
  101.5 9.3 %collective-permute-start.6 = (f32[2,8,1024]{2,1,0:T(8,128)}, f32[2,8,1024]{2,1,0:T(8,128)S(1)}, u32[]{:S(2)}, u32[]{:S(2)}) collective-permute-start(f32[2,8,1024]{2,1,0:T(8,128)} %get-tuple-element.163), channel_id=1, source_target_pairs={{0,1},{1,2},{2,3},{3,4},{4,5},{5,6},{6,7},{7,8},{8,9},{9,10},{10,1... | collective-permute-start | bytes 196616 | tf_op jit(solution)/shard_map/ppermute | solution.py:1171
  103.5 7.3 %collective-permute-start.7 = (f32[2,8,1024]{2,1,0:T(8,128)}, f32[2,8,1024]{2,1,0:T(8,128)S(1)}, u32[]{:S(2)}, u32[]{:S(2)}) collective-permute-start(f32[2,8,1024]{2,1,0:T(8,128)} %get-tuple-element.164), channel_id=1, source_target_pairs={{1,0},{2,1},{3,2},{4,3},{5,4},{6,5},{7,6},{8,7},{9,8},{10,9},{11,1... | collective-permute-start | bytes 196616 | tf_op jit(solution)/shard_map/ppermute | solution.py:1171
  136.8 15.4 %copy-start.38 = (bf16[128,1024]{1,0:T(8,128)(2,1)S(1)}, bf16[128,1024]{1,0:T(8,128)(2,1)}, u32[]{:S(2)}) copy-start(bf16[128,1024]{1,0:T(8,128)(2,1)} %get-tuple-element.182) | copy-start | bytes 786436
  136.8 19.7 %copy-start.37 = (bf16[128,1024]{1,0:T(8,128)(2,1)S(1)}, bf16[128,1024]{1,0:T(8,128)(2,1)}, u32[]{:S(2)}) copy-start(bf16[128,1024]{1,0:T(8,128)(2,1)} %get-tuple-element.184) | copy-start | bytes 786436
  146.5 11.3 %collective-permute-start.10 = (bf16[128,1024]{1,0:T(8,128)(2,1)}, bf16[128,1024]{1,0:T(8,128)(2,1)S(1)}, u32[]{:S(2)}, u32[]{:S(2)}) collective-permute-start(bf16[128,1024]{1,0:T(8,128)(2,1)} %get-tuple-element.192), channel_id=1, source_target_pairs={{0,1},{1,2},{2,3},{3,4},{4,5},{5,6},{6,7},{7,8},{8,9},{9,10},{10,1... | collective-permute-start | bytes 786440 | tf_op jit(solution)/shard_map/ppermute | solution.py:1171
  150.9 7.0 %collective-permute-start.11 = (bf16[128,1024]{1,0:T(8,128)(2,1)}, bf16[128,1024]{1,0:T(8,128)(2,1)S(1)}, u32[]{:S(2)}, u32[]{:S(2)}) collective-permute-start(bf16[128,1024]{1,0:T(8,128)(2,1)} %get-tuple-element.194), channel_id=1, source_target_pairs={{1,0},{2,1},{3,2},{4,3},{5,4},{6,5},{7,6},{8,7},{9,8},{10,9},{11,1... | collective-permute-start | bytes 786440 | tf_op jit(solution)/shard_map/ppermute | solution.py:1171
  152.2 10.5 %collective-permute-start.8 = (bf16[128,1024]{1,0:T(8,128)(2,1)S(1)}, bf16[128,1024]{1,0:T(8,128)(2,1)S(1)}, u32[]{:S(2)}, u32[]{:S(2)}) collective-permute-start(bf16[128,1024]{1,0:T(8,128)(2,1)S(1)} %copy-done.38), channel_id=1, source_target_pairs={{0,1},{1,2},{2,3},{3,4},{4,5},{5,6},{6,7},{7,8},{8,9},{9,10},{10,1... | collective-permute-start | bytes 786440 | tf_op jit(solution)/shard_map/ppermute | solution.py:1171
  156.5 6.2 %collective-permute-start.9 = (bf16[128,1024]{1,0:T(8,128)(2,1)S(1)}, bf16[128,1024]{1,0:T(8,128)(2,1)S(1)}, u32[]{:S(2)}, u32[]{:S(2)}) collective-permute-start(bf16[128,1024]{1,0:T(8,128)(2,1)S(1)} %copy-done.37), channel_id=1, source_target_pairs={{1,0},{2,1},{3,2},{4,3},{5,4},{6,5},{7,6},{8,7},{9,8},{10,9},{11,1... | collective-permute-start | bytes 786440 | tf_op jit(solution)/shard_map/ppermute | solution.py:1171
  174.2 17.1 %collective-permute-start.14 = (bf16[8,224,512]{2,1,0:T(8,128)(2,1)}, bf16[8,224,512]{2,1,0:T(8,128)(2,1)}, u32[]{:S(2)}, u32[]{:S(2)}) collective-permute-start(bf16[8,224,512]{2,1,0:T(8,128)(2,1)} %get-tuple-element.217), channel_id=1, source_target_pairs={{0,1},{1,0},{2,3},{3,2},{4,5},{5,4},{6,7},{7,6},{8,9},{9,8},{10,11... | collective-permute-start | bytes 5505032 | tf_op jit(solution)/shard_map/ppermute | solution.py:1187
  189.9 8.6 %collective-permute-start.12 = (bf16[8,160,512]{2,1,0:T(8,128)(2,1)}, bf16[8,160,512]{2,1,0:T(8,128)(2,1)S(1)}, u32[]{:S(2)}, u32[]{:S(2)}) collective-permute-start(bf16[8,160,512]{2,1,0:T(8,128)(2,1)} %get-tuple-element.204), channel_id=1, source_target_pairs={{0,1},{1,0},{2,3},{3,2},{4,5},{5,4},{6,7},{7,6},{8,9},{9,8},{10,11... | collective-permute-start | bytes 3932168 | tf_op jit(solution)/shard_map/ppermute | solution.py:1187
  196.1 14.1 %copy-start.27 = (f32[16,512]{1,0:T(8,128)S(1)}, f32[16,512]{1,0:T(8,128)}, u32[]{:S(2)}) copy-start(f32[16,512]{1,0:T(8,128)} %get-tuple-element.220) | copy-start | bytes 98308
  196.1 14.2 %copy-start.30 = (f32[8,512]{1,0:T(8,128)S(1)}, f32[8,512]{1,0:T(8,128)}, u32[]{:S(2)}) copy-start(f32[8,512]{1,0:T(8,128)} %get-tuple-element.223) | copy-start | bytes 49156
  196.1 14.2 %copy-start.31 = (f32[8,512]{1,0:T(8,128)S(1)}, f32[8,512]{1,0:T(8,128)}, u32[]{:S(2)}) copy-start(f32[8,512]{1,0:T(8,128)} %get-tuple-element.222) | copy-start | bytes 49156
  196.1 14.2 %copy-start.34 = (f32[1,2048]{1,0:T(1,128)S(1)}, f32[1,2048]{1,0:T(1,128)}, u32[]{:S(2)}) copy-start(f32[1,2048]{1,0:T(1,128)} %get-tuple-element.226) | copy-start | bytes 24580
  196.1 14.9 %copy-start = (bf16[2,256,512]{2,1,0:T(8,128)(2,1)S(1)}, bf16[2,256,512]{2,1,0:T(8,128)(2,1)}, u32[]{:S(2)}) copy-start(bf16[2,256,512]{2,1,0:T(8,128)(2,1)} %refs_1_.5) | copy-start | bytes 1572868
  196.2 14.9 %copy-start.3 = (f32[6,512]{1,0:T(8,128)S(1)}, f32[6,512]{1,0:T(8,128)}, u32[]{:S(2)}) copy-start(f32[6,512]{1,0:T(8,128)} %refs_0_.9) | copy-start | bytes 36868
  196.2 14.9 %copy-start.4 = (f32[512,512]{1,0:T(8,128)S(1)}, f32[512,512]{1,0:T(8,128)}, u32[]{:S(2)}) copy-start(f32[512,512]{1,0:T(8,128)} %get-tuple-element.206.refs_2_) | copy-start | bytes 3145732
  196.2 29.5 %collective-permute-start.15 = (bf16[8,224,256]{2,1,0:T(8,128)(2,1)}, bf16[8,224,256]{2,1,0:T(8,128)(2,1)}, u32[]{:S(2)}, u32[]{:S(2)}) collective-permute-start(bf16[8,224,256]{2,1,0:T(8,128)(2,1)} %get-tuple-element.219), channel_id=1, source_target_pairs={{0,16},{16,0},{1,17},{17,1},{2,18},{18,2},{3,19},{19,3},{4,20},{20... | collective-permute-start | bytes 2752520 | tf_op jit(solution)/shard_map/ppermute | solution.py:1381
  201.1 24.5 %copy-start.6 = (bf16[8,224,256]{2,1,0:T(8,128)(2,1)S(1)}, bf16[8,224,256]{2,1,0:T(8,128)(2,1)}, u32[]{:S(2)}) copy-start(bf16[8,224,256]{2,1,0:T(8,128)(2,1)} %copy-done.5) | copy-start | bytes 2752516
  201.1 24.5 %copy-start.8 = (bf16[4,1,160,512]{3,2,1,0:T(8,128)(2,1)S(1)}, bf16[4,1,160,512]{3,2,1,0:T(8,128)(2,1)}, u32[]{:S(2)}) copy-start(bf16[4,1,160,512]{3,2,1,0:T(8,128)(2,1)} %copy-done.7) | copy-start | bytes 1966084
  201.1 24.5 %collective-permute-start.13 = (bf16[4,160,512]{2,1,0:T(8,128)(2,1)}, bf16[4,160,512]{2,1,0:T(8,128)(2,1)}, u32[]{:S(2)}, u32[]{:S(2)}) collective-permute-start(bf16[4,160,512]{2,1,0:T(8,128)(2,1)} %bitcast.11), channel_id=1, source_target_pairs={{0,2},{1,3},{2,0},{3,1},{4,6},{5,7},{6,4},{7,5},{8,10},{9,11},{10,... | collective-permute-start | bytes 1966088 | tf_op jit(solution)/shard_map/ppermute | solution.py:1187
  215.6 1.3 collective-permute-start.16
  230.7 22.3 %collective-permute-start.20 = (bf16[4,224,256]{2,1,0:T(8,128)(2,1)}, bf16[4,224,256]{2,1,0:T(8,128)(2,1)S(1)}, u32[]{:S(2)}, u32[]{:S(2)}) collective-permute-start(bf16[4,224,256]{2,1,0:T(8,128)(2,1)} %bitcast.20), channel_id=1, source_target_pairs={{0,2},{1,3},{2,0},{3,1},{4,6},{5,7},{6,4},{7,5},{8,10},{9,11},{10,... | collective-permute-start | bytes 1376264 | tf_op jit(solution)/shard_map/ppermute | solution.py:1187
  233.5 19.5 %collective-permute-start.21 = (bf16[1,192,1024]{2,1,0:T(8,128)(2,1)}, bf16[1,192,1024]{2,1,0:T(8,128)(2,1)S(1)}, u32[]{:S(2)}, u32[]{:S(2)}) collective-permute-start(bf16[1,192,1024]{2,1,0:T(8,128)(2,1)} %reduce-scatter.2.cloned.1.call-done.refs_7_), channel_id=1, source_target_pairs={{0,16},{16,0},{1,17},{17,1},{2,18},{18,2},{3,19},{19,3},{4,20},{20... | collective-permute-start | bytes 1179656 | tf_op jit(solution)/shard_map/ppermute | solution.py:1414
  234.9 10.9 %collective-permute-start.22 = (f32[40,512]{1,0:T(8,128)S(1)}, f32[40,512]{1,0:T(8,128)S(1)}, u32[]{:S(2)}, u32[]{:S(2)}) collective-permute-start(f32[40,512]{1,0:T(8,128)S(1)} %get-tuple-element.236.refs_9_), channel_id=1, source_target_pairs={{0,2},{1,3},{2,0},{3,1},{4,6},{5,7},{6,4},{7,5},{8,10},{9,11},{10,... | collective-permute-start | bytes 245768 | tf_op jit(solution)/shard_map/ppermute | solution.py:1187
  235.0 13.1 %collective-permute-start.17 = (bf16[1,160,512]{2,1,0:T(8,128)(2,1)}, bf16[1,160,512]{2,1,0:T(8,128)(2,1)S(1)}, u32[]{:S(2)}, u32[]{:S(2)}) collective-permute-start(bf16[1,160,512]{2,1,0:T(8,128)(2,1)} %bitcast.62), channel_id=1, source_target_pairs={{0,4},{1,5},{2,6},{3,7},{4,0},{5,1},{6,2},{7,3},{8,12},{9,13},{10,... | collective-permute-start | bytes 491528 | tf_op jit(solution)/shard_map/ppermute | solution.py:1187
  235.5 12.5 %collective-permute-start.18 = (bf16[1,160,512]{2,1,0:T(8,128)(2,1)}, bf16[1,160,512]{2,1,0:T(8,128)(2,1)S(1)}, u32[]{:S(2)}, u32[]{:S(2)}) collective-permute-start(bf16[1,160,512]{2,1,0:T(8,128)(2,1)} %bitcast.61), channel_id=1, source_target_pairs={{0,8},{1,9},{2,10},{3,11},{4,12},{5,13},{6,14},{7,15},{8,0},{9,1},... | collective-permute-start | bytes 491528 | tf_op jit(solution)/shard_map/ppermute | solution.py:1187
  245.8 7.2 %collective-permute-start.19 = (bf16[1,160,512]{2,1,0:T(8,128)(2,1)S(1)}, bf16[1,160,512]{2,1,0:T(8,128)(2,1)S(1)}, u32[]{:S(2)}, u32[]{:S(2)}) collective-permute-start(bf16[1,160,512]{2,1,0:T(8,128)(2,1)S(1)} %bitcast.60), channel_id=1, source_target_pairs={{0,12},{1,13},{2,14},{3,15},{4,8},{5,9},{6,10},{7,11},{8,4},{9,5},... | collective-permute-start | bytes 491528 | tf_op jit(solution)/shard_map/ppermute | solution.py:1187
  258.0 8.0 %collective-permute-start.27 = (f32[40,512]{1,0:T(8,128)S(1)}, f32[40,512]{1,0:T(8,128)S(1)}, u32[]{:S(2)}, u32[]{:S(2)}) collective-permute-start(f32[40,512]{1,0:T(8,128)S(1)} %get-tuple-element.243.refs_5_), channel_id=1, source_target_pairs={{0,4},{1,5},{2,6},{3,7},{4,0},{5,1},{6,2},{7,3},{8,12},{9,13},{10,... | collective-permute-start | bytes 245768 | tf_op jit(solution)/shard_map/ppermute | solution.py:1187
  260.2 10.4 %collective-permute-start.28 = (f32[40,512]{1,0:T(8,128)S(1)}, f32[40,512]{1,0:T(8,128)S(1)}, u32[]{:S(2)}, u32[]{:S(2)}) collective-permute-start(f32[40,512]{1,0:T(8,128)S(1)} %get-tuple-element.243.refs_5_), channel_id=1, source_target_pairs={{0,8},{1,9},{2,10},{3,11},{4,12},{5,13},{6,14},{7,15},{8,0},{9,1},... | collective-permute-start | bytes 245768 | tf_op jit(solution)/shard_map/ppermute | solution.py:1187
  260.8 11.6 %collective-permute-start.29 = (f32[40,512]{1,0:T(8,128)S(1)}, f32[40,512]{1,0:T(8,128)S(1)}, u32[]{:S(2)}, u32[]{:S(2)}) collective-permute-start(f32[40,512]{1,0:T(8,128)S(1)} %get-tuple-element.243.refs_5_), channel_id=1, source_target_pairs={{0,12},{1,13},{2,14},{3,15},{4,8},{5,9},{6,10},{7,11},{8,4},{9,5},... | collective-permute-start | bytes 245768 | tf_op jit(solution)/shard_map/ppermute | solution.py:1187
  262.6 9.8 %collective-permute-start.24 = (bf16[1,224,256]{2,1,0:T(8,128)(2,1)S(1)}, bf16[1,224,256]{2,1,0:T(8,128)(2,1)S(1)}, u32[]{:S(2)}, u32[]{:S(2)}) collective-permute-start(bf16[1,224,256]{2,1,0:T(8,128)(2,1)S(1)} %bitcast.65), channel_id=1, source_target_pairs={{0,4},{1,5},{2,6},{3,7},{4,0},{5,1},{6,2},{7,3},{8,12},{9,13},{10,... | collective-permute-start | bytes 344072 | tf_op jit(solution)/shard_map/ppermute | solution.py:1187
  263.7 11.9 %collective-permute-start.25 = (bf16[1,224,256]{2,1,0:T(8,128)(2,1)S(1)}, bf16[1,224,256]{2,1,0:T(8,128)(2,1)S(1)}, u32[]{:S(2)}, u32[]{:S(2)}) collective-permute-start(bf16[1,224,256]{2,1,0:T(8,128)(2,1)S(1)} %bitcast.64), channel_id=1, source_target_pairs={{0,8},{1,9},{2,10},{3,11},{4,12},{5,13},{6,14},{7,15},{8,0},{9,1},... | collective-permute-start | bytes 344072 | tf_op jit(solution)/shard_map/ppermute | solution.py:1187
  265.9 9.6 %collective-permute-start.26 = (bf16[1,224,256]{2,1,0:T(8,128)(2,1)S(1)}, bf16[1,224,256]{2,1,0:T(8,128)(2,1)S(1)}, u32[]{:S(2)}, u32[]{:S(2)}) collective-permute-start(bf16[1,224,256]{2,1,0:T(8,128)(2,1)S(1)} %bitcast.63), channel_id=1, source_target_pairs={{0,12},{1,13},{2,14},{3,15},{4,8},{5,9},{6,10},{7,11},{8,4},{9,5},... | collective-permute-start | bytes 344072 | tf_op jit(solution)/shard_map/ppermute | solution.py:1187
  270.5 9.1 %collective-permute-start.23 = (bf16[1,160,512]{2,1,0:T(8,128)(2,1)S(1)}, bf16[1,160,512]{2,1,0:T(8,128)(2,1)S(1)}, u32[]{:S(2)}, u32[]{:S(2)}) collective-permute-start(bf16[1,160,512]{2,1,0:T(8,128)(2,1)S(1)} %get-tuple-element.237), channel_id=1, source_target_pairs={{0,16},{16,0},{1,17},{17,1},{2,18},{18,2},{3,19},{19,3},{4,20},{20... | collective-permute-start | bytes 491528 | tf_op jit(solution)/shard_map/ppermute | solution.py:1418
  277.5 4.5 %collective-permute-start.30 = (f32[40,512]{1,0:T(8,128)S(1)}, f32[40,512]{1,0:T(8,128)S(1)}, u32[]{:S(2)}, u32[]{:S(2)}) collective-permute-start(f32[40,512]{1,0:T(8,128)S(1)} %get-tuple-element.244), channel_id=1, source_target_pairs={{0,16},{16,0},{1,17},{17,1},{2,18},{18,2},{3,19},{19,3},{4,20},{20... | collective-permute-start | bytes 245768 | tf_op jit(solution)/shard_map/ppermute | solution.py:1423
  279.5 5.7 %collective-permute-start.31 = (bf16[1,224,256]{2,1,0:T(8,128)(2,1)S(1)}, bf16[1,224,256]{2,1,0:T(8,128)(2,1)S(1)}, u32[]{:S(2)}, u32[]{:S(2)}) collective-permute-start(bf16[1,224,256]{2,1,0:T(8,128)(2,1)S(1)} %get-tuple-element.245), channel_id=1, source_target_pairs={{0,16},{16,0},{1,17},{17,1},{2,18},{18,2},{3,19},{19,3},{4,20},{20... | collective-permute-start | bytes 344072 | tf_op jit(solution)/shard_map/ppermute | solution.py:1422
  (26 other events, 61.8 us)
Sparse Core Ops, SparseCore 0:
  128.3 96.7 reduce-scatter.1

commit v3 on v2

v3 whole, which is shorter than its diff:
```python
import functools
import math
import types

import jax
import jax.numpy as jnp
import ml_dtypes
import numpy as np
from jax import lax
from jax.experimental import pallas as pl
from jax.experimental.pallas import tpu as pltpu
from jax.sharding import PartitionSpec as P

H = 8
DH = 64
KERNEL = 9
WIN = 128

HALF = KERNEL // 2
SPAN = 3 * WIN
MANY = 4
GROUPS = H // MANY
WIDE = MANY * DH
RIM = 16
RIM_GRAD = 8
eps_norm = 1e-05
negative = -1e30
f32 = jnp.float32
bf16 = jnp.bfloat16
DEVICES = ("rows", "frames")
VMEM_LIMIT = 60 * 1024 * 1024
FOLD_LIMIT = 14 * 1024 * 1024


def dot(left, right):
    return jnp.dot(left, right, preferred_element_type=f32)


def dot_last(left, right):
    return lax.dot_general(left, right, (((1,), (1,)), ((), ())), preferred_element_type=f32)


def dot_first(left, right):
    return lax.dot_general(left, right, (((0,), (0,)), ((), ())), preferred_element_type=f32)


def sigmoid(x):
    return 0.5 * jnp.tanh(0.5 * x) + 0.5


def total(x):
    return jnp.sum(x, axis=0, keepdims=True)


def normalize(values):
    centered = values - jnp.mean(values, axis=-1, keepdims=True)
    inverse = lax.rsqrt(jnp.mean(centered * centered, axis=-1, keepdims=True) + eps_norm)
    return centered * inverse, inverse


def norm_back(grad_out, normal, inverse, gain):
    scaled = grad_out * gain
    centred = scaled - jnp.mean(scaled, axis=-1, keepdims=True)
    grad_in = inverse * (centred - normal * jnp.mean(scaled * normal, axis=-1, keepdims=True))
    return grad_in, total(grad_out * normal), total(grad_out)


def position_table(width, model):
    offsets = (np.arange(2 * width + 1) - width).astype(np.float32)
    rates = np.exp(
        np.arange(model // 2).astype(np.float32) * np.float32(-2.0 * math.log(10000.0) / model)
    )
    angles = (offsets[:, None] * rates[None, :]).astype(np.float32)
    both = np.stack([np.sin(angles), np.cos(angles)], axis=2).reshape(2 * width + 1, model)
    padded = np.zeros((3 * width, model), np.float32)
    padded[: 2 * width + 1] = both
    return padded.astype(ml_dtypes.bfloat16)


def bounds(ends, at, row_len):
    low = jnp.max(jnp.where(ends <= at, ends, 0.0), axis=1, keepdims=True)
    high = jnp.min(jnp.where(ends > at, ends, row_len), axis=1, keepdims=True)
    return low, high


def column(count, offset):
    return lax.broadcasted_iota(jnp.int32, (count, 1), 0).astype(f32) + offset


def head_lanes(rows):
    return lax.broadcasted_iota(jnp.int32, (rows, WIDE), 1) // DH


def heads_apart(group):
    at = head_lanes(group.shape[0])
    zero = jnp.zeros_like(group)
    return jnp.concatenate([jnp.where(at == k, group, zero) for k in range(MANY)], axis=0)


def heads_joined(stacked):
    rows = stacked.shape[0] // MANY
    at = head_lanes(rows)
    joined = stacked[:rows]
    for k in range(1, MANY):
        joined = jnp.where(at == k, stacked[k * rows : (k + 1) * rows], joined)
    return joined


def beside(stacked):
    rows = stacked.shape[0] // MANY
    return jnp.concatenate([stacked[k * rows : (k + 1) * rows] for k in range(MANY)], axis=1)


def below(joined):
    width = joined.shape[1] // MANY
    return jnp.concatenate([joined[:, k * width : (k + 1) * width] for k in range(MANY)], axis=0)


def flip(rows):
    i = lax.broadcasted_iota(jnp.int32, (rows, rows), 0)
    j = lax.broadcasted_iota(jnp.int32, (rows, rows), 1)
    return (i + j == rows - 1).astype(f32).astype(bf16)


class Load:
    def __init__(self, source, buffer, sem):
        self.buffer, self.waited = buffer, False
        self.copy = pltpu.make_async_copy(source, buffer, sem)
        self.copy.start()

    def ready(self):
        if not self.waited:
            self.copy.wait()
            self.waited = True
        return self.buffer


class Loads:
    def __init__(self, items):
        self.items = items

    def __getitem__(self, at):
        return self.items[at].ready()


class Stage:
    def __init__(self, loads, stores, sems):
        self.sems, self.used, self.pending, self.targets = sems, 0, [], []
        self.named, self.all_loads = {}, []
        for name, pairs, single in loads:
            items = [Load(source, buffer, self.sem()) for source, buffer in pairs]
            self.all_loads += items
            self.named[name] = items[0] if single else Loads(items)
        for name, pairs, single in stores:
            self.targets += [[target, buffer, False] for target, buffer in pairs]
            buffers = [buffer for _, buffer in pairs]
            self.named[name] = buffers[0] if single else buffers

    def sem(self):
        self.used += 1
        return self.sems.at[self.used - 1]

    def __getattr__(self, name):
        found = self.named[name]
        return found.ready() if isinstance(found, Load) else found

    def send(self, buffer, at=None):
        entry = next(entry for entry in self.targets if entry[1] is buffer)
        target = entry[0]
        entry[2] = True
        if at is not None:
            target, buffer = target.at[at], buffer.at[at]
        copy = pltpu.make_async_copy(buffer, target, self.sem())
        copy.start()
        self.pending.append(copy)

    def finish(self):
        for _, buffer, sent in self.targets:
            if not sent:
                self.send(buffer)
        for load in self.all_loads:
            load.ready()
        for copy in self.pending:
            copy.wait()


def staged(
    name, body, ins, outs, smem=(), scratch=(), flops=0, moved=0, sends=0, filled=None,
    limit=VMEM_LIMIT,
):
    operands, loads, stores = [], [], []
    for key, items in ins.items():
        single = not isinstance(items, list)
        entries = []
        for item in [items] if single else items:
            array, view, shape = item if isinstance(item, tuple) else (item, None, item.shape)
            at = next((i for i, other in enumerate(operands) if other is array), None)
            if at is None:
                at = len(operands)
                operands.append(array)
            entries.append((at, view, shape, array.dtype))
        loads.append((key, entries, single))
    for key, items in outs.items():
        single = not isinstance(items, list)
        entries = [
            item if isinstance(item, tuple) else (item, None, item.shape)
            for item in ([items] if single else items)
        ]
        stores.append((key, entries, single))
    aliases = {}
    if filled is not None:
        aliases = {len(smem) + len(operands): 0}
        operands.append(filled)
    every_load = [entry for _, entries, _ in loads for entry in entries]
    every_store = [entry for _, entries, _ in stores for entry in entries]
    n_smem, n_ops, n_outs, n_loads = len(smem), len(operands), len(every_store), len(every_load)

    def run(*refs):
        cuts = [n_smem, n_ops, n_outs, n_loads, n_outs, 1]
        taken, at = [], 0
        for cut in cuts:
            taken.append(refs[at : at + cut])
            at += cut
        scalars, given, targets, buffers, results, sems = taken
        buffers, places = iter(buffers), iter(zip(targets, results))
        placed_loads = [
            (
                key,
                [(given[i] if view is None else view(given[i]), next(buffers)) for i, view, _, _ in entries],
                single,
            )
            for key, entries, single in loads
        ]
        placed_stores = []
        for key, entries, single in stores:
            pairs = []
            for _, view, _ in entries:
                target, result = next(places)
                pairs.append((target if view is None else view(target), result))
            placed_stores.append((key, pairs, single))
        stage = Stage(placed_loads, placed_stores, sems[0])
        body(stage, *scalars, *refs[at:])
        stage.finish()

    hbm = pl.BlockSpec(memory_space=pl.ANY)
    got = iter(
        pl.pallas_call(
            run,
            in_specs=[pl.BlockSpec(memory_space=pltpu.SMEM)] * n_smem + [hbm] * n_ops,
            out_specs=[hbm] * n_outs,
            out_shape=[shape for shape, _, _ in every_store],
            scratch_shapes=[pltpu.VMEM(shape, dtype) for _, _, shape, dtype in every_load]
            + [pltpu.VMEM(shape, whole.dtype) for whole, _, shape in every_store]
            + [pltpu.SemaphoreType.DMA((n_loads + n_outs + sends,))]
            + list(scratch),
            input_output_aliases=aliases,
            compiler_params=pltpu.CompilerParams(vmem_limit_bytes=limit),
            cost_estimate=pl.CostEstimate(flops=flops, bytes_accessed=moved, transcendentals=0),
            name=name,
        )(*smem, *operands)
    )
    result = types.SimpleNamespace()
    for key, entries, single in stores:
        values = [next(got) for _ in entries]
        setattr(result, key, values[0] if single else values)
    return result


def sds(shape, dtype):
    return jax.ShapeDtypeStruct(shape, dtype)


def slab(array, *at):
    shape = tuple(a[1] for a in at if isinstance(a, tuple))
    index = tuple(pl.ds(*a) if isinstance(a, tuple) else a for a in at)
    return (array, lambda ref: ref.at[index], shape)


def by_row(array, rows):
    tokens, width = array.shape
    return [slab(array, (row * (tokens // rows), tokens // rows), (0, width)) for row in range(rows)]


def each_of(array):
    rows, size, width = array.shape
    return [slab(array, row, (0, size), (0, width)) for row in range(rows)]


PART = 1024


def activate(inner):
    half = 0.5 * inner
    turn = jnp.tanh(half)
    up = 1.0 + turn
    active = half * up
    return active, 0.5 * (up + active * (1.0 - turn))


def feed_slabs(feed_in, feed_out, module):
    _, model, hidden = feed_in.shape
    spans = [(part, PART) for part in range(0, hidden, PART)]
    w_in = [slab(feed_in, module, (0, model), span) for span in spans]
    w_out = [slab(feed_out, module, span, (0, model)) for span in spans]
    return w_in, w_out


def front(features, feed_in, feed_in_bias, feed_out, attend_in, gain, shift, bias):
    rows, frames, model = features.shape
    tokens = rows * frames
    hidden = feed_in.shape[2]
    parts = hidden // PART
    low = sds((tokens, model), bf16)

    def body(k):
        gain, shift = k.gain, k.shift
        x = k.x[...].reshape(tokens, model).astype(f32)
        normal, _ = normalize(x)
        k.n0[...] = (normal * gain[0:1] + shift[0:1]).astype(bf16)
        k.send(k.n0)
        for part in range(parts):
            cut = slice(part * PART, (part + 1) * PART)
            inner = dot(k.n0[...], k.w_in[part][...]) + k.b_in[0:1, cut]
            active, slope = activate(inner)
            k.act[:, cut] = active.astype(bf16)
            k.slope[:, cut] = slope.astype(bf16)
        k.send(k.slope)
        k.send(k.act)
        branch = k.bias[6:7]
        for part in range(parts):
            cut = slice(part * PART, (part + 1) * PART)
            branch = branch + dot(k.act[:, cut], k.w_out[part][...])
        after = x + 0.5 * branch
        k.after[...] = after
        k.send(k.after)
        normal, _ = normalize(after)
        normed = (normal * gain[1:2] + shift[1:2]).astype(bf16)
        k.na[...] = normed
        k.send(k.na)
        both = dot(normed, k.attend_in[...])
        keys = both[:, :model].astype(bf16)
        values = (both[:, model:] + k.bias[1:2]).astype(bf16)
        for row in range(rows):
            at = row * frames
            k.lo[row, :, :model] = keys[at : at + WIN]
            k.lo[row, :, model:] = values[at : at + WIN]
            k.hi[row, :, :model] = keys[at + WIN : at + frames]
            k.hi[row, :, model:] = values[at + WIN : at + frames]

    w_in, w_out = feed_slabs(feed_in, feed_out, 0)
    kv = sds((rows, WIN, 2 * model), bf16)
    return staged(
        "front",
        body,
        dict(
            x=features, gain=gain, shift=shift, b_in=feed_in_bias, w_in=w_in, bias=bias,
            w_out=w_out, attend_in=slab(attend_in, (0, model), (model, 2 * model)),
        ),
        dict(
            after=sds((tokens, model), f32), n0=low, na=low, lo=kv, hi=kv,
            act=sds((tokens, hidden), bf16), slope=sds((tokens, hidden), bf16),
        ),
        flops=2 * tokens * model * (2 * hidden + 2 * model),
        moved=16 << 20,
    )


def queries(na, attend_in, bias, sinusoid, proj):
    tokens, model = na.shape

    def body(k):
        query = dot(k.na[...], k.attend_in[...]) + k.bias[0:1]
        factor = 1.0 / math.sqrt(DH)
        k.qu[...] = ((query + k.bias[8:9]) * factor).astype(bf16)
        k.qv[...] = ((query + k.bias[9:10]) * factor).astype(bf16)
        k.table[...] = dot(k.sinusoid[...], k.proj[...]).astype(bf16)

    low = sds((tokens, model), bf16)
    return staged(
        "queries",
        body,
        dict(
            na=na, attend_in=slab(attend_in, (0, model), (0, model)), bias=bias,
            sinusoid=sinusoid, proj=proj,
        ),
        dict(qu=low, qv=low, table=sds((SPAN, model), bf16)),
        flops=2 * tokens * model * 2 * model,
        moved=4 << 20,
    )


def attend(
    row_len, info, ends, start, query, before, after, attend_out, convolve_in, gain, shift, bias
):
    rows = before.shape[0]
    tokens, model = start.after.shape
    frames = tokens // rows
    low = sds((tokens, model), bf16)

    def body(k, info):
        first_frame = info[0].astype(f32)
        turn = flip(WIN)
        key_at = lax.broadcasted_iota(jnp.int32, (WIN, SPAN), 1).astype(f32)
        table = k.table
        for row in range(rows):
            reach = info[1 + row].astype(f32)
            row_ends = k.ends[row : row + 1, :]
            for block in range(2):
                at = column(WIN, first_frame + WIN * block)
                lower, upper = bounds(row_ends, at, row_len)
                base = first_frame + (WIN * (block - 1))
                lower = jnp.maximum(lower, at - reach) - base
                upper = jnp.minimum(upper - 1.0, at + reach) - base
                allowed = ((key_at >= lower) & (key_at <= upper))[None]
                here = slice(row * frames + WIN * block, row * frames + WIN * (block + 1))
                some = [k.lo[row], k.hi[row]]
                some = some + [k.next[row]] if block else [k.before[row]] + some
                for group in range(GROUPS):
                    cut = slice(WIDE * group, WIDE * (group + 1))
                    cut_v = slice(model + WIDE * group, model + WIDE * (group + 1))
                    keys = jnp.concatenate([b[:, cut] for b in some], axis=0)
                    values = jnp.concatenate([b[:, cut_v] for b in some], axis=0)
                    spread = dot_last(heads_apart(k.qv[here, cut]), table[:, cut])
                    content = dot_last(heads_apart(k.qu[here, cut]), keys)
                    spread = pltpu.roll(
                        spread.reshape(MANY, WIN, SPAN), 0, 2, stride=1, stride_axis=1
                    )
                    scores = content.reshape(MANY, WIN, SPAN) + spread
                    scores = jnp.where(allowed, scores, negative)
                    powers = jnp.exp(scores - jnp.max(scores, axis=2, keepdims=True))
                    weights = powers * (1.0 / jnp.sum(powers, axis=2, keepdims=True))
                    weights = weights.astype(bf16).reshape(MANY * WIN, SPAN)
                    k.mixed[here, cut] = heads_joined(dot(weights, values)).astype(bf16)
                    k.prob[row][block, group] = dot(turn, beside(weights)).astype(bf16)
            k.send(k.prob[row])
        k.send(k.mixed)
        after_attend = k.after[...] + dot(k.mixed[...], k.attend_out[...]) + k.bias[2:3]
        k.out[...] = after_attend
        k.send(k.out)
        normal, _ = normalize(after_attend)
        normed = (normal * k.gain[2:3] + k.shift[2:3]).astype(bf16)
        k.nc[...] = normed
        k.send(k.nc)
        paired = dot(normed, k.convolve_in[...])
        value = paired[:, :model] + k.bias[3:4]
        gate = paired[:, model:] + k.bias[4:5]
        k.paired[:, :model] = value
        k.paired[:, model:] = gate
        k.send(k.paired)
        gated = (value * sigmoid(gate)).astype(bf16)
        k.gated[...] = gated
        for row in range(rows):
            k.first[row] = gated[row * frames : row * frames + RIM]
            k.last[row] = gated[(row + 1) * frames - RIM : (row + 1) * frames]

    rim = sds((rows, RIM, model), bf16)
    return staged(
        "attend",
        body,
        dict(
            ends=ends, table=query.table, qv=query.qv, qu=query.qu, lo=each_of(start.lo),
            hi=each_of(start.hi), before=each_of(before), next=each_of(after), after=start.after,
            attend_out=attend_out, bias=bias, gain=gain, shift=shift, convolve_in=convolve_in,
        ),
        dict(
            prob=[sds((2, GROUPS, WIN, MANY * SPAN), bf16)] * rows, mixed=low,
            out=sds((tokens, model), f32), nc=low, paired=sds((tokens, 2 * model), f32),
            gated=low, first=rim, last=rim,
        ),
        smem=[info],
        flops=16 * 8 * 256 * 384 * 128,
        moved=16 << 20,
    )


def valid_column(info, row, rows, frames):
    at = column(frames, info[0].astype(f32))
    return (at < info[1 + rows + row].astype(f32)).astype(f32)


def pack(ref, vectors):
    at = 0
    for vector in vectors:
        for k in range(0, vector.shape[1], 128):
            ref[at : at + 1, :] = vector[:, k : k + 128]
            at += 1


def by_rows(count, size, step, init=None):
    def one(i, carry):
        return step(pl.ds(pl.multiple_of(i * size, size), size), carry)

    return lax.fori_loop(0, count // size, one, init)


def by_lanes(width, step):
    def one(i, carry):
        step(pl.ds(pl.multiple_of(i * 128, 128), 128))
        return carry

    lax.fori_loop(0, width // 128, one, 0)


def spread(column):
    return jnp.broadcast_to(column, (column.shape[0], 128))


def tap_masks(keep_s, at, low, high):
    for tap in range(KERNEL):
        off = tap - HALF
        keep_s[tap] = spread(((at + off >= low) & (at + off < high)).astype(f32))


def depth_conv(row_len, devices, info, ends, gated, before, after, taps):
    rows = before.shape[0]
    tokens, model = gated.shape
    frames = tokens // rows

    def body(k, info, rim, keep_s, valid_s, sums, tile):
        start = info[0].astype(f32)
        counts = 0.0
        taps = k.taps
        for row in range(rows):
            here = slice(row * frames, (row + 1) * frames)
            at = column(frames, start)
            low, high = bounds(k.ends[row : row + 1, :], at, row_len)
            tap_masks(keep_s, at, low, high)
            valid = valid_column(info, row, rows, frames)
            valid_s[here] = spread(valid)
            counts += total(valid)
            rim[0:RIM] = k.before[row].astype(f32)
            rim[RIM : RIM + frames] = k.gated[row][...].astype(f32)
            rim[RIM + frames :] = k.after[row].astype(f32)

            def one(lanes):
                depth = jnp.zeros((frames, 128), f32)
                for tap in range(KERNEL):
                    off = tap - HALF
                    part = rim[RIM + off : RIM + off + frames, lanes] * keep_s[tap]
                    depth += taps[tap : tap + 1, lanes] * part
                k.depth[here, lanes] = depth
                sums[row : row + 1, lanes] = total(depth * valid_s[here])

            by_lanes(model, one)
            k.send(k.depth, pl.ds(row * frames, frames))
        first = total(sums[0:rows, :])
        mean = first / jnp.maximum(counts, 1.0)
        sums[rows : rows + 1, :] = mean

        def two(lanes):
            centered = k.depth[:, lanes] - sums[rows : rows + 1, lanes]
            sums[rows + 1 : rows + 2, lanes] = total(centered * centered * valid_s[...])

        by_lanes(model, two)
        pack(tile, [first, sums[rows + 1 : rows + 2, :]])
        k.stats[...] = jnp.broadcast_to(tile[...][None], k.stats.shape)

    return staged(
        "depth_conv",
        body,
        dict(ends=ends, before=before, taps=taps, gated=by_row(gated, rows), after=after),
        dict(depth=sds((rows * frames, model), f32), stats=sds((devices, 8, 128), f32)),
        smem=[info],
        scratch=[
            pltpu.VMEM((frames + 2 * RIM, model), f32),
            pltpu.VMEM((KERNEL, frames, 128), f32),
            pltpu.VMEM((rows * frames, 128), f32),
            pltpu.VMEM((8, model), f32),
            pltpu.VMEM((8, 128), f32),
        ],
        flops=rows * frames * model * 30,
        moved=2 << 20,
        sends=rows - 1,
    )


def middle(
    devices, rows, info, stats, counts, depth, stream, feed_in, feed_in_bias, feed_out,
    convolve_out, gain, shift, bias, cotangent,
):
    tokens, model = depth.shape
    frames = tokens // rows
    hidden = feed_in.shape[2]
    parts = hidden // PART

    def body(k, info, conv_s, slope_s, tile):
        stats, each = k.stats, k.counts[:, 0:1]
        gain, shift, bias = k.gain, k.shift, k.bias
        count = total(each)
        means, inverses = [], []
        for at in range(model // 128):
            sums = stats[:, at, :]
            mean = total(sums) / count
            off = sums / jnp.maximum(each, 1.0) - mean
            spread = total(stats[:, model // 128 + at, :]) + total(each * off * off)
            means.append(mean)
            inverses.append(lax.rsqrt(spread / count + eps_norm))
        mean = jnp.concatenate(means, axis=1)
        inverse = jnp.concatenate(inverses, axis=1)
        k.inv[0:1] = inverse
        k.inv[1:2] = jnp.broadcast_to(1.0 / count, (1, model))
        normal = (k.depth[...] - mean) * inverse
        k.bn[...] = normal
        k.send(k.bn)
        batch = normal * gain[5:6] + shift[5:6]
        swished = (batch * sigmoid(batch)).astype(bf16)
        k.sw[...] = swished
        k.send(k.sw)
        after_conv = k.stream[...] + dot(swished, k.convolve_out[...]) + bias[5:6]
        conv_s[...] = after_conv
        normal, _ = normalize(after_conv)
        k.nf[...] = (normal * gain[3:4] + shift[3:4]).astype(bf16)
        k.send(k.nf)
        for part in range(parts):
            cut = slice(part * PART, (part + 1) * PART)
            inner = dot(k.nf[...], k.w_in[part][...]) + k.b_in[1:2, cut]
            active, slope = activate(inner)
            k.act[:, cut] = active.astype(bf16)
            slope_s[:, cut] = slope
        k.send(k.act)
        branch = bias[7:8]
        for part in range(parts):
            cut = slice(part * PART, (part + 1) * PART)
            branch = branch + dot(k.act[:, cut], k.w_out[part][...])
        normal, inverse = normalize(conv_s[...] + 0.5 * branch)
        valid = jnp.concatenate(
            [valid_column(info, row, rows, frames) for row in range(rows)], axis=0
        )
        k.out[...] = (valid * (normal * gain[4:5] + shift[4:5])).astype(bf16)
        k.send(k.out)
        grad = valid * k.cotangent[...].astype(f32)
        grad, gain_grad, shift_grad = norm_back(grad, normal, inverse, gain[4:5])
        k.gcs[...] = grad
        low = (0.5 * grad).astype(bf16)
        k.gl[...] = low
        k.send(k.gl)
        vec = k.vec
        vec[2:3] = gain_grad
        vec[3:4] = shift_grad
        vec[5:6] = total(low.astype(f32))
        back = 0.0
        for part in range(parts):
            cut = slice(part * PART, (part + 1) * PART)
            grad = (dot_last(k.gl[...], k.w_out[part][...]) * slope_s[:, cut]).astype(bf16)
            k.gi[:, cut] = grad
            k.fb[:, cut] = total(grad.astype(f32))
            back = back + dot_last(grad, k.w_in[part][...])
        k.send(k.gi)
        normal, inverse = normalize(conv_s[...])
        grad, gain_grad, shift_grad = norm_back(back, normal, inverse, gain[3:4])
        vec[0:1] = gain_grad
        vec[1:2] = shift_grad
        grad = k.gcs[...] + grad
        k.gcs[...] = grad
        k.send(k.gcs)
        low = grad.astype(bf16)
        k.gcl[...] = low
        k.send(k.gcl)
        vec[4:5] = total(low.astype(f32))
        bn = k.bn[...]
        batch = bn * gain[5:6] + shift[5:6]
        _, slope = activate(batch)
        grad = dot_last(low, k.convolve_out[...]) * slope
        k.gb[...] = grad
        k.send(k.gb)
        pack(tile, [total(grad), total(grad * bn)])
        k.totals[...] = jnp.broadcast_to(tile[...][None], k.totals.shape)
        k.send(k.totals)
        for row in range(rows):
            at, end = row * frames, (row + 1) * frames
            k.first[row, :, :model] = k.gb[at : at + RIM_GRAD]
            k.first[row, :, model:] = k.bn[at : at + RIM_GRAD]
            k.last[row, :, :model] = k.gb[end - RIM_GRAD : end]
            k.last[row, :, model:] = k.bn[end - RIM_GRAD : end]

    w_in, w_out = feed_slabs(feed_in, feed_out, 1)
    ins = dict(
        stats=stats, counts=counts, gain=gain, shift=shift, depth=depth, bias=bias,
        convolve_out=convolve_out, stream=stream, b_in=feed_in_bias, w_in=w_in, w_out=w_out,
        cotangent=cotangent,
    )
    low = sds((tokens, model), bf16)
    wide = sds((tokens, model), f32)
    rim = sds((rows, RIM_GRAD, 2 * model), f32)
    return staged(
        "middle",
        body,
        ins,
        dict(
            out=low, act=sds((tokens, hidden), bf16), gi=sds((tokens, hidden), bf16), nf=low,
            gl=low, sw=low, gcl=low, gcs=wide, gb=wide, bn=wide, inv=sds((8, model), f32),
            totals=sds((devices, 8, 128), f32), first=rim, last=rim, vec=sds((8, model), f32),
            fb=sds((1, hidden), f32),
        ),
        smem=[info],
        scratch=[
            pltpu.VMEM((tokens, model), f32),
            pltpu.VMEM((tokens, hidden), f32),
            pltpu.VMEM((8, 128), f32),
        ],
        flops=2 * tokens * model * (4 * hidden + 2 * model),
        moved=24 << 20,
    )


def conv_back(
    row_len, n, info, ends, taps, convolve_in, attend_out, gain, totals, mid, edge_before,
    edge_after, rim_before, rim_after, mix, early,
):
    tokens, model = mid.gb.shape
    rows = rim_before.shape[0]
    frames = tokens // rows
    slim = model // n
    room = slim % 8 == 0

    def body(k, info, grads, rim, keep_s, gp, gal):
        start = info[0].astype(f32)
        parts = model // 128
        sums = [total(k.totals[:, at, :]) for at in range(2 * parts)]
        total_a = jnp.concatenate(sums[:parts], axis=1)
        total_b = jnp.concatenate(sums[parts:], axis=1)
        inverse, per_count = k.inv[0:1], k.inv[1:2]
        gain, taps, vec = k.gain, k.taps, k.vec
        own_scale = inverse * gain[5:6]
        share_a = own_scale * total_a * per_count
        share_b = own_scale * total_b * per_count
        vec[14:15] = total_a
        vec[15:16] = total_b
        vec[0:9] = jnp.zeros((9, model), f32)
        vec[9:14] = jnp.zeros((5, model), f32)

        def grad_of(grad, normal, valid):
            grad = grad * own_scale - valid * (share_a + normal * share_b)
            return grad.astype(bf16).astype(f32)

        for row in range(rows):
            first = row * frames
            last = info[1 + rows + row].astype(f32)
            at = column(frames, start)
            low, high = bounds(k.ends[row : row + 1, :], at, row_len)
            tap_masks(keep_s, at, low, high)
            before, after = k.edge_before, k.edge_after
            edge_at = column(RIM_GRAD, start - RIM_GRAD)
            grads[0:RIM_GRAD] = grad_of(
                before[row, :, :model], before[row, :, model:], (edge_at < last).astype(f32)
            )
            for step in range(0, frames, 32):
                here = slice(step, step + 32)
                at = column(32, start + step)
                grads[RIM_GRAD + step : RIM_GRAD + step + 32] = grad_of(
                    k.gb[row][here], k.bn[row][here], (at < last).astype(f32)
                )
            edge_at = column(RIM_GRAD, start + frames)
            grads[RIM_GRAD + frames :] = grad_of(
                after[row, :, :model], after[row, :, model:], (edge_at < last).astype(f32)
            )
            rim[0:RIM] = k.rim_before[row].astype(f32)
            rim[RIM : RIM + frames] = k.gated[row][...].astype(f32)
            rim[RIM + frames :] = k.rim_after[row].astype(f32)
            paired = k.paired[row]
            half = frames // 2

            def one(i, carry):
                lane = pl.multiple_of(i * 128, 128)
                lanes, gates = pl.ds(lane, 128), pl.ds(model + lane, 128)
                for base in range(0, frames, half):
                    own = grads[RIM_GRAD + base : RIM_GRAD + base + half, lanes]
                    grad = jnp.zeros((half, 128), f32)
                    for tap in range(KERNEL):
                        off = base + tap - HALF
                        keep = keep_s[tap, base : base + half]
                        part = own * (rim[RIM + off : RIM + off + half, lanes] * keep)
                        vec[tap : tap + 1, lanes] += total(part)
                        mirror = KERNEL - 1 - tap
                        part = grads[RIM_GRAD + off : RIM_GRAD + off + half, lanes] * keep
                        grad += taps[mirror : mirror + 1, lanes] * part
                    sigma = sigmoid(paired[base : base + half, gates])
                    one = (grad * sigma).astype(bf16)
                    value = paired[base : base + half, lanes]
                    two = (grad * sigma * value * (1.0 - sigma)).astype(bf16)
                    here = slice(first + base, first + base + half)
                    gp[here, lanes] = one
                    gp[here, gates] = two
                    vec[11:12, lanes] += total(one.astype(f32))
                    vec[12:13, lanes] += total(two.astype(f32))
                return carry

            lax.fori_loop(0, model // 128, one, 0)
        grad = dot_last(gp[...], k.convolve_in[...])
        normal, inverse = normalize(k.after[...])
        grad, gain_grad, shift_grad = norm_back(grad, normal, inverse, gain[2:3])
        vec[9:10] = gain_grad
        vec[10:11] = shift_grad
        grad = k.gcs[...] + grad
        k.gas[...] = grad
        k.send(k.gas)
        low = grad.astype(bf16)
        gal[...] = low
        vec[13:14] = total(low.astype(f32))
        k.gm[...] = dot_last(gal[...], k.attend_out[...]).astype(bf16)
        k.send(k.gm)
        out = k.early
        out[:, :slim] = dot_first(k.nc[...], gp[...]).astype(bf16).reshape(n, slim, 2 * model)
        block = dot_first(k.sw[...], k.gcl[...]).astype(bf16)
        out[:, slim:, :model] = block.reshape(n, slim, model)
        block = dot_first(k.mixed[...], gal[...]).astype(bf16)
        out[:, slim:, model:] = block.reshape(n, slim, model)

    own = (n, 2 * slim, 2 * model)
    size = early.shape[1] - 2 * slim
    if room:
        out = (sds(early.shape, bf16), lambda ref: ref.at[:, pl.ds(size, 2 * slim)], own)
    else:
        out = sds(own, bf16)
    got = staged(
        "conv_back",
        body,
        dict(
            totals=totals, inv=mid.inv, gain=gain, ends=ends, taps=taps, edge_before=edge_before,
            edge_after=edge_after, rim_before=rim_before, rim_after=rim_after,
            gb=by_row(mid.gb, rows), bn=by_row(mid.bn, rows), gated=by_row(mix.gated, rows),
            paired=by_row(mix.paired, rows), convolve_in=convolve_in, after=mix.out, gcs=mid.gcs,
            attend_out=attend_out, nc=mix.nc, sw=mid.sw, gcl=mid.gcl, mixed=mix.mixed,
        ),
        dict(
            early=out, gas=sds((tokens, model), f32), gm=sds((tokens, model), bf16),
            vec=sds((16, model), f32),
        ),
        smem=[info],
        scratch=[
            pltpu.VMEM((frames + 2 * RIM_GRAD, model), f32),
            pltpu.VMEM((frames + 2 * RIM, model), f32),
            pltpu.VMEM((KERNEL, frames, 128), f32),
            pltpu.VMEM((tokens, 2 * model), bf16),
            pltpu.VMEM((tokens, model), bf16),
        ],
        flops=2 * tokens * model * 7 * model,
        moved=16 << 20,
        filled=early if room else None,
    )
    if not room:
        got.early = jnp.concatenate([early, got.early], axis=1)
    return got


def attend_back(start, query, before, after, probs, gm):
    rows = before.shape[0]
    tokens, model = query.qu.shape
    frames = tokens // rows
    factor = 1.0 / math.sqrt(DH)

    def body(k, acc, turned):
        g_table, vec, table = k.g_table, k.vec, k.table
        g_table[...] = jnp.zeros_like(g_table)
        vec[...] = jnp.zeros_like(vec)
        turn = flip(WIN)
        for row in range(rows):
            acc[...] = jnp.zeros_like(acc)
            for block in range(2):
                here = slice(WIN * block, WIN * (block + 1))
                span = slice(WIN * block, WIN * block + SPAN)
                turned[0] = dot(turn, k.gm[row][here]).astype(bf16)
                turned[1] = dot(turn, k.qu[row][here]).astype(bf16)
                turned[2] = dot(turn, k.qv[row][here]).astype(bf16)
                blocks = [k.lo[row], k.hi[row]]
                blocks = blocks + [k.next[row]] if block else [k.before[row]] + blocks
                prob = k.prob[2 * row + block]
                for group in range(GROUPS):
                    cut = slice(WIDE * group, WIDE * (group + 1))
                    cut_v = slice(model + WIDE * group, model + WIDE * (group + 1))
                    keys = jnp.concatenate([b[:, cut] for b in blocks], axis=0)
                    values = jnp.concatenate([b[:, cut_v] for b in blocks], axis=0)
                    weights = below(prob[group])
                    grad_mixed = heads_apart(turned[0, :, cut])
                    grad = dot_last(grad_mixed, values)
                    wide = weights.astype(f32)
                    delta = jnp.sum(wide * grad, axis=1, keepdims=True)
                    raw = (wide * (grad - delta)).astype(bf16)
                    acc[span, cut_v] += dot_first(weights, grad_mixed)
                    acc[span, cut] += dot_first(raw, heads_apart(turned[1, :, cut]))
                    grad_u = heads_joined(dot(raw, keys)) * factor
                    band = pltpu.roll(
                        raw.astype(f32).reshape(MANY, WIN, SPAN),
                        SPAN - (WIN - 1),
                        2,
                        stride=1,
                        stride_axis=1,
                    )
                    band = band.astype(bf16).reshape(MANY * WIN, SPAN)
                    grad_v = heads_joined(dot(band, table[:, cut])) * factor
                    g_table[:, cut] += dot_first(band, heads_apart(turned[2, :, cut]))
                    vec[0:1, cut] += total(grad_u)
                    vec[1:2, cut] += total(grad_v)
                    both = (grad_u + grad_v).astype(bf16)
                    k.gq[row][here, cut] = dot(turn, both).astype(bf16)
                if block == 0:
                    k.g_before[row] = acc[0:WIN].astype(bf16)
                    k.send(k.g_before, row)
            k.g_after[row] = acc[3 * WIN :].astype(bf16)
            k.send(k.g_after, row)
            k.g_lo[row][...] = acc[WIN : 2 * WIN]
            k.send(k.g_lo[row])
            k.g_hi[row][...] = acc[2 * WIN : 3 * WIN]
            k.send(k.g_hi[row])
            k.send(k.gq[row])

    ins = dict(
        gm=by_row(gm, rows), qu=by_row(query.qu, rows), qv=by_row(query.qv, rows),
        before=each_of(before), lo=each_of(start.lo), hi=each_of(start.hi),
        prob=[
            slab(prob, block, (0, GROUPS), (0, WIN), (0, MANY * SPAN))
            for prob in probs
            for block in range(2)
        ],
        table=query.table, next=each_of(after),
    )
    kv = (WIN, 2 * model)
    return staged(
        "attend_back",
        body,
        ins,
        dict(
            gq=[sds((frames, model), bf16)] * rows, g_before=sds((rows,) + kv, bf16),
            g_lo=[sds(kv, f32)] * rows, g_hi=[sds(kv, f32)] * rows,
            g_after=sds((rows,) + kv, bf16), g_table=sds((SPAN, model), f32),
            vec=sds((8, model), f32),
        ),
        scratch=[
            pltpu.VMEM((4 * WIN, 2 * model), f32),
            pltpu.VMEM((3, WIN, model), bf16),
        ],
        flops=16 * 14 * 256 * 384 * 128,
        moved=16 << 20,
        sends=2 * rows - 2,
    )


def back(info, core_at, n, grads, halo, attend_in, start, gas, gain, sinusoid):
    rows = len(grads.gq)
    tokens, model = start.after.shape
    frames = tokens // rows
    hidden = start.act.shape[1]
    parts = hidden // PART
    width, slim = hidden // n, model // n

    def body(k, info, joined):
        core = info[core_at]
        vec, gain = k.vec, k.gain
        sums = [0.0] * 5
        for row in range(rows):
            here = slice(row * frames, (row + 1) * frames)
            low_half = slice(row * frames, row * frames + WIN)
            high_half = slice(row * frames + WIN, (row + 1) * frames)
            joined[here, :model] = k.gq[row][...]
            pair = (k.g_lo[row][...] + k.left[row][...].astype(f32)).astype(bf16)
            joined[low_half, model:] = pair
            pair = (k.g_hi[row][...] + k.right[row][...].astype(f32)).astype(bf16)
            joined[high_half, model:] = pair
            both = joined[here]
            k.gv[here] = both[:, 2 * model :]
            sums[0] += total(both[:, :model].astype(f32))
            sums[1] += total(both[:, 2 * model :].astype(f32))
            grad = dot_last(both, k.attend_in[...])
            normal, inverse = normalize(k.after[row][...])
            grad, gain_grad, shift_grad = norm_back(grad, normal, inverse, gain[1:2])
            sums[2] += gain_grad
            sums[3] += shift_grad
            grad = k.gas[row][...] + grad
            k.gfs[row][...] = grad
            k.send(k.gfs[row])
            low = (0.5 * grad).astype(bf16)
            k.gl[here] = low
            sums[4] += total(low.astype(f32))
        k.send(k.gv)
        k.send(k.gl)
        for at in range(5):
            vec[at : at + 1] = sums[at]
        pairs = (0, n // 2)
        block = dot_first(k.na[...], joined[:, : 2 * model])
        for part in range(2):
            cut = slice(part * model, (part + 1) * model)
            keep_half(block[:, cut], core, k.mine, k.other, pairs, width + part * slim)
        high = k.g_table[...].astype(bf16)
        low = (k.g_table[...] - high.astype(f32)).astype(bf16)
        place = dot_first(k.sinusoid[...], high) + dot_first(k.sinusoid[...], low)
        keep_half(place, core, k.mine, k.other, pairs, width + 2 * slim)
        step = n // 2 // parts
        for part in range(parts):
            block = dot_first(k.act[part][...], k.gl[...])
            some = (part * step, (part + 1) * step)
            keep_half(block, core, k.mine, k.other, some)
            k.send(k.other, pl.ds(part * step, step))
            k.send(k.mine, pl.ds(part * step, step))

    half = sds((n // 2, width + 3 * slim, model), bf16)
    low = sds((tokens, model), bf16)
    return staged(
        "back",
        body,
        dict(
            gain=gain, gq=grads.gq, g_lo=grads.g_lo, left=each_of(halo[0]), g_hi=grads.g_hi,
            right=each_of(halo[1]), attend_in=attend_in, after=by_row(start.after, rows),
            gas=by_row(gas, rows), na=start.na, g_table=grads.g_table, sinusoid=sinusoid,
            act=[slab(start.act, (0, tokens), (at, PART)) for at in range(0, hidden, PART)],
        ),
        dict(
            other=half, mine=half, gv=low, gl=low, gfs=[sds((frames, model), f32)] * rows,
            vec=sds((8, model), f32),
        ),
        smem=[info],
        scratch=[pltpu.VMEM((tokens, 3 * model), bf16)],
        flops=2 * tokens * model * (hidden + 6 * model),
        moved=18 << 20,
        sends=2 * parts - 2,
    )


def keep_half(block, core, mine_ref, other_ref, rows, at=0):
    model = mine_ref.shape[2]
    pairs = rows[1] - rows[0]
    size = block.shape[0] // (2 * pairs)
    shaped = block.reshape(pairs, 2, size, model)
    even, odd = shaped[:, 0], shaped[:, 1]
    here = slice(*rows)
    mine_ref[here, at : at + size] = jnp.where(core == 0, even, odd).astype(bf16)
    other_ref[here, at : at + size] = jnp.where(core == 0, odd, even).astype(bf16)


def first_back(info, core_at, n, gl, feed_in, feed_out, start, gv):
    tokens, hidden = start.slope.shape
    model = gl.shape[1]
    parts = hidden // PART

    def body(k, info):
        core = info[core_at]
        step = n // 2 // parts
        back = 0.0
        block = dot_first(k.na[...], k.gv[...])
        keep_half(block, core, k.mine, k.other, (0, n // 2), hidden // n)
        for part in range(parts):
            cut = slice(part * PART, (part + 1) * PART)
            grad = dot_last(k.gl[...], k.w_out[part][...])
            grad = (grad * k.slope[part][...].astype(f32)).astype(bf16)
            k.fb[:, cut] = total(grad.astype(f32))
            block = dot_first(grad, k.n0[...])
            some = (part * step, (part + 1) * step)
            keep_half(block, core, k.mine, k.other, some)
            k.send(k.other, pl.ds(part * step, step))
            k.send(k.mine, pl.ds(part * step, step))
            back = back + dot_last(grad, k.w_in[part][...])
        k.gn[...] = back

    half = sds((n // 2, hidden // n + model // n, model), bf16)
    w_in, w_out = feed_slabs(feed_in, feed_out, 0)
    return staged(
        "first_back",
        body,
        dict(
            na=start.na, gv=gv, gl=gl, w_out=w_out,
            slope=[slab(start.slope, (0, tokens), (at, PART)) for at in range(0, hidden, PART)],
            n0=start.n0, w_in=w_in,
        ),
        dict(other=half, mine=half, fb=sds((1, hidden), f32), gn=sds((tokens, model), f32)),
        smem=[info],
        flops=2 * tokens * model * hidden * 3,
        moved=12 << 20,
        sends=2 * parts - 2,
    )


def last(features, gn, gfs, gain):
    rows, frames, model = features.shape

    def body(k):
        gain_grads, shift_grads = 0.0, 0.0
        for row in range(rows):
            here = slice(row * frames, (row + 1) * frames)
            normal, inverse = normalize(k.x[row][...].astype(f32))
            grad = k.gn[row][...]
            grad, gain_grad, shift_grad = norm_back(grad, normal, inverse, k.gain[0:1])
            k.out[row] = k.gfs[row][...] + grad
            k.send(k.out, row)
            gain_grads += gain_grad
            shift_grads += shift_grad
        k.vec[0:1] = gain_grads
        k.vec[1:2] = shift_grads

    ins = dict(
        gain=gain, x=[slab(features, row, (0, frames), (0, model)) for row in range(rows)],
        gn=[slab(gn, (row * frames, frames), (0, model)) for row in range(rows)], gfs=list(gfs),
    )
    return staged(
        "last",
        body,
        ins,
        dict(out=sds(features.shape, f32), vec=sds((8, model), f32)),
        flops=rows * frames * model * 20,
        moved=4 << 20,
        sends=rows - 1,
        limit=FOLD_LIMIT,
    )


def feed_weights(n, gi, nf, act, gl):
    tokens, model = nf.shape
    hidden = gi.shape[1]
    parts = hidden // PART
    size, slim = hidden // n, model // n
    step = n // parts
    room = 2 * slim if slim % 8 == 0 else 0

    def body(k):
        for part in range(parts):
            here = slice(part * step, (part + 1) * step)
            block = dot_first(k.gi[part][...], k.nf[...]).astype(bf16)
            k.out[here, :, :model] = block.reshape(step, size, model)
            block = dot_first(k.act[part][...], k.gl[...]).astype(bf16)
            k.out[here, :, model:] = block.reshape(step, size, model)
            k.send(k.out, pl.ds(part * step, step))

    ins = dict(
        nf=nf, gi=[slab(gi, (0, tokens), (at, PART)) for at in range(0, hidden, PART)], gl=gl,
        act=[slab(act, (0, tokens), (at, PART)) for at in range(0, hidden, PART)],
    )
    own = (n, size, 2 * model)
    shape = sds((n, size + room, 2 * model), bf16)
    return staged(
        "feed_weights",
        body,
        ins,
        dict(out=(shape, lambda ref: ref.at[:, pl.ds(0, size)] if room else ref, own)),
        flops=4 * tokens * model * hidden,
        moved=10 << 20,
        sends=parts - 1,
    ).out


def neighbours(last_block, first_block):
    devices = lax.axis_size("frames")
    up = [(i, i + 1) for i in range(devices - 1)]
    down = [(i + 1, i) for i in range(devices - 1)]
    return lax.ppermute(last_block, "frames", up), lax.ppermute(first_block, "frames", down)


def gather(copies):
    return lax.all_to_all(copies, DEVICES, 0, 0, tiled=True)


def scatter_sum(grads):
    return lax.psum_scatter(grads, "frames", scatter_dimension=0, tiled=True)


ROW_PAIR = [(0, 1), (1, 0)]
COLUMNS, IN_FLOAT = 1, 2


def swap(x, k):
    n = lax.axis_size("frames")
    return lax.ppermute(x, "frames", [(i, i ^ k) for i in range(n)])


def swaps(sends, group):
    k, size = group
    return [swap(send, k * one) for one, send in zip(range(1, size), sends)]


def fold(name, info, row_at, states, small=None):
    mines, gots, keeps, sends, plans = [], [], [], [], []
    for mine, got, how in states:
        size, height, model = mine.shape
        if isinstance(how, tuple):
            _, place, digits = how
            view = (size // (digits * place), digits, place, height, model)
            half = (view[0], place, height, model)
        else:
            view = mine.shape
            half = (size, height, model // 2) if how == COLUMNS else mine.shape
        n_sends = how[2] - 1 if isinstance(how, tuple) else int(how == COLUMNS)
        plans.append((len(gots), len(got), len(sends), n_sends, how))
        mines.append(mine.reshape(view))
        gots += [one.reshape(view) for one in got]
        keeps.append(sds(half, f32 if how == IN_FLOAT else bf16))
        sends += [sds(half, bf16)] * n_sends

    def body(k, info):
        for at, (got_at, n_got, send_at, _, how) in enumerate(plans):
            parts = [k.mine[at]] + [k.got[got_at + one] for one in range(n_got)]

            def added(*index):
                return sum(part[index].astype(f32) for part in parts)

            keep = k.keep[at]
            if how is None or how == IN_FLOAT:
                keep[...] = added(...).astype(keep.dtype)
            elif how == COLUMNS:
                half = keep.shape[2]
                both = [
                    added(slice(None), slice(None), slice(one * half, (one + 1) * half))
                    for one in range(2)
                ]
                first = info[row_at] == 0
                k.away[send_at][...] = jnp.where(first, both[1], both[0]).astype(bf16)
                k.send(k.away[send_at])
                keep[...] = jnp.where(first, both[0], both[1]).astype(bf16)
            else:
                digit = info[how[0]]
                for one in range(1, how[2]):
                    other = digit
                    for bit in (1, 2):
                        if one & bit:
                            other = other + bit * (1 - 2 * ((digit // bit) % 2))
                    k.away[send_at + one - 1][...] = added(slice(None), other).astype(bf16)
                    k.send(k.away[send_at + one - 1])
                keep[...] = added(slice(None), digit).astype(bf16)
        if small is not None:
            k.total[...] = sum(k.small[one][...] for one in range(len(small)))

    ins, outs = dict(mine=mines, got=gots), dict(keep=keeps, away=sends)
    if small is not None:
        ins |= dict(small=list(small))
        outs |= dict(total=sds(small[0].shape, f32))
    got = staged(name, body, ins, outs, smem=[info], flops=1 << 20, moved=2 << 20, limit=FOLD_LIMIT)
    results = []
    for at, (mine, _, how) in enumerate(states):
        size, height, model = mine.shape
        shape = (size // how[2], height, model) if isinstance(how, tuple) else got.keep[at].shape
        _, _, send_at, n_sends, _ = plans[at]
        away = [one.reshape(shape) for one in got.away[send_at : send_at + n_sends]]
        results.append((got.keep[at].reshape(shape), away))
    if small is not None:
        results.append(got.total)
    return results


def finish(info, row_at, a, b, b_got, early, width, slim):
    model = a.shape[1]

    def body(info, a, b, b_got, early, feed_in, feed_out, joined, attend, place, con_in, con_out):
        feed_in[0] = a[:width].T
        feed_in[1] = early[:width, :model].T
        first = info[row_at] == 0
        one, two = b[...].astype(f32), b_got[...].astype(f32)
        whole = jnp.concatenate([jnp.where(first, one, two), jnp.where(first, two, one)], axis=1)
        feed_out[0] = whole[:width]
        feed_out[1] = early[:width, model:]
        joined[:, :model] = whole[width : width + slim]
        joined[:, model : 2 * model] = whole[width + slim : width + 2 * slim]
        joined[:, 2 * model :] = a[width:]
        place[...] = whole[width + 2 * slim :]
        con_in[...] = early[width : width + slim]
        con_out[...] = early[width + slim :, :model]
        attend[...] = early[width + slim :, model:]

    def full(shape):
        return pl.BlockSpec(shape, lambda i: (0,) * len(shape))

    shapes = [
        (2, model, width), (2, width, model), (slim, 3 * model), (slim, model), (slim, model),
        (slim, 2 * model), (slim, model),
    ]
    return pl.pallas_call(
        body,
        grid=(1,),
        in_specs=[pl.BlockSpec(memory_space=pltpu.SMEM)]
        + [full(one.shape) for one in (a, b, b_got, early)],
        out_specs=[full(shape) for shape in shapes],
        out_shape=[sds(shape, f32) for shape in shapes],
        compiler_params=pltpu.CompilerParams(vmem_limit_bytes=FOLD_LIMIT),
        name="finish",
    )(info, a, b, b_got, early)


def per_device(
    features,
    lengths,
    windows,
    feed_in,
    feed_in_bias,
    feed_out,
    attend_in,
    attend_out,
    position_proj,
    convolve_in,
    convolve_out,
    depthwise,
    norm_gain,
    norm_shift,
    biases,
    cotangent,
):
    rows, frames, model = features.shape
    tokens = rows * frames
    n = lax.axis_size("frames")
    devices = lax.axis_size("rows") * n
    row_len = float(frames * n)
    me = lax.axis_index("frames")
    first_frame = me * frames
    hidden = feed_in.shape[2]
    ends_every = jnp.cumsum(lengths, axis=1, dtype=jnp.int32)
    ends_here = lax.dynamic_slice_in_dim(ends_every, lax.axis_index("rows") * rows, rows, 0)
    slots = ends_here.shape[1]
    ends = jnp.pad(
        ends_here.astype(f32), ((0, 8 - rows), (0, -slots % 128)), constant_values=row_len
    )
    groups, k = [(2, 2)], 4
    while k < n:
        groups.append((k, min(4, n // k)))
        k *= groups[-1][1]
    places = [lax.axis_index("rows"), me % 2] + [(me // k) % size for k, size in groups]
    info = jnp.concatenate(
        [first_frame[None].astype(jnp.int32), windows, ends_here[:, -1], jnp.stack(places)]
    )
    row_at = 1 + 2 * rows
    core_at = row_at + 1
    starts = jnp.arange(n, dtype=jnp.int32) * frames
    counts = jnp.clip(ends_every[:, -1][:, None] - starts[None, :], 0, frames)
    counts = jnp.sum(counts.reshape(-1, rows, n), axis=1).astype(f32).reshape(devices, 1)
    counts = jnp.broadcast_to(counts, (devices, 128))
    sinusoid = jnp.asarray(position_table(WIN, model))

    start = front(
        features, feed_in, feed_in_bias, feed_out, attend_in, norm_gain, norm_shift, biases
    )
    before, after = neighbours(start.hi, start.lo)
    query = queries(start.na, attend_in, biases, sinusoid, position_proj)
    mix = attend(
        row_len, info, ends, start, query, before, after, attend_out, convolve_in, norm_gain,
        norm_shift, biases,
    )
    rim_before, rim_after = neighbours(mix.last, mix.first)
    got = depth_conv(row_len, devices, info, ends, mix.gated, rim_before, rim_after, depthwise)
    mid = middle(
        devices, rows, info, gather(got.stats), counts, got.depth, mix.out, feed_in,
        feed_in_bias, feed_out, convolve_out, norm_gain, norm_shift, biases,
        cotangent.reshape(tokens, model),
    )
    edge_before, edge_after = neighbours(mid.last, mid.first)
    totals = gather(mid.totals)
    early = feed_weights(n, mid.gi, mid.nf, mid.act, mid.gl)
    totals, early = lax.optimization_barrier((totals, early))
    conv = conv_back(
        row_len, n, info, ends, depthwise, convolve_in, attend_out, norm_gain, totals, mid,
        edge_before, edge_after, rim_before, rim_after, mix, early,
    )
    early, gm = lax.optimization_barrier((conv.early, conv.gm))
    early = scatter_sum(early)
    grads = attend_back(start, query, before, after, mix.prob, gm)
    halo = neighbours(grads.g_after, grads.g_before)
    end = back(
        info, core_at, n, grads, halo, attend_in, start, conv.gas, norm_gain, sinusoid
    )
    b, b_got = end.mine, [swap(end.other, 1)]
    got = first_back(info, core_at, n, end.gl, feed_in, feed_out, start, end.gv)
    a, a_got = got.mine, [swap(got.other, 1)]
    ((b, b_send),) = fold("fold_b", info, row_at, [(b, b_got, COLUMNS)])
    b_got = [lax.ppermute(b_send[0], "rows", ROW_PAIR)]
    ((a, a_send),) = fold("fold_a", info, row_at, [(a, a_got, (core_at + 1, 1, 2))])
    a_got = swaps(a_send, groups[0])
    gn, a = lax.optimization_barrier((got.gn, a))
    ending = last(features, gn, end.gfs, norm_gain)

    vec_conv, vec_mid, vec_back, vec_last = conv.vec, mid.vec, end.vec, ending.vec
    small = jnp.concatenate(
        [
            vec_conv[:KERNEL],
            vec_last[0:1], vec_back[2:3], vec_conv[9:10], vec_mid[0:1], vec_mid[2:3],
            vec_last[1:2], vec_back[3:4], vec_conv[10:11], vec_mid[1:2], vec_mid[3:4],
            vec_back[0:2], vec_conv[13:14], vec_conv[11:13], vec_mid[4:5], vec_back[4:5],
            vec_mid[5:6], grads.vec[0:2],
            got.fb.reshape(-1, model), mid.fb.reshape(-1, model),
            jnp.zeros((3, model), f32),
        ],
        axis=0,
    )
    small = [small] + swaps([small] * 3, (1, 4))
    last_group = groups[-1]
    for at, group in enumerate(groups):
        deeper = at + 1 < len(groups)
        a_how = (core_at + 2 + at, 1, groups[at + 1][1]) if deeper else None
        states = [(a, a_got, a_how), (b, b_got, (core_at + 1 + at, 1, group[1]))]
        (a, a_send), (b, b_send), one = fold(f"fold_{at}", info, row_at, states, small)
        if deeper:
            a_got = swaps(a_send, groups[at + 1])
        else:
            early, a = lax.optimization_barrier((early, a))
            a_got = [lax.ppermute(a, "rows", ROW_PAIR)]
            early_got = [lax.ppermute(early, "rows", ROW_PAIR)]
        b_got = swaps(b_send, group)
        if at == 0:
            small = [one, lax.ppermute(one, "rows", ROW_PAIR)]
        elif deeper:
            small = [one] + swaps([one] * (group[1] - 1), group)
    states = [(b, b_got, None), (a, a_got, IN_FLOAT), (early, early_got, IN_FLOAT)]
    (b, _), (a, _), (early, _) = fold("fold_last", info, row_at, states)
    b_got = lax.ppermute(b, "rows", ROW_PAIR)
    small = [one] + swaps([one] * (last_group[1] - 1), last_group)
    slim = model // n
    width = hidden // n
    feed_in_grad, feed_out_grad, joined, *rest = finish(
        info, row_at, a[0], b[0], b_got[0], early[0], width, slim
    )
    small = sum(small)
    n_vectors = small.shape[0] - 3 - 2 * (hidden // model)
    vectors = jnp.concatenate([small[:n_vectors], vec_conv[14:16]], axis=0)
    thin = lax.dynamic_slice_in_dim(vectors, me * slim, slim, 1)
    feed_bias = small[n_vectors:-3].reshape(2, hidden)
    feed_bias = lax.dynamic_slice_in_dim(feed_bias, me * width, width, 1)
    return (
        mid.out.reshape(rows, frames, model),
        ending.out,
        feed_in_grad,
        feed_bias,
        feed_out_grad,
        joined,
        *rest,
        thin[:KERNEL],
        jnp.concatenate([thin[KERNEL : KERNEL + 5], thin[n_vectors + 1 :]], axis=0),
        jnp.concatenate([thin[KERNEL + 5 : KERNEL + 10], thin[n_vectors : n_vectors + 1]], axis=0),
        thin[KERNEL + 10 : n_vectors],
    )


def solution(mesh):
    placed = (
        P("rows", "frames", None),
        P(),
        P("rows"),
        P(),
        P(),
        P(),
        P(),
        P(),
        P(),
        P(),
        P(),
        P(),
        P(),
        P(),
        P(),
        P("rows", "frames", None),
    )
    return jax.shard_map(
        per_device,
        mesh=mesh,
        in_specs=placed,
        out_specs=(
            P("rows", "frames", None),
            P("rows", "frames", None),
            P(None, None, "frames"),
            P(None, "frames"),
            P(None, "frames", None),
            P("frames", None),
            P("frames", None),
            P("frames", None),
            P("frames", None),
            P("frames", None),
            P(None, "frames"),
            P(None, "frames"),
            P(None, "frames"),
            P(None, "frames"),
        ),
        check_vma=False,
    )
```

time: 300 us -> 283 us (0.943)
  the two profiles are of different devices: /device:TPU:0 before, /device:TPU:16 now
where the time goes in v3:
time: 283 us; the launch traced here: 278 us
  Pallas kernels  122 us (43%)
  waiting for transfers between devices  66.2 us (23%)
  starting transfers between devices  59.5 us (21%)
  between operations  14.9 us (5%)
  local copies, waits for them, and re-layouts  13.4 us (5%)
    pallas_call x16, Pallas kernels, staged(): pl.pallas_call(run, in_specs=[pl.BlockSpec(memory_space=pltpu.SMEM)] * n_...  120 us
    ppermute x16, waiting for transfers between devices, swap(): return lax.ppermute(x, 'frames', [(i, i ^ k) for i in range(n)])  37.2 us
    ppermute x16, starting transfers between devices, swap(): return lax.ppermute(x, 'frames', [(i, i ^ k) for i in range(n)])  16.4 us
    ppermute x4, starting transfers between devices, neighbours(): lax.ppermute(first_block, 'frames', down)  16.2 us
    ppermute x4, starting transfers between devices, neighbours(): lax.ppermute(last_block, 'frames', up)  11.3 us
    all_to_all x2, starting transfers between devices, gather(): return lax.all_to_all(copies, DEVICES, 0, 0, tiled=True)  10.8 us
    unnamed x60, local copies, waits for them, and re-layouts  7.73 us
    ppermute x1, waiting for transfers between devices, per_device(): a_got = [lax.ppermute(a, 'rows', ROW_PAIR)]  6.78 us
  transfers between devices with their start and end apart: 32, of which 17 were waited for; matrix products, arithmetic and copies ran while one was open for 3% of the time, Pallas kernels for 21%

profile of v3, /device:TPU:16, one launch (start us, length us, event | category | flops | bytes accessed | tf_op | source)
XLA Modules:
  0.0 278.2 jit_solution(5496621944229570819)
XLA Ops:
  7.2 7.5 %front.1 = (f32[512,512]{1,0:T(8,128)}, bf16[512,512]{1,0:T(8,128)(2,1)}, bf16[512,512]{1,0:T(8,128)(2,1)}, bf16[2,128,1024]{2,1,0:T(8,128)(2,1)}, bf16[2,128,10...) custom-call(bf16[2,256,512]{2,1,0:T(8,128)(2,1)} %refs_1_.7, f32[6,512]{1,0:T(8,128)} %refs_0_.3, ...), custom_call_target="tpu_custom_call" | custom-call | flops 2684354560 | bytes 16777216 | tf_op jit(solution)/shard_map/front/pallas_call | solution.py:247
  14.7 1.9 collective-permute-start
  16.6 4.7 %collective-permute-start.1 = (bf16[2,128,1024]{2,1,0:T(8,128)(2,1)}, bf16[2,128,1024]{2,1,0:T(8,128)(2,1)S(1)}, u32[]{:S(2)}, u32[]{:S(2)}) collective-permute-start(bf16[2,128,1024]{2,1,0:T(8,128)(2,1)} %get-tuple-element.117.refs_5_.refs_4_), channel_id=1, source_target_pairs={{1,0},{2,1},{3,2},{4,3},{5,4},{6,5},{7,6},{8,7},{9,8},{10,9},{11,1... | collective-permute-start | bytes 1572872 | tf_op jit(solution)/shard_map/ppermute | solution.py:1142
  23.0 3.0 %queries.1 = (bf16[512,512]{1,0:T(8,128)(2,1)}, bf16[512,512]{1,0:T(8,128)(2,1)}, bf16[384,512]{1,0:T(8,128)(2,1)}) custom-call(bf16[512,512]{1,0:T(8,128)(2,1)} %get-tuple-element.113.refs_0_.refs_13_.refs_1_, bf16[512,1536]{1,0:T(8,128)(2,1)} %refs_10_.5, f32[10,512]{1,0:T(8,128)} %refs_6_.3, bf16[384,512]{1,0:T(8,128)(2,1)} %constant.76.clone.refs_3_.refs_15_, ...), custom_call_target="tpu_custom_call" | custom-call | flops 536870912 | bytes 4194304 | tf_op jit(solution)/shard_map/queries/pallas_call | solution.py:247
  26.4 1.8 collective-permute-done.1.refs_8_.refs_9_
  29.0 17.2 %attend.1 = (bf16[2,2,128,1536]{3,2,1,0:T(8,128)(2,1)}, bf16[2,2,128,1536]{3,2,1,0:T(8,128)(2,1)}, bf16[512,512]{1,0:T(8,128)(2,1)}, f32[512,512]{1,0:T(8,128)},...) custom-call(s32[9]{0:T(128)} %concatenate.15.refs_0_.info, ...), custom_call_target="tpu_custom_call" | custom-call | flops 1610612736 | bytes 16777216 | tf_op jit(solution)/shard_map/attend/pallas_call | solution.py:247
  46.2 5.4 %collective-permute-start.2 = (bf16[2,16,512]{2,1,0:T(8,128)(2,1)}, bf16[2,16,512]{2,1,0:T(8,128)(2,1)S(1)}, u32[]{:S(2)}, u32[]{:S(2)}) collective-permute-start(bf16[2,16,512]{2,1,0:T(8,128)(2,1)} %get-tuple-element.120), channel_id=1, source_target_pairs={{0,1},{1,2},{2,3},{3,4},{4,5},{5,6},{6,7},{7,8},{8,9},{9,10},{10,1... | collective-permute-start | bytes 98312 | tf_op jit(solution)/shard_map/ppermute | solution.py:1142
  51.6 2.3 collective-permute-start.3
  54.0 1.6 collective-permute-done.3.refs_5_.refs_9_
  56.1 5.9 %depth_conv.1 = (f32[512,512]{1,0:T(8,128)}, f32[32,8,128]{2,1,0:T(8,128)}) custom-call(s32[9]{0:T(128)} %concatenate.15.refs_0_.info, f32[8,128]{1,0:T(8,128)} %pad.4.refs_1_.refs_4_, bf16[2,16,512]{2,1,0:T(8,128)(2,1)} %copy-done.18, f32[9,512]{1,0:T(8,128)} %refs_5_.3, bf16[512,512]{1,0:T(8,128)(2,1)} %get-tuple-element.121.refs_4_.refs_12_, ...), custom_call_target="tpu_custom_call" | custom-call | flops 7864320 | bytes 2097152 | tf_op jit(solution)/shard_map/depth_conv/pallas_call | solution.py:247
  62.0 6.2 %all-to-all-start = ((f32[32,8,128]{2,1,0:T(8,128)}), f32[32,8,128]{2,1,0:T(8,128)S(1)}, u32[]{:S(2)}, u32[]{:S(2)}) async-start(f32[32,8,128]{2,1,0:T(8,128)} %get-tuple-element.123), calls=%async_computation | async-start | bytes 262144 | tf_op jit(solution)/shard_map/all_to_all | solution.py:1146
  68.7 5.8 %all-to-all-done.refs_1_ = f32[32,8,128]{2,1,0:T(8,128)S(1)} async-done(((f32[32,8,128]{2,1,0:T(8,128)}), f32[32,8,128]{2,1,0:T(8,128)S(1)}, u32[]{:S(2)}, u32[]{:S(2)}) %all-to-all-start) | async-done | bytes 131104 | tf_op jit(solution)/shard_map/all_to_all | solution.py:1146
  75.1 12.6 %middle.1 = (bf16[512,512]{1,0:T(8,128)(2,1)}, bf16[512,2048]{1,0:T(8,128)(2,1)}, bf16[512,2048]{1,0:T(8,128)(2,1)}, bf16[512,512]{1,0:T(8,128)(2,1)}, bf16[512,...) custom-call(s32[9]{0:T(128)} %concatenate.15.refs_0_.info, ...), custom_call_target="tpu_custom_call" | custom-call | flops 4831838208 | bytes 25165824 | tf_op jit(solution)/shard_map/middle/pallas_call | solution.py:247
  87.8 4.6 %all-to-all-start.1 = ((f32[32,8,128]{2,1,0:T(8,128)}), f32[32,8,128]{2,1,0:T(8,128)S(1)}, u32[]{:S(2)}, u32[]{:S(2)}) async-start(f32[32,8,128]{2,1,0:T(8,128)} %get-tuple-element.127), calls=%async_computation.1 | async-start | bytes 262144 | tf_op jit(solution)/shard_map/all_to_all | solution.py:1146
  92.4 2.1 collective-permute-start.4
  94.5 4.4 %collective-permute-start.5 = (f32[2,8,1024]{2,1,0:T(8,128)}, f32[2,8,1024]{2,1,0:T(8,128)S(1)}, u32[]{:S(2)}, u32[]{:S(2)}) collective-permute-start(f32[2,8,1024]{2,1,0:T(8,128)} %get-tuple-element.135), channel_id=1, source_target_pairs={{1,0},{2,1},{3,2},{4,3},{5,4},{6,5},{7,6},{8,7},{9,8},{10,9},{11,1... | collective-permute-start | bytes 196616 | tf_op jit(solution)/shard_map/ppermute | solution.py:1142
  98.9 6.0 %feed_weights.1.refs_22_ = bf16[16,192,1024]{2,1,0:T(8,128)(2,1)} custom-call(bf16[512,512]{1,0:T(8,128)(2,1)} %get-tuple-element.128.refs_0_, bf16[512,2048]{1,0:T(8,128)(2,1)} %get-tuple-element.129.refs_1_, bf16[512,512]{1,0:T(8,128)(2,1)} %get-tuple-element.130.refs_2_, bf16[512,2048]{1,0:T(8,128)(2,1)} %get-tuple-element.131.refs_3_), custom_call_target="tpu_custom_call" | custom-call | flops 2147483648 | bytes 10485760 | tf_op jit(solution)/shard_map/feed_weights/pallas_call | solution.py:247
  105.5 14.6 %conv_back.1 = (bf16[16,192,1024]{2,1,0:T(8,128)(2,1)}, f32[512,512]{1,0:T(8,128)}, bf16[512,512]{1,0:T(8,128)(2,1)}, f32[16,512]{1,0:T(8,128)}) custom-call(s32[9]{0:T(128)} %concatenate.15.refs_0_.info, f32[32,8,128]{2,1,0:T(8,128)} %copy-done.13, f32[8,512]{1,0:T(8,128)} %get-tuple-element.133.refs_2_, ...), custom_call_target="tpu_custom_call", output_to_operand_aliasing={{0}: (22, {})} | custom-call | flops 1879048192 | bytes 16777216 | tf_op jit(solution)/shard_map/conv_back/pallas_call | solution.py:247
  120.2 14.7 %attend_back.1 = (bf16[256,512]{1,0:T(8,128)(2,1)}, bf16[256,512]{1,0:T(8,128)(2,1)}, bf16[2,128,1024]{2,1,0:T(8,128)(2,1)}, f32[128,1024]{1,0:T(8,128)}, f32[12...) custom-call(bf16[512,512]{1,0:T(8,128)(2,1)} %get-tuple-element.147., ...), custom_call_target="tpu_custom_call" | custom-call | flops 2818572288 | bytes 16777216 | tf_op jit(solution)/shard_map/attend_back/pallas_call | solution.py:247
  134.9 1.9 collective-permute-start.6
  136.8 4.8 %collective-permute-start.7 = (bf16[2,128,1024]{2,1,0:T(8,128)(2,1)}, bf16[2,128,1024]{2,1,0:T(8,128)(2,1)S(1)}, u32[]{:S(2)}, u32[]{:S(2)}) collective-permute-start(bf16[2,128,1024]{2,1,0:T(8,128)(2,1)} %get-tuple-element.157), channel_id=1, source_target_pairs={{1,0},{2,1},{3,2},{4,3},{5,4},{6,5},{7,6},{8,7},{9,8},{10,9},{11,1... | collective-permute-start | bytes 1572872 | tf_op jit(solution)/shard_map/ppermute | solution.py:1142
  141.6 5.0 %collective-permute-done.6.refs_6_ = bf16[2,128,1024]{2,1,0:T(8,128)(2,1)S(1)} collective-permute-done((bf16[2,128,1024]{2,1,0:T(8,128)(2,1)}, bf16[2,128,1024]{2,1,0:T(8,128)(2,1)S(1)}, u32[]{:S(2)}, u32[]{:S(2)}) %collective-permute-start.6) | collective-permute-done | bytes 524320 | tf_op jit(solution)/shard_map/ppermute | solution.py:1142
  146.6 1.8 collective-permute-done.7.refs_9_
  149.2 10.9 %back.1 = (bf16[8,224,512]{2,1,0:T(8,128)(2,1)}, bf16[8,224,512]{2,1,0:T(8,128)(2,1)}, bf16[512,512]{1,0:T(8,128)(2,1)}, bf16[512,512]{1,0:T(8,128)(2,1)}, f32[2...) custom-call(s32[9]{0:T(128)} %concatenate.15.refs_0_.info, f32[6,512]{1,0:T(8,128)} %refs_0_.3, ...), custom_call_target="tpu_custom_call" | custom-call | flops 2684354560 | bytes 18874368 | tf_op jit(solution)/shard_map/back/pallas_call | solution.py:247
  160.1 3.0 %collective-permute-start.9 = (bf16[8,224,512]{2,1,0:T(8,128)(2,1)}, bf16[8,224,512]{2,1,0:T(8,128)(2,1)}, u32[]{:S(2)}, u32[]{:S(2)}) collective-permute-start(bf16[8,224,512]{2,1,0:T(8,128)(2,1)} %get-tuple-element.175), channel_id=1, source_target_pairs={{0,1},{1,0},{2,3},{3,2},{4,5},{5,4},{6,7},{7,6},{8,9},{9,8},{10,11... | collective-permute-start | bytes 5505032 | tf_op jit(solution)/shard_map/ppermute | solution.py:1159
  163.1 8.5 %first_back.1 = (bf16[8,160,512]{2,1,0:T(8,128)(2,1)}, bf16[8,160,512]{2,1,0:T(8,128)(2,1)}, f32[1,2048]{1,0:T(1,128)}, f32[512,512]{1,0:T(8,128)}) custom-call(s32[9]{0:T(128)} %concatenate.15.refs_0_.info, bf16[512,512]{1,0:T(8,128)(2,1)} %get-tuple-element.113.refs_0_.refs_13_.refs_1_, bf16[512,512]{1,0:T(8,128)(2,1)} %get-tuple-element.161.refs_2_, ...), custom_call_target="tpu_custom_call" | custom-call | flops 3221225472 | bytes 12582912 | tf_op jit(solution)/shard_map/first_back/pallas_call | solution.py:247
  173.8 3.8 %fold_b.1 = (bf16[8,224,256]{2,1,0:T(8,128)(2,1)S(1)}, bf16[8,224,256]{2,1,0:T(8,128)(2,1)}) custom-call(s32[9]{0:T(128)S(1)} %copy-done.12, bf16[8,224,512]{2,1,0:T(8,128)(2,1)S(1)} %copy-done.1, bf16[8,224,512]{2,1,0:T(8,128)(2,1)} %collective-permute-done.9.refs_2_), custom_call_target="tpu_custom_call" | custom-call | flops 1048576 | bytes 2097152 | tf_op jit(solution)/shard_map/fold_b/pallas_call | solution.py:247
  178.6 1.6 collective-permute-start.11
  180.2 3.0 %fold_a.1 = (bf16[4,1,160,512]{3,2,1,0:T(8,128)(2,1)S(1)}, bf16[4,1,160,512]{3,2,1,0:T(8,128)(2,1)}) custom-call(s32[9]{0:T(128)S(1)} %copy-done.12, bf16[4,2,1,160,512]{4,3,2,1,0:T(8,128)(2,1)S(1)} %bitcast.31, bf16[4,2,1,160,512]{4,3,2,1,0:T(8,128)(2,1)} %bitcast.8.refs_2_), custom_call_target="tpu_custom_call" | custom-call | flops 1048576 | bytes 2097152 | tf_op jit(solution)/shard_map/fold_a/pallas_call | solution.py:247
  187.4 2.2 last.1
  189.9 1.6 collective-permute-start.13
  191.8 16.0 %collective-permute-done.13.refs_7_ = f32[40,512]{1,0:T(8,128)S(1)} collective-permute-done((f32[40,512]{1,0:T(8,128)S(1)}, f32[40,512]{1,0:T(8,128)S(1)}, u32[]{:S(2)}, u32[]{:S(2)}) %collective-permute-start.13) | collective-permute-done | bytes 81952 | tf_op jit(solution)/shard_map/ppermute | solution.py:1159
  208.0 4.1 %fold_0.1 = (bf16[1,1,160,512]{3,2,1,0:T(8,128)(2,1)S(1)}, bf16[4,1,224,256]{3,2,1,0:T(8,128)(2,1)S(1)}, bf16[1,1,160,512]{3,2,1,0:T(8,128)(2,1)S(1)}, bf16[1,1,...) custom-call(s32[9]{0:T(128)S(1)} %copy-done.12, ...), custom_call_target="tpu_custom_call" | custom-call | flops 1048576 | bytes 2097152 | tf_op jit(solution)/shard_map/fold_0/pallas_call | solution.py:247
  212.5 1.5 collective-permute-start.15
  214.5 1.5 collective-permute-start.17
  216.5 3.9 %collective-permute-done.19.refs_8_ = f32[40,512]{1,0:T(8,128)S(1)} collective-permute-done((f32[40,512]{1,0:T(8,128)S(1)}, f32[40,512]{1,0:T(8,128)S(1)}, u32[]{:S(2)}, u32[]{:S(2)}) %collective-permute-start.19) | collective-permute-done | bytes 81952 | tf_op jit(solution)/shard_map/ppermute | solution.py:1390
  220.7 5.4 %collective-permute-done.16.refs_4_ = bf16[1,160,512]{2,1,0:T(8,128)(2,1)S(1)} collective-permute-done((bf16[1,160,512]{2,1,0:T(8,128)(2,1)S(1)}, bf16[1,160,512]{2,1,0:T(8,128)(2,1)S(1)}, u32[]{:S(2)}, u32[]{:S(2)}) %collective-permute-start.16) | collective-permute-done | bytes 163872 | tf_op jit(solution)/shard_map/ppermute | solution.py:1159
  226.1 4.7 %collective-permute-done.17.refs_5_ = bf16[1,160,512]{2,1,0:T(8,128)(2,1)S(1)} collective-permute-done((bf16[1,160,512]{2,1,0:T(8,128)(2,1)S(1)}, bf16[1,160,512]{2,1,0:T(8,128)(2,1)S(1)}, u32[]{:S(2)}, u32[]{:S(2)}) %collective-permute-start.17) | collective-permute-done | bytes 163872 | tf_op jit(solution)/shard_map/ppermute | solution.py:1159
  230.8 3.4 %fold_1.1 = (bf16[1,160,512]{2,1,0:T(8,128)(2,1)S(1)}, bf16[1,1,224,256]{3,2,1,0:T(8,128)(2,1)S(1)}, bf16[1,1,224,256]{3,2,1,0:T(8,128)(2,1)S(1)}, bf16[1,1,224,...) custom-call(s32[9]{0:T(128)S(1)} %copy-done.12, ...), custom_call_target="tpu_custom_call" | custom-call | flops 1048576 | bytes 2097152 | tf_op jit(solution)/shard_map/fold_1/pallas_call | solution.py:247
  234.2 2.3 collective-permute-start.27
  236.6 1.2 collective-permute-start.28
  238.7 1.3 collective-permute-start.21
  241.7 8.5 %collective-permute-done.28 = f32[40,512]{1,0:T(8,128)S(1)} collective-permute-done((f32[40,512]{1,0:T(8,128)S(1)}, f32[40,512]{1,0:T(8,128)S(1)}, u32[]{:S(2)}, u32[]{:S(2)}) %collective-permute-start.28) | collective-permute-done | bytes 81952 | tf_op jit(solution)/shard_map/ppermute | solution.py:1159
  252.4 1.6 collective-permute-done.22.refs_6_
  254.1 6.8 %collective-permute-done.23.refs_7_ = bf16[1,160,512]{2,1,0:T(8,128)(2,1)S(1)} collective-permute-done((bf16[1,160,512]{2,1,0:T(8,128)(2,1)S(1)}, bf16[1,160,512]{2,1,0:T(8,128)(2,1)S(1)}, u32[]{:S(2)}, u32[]{:S(2)}) %collective-permute-start.23) | collective-permute-done | bytes 163872 | tf_op jit(solution)/shard_map/ppermute | solution.py:1386
  261.9 2.5 fold_last.1
  267.4 1.9 collective-permute-done.25
  269.2 1.9 finish.1
  (131 shorter events, 24.3 us)
Async XLA Ops:
  7.2 14.2 %copy-start.28 = (s32[4,17]{1,0:T(4,128)S(1)}, s32[4,17]{1,0:T(4,128)}, u32[]{:S(2)}) copy-start(s32[4,17]{1,0:T(4,128)} %param.18) | copy-start | bytes 820
  7.2 15.2 %copy-start.29 = (s32[2]{0:T(128)S(1)}, s32[2]{0:T(128)}, u32[]{:S(2)}) copy-start(s32[2]{0:T(128)} %param.19) | copy-start | bytes 28
  14.7 11.7 %collective-permute-start = (bf16[2,128,1024]{2,1,0:T(8,128)(2,1)}, bf16[2,128,1024]{2,1,0:T(8,128)(2,1)S(1)}, u32[]{:S(2)}, u32[]{:S(2)}) collective-permute-start(bf16[2,128,1024]{2,1,0:T(8,128)(2,1)} %get-tuple-element.118.refs_6_.refs_5_), channel_id=1, source_target_pairs={{0,1},{1,2},{2,3},{3,4},{4,5},{5,6},{6,7},{7,8},{8,9},{9,10},{10,1... | collective-permute-start | bytes 1572872 | tf_op jit(solution)/shard_map/ppermute | solution.py:1142
  16.6 11.6 %collective-permute-start.1 = (bf16[2,128,1024]{2,1,0:T(8,128)(2,1)}, bf16[2,128,1024]{2,1,0:T(8,128)(2,1)S(1)}, u32[]{:S(2)}, u32[]{:S(2)}) collective-permute-start(bf16[2,128,1024]{2,1,0:T(8,128)(2,1)} %get-tuple-element.117.refs_5_.refs_4_), channel_id=1, source_target_pairs={{1,0},{2,1},{3,2},{4,3},{5,4},{6,5},{7,6},{8,7},{9,8},{10,9},{11,1... | collective-permute-start | bytes 1572872 | tf_op jit(solution)/shard_map/ppermute | solution.py:1142
  46.2 7.8 %collective-permute-start.2 = (bf16[2,16,512]{2,1,0:T(8,128)(2,1)}, bf16[2,16,512]{2,1,0:T(8,128)(2,1)S(1)}, u32[]{:S(2)}, u32[]{:S(2)}) collective-permute-start(bf16[2,16,512]{2,1,0:T(8,128)(2,1)} %get-tuple-element.120), channel_id=1, source_target_pairs={{0,1},{1,2},{2,3},{3,4},{4,5},{5,6},{6,7},{7,8},{8,9},{9,10},{10,1... | collective-permute-start | bytes 98312 | tf_op jit(solution)/shard_map/ppermute | solution.py:1142
  51.6 3.9 %collective-permute-start.3 = (bf16[2,16,512]{2,1,0:T(8,128)(2,1)}, bf16[2,16,512]{2,1,0:T(8,128)(2,1)S(1)}, u32[]{:S(2)}, u32[]{:S(2)}) collective-permute-start(bf16[2,16,512]{2,1,0:T(8,128)(2,1)} %get-tuple-element.122), channel_id=1, source_target_pairs={{1,0},{2,1},{3,2},{4,3},{5,4},{6,5},{7,6},{8,7},{9,8},{10,9},{11,1... | collective-permute-start | bytes 98312 | tf_op jit(solution)/shard_map/ppermute | solution.py:1142
  62.0 12.5 %all-to-all-start = ((f32[32,8,128]{2,1,0:T(8,128)}), f32[32,8,128]{2,1,0:T(8,128)S(1)}, u32[]{:S(2)}, u32[]{:S(2)}) async-start(f32[32,8,128]{2,1,0:T(8,128)} %get-tuple-element.123), calls=%async_computation | async-start | bytes 262144 | tf_op jit(solution)/shard_map/all_to_all | solution.py:1146
  87.8 17.1 %all-to-all-start.1 = ((f32[32,8,128]{2,1,0:T(8,128)}), f32[32,8,128]{2,1,0:T(8,128)S(1)}, u32[]{:S(2)}, u32[]{:S(2)}) async-start(f32[32,8,128]{2,1,0:T(8,128)} %get-tuple-element.127), calls=%async_computation.1 | async-start | bytes 262144 | tf_op jit(solution)/shard_map/all_to_all | solution.py:1146
  92.3 158.0 %reduce-scatter.2.cloned.1.call-start = ((), (), s32[]{:S(2)}) async-start(), calls=%async_computation.3 | async-start | bytes 6684672 | tf_op jit(solution)/shard_map/reduce_scatter | solution.py:1150
  92.4 12.5 %collective-permute-start.4 = (f32[2,8,1024]{2,1,0:T(8,128)}, f32[2,8,1024]{2,1,0:T(8,128)S(1)}, u32[]{:S(2)}, u32[]{:S(2)}) collective-permute-start(f32[2,8,1024]{2,1,0:T(8,128)} %get-tuple-element.134), channel_id=1, source_target_pairs={{0,1},{1,2},{2,3},{3,4},{4,5},{5,6},{6,7},{7,8},{8,9},{9,10},{10,1... | collective-permute-start | bytes 196616 | tf_op jit(solution)/shard_map/ppermute | solution.py:1142
  94.5 10.4 %collective-permute-start.5 = (f32[2,8,1024]{2,1,0:T(8,128)}, f32[2,8,1024]{2,1,0:T(8,128)S(1)}, u32[]{:S(2)}, u32[]{:S(2)}) collective-permute-start(f32[2,8,1024]{2,1,0:T(8,128)} %get-tuple-element.135), channel_id=1, source_target_pairs={{1,0},{2,1},{3,2},{4,3},{5,4},{6,5},{7,6},{8,7},{9,8},{10,9},{11,1... | collective-permute-start | bytes 196616 | tf_op jit(solution)/shard_map/ppermute | solution.py:1142
  134.9 11.7 %collective-permute-start.6 = (bf16[2,128,1024]{2,1,0:T(8,128)(2,1)}, bf16[2,128,1024]{2,1,0:T(8,128)(2,1)S(1)}, u32[]{:S(2)}, u32[]{:S(2)}) collective-permute-start(bf16[2,128,1024]{2,1,0:T(8,128)(2,1)} %get-tuple-element.154), channel_id=1, source_target_pairs={{0,1},{1,2},{2,3},{3,4},{4,5},{5,6},{6,7},{7,8},{8,9},{9,10},{10,1... | collective-permute-start | bytes 1572872 | tf_op jit(solution)/shard_map/ppermute | solution.py:1142
  136.8 11.6 %collective-permute-start.7 = (bf16[2,128,1024]{2,1,0:T(8,128)(2,1)}, bf16[2,128,1024]{2,1,0:T(8,128)(2,1)S(1)}, u32[]{:S(2)}, u32[]{:S(2)}) collective-permute-start(bf16[2,128,1024]{2,1,0:T(8,128)(2,1)} %get-tuple-element.157), channel_id=1, source_target_pairs={{1,0},{2,1},{3,2},{4,3},{5,4},{6,5},{7,6},{8,7},{9,8},{10,9},{11,1... | collective-permute-start | bytes 1572872 | tf_op jit(solution)/shard_map/ppermute | solution.py:1142
  146.6 1.8 copy-start.14
  160.1 13.7 %collective-permute-start.9 = (bf16[8,224,512]{2,1,0:T(8,128)(2,1)}, bf16[8,224,512]{2,1,0:T(8,128)(2,1)}, u32[]{:S(2)}, u32[]{:S(2)}) collective-permute-start(bf16[8,224,512]{2,1,0:T(8,128)(2,1)} %get-tuple-element.175), channel_id=1, source_target_pairs={{0,1},{1,0},{2,3},{3,2},{4,5},{5,4},{6,7},{7,6},{8,9},{9,8},{10,11... | collective-permute-start | bytes 5505032 | tf_op jit(solution)/shard_map/ppermute | solution.py:1159
  163.1 9.2 %copy-start.25 = (f32[1,2048]{1,0:T(1,128)S(1)}, f32[1,2048]{1,0:T(1,128)}, u32[]{:S(2)}) copy-start(f32[1,2048]{1,0:T(1,128)} %get-tuple-element.185) | copy-start | bytes 24580
  163.1 9.9 %copy-start.24 = (f32[8,512]{1,0:T(8,128)S(1)}, f32[8,512]{1,0:T(8,128)}, u32[]{:S(2)}) copy-start(f32[8,512]{1,0:T(8,128)} %get-tuple-element.182) | copy-start | bytes 49156
  163.1 10.7 %copy-start.1 = (bf16[8,224,512]{2,1,0:T(8,128)(2,1)S(1)}, bf16[8,224,512]{2,1,0:T(8,128)(2,1)}, u32[]{:S(2)}) copy-start(bf16[8,224,512]{2,1,0:T(8,128)(2,1)} %get-tuple-element.174.refs_1_) | copy-start | bytes 5505028
  163.1 10.7 %copy-start.12 = (s32[9]{0:T(128)S(1)}, s32[9]{0:T(128)}, u32[]{:S(2)}) copy-start(s32[9]{0:T(128)} %concatenate.15.refs_0_.info) | copy-start | bytes 112
  171.7 8.5 %copy-start.21 = (f32[16,512]{1,0:T(8,128)S(1)}, f32[16,512]{1,0:T(8,128)}, u32[]{:S(2)}) copy-start(f32[16,512]{1,0:T(8,128)} %get-tuple-element.179) | copy-start | bytes 98308
  171.7 8.5 %copy-start.2 = (bf16[8,160,512]{2,1,0:T(8,128)(2,1)S(1)}, bf16[8,160,512]{2,1,0:T(8,128)(2,1)}, u32[]{:S(2)}) copy-start(bf16[8,160,512]{2,1,0:T(8,128)(2,1)} %get-tuple-element.166) | copy-start | bytes 3932164
  171.7 8.5 %collective-permute-start.8 = (bf16[8,160,512]{2,1,0:T(8,128)(2,1)}, bf16[8,160,512]{2,1,0:T(8,128)(2,1)}, u32[]{:S(2)}, u32[]{:S(2)}) collective-permute-start(bf16[8,160,512]{2,1,0:T(8,128)(2,1)} %get-tuple-element.167), channel_id=1, source_target_pairs={{0,1},{1,0},{2,3},{3,2},{4,5},{5,4},{6,7},{7,6},{8,9},{9,8},{10,11... | collective-permute-start | bytes 3932168 | tf_op jit(solution)/shard_map/ppermute | solution.py:1159
  178.6 6.0 %copy-start.26 = (f32[1,2048]{1,0:T(1,128)S(1)}, f32[1,2048]{1,0:T(1,128)}, u32[]{:S(2)}) copy-start(f32[1,2048]{1,0:T(1,128)} %get-tuple-element.184) | copy-start | bytes 24580
  178.6 6.7 %copy-start.27 = (f32[8,512]{1,0:T(8,128)S(1)}, f32[8,512]{1,0:T(8,128)}, u32[]{:S(2)}) copy-start(f32[8,512]{1,0:T(8,128)} %get-tuple-element.181) | copy-start | bytes 49156
  178.6 6.7 %copy-start = (bf16[2,256,512]{2,1,0:T(8,128)(2,1)S(1)}, bf16[2,256,512]{2,1,0:T(8,128)(2,1)}, u32[]{:S(2)}) copy-start(bf16[2,256,512]{2,1,0:T(8,128)(2,1)} %refs_1_.7) | copy-start | bytes 1572868
  178.6 6.7 %copy-start.3 = (f32[512,512]{1,0:T(8,128)S(1)}, f32[512,512]{1,0:T(8,128)}, u32[]{:S(2)}) copy-start(f32[512,512]{1,0:T(8,128)} %get-tuple-element.169.refs_2_) | copy-start | bytes 3145732
  178.6 6.7 %copy-start.10 = (f32[6,512]{1,0:T(8,128)S(1)}, f32[6,512]{1,0:T(8,128)}, u32[]{:S(2)}) copy-start(f32[6,512]{1,0:T(8,128)} %refs_0_.3) | copy-start | bytes 36868
  178.6 29.4 %collective-permute-start.11 = (bf16[8,224,256]{2,1,0:T(8,128)(2,1)}, bf16[8,224,256]{2,1,0:T(8,128)(2,1)}, u32[]{:S(2)}, u32[]{:S(2)}) collective-permute-start(bf16[8,224,256]{2,1,0:T(8,128)(2,1)} %get-tuple-element.178), channel_id=1, source_target_pairs={{0,16},{16,0},{1,17},{17,1},{2,18},{18,2},{3,19},{19,3},{4,20},{20... | collective-permute-start | bytes 2752520 | tf_op jit(solution)/shard_map/ppermute | solution.py:1356
  184.1 24.0 %copy-start.5 = (bf16[8,224,256]{2,1,0:T(8,128)(2,1)S(1)}, bf16[8,224,256]{2,1,0:T(8,128)(2,1)}, u32[]{:S(2)}) copy-start(bf16[8,224,256]{2,1,0:T(8,128)(2,1)} %copy-done.4) | copy-start | bytes 2752516
  184.1 24.0 %copy-start.7 = (bf16[4,1,160,512]{3,2,1,0:T(8,128)(2,1)S(1)}, bf16[4,1,160,512]{3,2,1,0:T(8,128)(2,1)}, u32[]{:S(2)}) copy-start(bf16[4,1,160,512]{3,2,1,0:T(8,128)(2,1)} %copy-done.6) | copy-start | bytes 1966084
  184.1 23.9 %collective-permute-start.10 = (bf16[4,160,512]{2,1,0:T(8,128)(2,1)}, bf16[4,160,512]{2,1,0:T(8,128)(2,1)}, u32[]{:S(2)}, u32[]{:S(2)}) collective-permute-start(bf16[4,160,512]{2,1,0:T(8,128)(2,1)} %bitcast.12), channel_id=1, source_target_pairs={{0,2},{1,3},{2,0},{3,1},{4,6},{5,7},{6,4},{7,5},{8,10},{9,11},{10,... | collective-permute-start | bytes 1966088 | tf_op jit(solution)/shard_map/ppermute | solution.py:1159
  189.8 1.9 collective-permute-start.12
  189.9 17.9 %collective-permute-start.13 = (f32[40,512]{1,0:T(8,128)S(1)}, f32[40,512]{1,0:T(8,128)S(1)}, u32[]{:S(2)}, u32[]{:S(2)}) collective-permute-start(f32[40,512]{1,0:T(8,128)S(1)} %concatenate.16.refs_5_), channel_id=1, source_target_pairs={{0,2},{1,3},{2,0},{3,1},{4,6},{5,7},{6,4},{7,5},{8,10},{9,11},{10,... | collective-permute-start | bytes 245768 | tf_op jit(solution)/shard_map/ppermute | solution.py:1159
  191.5 16.5 %collective-permute-start.14 = (f32[40,512]{1,0:T(8,128)S(1)}, f32[40,512]{1,0:T(8,128)S(1)}, u32[]{:S(2)}, u32[]{:S(2)}) collective-permute-start(f32[40,512]{1,0:T(8,128)S(1)} %concatenate.16.refs_5_), channel_id=1, source_target_pairs={{0,3},{1,2},{2,1},{3,0},{4,7},{5,6},{6,5},{7,4},{8,11},{9,10},{10,... | collective-permute-start | bytes 245768 | tf_op jit(solution)/shard_map/ppermute | solution.py:1159
  212.1 18.6 %collective-permute-start.18 = (bf16[4,224,256]{2,1,0:T(8,128)(2,1)S(1)}, bf16[4,224,256]{2,1,0:T(8,128)(2,1)S(1)}, u32[]{:S(2)}, u32[]{:S(2)}) collective-permute-start(bf16[4,224,256]{2,1,0:T(8,128)(2,1)S(1)} %bitcast.42), channel_id=1, source_target_pairs={{0,2},{1,3},{2,0},{3,1},{4,6},{5,7},{6,4},{7,5},{8,10},{9,11},{10,... | collective-permute-start | bytes 1376264 | tf_op jit(solution)/shard_map/ppermute | solution.py:1159
  212.5 8.2 %collective-permute-start.15 = (bf16[1,160,512]{2,1,0:T(8,128)(2,1)S(1)}, bf16[1,160,512]{2,1,0:T(8,128)(2,1)S(1)}, u32[]{:S(2)}, u32[]{:S(2)}) collective-permute-start(bf16[1,160,512]{2,1,0:T(8,128)(2,1)S(1)} %bitcast.45), channel_id=1, source_target_pairs={{0,4},{1,5},{2,6},{3,7},{4,0},{5,1},{6,2},{7,3},{8,12},{9,13},{10,... | collective-permute-start | bytes 491528 | tf_op jit(solution)/shard_map/ppermute | solution.py:1159
  214.1 12.0 %collective-permute-start.16 = (bf16[1,160,512]{2,1,0:T(8,128)(2,1)S(1)}, bf16[1,160,512]{2,1,0:T(8,128)(2,1)S(1)}, u32[]{:S(2)}, u32[]{:S(2)}) collective-permute-start(bf16[1,160,512]{2,1,0:T(8,128)(2,1)S(1)} %bitcast.44), channel_id=1, source_target_pairs={{0,8},{1,9},{2,10},{3,11},{4,12},{5,13},{6,14},{7,15},{8,0},{9,1},... | collective-permute-start | bytes 491528 | tf_op jit(solution)/shard_map/ppermute | solution.py:1159
  214.5 16.3 %collective-permute-start.17 = (bf16[1,160,512]{2,1,0:T(8,128)(2,1)S(1)}, bf16[1,160,512]{2,1,0:T(8,128)(2,1)S(1)}, u32[]{:S(2)}, u32[]{:S(2)}) collective-permute-start(bf16[1,160,512]{2,1,0:T(8,128)(2,1)S(1)} %bitcast.43), channel_id=1, source_target_pairs={{0,12},{1,13},{2,14},{3,15},{4,8},{5,9},{6,10},{7,11},{8,4},{9,5},... | collective-permute-start | bytes 491528 | tf_op jit(solution)/shard_map/ppermute | solution.py:1159
  216.0 4.4 %collective-permute-start.19 = (f32[40,512]{1,0:T(8,128)S(1)}, f32[40,512]{1,0:T(8,128)S(1)}, u32[]{:S(2)}, u32[]{:S(2)}) collective-permute-start(f32[40,512]{1,0:T(8,128)S(1)} %get-tuple-element.192.refs_7_), channel_id=1, source_target_pairs={{0,16},{16,0},{1,17},{17,1},{2,18},{18,2},{3,19},{19,3},{4,20},{20... | collective-permute-start | bytes 245768 | tf_op jit(solution)/shard_map/ppermute | solution.py:1390
  234.2 5.9 %collective-permute-start.26 = (f32[40,512]{1,0:T(8,128)S(1)}, f32[40,512]{1,0:T(8,128)S(1)}, u32[]{:S(2)}, u32[]{:S(2)}) collective-permute-start(f32[40,512]{1,0:T(8,128)S(1)} %get-tuple-element.205), channel_id=1, source_target_pairs={{0,4},{1,5},{2,6},{3,7},{4,0},{5,1},{6,2},{7,3},{8,12},{9,13},{10,... | collective-permute-start | bytes 245768 | tf_op jit(solution)/shard_map/ppermute | solution.py:1159
  234.2 7.4 %collective-permute-start.27 = (f32[40,512]{1,0:T(8,128)S(1)}, f32[40,512]{1,0:T(8,128)S(1)}, u32[]{:S(2)}, u32[]{:S(2)}) collective-permute-start(f32[40,512]{1,0:T(8,128)S(1)} %get-tuple-element.205), channel_id=1, source_target_pairs={{0,8},{1,9},{2,10},{3,11},{4,12},{5,13},{6,14},{7,15},{8,0},{9,1},... | collective-permute-start | bytes 245768 | tf_op jit(solution)/shard_map/ppermute | solution.py:1159
  236.6 13.6 %collective-permute-start.28 = (f32[40,512]{1,0:T(8,128)S(1)}, f32[40,512]{1,0:T(8,128)S(1)}, u32[]{:S(2)}, u32[]{:S(2)}) collective-permute-start(f32[40,512]{1,0:T(8,128)S(1)} %get-tuple-element.205), channel_id=1, source_target_pairs={{0,12},{1,13},{2,14},{3,15},{4,8},{5,9},{6,10},{7,11},{8,4},{9,5},... | collective-permute-start | bytes 245768 | tf_op jit(solution)/shard_map/ppermute | solution.py:1159
  237.7 14.7 %collective-permute-start.20 = (bf16[1,224,256]{2,1,0:T(8,128)(2,1)S(1)}, bf16[1,224,256]{2,1,0:T(8,128)(2,1)S(1)}, u32[]{:S(2)}, u32[]{:S(2)}) collective-permute-start(bf16[1,224,256]{2,1,0:T(8,128)(2,1)S(1)} %bitcast.48), channel_id=1, source_target_pairs={{0,4},{1,5},{2,6},{3,7},{4,0},{5,1},{6,2},{7,3},{8,12},{9,13},{10,... | collective-permute-start | bytes 344072 | tf_op jit(solution)/shard_map/ppermute | solution.py:1159
  238.7 13.7 %collective-permute-start.21 = (bf16[1,224,256]{2,1,0:T(8,128)(2,1)S(1)}, bf16[1,224,256]{2,1,0:T(8,128)(2,1)S(1)}, u32[]{:S(2)}, u32[]{:S(2)}) collective-permute-start(bf16[1,224,256]{2,1,0:T(8,128)(2,1)S(1)} %bitcast.47), channel_id=1, source_target_pairs={{0,8},{1,9},{2,10},{3,11},{4,12},{5,13},{6,14},{7,15},{8,0},{9,1},... | collective-permute-start | bytes 344072 | tf_op jit(solution)/shard_map/ppermute | solution.py:1159
  240.1 14.0 %collective-permute-start.22 = (bf16[1,224,256]{2,1,0:T(8,128)(2,1)S(1)}, bf16[1,224,256]{2,1,0:T(8,128)(2,1)S(1)}, u32[]{:S(2)}, u32[]{:S(2)}) collective-permute-start(bf16[1,224,256]{2,1,0:T(8,128)(2,1)S(1)} %bitcast.46), channel_id=1, source_target_pairs={{0,12},{1,13},{2,14},{3,15},{4,8},{5,9},{6,10},{7,11},{8,4},{9,5},... | collective-permute-start | bytes 344072 | tf_op jit(solution)/shard_map/ppermute | solution.py:1159
  250.4 10.5 %collective-permute-start.24 = (bf16[1,192,1024]{2,1,0:T(8,128)(2,1)}, bf16[1,192,1024]{2,1,0:T(8,128)(2,1)S(1)}, u32[]{:S(2)}, u32[]{:S(2)}) collective-permute-start(bf16[1,192,1024]{2,1,0:T(8,128)(2,1)} %reduce-scatter.2.cloned.1.call-done.refs_3_), channel_id=1, source_target_pairs={{0,16},{16,0},{1,17},{17,1},{2,18},{18,2},{3,19},{19,3},{4,20},{20... | collective-permute-start | bytes 1179656 | tf_op jit(solution)/shard_map/ppermute | solution.py:1387
  251.4 9.5 %collective-permute-start.23 = (bf16[1,160,512]{2,1,0:T(8,128)(2,1)S(1)}, bf16[1,160,512]{2,1,0:T(8,128)(2,1)S(1)}, u32[]{:S(2)}, u32[]{:S(2)}) collective-permute-start(bf16[1,160,512]{2,1,0:T(8,128)(2,1)S(1)} %get-tuple-element.196.refs_2_), channel_id=1, source_target_pairs={{0,16},{16,0},{1,17},{17,1},{2,18},{18,2},{3,19},{19,3},{4,20},{20... | collective-permute-start | bytes 491528 | tf_op jit(solution)/shard_map/ppermute | solution.py:1386
  264.4 4.9 %collective-permute-start.25 = (bf16[1,224,256]{2,1,0:T(8,128)(2,1)S(1)}, bf16[1,224,256]{2,1,0:T(8,128)(2,1)S(1)}, u32[]{:S(2)}, u32[]{:S(2)}) collective-permute-start(bf16[1,224,256]{2,1,0:T(8,128)(2,1)S(1)} %get-tuple-element.202), channel_id=1, source_target_pairs={{0,16},{16,0},{1,17},{17,1},{2,18},{18,2},{3,19},{19,3},{4,20},{20... | collective-permute-start | bytes 344072 | tf_op jit(solution)/shard_map/ppermute | solution.py:1395
  (14 other events, 13.1 us)
Sparse Core Ops, SparseCore 0:
  120.3 88.7 reduce-scatter.1

commit v4 on v3

--- a/solution.py
+++ b/solution.py
@@ -186,9 +186,9 @@
 
 def staged(
     name, body, ins, outs, smem=(), scratch=(), flops=0, moved=0, sends=0, filled=None,
-    limit=VMEM_LIMIT,
+    limit=VMEM_LIMIT, kept=None,
 ):
-    operands, loads, stores = [], [], []
+    operands, loads, stores, kept = [], [], [], kept or {}
     for key, items in ins.items():
         single = not isinstance(items, list)
         entries = []
@@ -209,19 +209,19 @@
         stores.append((key, entries, single))
     aliases = {}
     if filled is not None:
-        aliases = {len(smem) + len(operands): 0}
+        aliases = {len(smem) + len(kept) + len(operands): 0}
         operands.append(filled)
     every_load = [entry for _, entries, _ in loads for entry in entries]
     every_store = [entry for _, entries, _ in stores for entry in entries]
     n_smem, n_ops, n_outs, n_loads = len(smem), len(operands), len(every_store), len(every_load)
 
     def run(*refs):
-        cuts = [n_smem, n_ops, n_outs, n_loads, n_outs, 1]
+        cuts = [n_smem, len(kept), n_ops, n_outs, n_loads, n_outs, 1]
         taken, at = [], 0
         for cut in cuts:
             taken.append(refs[at : at + cut])
             at += cut
-        scalars, given, targets, buffers, results, sems = taken
+        scalars, here, given, targets, buffers, results, sems = taken
         buffers, places = iter(buffers), iter(zip(targets, results))
         placed_loads = [
             (
@@ -239,6 +239,7 @@
                 pairs.append((target if view is None else view(target), result))
             placed_stores.append((key, pairs, single))
         stage = Stage(placed_loads, placed_stores, sems[0])
+        stage.named.update(zip(kept, here))
         body(stage, *scalars, *refs[at:])
         stage.finish()
 
@@ -246,7 +247,9 @@
     got = iter(
         pl.pallas_call(
             run,
-            in_specs=[pl.BlockSpec(memory_space=pltpu.SMEM)] * n_smem + [hbm] * n_ops,
+            in_specs=[pl.BlockSpec(memory_space=pltpu.SMEM)] * n_smem
+            + [pl.BlockSpec(memory_space=pltpu.VMEM)] * len(kept)
+            + [hbm] * n_ops,
             out_specs=[hbm] * n_outs,
             out_shape=[shape for shape, _, _ in every_store],
             scratch_shapes=[pltpu.VMEM(shape, dtype) for _, _, shape, dtype in every_load]
@@ -257,7 +260,7 @@
             compiler_params=pltpu.CompilerParams(vmem_limit_bytes=limit),
             cost_estimate=pl.CostEstimate(flops=flops, bytes_accessed=moved, transcendentals=0),
             name=name,
-        )(*smem, *operands)
+        )(*smem, *kept.values(), *operands)
     )
     result = types.SimpleNamespace()
     for key, entries, single in stores:
@@ -478,6 +481,14 @@
     return (at < info[1 + rows + row].astype(f32)).astype(f32)
 
 
+def put_rows(ref, part, vector):
+    model = ref.shape[1]
+    per = vector.shape[1] // model
+    for one in range(per):
+        at = part * per + one
+        ref[at : at + 1] = vector[:, one * model : (one + 1) * model]
+
+
 def pack(ref, vectors):
     at = 0
     for vector in vectors:
@@ -558,7 +569,7 @@
     return staged(
         "depth_conv",
         body,
-        dict(ends=ends, before=before, taps=taps, gated=by_row(gated, rows), after=after),
+        dict(ends=ends, taps=taps, gated=by_row(gated, rows)),
         dict(depth=sds((rows * frames, model), f32), stats=sds((devices, 8, 128), f32)),
         smem=[info],
         scratch=[
@@ -568,6 +579,7 @@
             pltpu.VMEM((8, model), f32),
             pltpu.VMEM((8, 128), f32),
         ],
+        kept=dict(before=before, after=after),
         flops=rows * frames * model * 30,
         moved=2 << 20,
         sends=rows - 1,
@@ -643,7 +655,7 @@
             cut = slice(part * PART, (part + 1) * PART)
             grad = (dot_last(k.gl[...], k.w_out[part][...]) * slope_s[:, cut]).astype(bf16)
             k.gi[:, cut] = grad
-            k.fb[:, cut] = total(grad.astype(f32))
+            put_rows(k.fb, part, total(grad.astype(f32)))
             back = back + dot_last(grad, k.w_in[part][...])
         k.send(k.gi)
         normal, inverse = normalize(conv_s[...])
@@ -675,7 +687,7 @@
 
     w_in, w_out = feed_slabs(feed_in, feed_out, 1)
     ins = dict(
-        stats=stats, counts=counts, gain=gain, shift=shift, depth=depth, bias=bias,
+        gain=gain, shift=shift, depth=depth, bias=bias,
         convolve_out=convolve_out, stream=stream, b_in=feed_in_bias, w_in=w_in, w_out=w_out,
         cotangent=cotangent,
     )
@@ -690,7 +702,7 @@
             out=low, act=sds((tokens, hidden), bf16), gi=sds((tokens, hidden), bf16), nf=low,
             gl=low, sw=low, gcl=low, gcs=wide, gb=wide, bn=wide, inv=sds((8, model), f32),
             totals=sds((devices, 8, 128), f32), first=rim, last=rim, vec=sds((8, model), f32),
-            fb=sds((1, hidden), f32),
+            fb=sds((hidden // model, model), f32),
         ),
         smem=[info],
         scratch=[
@@ -698,6 +710,7 @@
             pltpu.VMEM((tokens, hidden), f32),
             pltpu.VMEM((8, 128), f32),
         ],
+        kept=dict(stats=stats, counts=counts),
         flops=2 * tokens * model * (4 * hidden + 2 * model),
         moved=24 << 20,
     )
@@ -816,9 +829,8 @@
         "conv_back",
         body,
         dict(
-            totals=totals, inv=mid.inv, gain=gain, ends=ends, taps=taps, edge_before=edge_before,
-            edge_after=edge_after, rim_before=rim_before, rim_after=rim_after,
-            gb=by_row(mid.gb, rows), bn=by_row(mid.bn, rows), gated=by_row(mix.gated, rows),
+            inv=mid.inv, gain=gain, ends=ends, taps=taps, rim_before=rim_before,
+            rim_after=rim_after, gb=by_row(mid.gb, rows), bn=by_row(mid.bn, rows), gated=by_row(mix.gated, rows),
             paired=by_row(mix.paired, rows), convolve_in=convolve_in, after=mix.out, gcs=mid.gcs,
             attend_out=attend_out, nc=mix.nc, sw=mid.sw, gcl=mid.gcl, mixed=mix.mixed,
         ),
@@ -834,6 +846,7 @@
             pltpu.VMEM((tokens, 2 * model), bf16),
             pltpu.VMEM((tokens, model), bf16),
         ],
+        kept=dict(totals=totals, edge_before=edge_before, edge_after=edge_after),
         flops=2 * tokens * model * 7 * model,
         moved=16 << 20,
         filled=early if room else None,
@@ -952,9 +965,9 @@
             low_half = slice(row * frames, row * frames + WIN)
             high_half = slice(row * frames + WIN, (row + 1) * frames)
             joined[here, :model] = k.gq[row][...]
-            pair = (k.g_lo[row][...] + k.left[row][...].astype(f32)).astype(bf16)
+            pair = (k.g_lo[row][...] + k.left[row].astype(f32)).astype(bf16)
             joined[low_half, model:] = pair
-            pair = (k.g_hi[row][...] + k.right[row][...].astype(f32)).astype(bf16)
+            pair = (k.g_hi[row][...] + k.right[row].astype(f32)).astype(bf16)
             joined[high_half, model:] = pair
             both = joined[here]
             k.gv[here] = both[:, 2 * model :]
@@ -998,8 +1011,7 @@
         "back",
         body,
         dict(
-            gain=gain, gq=grads.gq, g_lo=grads.g_lo, left=each_of(halo[0]), g_hi=grads.g_hi,
-            right=each_of(halo[1]), attend_in=attend_in, after=by_row(start.after, rows),
+            gain=gain, gq=grads.gq, g_lo=grads.g_lo, g_hi=grads.g_hi, attend_in=attend_in, after=by_row(start.after, rows),
             gas=by_row(gas, rows), na=start.na, g_table=grads.g_table, sinusoid=sinusoid,
             act=[slab(start.act, (0, tokens), (at, PART)) for at in range(0, hidden, PART)],
         ),
@@ -1009,6 +1021,7 @@
         ),
         smem=[info],
         scratch=[pltpu.VMEM((tokens, 3 * model), bf16)],
+        kept=dict(left=halo[0], right=halo[1]),
         flops=2 * tokens * model * (hidden + 6 * model),
         moved=18 << 20,
         sends=2 * parts - 2,
@@ -1041,7 +1054,7 @@
             cut = slice(part * PART, (part + 1) * PART)
             grad = dot_last(k.gl[...], k.w_out[part][...])
             grad = (grad * k.slope[part][...].astype(f32)).astype(bf16)
-            k.fb[:, cut] = total(grad.astype(f32))
+            put_rows(k.fb, part, total(grad.astype(f32)))
             block = dot_first(grad, k.n0[...])
             some = (part * step, (part + 1) * step)
             keep_half(block, core, k.mine, k.other, some)
@@ -1060,7 +1073,7 @@
             slope=[slab(start.slope, (0, tokens), (at, PART)) for at in range(0, hidden, PART)],
             n0=start.n0, w_in=w_in,
         ),
-        dict(other=half, mine=half, fb=sds((1, hidden), f32), gn=sds((tokens, model), f32)),
+        dict(other=half, mine=half, fb=sds((hidden // model, model), f32), gn=sds((tokens, model), f32)),
         smem=[info],
         flops=2 * tokens * model * hidden * 3,
         moved=12 << 20,
@@ -1152,6 +1165,7 @@
 
 ROW_PAIR = [(0, 1), (1, 0)]
 COLUMNS, IN_FLOAT = 1, 2
+N_VECTORS = KERNEL + 5 + 5 + 10
 
 
 def swap(x, k):
@@ -1182,14 +1196,22 @@
         keeps.append(sds(half, f32 if how == IN_FLOAT else bf16))
         sends += [sds(half, bf16)] * n_sends
 
-    def body(k, info):
+    n_small = 0 if small is None else len(small)
+
+    def body(info, *refs):
+        cuts = [len(mines), len(gots), n_small, len(keeps), len(sends)]
+        taken, at = [], 0
+        for cut in cuts:
+            taken.append(refs[at : at + cut])
+            at += cut
+        mine_refs, got_refs, small_refs, keep_refs, send_refs = taken
         for at, (got_at, n_got, send_at, _, how) in enumerate(plans):
-            parts = [k.mine[at]] + [k.got[got_at + one] for one in range(n_got)]
+            parts = [mine_refs[at], *got_refs[got_at : got_at + n_got]]
 
             def added(*index):
                 return sum(part[index].astype(f32) for part in parts)
 
-            keep = k.keep[at]
+            keep = keep_refs[at]
             if how is None or how == IN_FLOAT:
                 keep[...] = added(...).astype(keep.dtype)
             elif how == COLUMNS:
@@ -1199,8 +1221,7 @@
                     for one in range(2)
                 ]
                 first = info[row_at] == 0
-                k.away[send_at][...] = jnp.where(first, both[1], both[0]).astype(bf16)
-                k.send(k.away[send_at])
+                send_refs[send_at][...] = jnp.where(first, both[1], both[0]).astype(bf16)
                 keep[...] = jnp.where(first, both[0], both[1]).astype(bf16)
             else:
                 digit = info[how[0]]
@@ -1209,33 +1230,45 @@
                     for bit in (1, 2):
                         if one & bit:
                             other = other + bit * (1 - 2 * ((digit // bit) % 2))
-                    k.away[send_at + one - 1][...] = added(slice(None), other).astype(bf16)
-                    k.send(k.away[send_at + one - 1])
+                    send_refs[send_at + one - 1][...] = added(slice(None), other).astype(bf16)
                 keep[...] = added(slice(None), digit).astype(bf16)
-        if small is not None:
-            k.total[...] = sum(k.small[one][...] for one in range(len(small)))
-
-    ins, outs = dict(mine=mines, got=gots), dict(keep=keeps, away=sends)
-    if small is not None:
-        ins |= dict(small=list(small))
-        outs |= dict(total=sds(small[0].shape, f32))
-    got = staged(name, body, ins, outs, smem=[info], flops=1 << 20, moved=2 << 20, limit=FOLD_LIMIT)
+        if n_small:
+            refs[-1][...] = sum(one[...] for one in small_refs)
+
+    shapes = keeps + sends + ([sds(small[0].shape, f32)] if n_small else [])
+    here = pl.BlockSpec(memory_space=pltpu.VMEM)
+    given = mines + gots + (list(small) if n_small else [])
+    got = pl.pallas_call(
+        body,
+        in_specs=[pl.BlockSpec(memory_space=pltpu.SMEM)] + [here] * len(given),
+        out_specs=[here] * len(shapes),
+        out_shape=shapes,
+        compiler_params=pltpu.CompilerParams(vmem_limit_bytes=FOLD_LIMIT),
+        cost_estimate=pl.CostEstimate(flops=1 << 20, bytes_accessed=2 << 20, transcendentals=0),
+        name=name,
+    )(info, *given)
+    kept, away = got[: len(keeps)], got[len(keeps) : len(keeps) + len(sends)]
     results = []
     for at, (mine, _, how) in enumerate(states):
         size, height, model = mine.shape
-        shape = (size // how[2], height, model) if isinstance(how, tuple) else got.keep[at].shape
+        shape = (size // how[2], height, model) if isinstance(how, tuple) else kept[at].shape
         _, _, send_at, n_sends, _ = plans[at]
-        away = [one.reshape(shape) for one in got.away[send_at : send_at + n_sends]]
-        results.append((got.keep[at].reshape(shape), away))
-    if small is not None:
-        results.append(got.total)
+        some = [one.reshape(shape) for one in away[send_at : send_at + n_sends]]
+        results.append((kept[at].reshape(shape), some))
+    if n_small:
+        results.append(got[-1])
     return results
 
 
-def finish(info, row_at, a, b, b_got, early, width, slim):
+def finish(info, row_at, frames, a, b, b_got, early, small, totals, width, slim):
     model = a.shape[1]
-
-    def body(info, a, b, b_got, early, feed_in, feed_out, joined, attend, place, con_in, con_out):
+    feed_rows = small[0].shape[0] - N_VECTORS
+    per = feed_rows // 2
+
+    def body(info, a, b, b_got, early, totals, *refs):
+        sums, refs = refs[: len(small)], refs[len(small) :]
+        feed_in, feed_out, joined, attend, place, con_in, con_out, *refs = refs
+        depth, gain, shift, bias, feed_bias, vectors = refs
         feed_in[0] = a[:width].T
         feed_in[1] = early[:width, :model].T
         first = info[row_at] == 0
@@ -1250,24 +1283,43 @@
         con_in[...] = early[width : width + slim]
         con_out[...] = early[width + slim :, :model]
         attend[...] = early[width + slim :, model:]
+        me = info[0] // frames
+        end = N_VECTORS + feed_rows
+        vectors[end:] = jnp.zeros((vectors.shape[0] - end, model), f32)
+        vectors[:end] = sum(one[...] for one in sums)
+        vectors[end : end + 2] = totals[...]
+        own = pltpu.roll(vectors[...], lax.rem(model - me * slim, model), 1)[:, :slim]
+        depth[...] = own[:KERNEL]
+        gain[0:5] = own[KERNEL : KERNEL + 5]
+        gain[5:6] = own[end + 1 : end + 2]
+        shift[0:5] = own[KERNEL + 5 : KERNEL + 10]
+        shift[5:6] = own[end : end + 1]
+        bias[...] = own[KERNEL + 10 : N_VECTORS]
+        at = me * width
+        for module in range(2):
+            row = vectors[pl.ds(N_VECTORS + module * per + at // model, 1), :]
+            row = pltpu.roll(row, lax.rem(model - lax.rem(at, model), model), 1)
+            feed_bias[module : module + 1] = row[:, :width]
 
     def full(shape):
         return pl.BlockSpec(shape, lambda i: (0,) * len(shape))
 
     shapes = [
         (2, model, width), (2, width, model), (slim, 3 * model), (slim, model), (slim, model),
-        (slim, 2 * model), (slim, model),
+        (slim, 2 * model), (slim, model), (KERNEL, slim), (6, slim), (6, slim), (10, slim),
+        (2, width),
     ]
+    given = (a, b, b_got, early, totals, *small)
     return pl.pallas_call(
         body,
         grid=(1,),
-        in_specs=[pl.BlockSpec(memory_space=pltpu.SMEM)]
-        + [full(one.shape) for one in (a, b, b_got, early)],
+        in_specs=[pl.BlockSpec(memory_space=pltpu.SMEM)] + [full(one.shape) for one in given],
         out_specs=[full(shape) for shape in shapes],
         out_shape=[sds(shape, f32) for shape in shapes],
+        scratch_shapes=[pltpu.VMEM((-(-(N_VECTORS + feed_rows + 2) // 8) * 8, model), f32)],
         compiler_params=pltpu.CompilerParams(vmem_limit_bytes=FOLD_LIMIT),
         name="finish",
-    )(info, a, b, b_got, early)
+    )(info, *given)
 
 
 def per_device(
@@ -1367,8 +1419,7 @@
             vec_last[1:2], vec_back[3:4], vec_conv[10:11], vec_mid[1:2], vec_mid[3:4],
             vec_back[0:2], vec_conv[13:14], vec_conv[11:13], vec_mid[4:5], vec_back[4:5],
             vec_mid[5:6], grads.vec[0:2],
-            got.fb.reshape(-1, model), mid.fb.reshape(-1, model),
-            jnp.zeros((3, model), f32),
+            got.fb, mid.fb,
         ],
         axis=0,
     )
@@ -1396,15 +1447,9 @@
     small = [one] + swaps([one] * (last_group[1] - 1), last_group)
     slim = model // n
     width = hidden // n
-    feed_in_grad, feed_out_grad, joined, *rest = finish(
-        info, row_at, a[0], b[0], b_got[0], early[0], width, slim
-    )
-    small = sum(small)
-    n_vectors = small.shape[0] - 3 - 2 * (hidden // model)
-    vectors = jnp.concatenate([small[:n_vectors], vec_conv[14:16]], axis=0)
-    thin = lax.dynamic_slice_in_dim(vectors, me * slim, slim, 1)
-    feed_bias = small[n_vectors:-3].reshape(2, hidden)
-    feed_bias = lax.dynamic_slice_in_dim(feed_bias, me * width, width, 1)
+    feed_in_grad, feed_out_grad, joined, *rest, depth, gain, shift, bias, feed_bias = finish(
+        info, row_at, frames, a[0], b[0], b_got[0], early[0], small, vec_conv[14:16], width, slim
+    )
     return (
         mid.out.reshape(rows, frames, model),
         ending.out,
@@ -1413,10 +1458,10 @@
         feed_out_grad,
         joined,
         *rest,
-        thin[:KERNEL],
-        jnp.concatenate([thin[KERNEL : KERNEL + 5], thin[n_vectors + 1 :]], axis=0),
-        jnp.concatenate([thin[KERNEL + 5 : KERNEL + 10], thin[n_vectors : n_vectors + 1]], axis=0),
-        thin[KERNEL + 10 : n_vectors],
+        depth,
+        gain,
+        shift,
+        bias,
     )
 
 

time: 283 us -> 266 us (0.940)
  the two profiles are of different devices: /device:TPU:16 before, /device:TPU:0 now
where the time goes in v4:
time: 266 us; the launch traced here: 261 us
  Pallas kernels  111 us (42%)
  starting transfers between devices  70.2 us (26%)
  waiting for transfers between devices  56.9 us (21%)
  between operations  14.9 us (6%)
  local copies, waits for them, and re-layouts  7.6 us (3%)
    pallas_call x11, Pallas kernels, staged(): pl.pallas_call(run, in_specs=[pl.BlockSpec(memory_space=pltpu.SMEM)] * n_...  103 us
    ppermute x16, waiting for transfers between devices, swap(): return lax.ppermute(x, 'frames', [(i, i ^ k) for i in range(n)])  38 us
    ppermute x16, starting transfers between devices, swap(): return lax.ppermute(x, 'frames', [(i, i ^ k) for i in range(n)])  29.7 us
    ppermute x4, starting transfers between devices, neighbours(): lax.ppermute(last_block, 'frames', up)  19.9 us
    all_to_all x2, starting transfers between devices, gather(): return lax.all_to_all(copies, DEVICES, 0, 0, tiled=True)  8.72 us
    all_to_all x2, waiting for transfers between devices, gather(): return lax.all_to_all(copies, DEVICES, 0, 0, tiled=True)  7.78 us
    ppermute x4, waiting for transfers between devices, neighbours(): lax.ppermute(first_block, 'frames', down)  6.98 us
    pallas_call x5, Pallas kernels, fold(): pl.pallas_call(body, in_specs=[pl.BlockSpec(memory_space=pltpu.SMEM)] + [...  5.91 us
  transfers between devices with their start and end apart: 32, of which 13 were waited for; matrix products, arithmetic and copies ran while one was open for 1% of the time, Pallas kernels for 19%

profile of v4, /device:TPU:0, one launch (start us, length us, event | category | flops | bytes accessed | tf_op | source)
XLA Modules:
  0.0 260.9 jit_solution(17558046095988032813)
XLA Ops:
  7.2 7.5 %front.1 = (f32[512,512]{1,0:T(8,128)}, bf16[512,512]{1,0:T(8,128)(2,1)}, bf16[512,512]{1,0:T(8,128)(2,1)}, bf16[2,128,1024]{2,1,0:T(8,128)(2,1)}, bf16[2,128,10...) custom-call(bf16[2,256,512]{2,1,0:T(8,128)(2,1)} %refs_1_.5, f32[6,512]{1,0:T(8,128)} %refs_0_.3, ...), custom_call_target="tpu_custom_call" | custom-call | flops 2684354560 | bytes 16777216 | tf_op jit(solution)/shard_map/front/pallas_call | solution.py:248
  14.7 1.3 collective-permute-start.1
  16.0 3.2 %collective-permute-start = (bf16[2,128,1024]{2,1,0:T(8,128)(2,1)}, bf16[2,128,1024]{2,1,0:T(8,128)(2,1)S(1)}, u32[]{:S(2)}, u32[]{:S(2)}) collective-permute-start(bf16[2,128,1024]{2,1,0:T(8,128)(2,1)} %get-tuple-element.123.refs_6_.refs_5_), channel_id=1, source_target_pairs={{0,1},{1,2},{2,3},{3,4},{4,5},{5,6},{6,7},{7,8},{8,9},{9,10},{10,1... | collective-permute-start | bytes 1572872 | tf_op jit(solution)/shard_map/ppermute | solution.py:1155
  21.0 3.0 %queries.1 = (bf16[512,512]{1,0:T(8,128)(2,1)}, bf16[512,512]{1,0:T(8,128)(2,1)}, bf16[384,512]{1,0:T(8,128)(2,1)}) custom-call(bf16[512,512]{1,0:T(8,128)(2,1)} %get-tuple-element.118.refs_0_.refs_13_.refs_1_, bf16[512,1536]{1,0:T(8,128)(2,1)} %refs_10_.5, f32[10,512]{1,0:T(8,128)} %refs_6_.3, bf16[384,512]{1,0:T(8,128)(2,1)} %constant.66.clone.refs_3_.refs_15_, ...), custom_call_target="tpu_custom_call" | custom-call | flops 536870912 | bytes 4194304 | tf_op jit(solution)/shard_map/queries/pallas_call | solution.py:248
  24.9 17.1 %attend.1 = (bf16[2,2,128,1536]{3,2,1,0:T(8,128)(2,1)}, bf16[2,2,128,1536]{3,2,1,0:T(8,128)(2,1)}, bf16[512,512]{1,0:T(8,128)(2,1)}, f32[512,512]{1,0:T(8,128)},...) custom-call(s32[9]{0:T(128)} %concatenate.6.refs_0_.info, ...), custom_call_target="tpu_custom_call" | custom-call | flops 1610612736 | bytes 16777216 | tf_op jit(solution)/shard_map/attend/pallas_call | solution.py:248
  42.1 10.4 %collective-permute-start.2 = (bf16[2,16,512]{2,1,0:T(8,128)(2,1)}, bf16[2,16,512]{2,1,0:T(8,128)(2,1)S(1)}, u32[]{:S(2)}, u32[]{:S(2)}) collective-permute-start(bf16[2,16,512]{2,1,0:T(8,128)(2,1)} %get-tuple-element.125), channel_id=1, source_target_pairs={{0,1},{1,2},{2,3},{3,4},{4,5},{5,6},{6,7},{7,8},{8,9},{9,10},{10,1... | collective-permute-start | bytes 98312 | tf_op jit(solution)/shard_map/ppermute | solution.py:1155
  52.5 1.7 collective-permute-start.3
  54.3 3.5 %collective-permute-done.3.refs_2_.refs_9_ = bf16[2,16,512]{2,1,0:T(8,128)(2,1)S(1)} collective-permute-done((bf16[2,16,512]{2,1,0:T(8,128)(2,1)}, bf16[2,16,512]{2,1,0:T(8,128)(2,1)S(1)}, u32[]{:S(2)}, u32[]{:S(2)}) %collective-permute-start.3) | collective-permute-done | bytes 32800 | tf_op jit(solution)/shard_map/ppermute | solution.py:1155
  58.3 6.0 %depth_conv.1 = (f32[512,512]{1,0:T(8,128)}, f32[32,8,128]{2,1,0:T(8,128)}) custom-call(s32[9]{0:T(128)} %concatenate.6.refs_0_.info, bf16[2,16,512]{2,1,0:T(8,128)(2,1)} %copy-done.16, bf16[2,16,512]{2,1,0:T(8,128)(2,1)} %copy-done.17, f32[8,128]{1,0:T(8,128)} %pad.4.refs_1_.refs_3_.refs_6_, f32[9,512]{1,0:T(8,128)} %refs_7_.6, ...), custom_call_target="tpu_custom_call" | custom-call | flops 7864320 | bytes 2097152 | tf_op jit(solution)/shard_map/depth_conv/pallas_call | solution.py:248
  64.3 6.1 %all-to-all-start = ((f32[32,8,128]{2,1,0:T(8,128)}), f32[32,8,128]{2,1,0:T(8,128)S(1)}, u32[]{:S(2)}, u32[]{:S(2)}) async-start(f32[32,8,128]{2,1,0:T(8,128)} %get-tuple-element.128), calls=%async_computation | async-start | bytes 262144 | tf_op jit(solution)/shard_map/all_to_all | solution.py:1159
  70.9 7.8 %all-to-all-done.refs_1_ = f32[32,8,128]{2,1,0:T(8,128)S(1)} async-done(((f32[32,8,128]{2,1,0:T(8,128)}), f32[32,8,128]{2,1,0:T(8,128)S(1)}, u32[]{:S(2)}, u32[]{:S(2)}) %all-to-all-start) | async-done | bytes 131104 | tf_op jit(solution)/shard_map/all_to_all | solution.py:1159
  79.3 12.8 %middle.1 = (bf16[512,512]{1,0:T(8,128)(2,1)}, bf16[512,2048]{1,0:T(8,128)(2,1)}, bf16[512,2048]{1,0:T(8,128)(2,1)}, bf16[512,512]{1,0:T(8,128)(2,1)}, bf16[512,...) custom-call(s32[9]{0:T(128)} %concatenate.6.refs_0_.info, ...), custom_call_target="tpu_custom_call" | custom-call | flops 4831838208 | bytes 25165824 | tf_op jit(solution)/shard_map/middle/pallas_call | solution.py:248
  92.1 2.6 all-to-all-start.1
  94.8 2.0 collective-permute-start.4
  96.8 1.3 collective-permute-start.5
  98.1 6.0 %feed_weights.1.refs_22_ = bf16[16,192,1024]{2,1,0:T(8,128)(2,1)} custom-call(bf16[512,512]{1,0:T(8,128)(2,1)} %get-tuple-element.133.refs_0_, bf16[512,2048]{1,0:T(8,128)(2,1)} %get-tuple-element.134.refs_1_, bf16[512,512]{1,0:T(8,128)(2,1)} %get-tuple-element.135.refs_2_, bf16[512,2048]{1,0:T(8,128)(2,1)} %get-tuple-element.136.refs_3_), custom_call_target="tpu_custom_call" | custom-call | flops 2147483648 | bytes 10485760 | tf_op jit(solution)/shard_map/feed_weights/pallas_call | solution.py:248
  104.8 14.7 %conv_back.1 = (bf16[16,192,1024]{2,1,0:T(8,128)(2,1)}, f32[512,512]{1,0:T(8,128)}, bf16[512,512]{1,0:T(8,128)(2,1)}, f32[16,512]{1,0:T(8,128)}) custom-call(s32[9]{0:T(128)} %concatenate.6.refs_0_.info, f32[32,8,128]{2,1,0:T(8,128)} %copy-done.11, f32[2,8,1024]{2,1,0:T(8,128)} %copy-done.20, ...), custom_call_target="tpu_custom_call", output_to_operand_aliasing={{0}: (22, {})} | custom-call | flops 1879048192 | bytes 16777216 | tf_op jit(solution)/shard_map/conv_back/pallas_call | solution.py:248
  119.6 14.7 %attend_back.1 = (bf16[256,512]{1,0:T(8,128)(2,1)}, bf16[256,512]{1,0:T(8,128)(2,1)}, bf16[2,128,1024]{2,1,0:T(8,128)(2,1)}, f32[128,1024]{1,0:T(8,128)}, f32[12...) custom-call(bf16[512,512]{1,0:T(8,128)(2,1)} %get-tuple-element.152., ...), custom_call_target="tpu_custom_call" | custom-call | flops 2818572288 | bytes 16777216 | tf_op jit(solution)/shard_map/attend_back/pallas_call | solution.py:248
  134.3 4.2 %collective-permute-start.6 = (bf16[2,128,1024]{2,1,0:T(8,128)(2,1)}, bf16[2,128,1024]{2,1,0:T(8,128)(2,1)S(1)}, u32[]{:S(2)}, u32[]{:S(2)}) collective-permute-start(bf16[2,128,1024]{2,1,0:T(8,128)(2,1)} %get-tuple-element.155), channel_id=1, source_target_pairs={{0,1},{1,2},{2,3},{3,4},{4,5},{5,6},{6,7},{7,8},{8,9},{9,10},{10,1... | collective-permute-start | bytes 1572872 | tf_op jit(solution)/shard_map/ppermute | solution.py:1155
  138.5 1.5 collective-permute-start.7
  140.2 3.5 %collective-permute-done.7.refs_2_ = bf16[2,128,1024]{2,1,0:T(8,128)(2,1)S(1)} collective-permute-done((bf16[2,128,1024]{2,1,0:T(8,128)(2,1)}, bf16[2,128,1024]{2,1,0:T(8,128)(2,1)S(1)}, u32[]{:S(2)}, u32[]{:S(2)}) %collective-permute-start.7) | collective-permute-done | bytes 524320 | tf_op jit(solution)/shard_map/ppermute | solution.py:1155
  144.5 10.5 %back.1 = (bf16[8,224,512]{2,1,0:T(8,128)(2,1)}, bf16[8,224,512]{2,1,0:T(8,128)(2,1)}, bf16[512,512]{1,0:T(8,128)(2,1)}, bf16[512,512]{1,0:T(8,128)(2,1)}, f32[2...) custom-call(s32[9]{0:T(128)} %concatenate.6.refs_0_.info, bf16[2,128,1024]{2,1,0:T(8,128)(2,1)} %copy-done.12, ...), custom_call_target="tpu_custom_call" | custom-call | flops 2684354560 | bytes 18874368 | tf_op jit(solution)/shard_map/back/pallas_call | solution.py:248
  155.0 7.9 %collective-permute-start.9 = (bf16[8,224,512]{2,1,0:T(8,128)(2,1)}, bf16[8,224,512]{2,1,0:T(8,128)(2,1)S(1)}, u32[]{:S(2)}, u32[]{:S(2)}) collective-permute-start(bf16[8,224,512]{2,1,0:T(8,128)(2,1)} %get-tuple-element.180), channel_id=1, source_target_pairs={{0,1},{1,0},{2,3},{3,2},{4,5},{5,4},{6,7},{7,6},{8,9},{9,8},{10,11... | collective-permute-start | bytes 5505032 | tf_op jit(solution)/shard_map/ppermute | solution.py:1173
  162.9 8.6 %first_back.1 = (bf16[8,160,512]{2,1,0:T(8,128)(2,1)}, bf16[8,160,512]{2,1,0:T(8,128)(2,1)}, f32[4,512]{1,0:T(4,128)}, f32[512,512]{1,0:T(8,128)}) custom-call(s32[9]{0:T(128)} %concatenate.6.refs_0_.info, bf16[512,512]{1,0:T(8,128)(2,1)} %get-tuple-element.118.refs_0_.refs_13_.refs_1_, bf16[512,512]{1,0:T(8,128)(2,1)} %get-tuple-element.166.refs_2_, ...), custom_call_target="tpu_custom_call" | custom-call | flops 3221225472 | bytes 12582912 | tf_op jit(solution)/shard_map/first_back/pallas_call | solution.py:248
  172.4 1.9 fold_b.1
  174.4 1.3 collective-permute-start.11
  175.7 1.6 fold_a.1
  177.4 4.0 %collective-permute-start.10 = (bf16[4,160,512]{2,1,0:T(8,128)(2,1)}, bf16[4,160,512]{2,1,0:T(8,128)(2,1)S(1)}, u32[]{:S(2)}, u32[]{:S(2)}) collective-permute-start(bf16[4,160,512]{2,1,0:T(8,128)(2,1)} %bitcast.12), channel_id=1, source_target_pairs={{0,2},{1,3},{2,0},{3,1},{4,6},{5,7},{6,4},{7,5},{8,10},{9,11},{10,... | collective-permute-start | bytes 1966088 | tf_op jit(solution)/shard_map/ppermute | solution.py:1173
  181.5 2.4 last.1
  184.3 1.2 collective-permute-start.13
  186.1 16.4 %collective-permute-done.14.refs_7_ = f32[37,512]{1,0:T(8,128)S(1)} collective-permute-done((f32[37,512]{1,0:T(8,128)S(1)}, f32[37,512]{1,0:T(8,128)S(1)}, u32[]{:S(2)}, u32[]{:S(2)}) %collective-permute-start.14) | collective-permute-done | bytes 75808 | tf_op jit(solution)/shard_map/ppermute | solution.py:1173
  202.5 1.6 collective-permute-done.13.refs_6_
  205.1 1.8 collective-permute-start.18
  206.9 1.5 collective-permute-start.15
  208.4 2.3 collective-permute-start.16
  211.8 3.9 %collective-permute-done.19.refs_7_ = f32[37,512]{1,0:T(8,128)S(1)} collective-permute-done((f32[37,512]{1,0:T(8,128)S(1)}, f32[37,512]{1,0:T(8,128)S(1)}, u32[]{:S(2)}, u32[]{:S(2)}) %collective-permute-start.19) | collective-permute-done | bytes 75808 | tf_op jit(solution)/shard_map/ppermute | solution.py:1441
  215.7 2.0 collective-permute-done.15.refs_2_
  217.8 6.0 %collective-permute-done.16.refs_3_ = bf16[1,160,512]{2,1,0:T(8,128)(2,1)S(1)} collective-permute-done((bf16[1,160,512]{2,1,0:T(8,128)(2,1)S(1)}, bf16[1,160,512]{2,1,0:T(8,128)(2,1)S(1)}, u32[]{:S(2)}, u32[]{:S(2)}) %collective-permute-start.16) | collective-permute-done | bytes 163872 | tf_op jit(solution)/shard_map/ppermute | solution.py:1173
  226.6 2.8 %collective-permute-start.20 = (bf16[1,224,256]{2,1,0:T(8,128)(2,1)S(1)}, bf16[1,224,256]{2,1,0:T(8,128)(2,1)S(1)}, u32[]{:S(2)}, u32[]{:S(2)}) collective-permute-start(bf16[1,224,256]{2,1,0:T(8,128)(2,1)S(1)} %bitcast.51), channel_id=1, source_target_pairs={{0,4},{1,5},{2,6},{3,7},{4,0},{5,1},{6,2},{7,3},{8,12},{9,13},{10,... | collective-permute-start | bytes 344072 | tf_op jit(solution)/shard_map/ppermute | solution.py:1173
  229.7 2.1 collective-permute-start.22
  231.8 2.9 %collective-permute-done.20.refs_3_ = bf16[1,224,256]{2,1,0:T(8,128)(2,1)S(1)} collective-permute-done((bf16[1,224,256]{2,1,0:T(8,128)(2,1)S(1)}, bf16[1,224,256]{2,1,0:T(8,128)(2,1)S(1)}, u32[]{:S(2)}, u32[]{:S(2)}) %collective-permute-start.20) | collective-permute-done | bytes 114720 | tf_op jit(solution)/shard_map/ppermute | solution.py:1173
  234.7 4.1 %collective-permute-done.21.refs_4_ = bf16[1,224,256]{2,1,0:T(8,128)(2,1)S(1)} collective-permute-done((bf16[1,224,256]{2,1,0:T(8,128)(2,1)S(1)}, bf16[1,224,256]{2,1,0:T(8,128)(2,1)S(1)}, u32[]{:S(2)}, u32[]{:S(2)}) %collective-permute-start.21) | collective-permute-done | bytes 114720 | tf_op jit(solution)/shard_map/ppermute | solution.py:1173
  240.6 2.1 collective-permute-start.25
  242.7 1.7 collective-permute-start.28
  244.3 1.8 collective-permute-start.27
  247.0 2.2 collective-permute-done.28.refs_3_
  249.2 2.7 %collective-permute-done.27.refs_2_ = f32[37,512]{1,0:T(8,128)S(1)} collective-permute-done((f32[37,512]{1,0:T(8,128)S(1)}, f32[37,512]{1,0:T(8,128)S(1)}, u32[]{:S(2)}, u32[]{:S(2)}) %collective-permute-start.27) | collective-permute-done | bytes 75808 | tf_op jit(solution)/shard_map/ppermute | solution.py:1173
  251.9 1.9 finish.1
  (110 shorter events, 15.8 us)
Async XLA Ops:
  7.2 12.1 %copy-start.26 = (s32[4,17]{1,0:T(4,128)S(1)}, s32[4,17]{1,0:T(4,128)}, u32[]{:S(2)}) copy-start(s32[4,17]{1,0:T(4,128)} %param.18) | copy-start | bytes 820
  7.2 13.1 %copy-start.27 = (s32[2]{0:T(128)S(1)}, s32[2]{0:T(128)}, u32[]{:S(2)}) copy-start(s32[2]{0:T(128)} %param.19) | copy-start | bytes 28
  14.7 9.3 %collective-permute-start.1 = (bf16[2,128,1024]{2,1,0:T(8,128)(2,1)}, bf16[2,128,1024]{2,1,0:T(8,128)(2,1)S(1)}, u32[]{:S(2)}, u32[]{:S(2)}) collective-permute-start(bf16[2,128,1024]{2,1,0:T(8,128)(2,1)} %get-tuple-element.122.refs_5_.refs_4_), channel_id=1, source_target_pairs={{1,0},{2,1},{3,2},{4,3},{5,4},{6,5},{7,6},{8,7},{9,8},{10,9},{11,1... | collective-permute-start | bytes 1572872 | tf_op jit(solution)/shard_map/ppermute | solution.py:1155
  16.0 8.0 %collective-permute-start = (bf16[2,128,1024]{2,1,0:T(8,128)(2,1)}, bf16[2,128,1024]{2,1,0:T(8,128)(2,1)S(1)}, u32[]{:S(2)}, u32[]{:S(2)}) collective-permute-start(bf16[2,128,1024]{2,1,0:T(8,128)(2,1)} %get-tuple-element.123.refs_6_.refs_5_), channel_id=1, source_target_pairs={{0,1},{1,2},{2,3},{3,4},{4,5},{5,6},{6,7},{7,8},{8,9},{9,10},{10,1... | collective-permute-start | bytes 1572872 | tf_op jit(solution)/shard_map/ppermute | solution.py:1155
  42.1 12.1 %collective-permute-start.2 = (bf16[2,16,512]{2,1,0:T(8,128)(2,1)}, bf16[2,16,512]{2,1,0:T(8,128)(2,1)S(1)}, u32[]{:S(2)}, u32[]{:S(2)}) collective-permute-start(bf16[2,16,512]{2,1,0:T(8,128)(2,1)} %get-tuple-element.125), channel_id=1, source_target_pairs={{0,1},{1,2},{2,3},{3,4},{4,5},{5,6},{6,7},{7,8},{8,9},{9,10},{10,1... | collective-permute-start | bytes 98312 | tf_op jit(solution)/shard_map/ppermute | solution.py:1155
  52.5 5.2 %collective-permute-start.3 = (bf16[2,16,512]{2,1,0:T(8,128)(2,1)}, bf16[2,16,512]{2,1,0:T(8,128)(2,1)S(1)}, u32[]{:S(2)}, u32[]{:S(2)}) collective-permute-start(bf16[2,16,512]{2,1,0:T(8,128)(2,1)} %get-tuple-element.126), channel_id=1, source_target_pairs={{1,0},{2,1},{3,2},{4,3},{5,4},{6,5},{7,6},{8,7},{9,8},{10,9},{11,1... | collective-permute-start | bytes 98312 | tf_op jit(solution)/shard_map/ppermute | solution.py:1155
  64.3 14.4 %all-to-all-start = ((f32[32,8,128]{2,1,0:T(8,128)}), f32[32,8,128]{2,1,0:T(8,128)S(1)}, u32[]{:S(2)}, u32[]{:S(2)}) async-start(f32[32,8,128]{2,1,0:T(8,128)} %get-tuple-element.128), calls=%async_computation | async-start | bytes 262144 | tf_op jit(solution)/shard_map/all_to_all | solution.py:1159
  92.1 12.0 %all-to-all-start.1 = ((f32[32,8,128]{2,1,0:T(8,128)}), f32[32,8,128]{2,1,0:T(8,128)S(1)}, u32[]{:S(2)}, u32[]{:S(2)}) async-start(f32[32,8,128]{2,1,0:T(8,128)} %get-tuple-element.132), calls=%async_computation.1 | async-start | bytes 262144 | tf_op jit(solution)/shard_map/all_to_all | solution.py:1159
  94.7 129.8 %reduce-scatter.2.cloned.1.call-start = ((), (), s32[]{:S(2)}) async-start(), calls=%async_computation.3 | async-start | bytes 6684672 | tf_op jit(solution)/shard_map/reduce_scatter | solution.py:1163
  94.8 9.3 %collective-permute-start.4 = (f32[2,8,1024]{2,1,0:T(8,128)}, f32[2,8,1024]{2,1,0:T(8,128)S(1)}, u32[]{:S(2)}, u32[]{:S(2)}) collective-permute-start(f32[2,8,1024]{2,1,0:T(8,128)} %get-tuple-element.138), channel_id=1, source_target_pairs={{0,1},{1,2},{2,3},{3,4},{4,5},{5,6},{6,7},{7,8},{8,9},{9,10},{10,1... | collective-permute-start | bytes 196616 | tf_op jit(solution)/shard_map/ppermute | solution.py:1155
  96.8 7.3 %collective-permute-start.5 = (f32[2,8,1024]{2,1,0:T(8,128)}, f32[2,8,1024]{2,1,0:T(8,128)S(1)}, u32[]{:S(2)}, u32[]{:S(2)}) collective-permute-start(f32[2,8,1024]{2,1,0:T(8,128)} %get-tuple-element.139), channel_id=1, source_target_pairs={{1,0},{2,1},{3,2},{4,3},{5,4},{6,5},{7,6},{8,7},{9,8},{10,9},{11,1... | collective-permute-start | bytes 196616 | tf_op jit(solution)/shard_map/ppermute | solution.py:1155
  134.3 5.9 %collective-permute-start.6 = (bf16[2,128,1024]{2,1,0:T(8,128)(2,1)}, bf16[2,128,1024]{2,1,0:T(8,128)(2,1)S(1)}, u32[]{:S(2)}, u32[]{:S(2)}) collective-permute-start(bf16[2,128,1024]{2,1,0:T(8,128)(2,1)} %get-tuple-element.155), channel_id=1, source_target_pairs={{0,1},{1,2},{2,3},{3,4},{4,5},{5,6},{6,7},{7,8},{8,9},{9,10},{10,1... | collective-permute-start | bytes 1572872 | tf_op jit(solution)/shard_map/ppermute | solution.py:1155
  138.5 5.2 %collective-permute-start.7 = (bf16[2,128,1024]{2,1,0:T(8,128)(2,1)}, bf16[2,128,1024]{2,1,0:T(8,128)(2,1)S(1)}, u32[]{:S(2)}, u32[]{:S(2)}) collective-permute-start(bf16[2,128,1024]{2,1,0:T(8,128)(2,1)} %get-tuple-element.156), channel_id=1, source_target_pairs={{1,0},{2,1},{3,2},{4,3},{5,4},{6,5},{7,6},{8,7},{9,8},{10,9},{11,1... | collective-permute-start | bytes 1572872 | tf_op jit(solution)/shard_map/ppermute | solution.py:1155
  155.0 17.4 %collective-permute-start.9 = (bf16[8,224,512]{2,1,0:T(8,128)(2,1)}, bf16[8,224,512]{2,1,0:T(8,128)(2,1)S(1)}, u32[]{:S(2)}, u32[]{:S(2)}) collective-permute-start(bf16[8,224,512]{2,1,0:T(8,128)(2,1)} %get-tuple-element.180), channel_id=1, source_target_pairs={{0,1},{1,0},{2,3},{3,2},{4,5},{5,4},{6,7},{7,6},{8,9},{9,8},{10,11... | collective-permute-start | bytes 5505032 | tf_op jit(solution)/shard_map/ppermute | solution.py:1173
  162.9 8.7 %copy-start.22 = (f32[8,512]{1,0:T(8,128)S(1)}, f32[8,512]{1,0:T(8,128)}, u32[]{:S(2)}) copy-start(f32[8,512]{1,0:T(8,128)} %get-tuple-element.187) | copy-start | bytes 49156
  162.9 9.5 %copy-start.1 = (bf16[8,224,512]{2,1,0:T(8,128)(2,1)S(1)}, bf16[8,224,512]{2,1,0:T(8,128)(2,1)}, u32[]{:S(2)}) copy-start(bf16[8,224,512]{2,1,0:T(8,128)(2,1)} %get-tuple-element.179.refs_0_) | copy-start | bytes 5505028
  162.9 9.5 %copy-start.10 = (s32[9]{0:T(128)S(1)}, s32[9]{0:T(128)}, u32[]{:S(2)}) copy-start(s32[9]{0:T(128)} %concatenate.6.refs_0_.info) | copy-start | bytes 112
  171.4 4.3 %copy-start.19 = (f32[16,512]{1,0:T(8,128)S(1)}, f32[16,512]{1,0:T(8,128)}, u32[]{:S(2)}) copy-start(f32[16,512]{1,0:T(8,128)} %get-tuple-element.184) | copy-start | bytes 98308
  171.4 4.3 %copy-start.2 = (bf16[8,160,512]{2,1,0:T(8,128)(2,1)S(1)}, bf16[8,160,512]{2,1,0:T(8,128)(2,1)}, u32[]{:S(2)}) copy-start(bf16[8,160,512]{2,1,0:T(8,128)(2,1)} %get-tuple-element.171) | copy-start | bytes 3932164
  171.5 4.3 %collective-permute-start.8 = (bf16[8,160,512]{2,1,0:T(8,128)(2,1)}, bf16[8,160,512]{2,1,0:T(8,128)(2,1)S(1)}, u32[]{:S(2)}, u32[]{:S(2)}) collective-permute-start(bf16[8,160,512]{2,1,0:T(8,128)(2,1)} %get-tuple-element.172), channel_id=1, source_target_pairs={{0,1},{1,0},{2,3},{3,2},{4,5},{5,4},{6,7},{7,6},{8,9},{9,8},{10,11... | collective-permute-start | bytes 3932168 | tf_op jit(solution)/shard_map/ppermute | solution.py:1173
  174.3 7.1 %copy-start.25 = (f32[8,512]{1,0:T(8,128)S(1)}, f32[8,512]{1,0:T(8,128)}, u32[]{:S(2)}) copy-start(f32[8,512]{1,0:T(8,128)} %get-tuple-element.186) | copy-start | bytes 49156
  174.3 7.1 %copy-start = (bf16[2,256,512]{2,1,0:T(8,128)(2,1)S(1)}, bf16[2,256,512]{2,1,0:T(8,128)(2,1)}, u32[]{:S(2)}) copy-start(bf16[2,256,512]{2,1,0:T(8,128)(2,1)} %refs_1_.5) | copy-start | bytes 1572868
  174.3 7.1 %copy-start.3 = (f32[512,512]{1,0:T(8,128)S(1)}, f32[512,512]{1,0:T(8,128)}, u32[]{:S(2)}) copy-start(f32[512,512]{1,0:T(8,128)} %get-tuple-element.174.refs_2_) | copy-start | bytes 3145732
  174.3 7.1 %copy-start.6 = (f32[256,512]{1,0:T(8,128)S(1)}, f32[256,512]{1,0:T(8,128)}, u32[]{:S(2)}) copy-start(f32[256,512]{1,0:T(8,128)} %get-tuple-element.175.refs_3_) | copy-start | bytes 1572868
  174.3 7.1 %copy-start.7 = (f32[256,512]{1,0:T(8,128)S(1)}, f32[256,512]{1,0:T(8,128)}, u32[]{:S(2)}) copy-start(f32[256,512]{1,0:T(8,128)} %get-tuple-element.176.refs_4_) | copy-start | bytes 1572868
  174.3 7.1 %copy-start.8 = (f32[6,512]{1,0:T(8,128)S(1)}, f32[6,512]{1,0:T(8,128)}, u32[]{:S(2)}) copy-start(f32[6,512]{1,0:T(8,128)} %refs_0_.3) | copy-start | bytes 36868
  174.4 29.8 %collective-permute-start.11 = (bf16[8,224,256]{2,1,0:T(8,128)(2,1)}, bf16[8,224,256]{2,1,0:T(8,128)(2,1)S(1)}, u32[]{:S(2)}, u32[]{:S(2)}) collective-permute-start(bf16[8,224,256]{2,1,0:T(8,128)(2,1)} %get-tuple-element.183), channel_id=1, source_target_pairs={{0,16},{16,0},{1,17},{17,1},{2,18},{18,2},{3,19},{19,3},{4,20},{20... | collective-permute-start | bytes 2752520 | tf_op jit(solution)/shard_map/ppermute | solution.py:1408
  175.7 8.2 %copy-start.23 = (f32[4,512]{1,0:T(4,128)S(1)}, f32[4,512]{1,0:T(4,128)}, u32[]{:S(2)}) copy-start(f32[4,512]{1,0:T(4,128)} %get-tuple-element.190) | copy-start | bytes 24580
  175.7 8.2 %copy-start.24 = (f32[4,512]{1,0:T(4,128)S(1)}, f32[4,512]{1,0:T(4,128)}, u32[]{:S(2)}) copy-start(f32[4,512]{1,0:T(4,128)} %get-tuple-element.189) | copy-start | bytes 24580
  177.4 26.8 %copy-start.5 = (bf16[8,224,256]{2,1,0:T(8,128)(2,1)S(1)}, bf16[8,224,256]{2,1,0:T(8,128)(2,1)}, u32[]{:S(2)}) copy-start(bf16[8,224,256]{2,1,0:T(8,128)(2,1)} %copy-done.4) | copy-start | bytes 2752516
  177.4 26.8 %collective-permute-start.10 = (bf16[4,160,512]{2,1,0:T(8,128)(2,1)}, bf16[4,160,512]{2,1,0:T(8,128)(2,1)S(1)}, u32[]{:S(2)}, u32[]{:S(2)}) collective-permute-start(bf16[4,160,512]{2,1,0:T(8,128)(2,1)} %bitcast.12), channel_id=1, source_target_pairs={{0,2},{1,3},{2,0},{3,1},{4,6},{5,7},{6,4},{7,5},{8,10},{9,11},{10,... | collective-permute-start | bytes 1966088 | tf_op jit(solution)/shard_map/ppermute | solution.py:1173
  184.2 18.3 %collective-permute-start.14 = (f32[37,512]{1,0:T(8,128)S(1)}, f32[37,512]{1,0:T(8,128)S(1)}, u32[]{:S(2)}, u32[]{:S(2)}) collective-permute-start(f32[37,512]{1,0:T(8,128)S(1)} %concatenate.7.refs_4_), channel_id=1, source_target_pairs={{0,3},{1,2},{2,1},{3,0},{4,7},{5,6},{6,5},{7,4},{8,11},{9,10},{10,... | collective-permute-start | bytes 227336 | tf_op jit(solution)/shard_map/ppermute | solution.py:1173
  184.3 19.9 %collective-permute-start.13 = (f32[37,512]{1,0:T(8,128)S(1)}, f32[37,512]{1,0:T(8,128)S(1)}, u32[]{:S(2)}, u32[]{:S(2)}) collective-permute-start(f32[37,512]{1,0:T(8,128)S(1)} %concatenate.7.refs_4_), channel_id=1, source_target_pairs={{0,2},{1,3},{2,0},{3,1},{4,6},{5,7},{6,4},{7,5},{8,10},{9,11},{10,... | collective-permute-start | bytes 227336 | tf_op jit(solution)/shard_map/ppermute | solution.py:1173
  185.5 18.6 %collective-permute-start.12 = (f32[37,512]{1,0:T(8,128)S(1)}, f32[37,512]{1,0:T(8,128)S(1)}, u32[]{:S(2)}, u32[]{:S(2)}) collective-permute-start(f32[37,512]{1,0:T(8,128)S(1)} %concatenate.7.refs_4_), channel_id=1, source_target_pairs={{0,1},{1,0},{2,3},{3,2},{4,5},{5,4},{6,7},{7,6},{8,9},{9,8},{10,11... | collective-permute-start | bytes 227336 | tf_op jit(solution)/shard_map/ppermute | solution.py:1173
  205.1 18.7 %collective-permute-start.18 = (bf16[4,224,256]{2,1,0:T(8,128)(2,1)S(1)}, bf16[4,224,256]{2,1,0:T(8,128)(2,1)S(1)}, u32[]{:S(2)}, u32[]{:S(2)}) collective-permute-start(bf16[4,224,256]{2,1,0:T(8,128)(2,1)S(1)} %bitcast.45), channel_id=1, source_target_pairs={{0,2},{1,3},{2,0},{3,1},{4,6},{5,7},{6,4},{7,5},{8,10},{9,11},{10,... | collective-permute-start | bytes 1376264 | tf_op jit(solution)/shard_map/ppermute | solution.py:1173
  206.9 10.9 %collective-permute-start.15 = (bf16[1,160,512]{2,1,0:T(8,128)(2,1)S(1)}, bf16[1,160,512]{2,1,0:T(8,128)(2,1)S(1)}, u32[]{:S(2)}, u32[]{:S(2)}) collective-permute-start(bf16[1,160,512]{2,1,0:T(8,128)(2,1)S(1)} %bitcast.48), channel_id=1, source_target_pairs={{0,4},{1,5},{2,6},{3,7},{4,0},{5,1},{6,2},{7,3},{8,12},{9,13},{10,... | collective-permute-start | bytes 491528 | tf_op jit(solution)/shard_map/ppermute | solution.py:1173
  208.4 15.3 %collective-permute-start.16 = (bf16[1,160,512]{2,1,0:T(8,128)(2,1)S(1)}, bf16[1,160,512]{2,1,0:T(8,128)(2,1)S(1)}, u32[]{:S(2)}, u32[]{:S(2)}) collective-permute-start(bf16[1,160,512]{2,1,0:T(8,128)(2,1)S(1)} %bitcast.47), channel_id=1, source_target_pairs={{0,8},{1,9},{2,10},{3,11},{4,12},{5,13},{6,14},{7,15},{8,0},{9,1},... | collective-permute-start | bytes 491528 | tf_op jit(solution)/shard_map/ppermute | solution.py:1173
  210.7 13.1 %collective-permute-start.17 = (bf16[1,160,512]{2,1,0:T(8,128)(2,1)S(1)}, bf16[1,160,512]{2,1,0:T(8,128)(2,1)S(1)}, u32[]{:S(2)}, u32[]{:S(2)}) collective-permute-start(bf16[1,160,512]{2,1,0:T(8,128)(2,1)S(1)} %bitcast.46), channel_id=1, source_target_pairs={{0,12},{1,13},{2,14},{3,15},{4,8},{5,9},{6,10},{7,11},{8,4},{9,5},... | collective-permute-start | bytes 491528 | tf_op jit(solution)/shard_map/ppermute | solution.py:1173
  211.3 4.4 %collective-permute-start.19 = (f32[37,512]{1,0:T(8,128)S(1)}, f32[37,512]{1,0:T(8,128)S(1)}, u32[]{:S(2)}, u32[]{:S(2)}) collective-permute-start(f32[37,512]{1,0:T(8,128)S(1)} %get-tuple-element.197.refs_6_), channel_id=1, source_target_pairs={{0,16},{16,0},{1,17},{17,1},{2,18},{18,2},{3,19},{19,3},{4,20},{20... | collective-permute-start | bytes 227336 | tf_op jit(solution)/shard_map/ppermute | solution.py:1441
  224.5 14.3 %collective-permute-start.24 = (bf16[1,192,1024]{2,1,0:T(8,128)(2,1)}, bf16[1,192,1024]{2,1,0:T(8,128)(2,1)S(1)}, u32[]{:S(2)}, u32[]{:S(2)}) collective-permute-start(bf16[1,192,1024]{2,1,0:T(8,128)(2,1)} %reduce-scatter.2.cloned.1.call-done.refs_2_), channel_id=1, source_target_pairs={{0,16},{16,0},{1,17},{17,1},{2,18},{18,2},{3,19},{19,3},{4,20},{20... | collective-permute-start | bytes 1179656 | tf_op jit(solution)/shard_map/ppermute | solution.py:1438
  225.6 13.2 %collective-permute-start.23 = (bf16[1,160,512]{2,1,0:T(8,128)(2,1)S(1)}, bf16[1,160,512]{2,1,0:T(8,128)(2,1)S(1)}, u32[]{:S(2)}, u32[]{:S(2)}) collective-permute-start(bf16[1,160,512]{2,1,0:T(8,128)(2,1)S(1)} %get-tuple-element.201.refs_1_), channel_id=1, source_target_pairs={{0,16},{16,0},{1,17},{17,1},{2,18},{18,2},{3,19},{19,3},{4,20},{20... | collective-permute-start | bytes 491528 | tf_op jit(solution)/shard_map/ppermute | solution.py:1437
  226.6 8.1 %collective-permute-start.20 = (bf16[1,224,256]{2,1,0:T(8,128)(2,1)S(1)}, bf16[1,224,256]{2,1,0:T(8,128)(2,1)S(1)}, u32[]{:S(2)}, u32[]{:S(2)}) collective-permute-start(bf16[1,224,256]{2,1,0:T(8,128)(2,1)S(1)} %bitcast.51), channel_id=1, source_target_pairs={{0,4},{1,5},{2,6},{3,7},{4,0},{5,1},{6,2},{7,3},{8,12},{9,13},{10,... | collective-permute-start | bytes 344072 | tf_op jit(solution)/shard_map/ppermute | solution.py:1173
  229.4 9.4 %collective-permute-start.21 = (bf16[1,224,256]{2,1,0:T(8,128)(2,1)S(1)}, bf16[1,224,256]{2,1,0:T(8,128)(2,1)S(1)}, u32[]{:S(2)}, u32[]{:S(2)}) collective-permute-start(bf16[1,224,256]{2,1,0:T(8,128)(2,1)S(1)} %bitcast.50), channel_id=1, source_target_pairs={{0,8},{1,9},{2,10},{3,11},{4,12},{5,13},{6,14},{7,15},{8,0},{9,1},... | collective-permute-start | bytes 344072 | tf_op jit(solution)/shard_map/ppermute | solution.py:1173
  229.7 9.2 %collective-permute-start.22 = (bf16[1,224,256]{2,1,0:T(8,128)(2,1)S(1)}, bf16[1,224,256]{2,1,0:T(8,128)(2,1)S(1)}, u32[]{:S(2)}, u32[]{:S(2)}) collective-permute-start(bf16[1,224,256]{2,1,0:T(8,128)(2,1)S(1)} %bitcast.49), channel_id=1, source_target_pairs={{0,12},{1,13},{2,14},{3,15},{4,8},{5,9},{6,10},{7,11},{8,4},{9,5},... | collective-permute-start | bytes 344072 | tf_op jit(solution)/shard_map/ppermute | solution.py:1173
  240.6 11.3 %collective-permute-start.25 = (bf16[1,224,256]{2,1,0:T(8,128)(2,1)S(1)}, bf16[1,224,256]{2,1,0:T(8,128)(2,1)S(1)}, u32[]{:S(2)}, u32[]{:S(2)}) collective-permute-start(bf16[1,224,256]{2,1,0:T(8,128)(2,1)S(1)} %get-tuple-element.207), channel_id=1, source_target_pairs={{0,16},{16,0},{1,17},{17,1},{2,18},{18,2},{3,19},{19,3},{4,20},{20... | collective-permute-start | bytes 344072 | tf_op jit(solution)/shard_map/ppermute | solution.py:1446
  242.7 6.6 %collective-permute-start.28 = (f32[37,512]{1,0:T(8,128)S(1)}, f32[37,512]{1,0:T(8,128)S(1)}, u32[]{:S(2)}, u32[]{:S(2)}) collective-permute-start(f32[37,512]{1,0:T(8,128)S(1)} %get-tuple-element.209.refs_0_), channel_id=1, source_target_pairs={{0,12},{1,13},{2,14},{3,15},{4,8},{5,9},{6,10},{7,11},{8,4},{9,5},... | collective-permute-start | bytes 227336 | tf_op jit(solution)/shard_map/ppermute | solution.py:1173
  244.3 7.6 %collective-permute-start.27 = (f32[37,512]{1,0:T(8,128)S(1)}, f32[37,512]{1,0:T(8,128)S(1)}, u32[]{:S(2)}, u32[]{:S(2)}) collective-permute-start(f32[37,512]{1,0:T(8,128)S(1)} %get-tuple-element.209.refs_0_), channel_id=1, source_target_pairs={{0,8},{1,9},{2,10},{3,11},{4,12},{5,13},{6,14},{7,15},{8,0},{9,1},... | collective-permute-start | bytes 227336 | tf_op jit(solution)/shard_map/ppermute | solution.py:1173
  246.1 5.8 %collective-permute-start.26 = (f32[37,512]{1,0:T(8,128)S(1)}, f32[37,512]{1,0:T(8,128)S(1)}, u32[]{:S(2)}, u32[]{:S(2)}) collective-permute-start(f32[37,512]{1,0:T(8,128)S(1)} %get-tuple-element.209.refs_0_), channel_id=1, source_target_pairs={{0,4},{1,5},{2,6},{3,7},{4,0},{5,1},{6,2},{7,3},{8,12},{9,13},{10,... | collective-permute-start | bytes 227336 | tf_op jit(solution)/shard_map/ppermute | solution.py:1173
  (12 other events, 16.8 us)
Sparse Core Ops, SparseCore 0:
  119.7 95.1 reduce-scatter.1

commit v5 on v4

--- a/solution.py
+++ b/solution.py
@@ -114,6 +114,10 @@
 def below(joined):
     width = joined.shape[1] // MANY
     return jnp.concatenate([joined[:, k * width : (k + 1) * width] for k in range(MANY)], axis=0)
+
+
+def windows(width):
+    return [slice(at, at + WIN) for at in range(0, width, WIN)]
 
 
 def flip(rows):
@@ -405,6 +409,7 @@
         turn = flip(WIN)
         key_at = lax.broadcasted_iota(jnp.int32, (WIN, SPAN), 1).astype(f32)
         table = k.table
+        ones = jnp.ones((SPAN, WIN), bf16)
         for row in range(rows):
             reach = info[1 + row].astype(f32)
             row_ends = k.ends[row : row + 1, :]
@@ -431,8 +436,11 @@
                     scores = content.reshape(MANY, WIN, SPAN) + spread
                     scores = jnp.where(allowed, scores, negative)
                     powers = jnp.exp(scores - jnp.max(scores, axis=2, keepdims=True))
-                    weights = powers * (1.0 / jnp.sum(powers, axis=2, keepdims=True))
-                    weights = weights.astype(bf16).reshape(MANY * WIN, SPAN)
+                    powers = powers.reshape(MANY * WIN, SPAN)
+                    inverse = 1.0 / dot(powers.astype(bf16), ones)
+                    weights = jnp.concatenate(
+                        [powers[:, cut] * inverse for cut in windows(SPAN)], axis=1
+                    ).astype(bf16)
                     k.mixed[here, cut] = heads_joined(dot(weights, values)).astype(bf16)
                     k.prob[row][block, group] = dot(turn, beside(weights)).astype(bf16)
             k.send(k.prob[row])
@@ -447,10 +455,12 @@
         paired = dot(normed, k.convolve_in[...])
         value = paired[:, :model] + k.bias[3:4]
         gate = paired[:, model:] + k.bias[4:5]
-        k.paired[:, :model] = value
-        k.paired[:, model:] = gate
-        k.send(k.paired)
-        gated = (value * sigmoid(gate)).astype(bf16)
+        sigma = sigmoid(gate)
+        gated = value * sigma
+        k.factors[:, :model] = sigma.astype(bf16)
+        k.factors[:, model:] = (gated * (1.0 - sigma)).astype(bf16)
+        k.send(k.factors)
+        gated = gated.astype(bf16)
         k.gated[...] = gated
         for row in range(rows):
             k.first[row] = gated[row * frames : row * frames + RIM]
@@ -467,7 +477,7 @@
         ),
         dict(
             prob=[sds((2, GROUPS, WIN, MANY * SPAN), bf16)] * rows, mixed=low,
-            out=sds((tokens, model), f32), nc=low, paired=sds((tokens, 2 * model), f32),
+            out=sds((tokens, model), f32), nc=low, factors=sds((tokens, 2 * model), bf16),
             gated=low, first=rim, last=rim,
         ),
         smem=[info],
@@ -595,7 +605,7 @@
     hidden = feed_in.shape[2]
     parts = hidden // PART
 
-    def body(k, info, conv_s, slope_s, tile):
+    def body(k, info, conv_s, bn_s, slope_s, tile):
         stats, each = k.stats, k.counts[:, 0:1]
         gain, shift, bias = k.gain, k.shift, k.bias
         count = total(each)
@@ -612,7 +622,8 @@
         k.inv[0:1] = inverse
         k.inv[1:2] = jnp.broadcast_to(1.0 / count, (1, model))
         normal = (k.depth[...] - mean) * inverse
-        k.bn[...] = normal
+        bn_s[...] = normal
+        k.bn[...] = normal.astype(bf16)
         k.send(k.bn)
         batch = normal * gain[5:6] + shift[5:6]
         swished = (batch * sigmoid(batch)).astype(bf16)
@@ -669,21 +680,21 @@
         k.gcl[...] = low
         k.send(k.gcl)
         vec[4:5] = total(low.astype(f32))
-        bn = k.bn[...]
+        bn = bn_s[...]
         batch = bn * gain[5:6] + shift[5:6]
         _, slope = activate(batch)
         grad = dot_last(low, k.convolve_out[...]) * slope
-        k.gb[...] = grad
+        k.gb[...] = grad.astype(bf16)
         k.send(k.gb)
         pack(tile, [total(grad), total(grad * bn)])
         k.totals[...] = jnp.broadcast_to(tile[...][None], k.totals.shape)
         k.send(k.totals)
         for row in range(rows):
             at, end = row * frames, (row + 1) * frames
-            k.first[row, :, :model] = k.gb[at : at + RIM_GRAD]
-            k.first[row, :, model:] = k.bn[at : at + RIM_GRAD]
-            k.last[row, :, :model] = k.gb[end - RIM_GRAD : end]
-            k.last[row, :, model:] = k.bn[end - RIM_GRAD : end]
+            k.first[row, :, :model] = grad[at : at + RIM_GRAD]
+            k.first[row, :, model:] = bn[at : at + RIM_GRAD]
+            k.last[row, :, :model] = grad[end - RIM_GRAD : end]
+            k.last[row, :, model:] = bn[end - RIM_GRAD : end]
 
     w_in, w_out = feed_slabs(feed_in, feed_out, 1)
     ins = dict(
@@ -700,12 +711,13 @@
         ins,
         dict(
             out=low, act=sds((tokens, hidden), bf16), gi=sds((tokens, hidden), bf16), nf=low,
-            gl=low, sw=low, gcl=low, gcs=wide, gb=wide, bn=wide, inv=sds((8, model), f32),
+            gl=low, sw=low, gcl=low, gcs=wide, gb=low, bn=low, inv=sds((8, model), f32),
             totals=sds((devices, 8, 128), f32), first=rim, last=rim, vec=sds((8, model), f32),
             fb=sds((hidden // model, model), f32),
         ),
         smem=[info],
         scratch=[
+            pltpu.VMEM((tokens, model), f32),
             pltpu.VMEM((tokens, model), f32),
             pltpu.VMEM((tokens, hidden), f32),
             pltpu.VMEM((8, 128), f32),
@@ -761,7 +773,9 @@
                 here = slice(step, step + 32)
                 at = column(32, start + step)
                 grads[RIM_GRAD + step : RIM_GRAD + step + 32] = grad_of(
-                    k.gb[row][here], k.bn[row][here], (at < last).astype(f32)
+                    k.gb[row][here].astype(f32),
+                    k.bn[row][here].astype(f32),
+                    (at < last).astype(f32),
                 )
             edge_at = column(RIM_GRAD, start + frames)
             grads[RIM_GRAD + frames :] = grad_of(
@@ -770,7 +784,7 @@
             rim[0:RIM] = k.rim_before[row].astype(f32)
             rim[RIM : RIM + frames] = k.gated[row][...].astype(f32)
             rim[RIM + frames :] = k.rim_after[row].astype(f32)
-            paired = k.paired[row]
+            factors = k.factors[row]
             half = frames // 2
 
             def one(i, carry):
@@ -787,10 +801,8 @@
                         mirror = KERNEL - 1 - tap
                         part = grads[RIM_GRAD + off : RIM_GRAD + off + half, lanes] * keep
                         grad += taps[mirror : mirror + 1, lanes] * part
-                    sigma = sigmoid(paired[base : base + half, gates])
-                    one = (grad * sigma).astype(bf16)
-                    value = paired[base : base + half, lanes]
-                    two = (grad * sigma * value * (1.0 - sigma)).astype(bf16)
+                    one = (grad * factors[base : base + half, lanes].astype(f32)).astype(bf16)
+                    two = (grad * factors[base : base + half, gates].astype(f32)).astype(bf16)
                     here = slice(first + base, first + base + half)
                     gp[here, lanes] = one
                     gp[here, gates] = two
@@ -831,7 +843,7 @@
         dict(
             inv=mid.inv, gain=gain, ends=ends, taps=taps, rim_before=rim_before,
             rim_after=rim_after, gb=by_row(mid.gb, rows), bn=by_row(mid.bn, rows), gated=by_row(mix.gated, rows),
-            paired=by_row(mix.paired, rows), convolve_in=convolve_in, after=mix.out, gcs=mid.gcs,
+            factors=by_row(mix.factors, rows), convolve_in=convolve_in, after=mix.out, gcs=mid.gcs,
             attend_out=attend_out, nc=mix.nc, sw=mid.sw, gcl=mid.gcl, mixed=mix.mixed,
         ),
         dict(
@@ -948,7 +960,34 @@
     )
 
 
-def back(info, core_at, n, grads, halo, attend_in, start, gas, gain, sinusoid):
+def place_weights(info, core_at, n, grads, start, sinusoid):
+    tokens, model = start.na.shape
+    slim = model // n
+
+    def body(k, info):
+        core = info[core_at]
+        pairs = (0, n // 2)
+        rows = [ref[...] for ref in (k.gq[at] for at in range(len(grads.gq)))]
+        block = dot_first(k.na[...], jnp.concatenate(rows, axis=0))
+        keep_half(block, core, k.mine, k.other, pairs)
+        high = k.g_table[...].astype(bf16)
+        low = (k.g_table[...] - high.astype(f32)).astype(bf16)
+        place = dot_first(k.sinusoid[...], high) + dot_first(k.sinusoid[...], low)
+        keep_half(place, core, k.mine, k.other, pairs, slim)
+
+    half = sds((n // 2, 2 * slim, model), bf16)
+    return staged(
+        "place_weights",
+        body,
+        dict(na=start.na, gq=list(grads.gq), g_table=grads.g_table, sinusoid=sinusoid),
+        dict(mine=half, other=half),
+        smem=[info],
+        flops=2 * tokens * model * 2 * model,
+        moved=4 << 20,
+    )
+
+
+def back(info, core_at, n, grads, halo, attend_in, start, gas, gain, placed):
     rows = len(grads.gq)
     tokens, model = start.after.shape
     frames = tokens // rows
@@ -989,14 +1028,11 @@
         for at in range(5):
             vec[at : at + 1] = sums[at]
         pairs = (0, n // 2)
-        block = dot_first(k.na[...], joined[:, : 2 * model])
-        for part in range(2):
-            cut = slice(part * model, (part + 1) * model)
-            keep_half(block[:, cut], core, k.mine, k.other, pairs, width + part * slim)
-        high = k.g_table[...].astype(bf16)
-        low = (k.g_table[...] - high.astype(f32)).astype(bf16)
-        place = dot_first(k.sinusoid[...], high) + dot_first(k.sinusoid[...], low)
-        keep_half(place, core, k.mine, k.other, pairs, width + 2 * slim)
+        block = dot_first(k.na[...], joined[:, model : 2 * model])
+        keep_half(block, core, k.mine, k.other, pairs, width + slim)
+        for mine, placed in ((k.mine, k.mine_placed), (k.other, k.other_placed)):
+            mine[:, width : width + slim] = placed[:, :slim]
+            mine[:, width + 2 * slim :] = placed[:, slim:]
         step = n // 2 // parts
         for part in range(parts):
             block = dot_first(k.act[part][...], k.gl[...])
@@ -1012,7 +1048,7 @@
         body,
         dict(
             gain=gain, gq=grads.gq, g_lo=grads.g_lo, g_hi=grads.g_hi, attend_in=attend_in, after=by_row(start.after, rows),
-            gas=by_row(gas, rows), na=start.na, g_table=grads.g_table, sinusoid=sinusoid,
+            gas=by_row(gas, rows), na=start.na, mine_placed=placed.mine, other_placed=placed.other,
             act=[slab(start.act, (0, tokens), (at, PART)) for at in range(0, hidden, PART)],
         ),
         dict(
@@ -1398,9 +1434,8 @@
     early = scatter_sum(early)
     grads = attend_back(start, query, before, after, mix.prob, gm)
     halo = neighbours(grads.g_after, grads.g_before)
-    end = back(
-        info, core_at, n, grads, halo, attend_in, start, conv.gas, norm_gain, sinusoid
-    )
+    placed = place_weights(info, core_at, n, grads, start, sinusoid)
+    end = back(info, core_at, n, grads, halo, attend_in, start, conv.gas, norm_gain, placed)
     b, b_got = end.mine, [swap(end.other, 1)]
     got = first_back(info, core_at, n, end.gl, feed_in, feed_out, start, end.gv)
     a, a_got = got.mine, [swap(got.other, 1)]

time: 266 us -> 262 us (0.985)
  waiting for transfers between devices: 56.9 us -> 54.2 us
    ppermute x4, waiting for transfers between devices: 6.98 us -> 3.48 us  [neighbours(): lax.ppermute(first_block, 'frames', down)]
    pallas_call x11 -> x12, Pallas kernels: 103 us -> 103 us  [staged(): pl.pallas_call(run, in_specs=[pl.BlockSpec(memory_space=pltpu.SMEM)] * n_...]
  transfers between devices with their start and end apart: 32 -> 32, of which waited for: 13 -> 11; matrix products, arithmetic and copies ran while one was open for 1% -> 1% of each run, Pallas kernels for 19% -> 21%
where the time goes in v5:
time: 262 us; the launch traced here: 258 us
  Pallas kernels  111 us (42%)
  starting transfers between devices  69.6 us (27%)
  waiting for transfers between devices  54.2 us (21%)
  between operations  14.9 us (6%)
  local copies, waits for them, and re-layouts  7.66 us (3%)
    pallas_call x12, Pallas kernels, staged(): pl.pallas_call(run, in_specs=[pl.BlockSpec(memory_space=pltpu.SMEM)] * n_...  103 us
    ppermute x16, waiting for transfers between devices, swap(): return lax.ppermute(x, 'frames', [(i, i ^ k) for i in range(n)])  39 us
    ppermute x16, starting transfers between devices, swap(): return lax.ppermute(x, 'frames', [(i, i ^ k) for i in range(n)])  29.6 us
    ppermute x4, starting transfers between devices, neighbours(): lax.ppermute(last_block, 'frames', up)  19.9 us
    all_to_all x2, starting transfers between devices, gather(): return lax.all_to_all(copies, DEVICES, 0, 0, tiled=True)  8.72 us
    all_to_all x2, waiting for transfers between devices, gather(): return lax.all_to_all(copies, DEVICES, 0, 0, tiled=True)  7.78 us
    pallas_call x5, Pallas kernels, fold(): pl.pallas_call(body, in_specs=[pl.BlockSpec(memory_space=pltpu.SMEM)] + [...  5.99 us
    ppermute x4, starting transfers between devices, neighbours(): lax.ppermute(first_block, 'frames', down)  5.79 us
  transfers between devices with their start and end apart: 32, of which 11 were waited for; matrix products, arithmetic and copies ran while one was open for 1% of the time, Pallas kernels for 21%

profile of v5, /device:TPU:0, one launch (start us, length us, event | category | flops | bytes accessed | tf_op | source)
XLA Modules:
  0.0 257.8 jit_solution(8618827277138733069)
XLA Ops:
  7.2 7.5 %front.1 = (f32[512,512]{1,0:T(8,128)}, bf16[512,512]{1,0:T(8,128)(2,1)}, bf16[512,512]{1,0:T(8,128)(2,1)}, bf16[2,128,1024]{2,1,0:T(8,128)(2,1)}, bf16[2,128,10...) custom-call(bf16[2,256,512]{2,1,0:T(8,128)(2,1)} %refs_1_.5, f32[6,512]{1,0:T(8,128)} %refs_0_.3, ...), custom_call_target="tpu_custom_call" | custom-call | flops 2684354560 | bytes 16777216 | tf_op jit(solution)/shard_map/front/pallas_call | solution.py:252
  14.7 1.3 collective-permute-start.1
  16.0 3.2 %collective-permute-start = (bf16[2,128,1024]{2,1,0:T(8,128)(2,1)}, bf16[2,128,1024]{2,1,0:T(8,128)(2,1)S(1)}, u32[]{:S(2)}, u32[]{:S(2)}) collective-permute-start(bf16[2,128,1024]{2,1,0:T(8,128)(2,1)} %get-tuple-element.125.refs_6_.refs_5_), channel_id=1, source_target_pairs={{0,1},{1,2},{2,3},{3,4},{4,5},{5,6},{6,7},{7,8},{8,9},{9,10},{10,1... | collective-permute-start | bytes 1572872 | tf_op jit(solution)/shard_map/ppermute | solution.py:1191
  20.9 3.0 %queries.1 = (bf16[512,512]{1,0:T(8,128)(2,1)}, bf16[512,512]{1,0:T(8,128)(2,1)}, bf16[384,512]{1,0:T(8,128)(2,1)}) custom-call(bf16[512,512]{1,0:T(8,128)(2,1)} %get-tuple-element.120.refs_0_.refs_1_.refs_13_, bf16[512,1536]{1,0:T(8,128)(2,1)} %refs_10_.5, f32[10,512]{1,0:T(8,128)} %refs_6_.3, bf16[384,512]{1,0:T(8,128)(2,1)} %constant.66.clone.refs_3_.refs_5_, ...), custom_call_target="tpu_custom_call" | custom-call | flops 536870912 | bytes 4194304 | tf_op jit(solution)/shard_map/queries/pallas_call | solution.py:252
  24.9 14.8 %attend.1 = (bf16[2,2,128,1536]{3,2,1,0:T(8,128)(2,1)}, bf16[2,2,128,1536]{3,2,1,0:T(8,128)(2,1)}, bf16[512,512]{1,0:T(8,128)(2,1)}, f32[512,512]{1,0:T(8,128)},...) custom-call(s32[9]{0:T(128)} %concatenate.6.refs_0_.info, ...), custom_call_target="tpu_custom_call" | custom-call | flops 1610612736 | bytes 16777216 | tf_op jit(solution)/shard_map/attend/pallas_call | solution.py:252
  39.7 10.4 %collective-permute-start.2 = (bf16[2,16,512]{2,1,0:T(8,128)(2,1)}, bf16[2,16,512]{2,1,0:T(8,128)(2,1)S(1)}, u32[]{:S(2)}, u32[]{:S(2)}) collective-permute-start(bf16[2,16,512]{2,1,0:T(8,128)(2,1)} %get-tuple-element.127), channel_id=1, source_target_pairs={{0,1},{1,2},{2,3},{3,4},{4,5},{5,6},{6,7},{7,8},{8,9},{9,10},{10,1... | collective-permute-start | bytes 98312 | tf_op jit(solution)/shard_map/ppermute | solution.py:1191
  50.1 1.7 collective-permute-start.3
  51.9 3.5 %collective-permute-done.3.refs_2_.refs_9_ = bf16[2,16,512]{2,1,0:T(8,128)(2,1)S(1)} collective-permute-done((bf16[2,16,512]{2,1,0:T(8,128)(2,1)}, bf16[2,16,512]{2,1,0:T(8,128)(2,1)S(1)}, u32[]{:S(2)}, u32[]{:S(2)}) %collective-permute-start.3) | collective-permute-done | bytes 32800 | tf_op jit(solution)/shard_map/ppermute | solution.py:1191
  56.0 6.0 %depth_conv.1 = (f32[512,512]{1,0:T(8,128)}, f32[32,8,128]{2,1,0:T(8,128)}) custom-call(s32[9]{0:T(128)} %concatenate.6.refs_0_.info, bf16[2,16,512]{2,1,0:T(8,128)(2,1)} %copy-done.16, bf16[2,16,512]{2,1,0:T(8,128)(2,1)} %copy-done.17, f32[8,128]{1,0:T(8,128)} %pad.4.refs_1_.refs_3_.refs_6_, f32[9,512]{1,0:T(8,128)} %refs_7_.6, ...), custom_call_target="tpu_custom_call" | custom-call | flops 7864320 | bytes 2097152 | tf_op jit(solution)/shard_map/depth_conv/pallas_call | solution.py:252
  61.9 6.1 %all-to-all-start = ((f32[32,8,128]{2,1,0:T(8,128)}), f32[32,8,128]{2,1,0:T(8,128)S(1)}, u32[]{:S(2)}, u32[]{:S(2)}) async-start(f32[32,8,128]{2,1,0:T(8,128)} %get-tuple-element.130), calls=%async_computation | async-start | bytes 262144 | tf_op jit(solution)/shard_map/all_to_all | solution.py:1195
  68.5 7.8 %all-to-all-done.refs_1_ = f32[32,8,128]{2,1,0:T(8,128)S(1)} async-done(((f32[32,8,128]{2,1,0:T(8,128)}), f32[32,8,128]{2,1,0:T(8,128)S(1)}, u32[]{:S(2)}, u32[]{:S(2)}) %all-to-all-start) | async-done | bytes 131104 | tf_op jit(solution)/shard_map/all_to_all | solution.py:1195
  77.0 12.6 %middle.1 = (bf16[512,512]{1,0:T(8,128)(2,1)}, bf16[512,2048]{1,0:T(8,128)(2,1)}, bf16[512,2048]{1,0:T(8,128)(2,1)}, bf16[512,512]{1,0:T(8,128)(2,1)}, bf16[512,...) custom-call(s32[9]{0:T(128)} %concatenate.6.refs_0_.info, ...), custom_call_target="tpu_custom_call" | custom-call | flops 4831838208 | bytes 25165824 | tf_op jit(solution)/shard_map/middle/pallas_call | solution.py:252
  89.6 2.6 %all-to-all-start.1 = ((f32[32,8,128]{2,1,0:T(8,128)}), f32[32,8,128]{2,1,0:T(8,128)S(1)}, u32[]{:S(2)}, u32[]{:S(2)}) async-start(f32[32,8,128]{2,1,0:T(8,128)} %get-tuple-element.134), calls=%async_computation.1 | async-start | bytes 262144 | tf_op jit(solution)/shard_map/all_to_all | solution.py:1195
  92.3 2.0 collective-permute-start.4
  94.3 1.3 collective-permute-start.5
  95.6 5.9 %feed_weights.1.refs_22_ = bf16[16,192,1024]{2,1,0:T(8,128)(2,1)} custom-call(bf16[512,512]{1,0:T(8,128)(2,1)} %get-tuple-element.135.refs_0_, bf16[512,2048]{1,0:T(8,128)(2,1)} %get-tuple-element.136.refs_1_, bf16[512,512]{1,0:T(8,128)(2,1)} %get-tuple-element.137.refs_2_, bf16[512,2048]{1,0:T(8,128)(2,1)} %get-tuple-element.138.refs_3_), custom_call_target="tpu_custom_call" | custom-call | flops 2147483648 | bytes 10485760 | tf_op jit(solution)/shard_map/feed_weights/pallas_call | solution.py:252
  102.2 14.0 %conv_back.1 = (bf16[16,192,1024]{2,1,0:T(8,128)(2,1)}, f32[512,512]{1,0:T(8,128)}, bf16[512,512]{1,0:T(8,128)(2,1)}, f32[16,512]{1,0:T(8,128)}) custom-call(s32[9]{0:T(128)} %concatenate.6.refs_0_.info, f32[32,8,128]{2,1,0:T(8,128)} %copy-done.11, f32[2,8,1024]{2,1,0:T(8,128)} %copy-done.20, ...), custom_call_target="tpu_custom_call", output_to_operand_aliasing={{0}: (22, {})} | custom-call | flops 1879048192 | bytes 16777216 | tf_op jit(solution)/shard_map/conv_back/pallas_call | solution.py:252
  116.3 14.7 %attend_back.1 = (bf16[256,512]{1,0:T(8,128)(2,1)}, bf16[256,512]{1,0:T(8,128)(2,1)}, bf16[2,128,1024]{2,1,0:T(8,128)(2,1)}, f32[128,1024]{1,0:T(8,128)}, f32[12...) custom-call(bf16[512,512]{1,0:T(8,128)(2,1)} %get-tuple-element.154., ...), custom_call_target="tpu_custom_call" | custom-call | flops 2818572288 | bytes 16777216 | tf_op jit(solution)/shard_map/attend_back/pallas_call | solution.py:252
  131.0 4.2 %collective-permute-start.6 = (bf16[2,128,1024]{2,1,0:T(8,128)(2,1)}, bf16[2,128,1024]{2,1,0:T(8,128)(2,1)S(1)}, u32[]{:S(2)}, u32[]{:S(2)}) collective-permute-start(bf16[2,128,1024]{2,1,0:T(8,128)(2,1)} %get-tuple-element.157), channel_id=1, source_target_pairs={{0,1},{1,2},{2,3},{3,4},{4,5},{5,6},{6,7},{7,8},{8,9},{9,10},{10,1... | collective-permute-start | bytes 1572872 | tf_op jit(solution)/shard_map/ppermute | solution.py:1191
  135.3 1.5 collective-permute-start.7
  136.8 4.3 %place_weights.1 = (bf16[8,64,512]{2,1,0:T(8,128)(2,1)}, bf16[8,64,512]{2,1,0:T(8,128)(2,1)}) custom-call(s32[9]{0:T(128)} %concatenate.6.refs_0_.info, bf16[512,512]{1,0:T(8,128)(2,1)} %get-tuple-element.120.refs_0_.refs_1_.refs_13_, bf16[256,512]{1,0:T(8,128)(2,1)} %get-tuple-element.159.refs_2_.refs_4_, ...), custom_call_target="tpu_custom_call" | custom-call | flops 536870912 | bytes 4194304 | tf_op jit(solution)/shard_map/place_weights/pallas_call | solution.py:252
  142.1 9.4 %back.1 = (bf16[8,224,512]{2,1,0:T(8,128)(2,1)}, bf16[8,224,512]{2,1,0:T(8,128)(2,1)}, bf16[512,512]{1,0:T(8,128)(2,1)}, bf16[512,512]{1,0:T(8,128)(2,1)}, f32[2...) custom-call(s32[9]{0:T(128)} %concatenate.6.refs_0_.info, bf16[2,128,1024]{2,1,0:T(8,128)(2,1)} %copy-done.12, ...), custom_call_target="tpu_custom_call" | custom-call | flops 2684354560 | bytes 18874368 | tf_op jit(solution)/shard_map/back/pallas_call | solution.py:252
  151.5 7.2 %collective-permute-start.9 = (bf16[8,224,512]{2,1,0:T(8,128)(2,1)}, bf16[8,224,512]{2,1,0:T(8,128)(2,1)S(1)}, u32[]{:S(2)}, u32[]{:S(2)}) collective-permute-start(bf16[8,224,512]{2,1,0:T(8,128)(2,1)} %get-tuple-element.184), channel_id=1, source_target_pairs={{0,1},{1,0},{2,3},{3,2},{4,5},{5,4},{6,7},{7,6},{8,9},{9,8},{10,11... | collective-permute-start | bytes 5505032 | tf_op jit(solution)/shard_map/ppermute | solution.py:1209
  158.6 8.6 %first_back.1 = (bf16[8,160,512]{2,1,0:T(8,128)(2,1)}, bf16[8,160,512]{2,1,0:T(8,128)(2,1)}, f32[4,512]{1,0:T(4,128)}, f32[512,512]{1,0:T(8,128)}) custom-call(s32[9]{0:T(128)} %concatenate.6.refs_0_.info, bf16[512,512]{1,0:T(8,128)(2,1)} %get-tuple-element.120.refs_0_.refs_1_.refs_13_, bf16[512,512]{1,0:T(8,128)(2,1)} %get-tuple-element.170.refs_2_, ...), custom_call_target="tpu_custom_call" | custom-call | flops 3221225472 | bytes 12582912 | tf_op jit(solution)/shard_map/first_back/pallas_call | solution.py:252
  168.0 2.0 fold_b.1
  170.1 1.3 collective-permute-start.11
  171.4 1.6 fold_a.1
  173.1 4.2 %collective-permute-start.10 = (bf16[4,160,512]{2,1,0:T(8,128)(2,1)}, bf16[4,160,512]{2,1,0:T(8,128)(2,1)S(1)}, u32[]{:S(2)}, u32[]{:S(2)}) collective-permute-start(bf16[4,160,512]{2,1,0:T(8,128)(2,1)} %bitcast.12), channel_id=1, source_target_pairs={{0,2},{1,3},{2,0},{3,1},{4,6},{5,7},{6,4},{7,5},{8,10},{9,11},{10,... | collective-permute-start | bytes 1966088 | tf_op jit(solution)/shard_map/ppermute | solution.py:1209
  177.3 2.4 last.1
  181.9 16.3 %collective-permute-done.14.refs_7_ = f32[37,512]{1,0:T(8,128)S(1)} collective-permute-done((f32[37,512]{1,0:T(8,128)S(1)}, f32[37,512]{1,0:T(8,128)S(1)}, u32[]{:S(2)}, u32[]{:S(2)}) %collective-permute-start.14) | collective-permute-done | bytes 75808 | tf_op jit(solution)/shard_map/ppermute | solution.py:1209
  198.2 1.6 collective-permute-done.13.refs_6_
  200.8 1.8 collective-permute-start.18
  202.6 1.4 collective-permute-start.15
  204.0 2.5 collective-permute-start.16
  207.6 3.9 %collective-permute-done.19.refs_7_ = f32[37,512]{1,0:T(8,128)S(1)} collective-permute-done((f32[37,512]{1,0:T(8,128)S(1)}, f32[37,512]{1,0:T(8,128)S(1)}, u32[]{:S(2)}, u32[]{:S(2)}) %collective-permute-start.19) | collective-permute-done | bytes 75808 | tf_op jit(solution)/shard_map/ppermute | solution.py:1476
  211.4 3.3 %collective-permute-done.15.refs_2_ = bf16[1,160,512]{2,1,0:T(8,128)(2,1)S(1)} collective-permute-done((bf16[1,160,512]{2,1,0:T(8,128)(2,1)S(1)}, bf16[1,160,512]{2,1,0:T(8,128)(2,1)S(1)}, u32[]{:S(2)}, u32[]{:S(2)}) %collective-permute-start.15) | collective-permute-done | bytes 163872 | tf_op jit(solution)/shard_map/ppermute | solution.py:1209
  214.8 5.2 %collective-permute-done.17.refs_4_ = bf16[1,160,512]{2,1,0:T(8,128)(2,1)S(1)} collective-permute-done((bf16[1,160,512]{2,1,0:T(8,128)(2,1)S(1)}, bf16[1,160,512]{2,1,0:T(8,128)(2,1)S(1)}, u32[]{:S(2)}, u32[]{:S(2)}) %collective-permute-start.17) | collective-permute-done | bytes 163872 | tf_op jit(solution)/shard_map/ppermute | solution.py:1209
  220.8 1.5 collective-permute-start.24
  222.9 3.3 %collective-permute-start.20 = (bf16[1,224,256]{2,1,0:T(8,128)(2,1)S(1)}, bf16[1,224,256]{2,1,0:T(8,128)(2,1)S(1)}, u32[]{:S(2)}, u32[]{:S(2)}) collective-permute-start(bf16[1,224,256]{2,1,0:T(8,128)(2,1)S(1)} %bitcast.51), channel_id=1, source_target_pairs={{0,4},{1,5},{2,6},{3,7},{4,0},{5,1},{6,2},{7,3},{8,12},{9,13},{10,... | collective-permute-start | bytes 344072 | tf_op jit(solution)/shard_map/ppermute | solution.py:1209
  226.2 2.4 collective-permute-start.22
  228.5 1.2 collective-permute-done.20.refs_3_
  229.8 6.8 %collective-permute-done.21.refs_4_ = bf16[1,224,256]{2,1,0:T(8,128)(2,1)S(1)} collective-permute-done((bf16[1,224,256]{2,1,0:T(8,128)(2,1)S(1)}, bf16[1,224,256]{2,1,0:T(8,128)(2,1)S(1)}, u32[]{:S(2)}, u32[]{:S(2)}) %collective-permute-start.21) | collective-permute-done | bytes 114720 | tf_op jit(solution)/shard_map/ppermute | solution.py:1209
  238.3 1.6 collective-permute-start.25
  239.9 1.5 collective-permute-start.28
  241.4 1.8 collective-permute-start.27
  244.3 1.9 collective-permute-done.28.refs_3_
  246.2 2.5 collective-permute-done.27.refs_2_
  248.8 1.9 finish.1
  (111 shorter events, 15.2 us)
Async XLA Ops:
  7.2 12.1 %copy-start.26 = (s32[4,17]{1,0:T(4,128)S(1)}, s32[4,17]{1,0:T(4,128)}, u32[]{:S(2)}) copy-start(s32[4,17]{1,0:T(4,128)} %param.18) | copy-start | bytes 820
  7.2 13.1 %copy-start.27 = (s32[2]{0:T(128)S(1)}, s32[2]{0:T(128)}, u32[]{:S(2)}) copy-start(s32[2]{0:T(128)} %param.19) | copy-start | bytes 28
  14.7 9.2 %collective-permute-start.1 = (bf16[2,128,1024]{2,1,0:T(8,128)(2,1)}, bf16[2,128,1024]{2,1,0:T(8,128)(2,1)S(1)}, u32[]{:S(2)}, u32[]{:S(2)}) collective-permute-start(bf16[2,128,1024]{2,1,0:T(8,128)(2,1)} %get-tuple-element.124.refs_5_.refs_4_), channel_id=1, source_target_pairs={{1,0},{2,1},{3,2},{4,3},{5,4},{6,5},{7,6},{8,7},{9,8},{10,9},{11,1... | collective-permute-start | bytes 1572872 | tf_op jit(solution)/shard_map/ppermute | solution.py:1191
  16.0 8.0 %collective-permute-start = (bf16[2,128,1024]{2,1,0:T(8,128)(2,1)}, bf16[2,128,1024]{2,1,0:T(8,128)(2,1)S(1)}, u32[]{:S(2)}, u32[]{:S(2)}) collective-permute-start(bf16[2,128,1024]{2,1,0:T(8,128)(2,1)} %get-tuple-element.125.refs_6_.refs_5_), channel_id=1, source_target_pairs={{0,1},{1,2},{2,3},{3,4},{4,5},{5,6},{6,7},{7,8},{8,9},{9,10},{10,1... | collective-permute-start | bytes 1572872 | tf_op jit(solution)/shard_map/ppermute | solution.py:1191
  39.7 12.1 %collective-permute-start.2 = (bf16[2,16,512]{2,1,0:T(8,128)(2,1)}, bf16[2,16,512]{2,1,0:T(8,128)(2,1)S(1)}, u32[]{:S(2)}, u32[]{:S(2)}) collective-permute-start(bf16[2,16,512]{2,1,0:T(8,128)(2,1)} %get-tuple-element.127), channel_id=1, source_target_pairs={{0,1},{1,2},{2,3},{3,4},{4,5},{5,6},{6,7},{7,8},{8,9},{9,10},{10,1... | collective-permute-start | bytes 98312 | tf_op jit(solution)/shard_map/ppermute | solution.py:1191
  50.1 5.2 %collective-permute-start.3 = (bf16[2,16,512]{2,1,0:T(8,128)(2,1)}, bf16[2,16,512]{2,1,0:T(8,128)(2,1)S(1)}, u32[]{:S(2)}, u32[]{:S(2)}) collective-permute-start(bf16[2,16,512]{2,1,0:T(8,128)(2,1)} %get-tuple-element.128), channel_id=1, source_target_pairs={{1,0},{2,1},{3,2},{4,3},{5,4},{6,5},{7,6},{8,7},{9,8},{10,9},{11,1... | collective-permute-start | bytes 98312 | tf_op jit(solution)/shard_map/ppermute | solution.py:1191
  51.9 3.5 %copy-start.16 = (bf16[2,16,512]{2,1,0:T(8,128)(2,1)}, bf16[2,16,512]{2,1,0:T(8,128)(2,1)S(1)}, u32[]{:S(2)}) copy-start(bf16[2,16,512]{2,1,0:T(8,128)(2,1)S(1)} %collective-permute-done.2.refs_1_.refs_8_) | copy-start | bytes 98308
  61.9 14.4 %all-to-all-start = ((f32[32,8,128]{2,1,0:T(8,128)}), f32[32,8,128]{2,1,0:T(8,128)S(1)}, u32[]{:S(2)}, u32[]{:S(2)}) async-start(f32[32,8,128]{2,1,0:T(8,128)} %get-tuple-element.130), calls=%async_computation | async-start | bytes 262144 | tf_op jit(solution)/shard_map/all_to_all | solution.py:1195
  89.6 11.9 %all-to-all-start.1 = ((f32[32,8,128]{2,1,0:T(8,128)}), f32[32,8,128]{2,1,0:T(8,128)S(1)}, u32[]{:S(2)}, u32[]{:S(2)}) async-start(f32[32,8,128]{2,1,0:T(8,128)} %get-tuple-element.134), calls=%async_computation.1 | async-start | bytes 262144 | tf_op jit(solution)/shard_map/all_to_all | solution.py:1195
  92.2 128.6 %reduce-scatter.2.cloned.1.call-start = ((), (), s32[]{:S(2)}) async-start(), calls=%async_computation.3 | async-start | bytes 6684672 | tf_op jit(solution)/shard_map/reduce_scatter | solution.py:1199
  92.3 9.3 %collective-permute-start.4 = (f32[2,8,1024]{2,1,0:T(8,128)}, f32[2,8,1024]{2,1,0:T(8,128)S(1)}, u32[]{:S(2)}, u32[]{:S(2)}) collective-permute-start(f32[2,8,1024]{2,1,0:T(8,128)} %get-tuple-element.140), channel_id=1, source_target_pairs={{0,1},{1,2},{2,3},{3,4},{4,5},{5,6},{6,7},{7,8},{8,9},{9,10},{10,1... | collective-permute-start | bytes 196616 | tf_op jit(solution)/shard_map/ppermute | solution.py:1191
  94.3 7.3 %collective-permute-start.5 = (f32[2,8,1024]{2,1,0:T(8,128)}, f32[2,8,1024]{2,1,0:T(8,128)S(1)}, u32[]{:S(2)}, u32[]{:S(2)}) collective-permute-start(f32[2,8,1024]{2,1,0:T(8,128)} %get-tuple-element.141), channel_id=1, source_target_pairs={{1,0},{2,1},{3,2},{4,3},{5,4},{6,5},{7,6},{8,7},{9,8},{10,9},{11,1... | collective-permute-start | bytes 196616 | tf_op jit(solution)/shard_map/ppermute | solution.py:1191
  131.0 10.0 %collective-permute-start.6 = (bf16[2,128,1024]{2,1,0:T(8,128)(2,1)}, bf16[2,128,1024]{2,1,0:T(8,128)(2,1)S(1)}, u32[]{:S(2)}, u32[]{:S(2)}) collective-permute-start(bf16[2,128,1024]{2,1,0:T(8,128)(2,1)} %get-tuple-element.157), channel_id=1, source_target_pairs={{0,1},{1,2},{2,3},{3,4},{4,5},{5,6},{6,7},{7,8},{8,9},{9,10},{10,1... | collective-permute-start | bytes 1572872 | tf_op jit(solution)/shard_map/ppermute | solution.py:1191
  135.3 5.8 %collective-permute-start.7 = (bf16[2,128,1024]{2,1,0:T(8,128)(2,1)}, bf16[2,128,1024]{2,1,0:T(8,128)(2,1)S(1)}, u32[]{:S(2)}, u32[]{:S(2)}) collective-permute-start(bf16[2,128,1024]{2,1,0:T(8,128)(2,1)} %get-tuple-element.158), channel_id=1, source_target_pairs={{1,0},{2,1},{3,2},{4,3},{5,4},{6,5},{7,6},{8,7},{9,8},{10,9},{11,1... | collective-permute-start | bytes 1572872 | tf_op jit(solution)/shard_map/ppermute | solution.py:1191
  151.5 16.6 %collective-permute-start.9 = (bf16[8,224,512]{2,1,0:T(8,128)(2,1)}, bf16[8,224,512]{2,1,0:T(8,128)(2,1)S(1)}, u32[]{:S(2)}, u32[]{:S(2)}) collective-permute-start(bf16[8,224,512]{2,1,0:T(8,128)(2,1)} %get-tuple-element.184), channel_id=1, source_target_pairs={{0,1},{1,0},{2,3},{3,2},{4,5},{5,4},{6,7},{7,6},{8,9},{9,8},{10,11... | collective-permute-start | bytes 5505032 | tf_op jit(solution)/shard_map/ppermute | solution.py:1209
  158.6 8.7 %copy-start.22 = (f32[8,512]{1,0:T(8,128)S(1)}, f32[8,512]{1,0:T(8,128)}, u32[]{:S(2)}) copy-start(f32[8,512]{1,0:T(8,128)} %get-tuple-element.191) | copy-start | bytes 49156
  158.6 9.4 %copy-start.1 = (bf16[8,224,512]{2,1,0:T(8,128)(2,1)S(1)}, bf16[8,224,512]{2,1,0:T(8,128)(2,1)}, u32[]{:S(2)}) copy-start(bf16[8,224,512]{2,1,0:T(8,128)(2,1)} %get-tuple-element.183.refs_0_) | copy-start | bytes 5505028
  158.6 9.4 %copy-start.10 = (s32[9]{0:T(128)S(1)}, s32[9]{0:T(128)}, u32[]{:S(2)}) copy-start(s32[9]{0:T(128)} %concatenate.6.refs_0_.info) | copy-start | bytes 112
  167.2 4.2 %collective-permute-start.8 = (bf16[8,160,512]{2,1,0:T(8,128)(2,1)}, bf16[8,160,512]{2,1,0:T(8,128)(2,1)S(1)}, u32[]{:S(2)}, u32[]{:S(2)}) collective-permute-start(bf16[8,160,512]{2,1,0:T(8,128)(2,1)} %get-tuple-element.176), channel_id=1, source_target_pairs={{0,1},{1,0},{2,3},{3,2},{4,5},{5,4},{6,7},{7,6},{8,9},{9,8},{10,11... | collective-permute-start | bytes 3932168 | tf_op jit(solution)/shard_map/ppermute | solution.py:1209
  168.0 3.4 %copy-start.2 = (bf16[8,160,512]{2,1,0:T(8,128)(2,1)S(1)}, bf16[8,160,512]{2,1,0:T(8,128)(2,1)}, u32[]{:S(2)}) copy-start(bf16[8,160,512]{2,1,0:T(8,128)(2,1)} %get-tuple-element.175) | copy-start | bytes 3932164
  170.0 7.2 %copy-start.25 = (f32[8,512]{1,0:T(8,128)S(1)}, f32[8,512]{1,0:T(8,128)}, u32[]{:S(2)}) copy-start(f32[8,512]{1,0:T(8,128)} %get-tuple-element.190) | copy-start | bytes 49156
  170.0 7.2 %copy-start = (bf16[2,256,512]{2,1,0:T(8,128)(2,1)S(1)}, bf16[2,256,512]{2,1,0:T(8,128)(2,1)}, u32[]{:S(2)}) copy-start(bf16[2,256,512]{2,1,0:T(8,128)(2,1)} %refs_1_.5) | copy-start | bytes 1572868
  170.0 7.2 %copy-start.3 = (f32[512,512]{1,0:T(8,128)S(1)}, f32[512,512]{1,0:T(8,128)}, u32[]{:S(2)}) copy-start(f32[512,512]{1,0:T(8,128)} %get-tuple-element.178.refs_2_) | copy-start | bytes 3145732
  170.0 7.3 %copy-start.6 = (f32[256,512]{1,0:T(8,128)S(1)}, f32[256,512]{1,0:T(8,128)}, u32[]{:S(2)}) copy-start(f32[256,512]{1,0:T(8,128)} %get-tuple-element.179.refs_3_) | copy-start | bytes 1572868
  170.0 7.3 %copy-start.7 = (f32[256,512]{1,0:T(8,128)S(1)}, f32[256,512]{1,0:T(8,128)}, u32[]{:S(2)}) copy-start(f32[256,512]{1,0:T(8,128)} %get-tuple-element.180.refs_4_) | copy-start | bytes 1572868
  170.1 7.3 %copy-start.8 = (f32[6,512]{1,0:T(8,128)S(1)}, f32[6,512]{1,0:T(8,128)}, u32[]{:S(2)}) copy-start(f32[6,512]{1,0:T(8,128)} %refs_0_.3) | copy-start | bytes 36868
  170.1 29.8 %collective-permute-start.11 = (bf16[8,224,256]{2,1,0:T(8,128)(2,1)}, bf16[8,224,256]{2,1,0:T(8,128)(2,1)S(1)}, u32[]{:S(2)}, u32[]{:S(2)}) collective-permute-start(bf16[8,224,256]{2,1,0:T(8,128)(2,1)} %get-tuple-element.187), channel_id=1, source_target_pairs={{0,16},{16,0},{1,17},{17,1},{2,18},{18,2},{3,19},{19,3},{4,20},{20... | collective-permute-start | bytes 2752520 | tf_op jit(solution)/shard_map/ppermute | solution.py:1443
  173.1 6.7 %copy-start.23 = (f32[4,512]{1,0:T(4,128)S(1)}, f32[4,512]{1,0:T(4,128)}, u32[]{:S(2)}) copy-start(f32[4,512]{1,0:T(4,128)} %get-tuple-element.194) | copy-start | bytes 24580
  173.1 6.7 %copy-start.24 = (f32[4,512]{1,0:T(4,128)S(1)}, f32[4,512]{1,0:T(4,128)}, u32[]{:S(2)}) copy-start(f32[4,512]{1,0:T(4,128)} %get-tuple-element.193) | copy-start | bytes 24580
  173.1 26.8 %copy-start.5 = (bf16[8,224,256]{2,1,0:T(8,128)(2,1)S(1)}, bf16[8,224,256]{2,1,0:T(8,128)(2,1)}, u32[]{:S(2)}) copy-start(bf16[8,224,256]{2,1,0:T(8,128)(2,1)} %copy-done.4) | copy-start | bytes 2752516
  173.1 26.8 %collective-permute-start.10 = (bf16[4,160,512]{2,1,0:T(8,128)(2,1)}, bf16[4,160,512]{2,1,0:T(8,128)(2,1)S(1)}, u32[]{:S(2)}, u32[]{:S(2)}) collective-permute-start(bf16[4,160,512]{2,1,0:T(8,128)(2,1)} %bitcast.12), channel_id=1, source_target_pairs={{0,2},{1,3},{2,0},{3,1},{4,6},{5,7},{6,4},{7,5},{8,10},{9,11},{10,... | collective-permute-start | bytes 1966088 | tf_op jit(solution)/shard_map/ppermute | solution.py:1209
  180.0 18.2 %collective-permute-start.14 = (f32[37,512]{1,0:T(8,128)S(1)}, f32[37,512]{1,0:T(8,128)S(1)}, u32[]{:S(2)}, u32[]{:S(2)}) collective-permute-start(f32[37,512]{1,0:T(8,128)S(1)} %concatenate.7.refs_4_), channel_id=1, source_target_pairs={{0,3},{1,2},{2,1},{3,0},{4,7},{5,6},{6,5},{7,4},{8,11},{9,10},{10,... | collective-permute-start | bytes 227336 | tf_op jit(solution)/shard_map/ppermute | solution.py:1209
  180.1 19.7 %collective-permute-start.13 = (f32[37,512]{1,0:T(8,128)S(1)}, f32[37,512]{1,0:T(8,128)S(1)}, u32[]{:S(2)}, u32[]{:S(2)}) collective-permute-start(f32[37,512]{1,0:T(8,128)S(1)} %concatenate.7.refs_4_), channel_id=1, source_target_pairs={{0,2},{1,3},{2,0},{3,1},{4,6},{5,7},{6,4},{7,5},{8,10},{9,11},{10,... | collective-permute-start | bytes 227336 | tf_op jit(solution)/shard_map/ppermute | solution.py:1209
  181.2 18.6 %collective-permute-start.12 = (f32[37,512]{1,0:T(8,128)S(1)}, f32[37,512]{1,0:T(8,128)S(1)}, u32[]{:S(2)}, u32[]{:S(2)}) collective-permute-start(f32[37,512]{1,0:T(8,128)S(1)} %concatenate.7.refs_4_), channel_id=1, source_target_pairs={{0,1},{1,0},{2,3},{3,2},{4,5},{5,4},{6,7},{7,6},{8,9},{9,8},{10,11... | collective-permute-start | bytes 227336 | tf_op jit(solution)/shard_map/ppermute | solution.py:1209
  200.8 19.2 %collective-permute-start.18 = (bf16[4,224,256]{2,1,0:T(8,128)(2,1)S(1)}, bf16[4,224,256]{2,1,0:T(8,128)(2,1)S(1)}, u32[]{:S(2)}, u32[]{:S(2)}) collective-permute-start(bf16[4,224,256]{2,1,0:T(8,128)(2,1)S(1)} %bitcast.45), channel_id=1, source_target_pairs={{0,2},{1,3},{2,0},{3,1},{4,6},{5,7},{6,4},{7,5},{8,10},{9,11},{10,... | collective-permute-start | bytes 1376264 | tf_op jit(solution)/shard_map/ppermute | solution.py:1209
  202.6 12.2 %collective-permute-start.15 = (bf16[1,160,512]{2,1,0:T(8,128)(2,1)S(1)}, bf16[1,160,512]{2,1,0:T(8,128)(2,1)S(1)}, u32[]{:S(2)}, u32[]{:S(2)}) collective-permute-start(bf16[1,160,512]{2,1,0:T(8,128)(2,1)S(1)} %bitcast.48), channel_id=1, source_target_pairs={{0,4},{1,5},{2,6},{3,7},{4,0},{5,1},{6,2},{7,3},{8,12},{9,13},{10,... | collective-permute-start | bytes 491528 | tf_op jit(solution)/shard_map/ppermute | solution.py:1209
  204.0 10.7 %collective-permute-start.16 = (bf16[1,160,512]{2,1,0:T(8,128)(2,1)S(1)}, bf16[1,160,512]{2,1,0:T(8,128)(2,1)S(1)}, u32[]{:S(2)}, u32[]{:S(2)}) collective-permute-start(bf16[1,160,512]{2,1,0:T(8,128)(2,1)S(1)} %bitcast.47), channel_id=1, source_target_pairs={{0,8},{1,9},{2,10},{3,11},{4,12},{5,13},{6,14},{7,15},{8,0},{9,1},... | collective-permute-start | bytes 491528 | tf_op jit(solution)/shard_map/ppermute | solution.py:1209
  206.5 13.5 %collective-permute-start.17 = (bf16[1,160,512]{2,1,0:T(8,128)(2,1)S(1)}, bf16[1,160,512]{2,1,0:T(8,128)(2,1)S(1)}, u32[]{:S(2)}, u32[]{:S(2)}) collective-permute-start(bf16[1,160,512]{2,1,0:T(8,128)(2,1)S(1)} %bitcast.46), channel_id=1, source_target_pairs={{0,12},{1,13},{2,14},{3,15},{4,8},{5,9},{6,10},{7,11},{8,4},{9,5},... | collective-permute-start | bytes 491528 | tf_op jit(solution)/shard_map/ppermute | solution.py:1209
  207.0 4.4 %collective-permute-start.19 = (f32[37,512]{1,0:T(8,128)S(1)}, f32[37,512]{1,0:T(8,128)S(1)}, u32[]{:S(2)}, u32[]{:S(2)}) collective-permute-start(f32[37,512]{1,0:T(8,128)S(1)} %get-tuple-element.201.refs_6_), channel_id=1, source_target_pairs={{0,16},{16,0},{1,17},{17,1},{2,18},{18,2},{3,19},{19,3},{4,20},{20... | collective-permute-start | bytes 227336 | tf_op jit(solution)/shard_map/ppermute | solution.py:1476
  220.8 15.8 %collective-permute-start.24 = (bf16[1,192,1024]{2,1,0:T(8,128)(2,1)}, bf16[1,192,1024]{2,1,0:T(8,128)(2,1)S(1)}, u32[]{:S(2)}, u32[]{:S(2)}) collective-permute-start(bf16[1,192,1024]{2,1,0:T(8,128)(2,1)} %reduce-scatter.2.cloned.1.call-done.refs_2_), channel_id=1, source_target_pairs={{0,16},{16,0},{1,17},{17,1},{2,18},{18,2},{3,19},{19,3},{4,20},{20... | collective-permute-start | bytes 1179656 | tf_op jit(solution)/shard_map/ppermute | solution.py:1473
  222.3 14.3 %collective-permute-start.23 = (bf16[1,160,512]{2,1,0:T(8,128)(2,1)S(1)}, bf16[1,160,512]{2,1,0:T(8,128)(2,1)S(1)}, u32[]{:S(2)}, u32[]{:S(2)}) collective-permute-start(bf16[1,160,512]{2,1,0:T(8,128)(2,1)S(1)} %get-tuple-element.205.refs_1_), channel_id=1, source_target_pairs={{0,16},{16,0},{1,17},{17,1},{2,18},{18,2},{3,19},{19,3},{4,20},{20... | collective-permute-start | bytes 491528 | tf_op jit(solution)/shard_map/ppermute | solution.py:1472
  222.9 6.9 %collective-permute-start.20 = (bf16[1,224,256]{2,1,0:T(8,128)(2,1)S(1)}, bf16[1,224,256]{2,1,0:T(8,128)(2,1)S(1)}, u32[]{:S(2)}, u32[]{:S(2)}) collective-permute-start(bf16[1,224,256]{2,1,0:T(8,128)(2,1)S(1)} %bitcast.51), channel_id=1, source_target_pairs={{0,4},{1,5},{2,6},{3,7},{4,0},{5,1},{6,2},{7,3},{8,12},{9,13},{10,... | collective-permute-start | bytes 344072 | tf_op jit(solution)/shard_map/ppermute | solution.py:1209
  226.2 10.4 %collective-permute-start.21 = (bf16[1,224,256]{2,1,0:T(8,128)(2,1)S(1)}, bf16[1,224,256]{2,1,0:T(8,128)(2,1)S(1)}, u32[]{:S(2)}, u32[]{:S(2)}) collective-permute-start(bf16[1,224,256]{2,1,0:T(8,128)(2,1)S(1)} %bitcast.50), channel_id=1, source_target_pairs={{0,8},{1,9},{2,10},{3,11},{4,12},{5,13},{6,14},{7,15},{8,0},{9,1},... | collective-permute-start | bytes 344072 | tf_op jit(solution)/shard_map/ppermute | solution.py:1209
  226.2 10.4 %collective-permute-start.22 = (bf16[1,224,256]{2,1,0:T(8,128)(2,1)S(1)}, bf16[1,224,256]{2,1,0:T(8,128)(2,1)S(1)}, u32[]{:S(2)}, u32[]{:S(2)}) collective-permute-start(bf16[1,224,256]{2,1,0:T(8,128)(2,1)S(1)} %bitcast.49), channel_id=1, source_target_pairs={{0,12},{1,13},{2,14},{3,15},{4,8},{5,9},{6,10},{7,11},{8,4},{9,5},... | collective-permute-start | bytes 344072 | tf_op jit(solution)/shard_map/ppermute | solution.py:1209
  238.3 10.5 %collective-permute-start.25 = (bf16[1,224,256]{2,1,0:T(8,128)(2,1)S(1)}, bf16[1,224,256]{2,1,0:T(8,128)(2,1)S(1)}, u32[]{:S(2)}, u32[]{:S(2)}) collective-permute-start(bf16[1,224,256]{2,1,0:T(8,128)(2,1)S(1)} %get-tuple-element.211), channel_id=1, source_target_pairs={{0,16},{16,0},{1,17},{17,1},{2,18},{18,2},{3,19},{19,3},{4,20},{20... | collective-permute-start | bytes 344072 | tf_op jit(solution)/shard_map/ppermute | solution.py:1481
  239.9 6.3 %collective-permute-start.28 = (f32[37,512]{1,0:T(8,128)S(1)}, f32[37,512]{1,0:T(8,128)S(1)}, u32[]{:S(2)}, u32[]{:S(2)}) collective-permute-start(f32[37,512]{1,0:T(8,128)S(1)} %get-tuple-element.213.refs_0_), channel_id=1, source_target_pairs={{0,12},{1,13},{2,14},{3,15},{4,8},{5,9},{6,10},{7,11},{8,4},{9,5},... | collective-permute-start | bytes 227336 | tf_op jit(solution)/shard_map/ppermute | solution.py:1209
  241.4 7.4 %collective-permute-start.27 = (f32[37,512]{1,0:T(8,128)S(1)}, f32[37,512]{1,0:T(8,128)S(1)}, u32[]{:S(2)}, u32[]{:S(2)}) collective-permute-start(f32[37,512]{1,0:T(8,128)S(1)} %get-tuple-element.213.refs_0_), channel_id=1, source_target_pairs={{0,8},{1,9},{2,10},{3,11},{4,12},{5,13},{6,14},{7,15},{8,0},{9,1},... | collective-permute-start | bytes 227336 | tf_op jit(solution)/shard_map/ppermute | solution.py:1209
  243.2 5.6 %collective-permute-start.26 = (f32[37,512]{1,0:T(8,128)S(1)}, f32[37,512]{1,0:T(8,128)S(1)}, u32[]{:S(2)}, u32[]{:S(2)}) collective-permute-start(f32[37,512]{1,0:T(8,128)S(1)} %get-tuple-element.213.refs_0_), channel_id=1, source_target_pairs={{0,4},{1,5},{2,6},{3,7},{4,0},{5,1},{6,2},{7,3},{8,12},{9,13},{10,... | collective-permute-start | bytes 227336 | tf_op jit(solution)/shard_map/ppermute | solution.py:1209
  (12 other events, 14.2 us)
Sparse Core Ops, SparseCore 0:
  116.4 97.0 reduce-scatter.1

commit v6 on v5

--- a/solution.py
+++ b/solution.py
@@ -151,10 +151,18 @@
     def __init__(self, loads, stores, sems):
         self.sems, self.used, self.pending, self.targets = sems, 0, [], []
         self.named, self.all_loads = {}, []
-        for name, pairs, single in loads:
-            items = [Load(source, buffer, self.sem()) for source, buffer in pairs]
-            self.all_loads += items
-            self.named[name] = items[0] if single else Loads(items)
+        while loads:
+            run = [loads.pop(0)]
+            while not run[0][2] and loads and len(loads[0][1]) == len(run[0][1]) > 1:
+                run.append(loads.pop(0))
+            items = [[] for _ in run]
+            for at in range(len(run[0][1])):
+                for (_, pairs, _), own in zip(run, items):
+                    source, buffer = pairs[at]
+                    own.append(Load(source, buffer, self.sem()))
+            for (name, _, single), own in zip(run, items):
+                self.all_loads += own
+                self.named[name] = own[0] if single else Loads(own)
         for name, pairs, single in stores:
             self.targets += [[target, buffer, False] for target, buffer in pairs]
             buffers = [buffer for _, buffer in pairs]
@@ -328,10 +336,8 @@
         for part in range(parts):
             cut = slice(part * PART, (part + 1) * PART)
             inner = dot(k.n0[...], k.w_in[part][...]) + k.b_in[0:1, cut]
-            active, slope = activate(inner)
+            active, _ = activate(inner)
             k.act[:, cut] = active.astype(bf16)
-            k.slope[:, cut] = slope.astype(bf16)
-        k.send(k.slope)
         k.send(k.act)
         branch = k.bias[6:7]
         for part in range(parts):
@@ -365,34 +371,48 @@
         ),
         dict(
             after=sds((tokens, model), f32), n0=low, na=low, lo=kv, hi=kv,
-            act=sds((tokens, hidden), bf16), slope=sds((tokens, hidden), bf16),
+            act=sds((tokens, hidden), bf16),
         ),
         flops=2 * tokens * model * (2 * hidden + 2 * model),
         moved=16 << 20,
     )
 
 
-def queries(na, attend_in, bias, sinusoid, proj):
-    tokens, model = na.shape
+def queries(start, feed_in, feed_in_bias, attend_in, bias, sinusoid, proj):
+    tokens, model = start.na.shape
+    hidden = feed_in.shape[2]
+    parts = hidden // PART
 
     def body(k):
         query = dot(k.na[...], k.attend_in[...]) + k.bias[0:1]
         factor = 1.0 / math.sqrt(DH)
         k.qu[...] = ((query + k.bias[8:9]) * factor).astype(bf16)
         k.qv[...] = ((query + k.bias[9:10]) * factor).astype(bf16)
+        k.send(k.qu)
+        k.send(k.qv)
         k.table[...] = dot(k.sinusoid[...], k.proj[...]).astype(bf16)
+        k.send(k.table)
+        for part in range(parts):
+            cut = slice(part * PART, (part + 1) * PART)
+            inner = dot(k.n0[...], k.w_in[part][...]) + k.b_in[0:1, cut]
+            _, slope = activate(inner)
+            k.slope[:, cut] = slope.astype(bf16)
 
     low = sds((tokens, model), bf16)
+    spans = [(at, PART) for at in range(0, hidden, PART)]
+    w_in = [slab(feed_in, 0, (0, model), span) for span in spans]
     return staged(
         "queries",
         body,
         dict(
-            na=na, attend_in=slab(attend_in, (0, model), (0, model)), bias=bias,
-            sinusoid=sinusoid, proj=proj,
+            na=start.na, attend_in=slab(attend_in, (0, model), (0, model)), bias=bias,
+            sinusoid=sinusoid, proj=proj, n0=start.n0, b_in=feed_in_bias, w_in=w_in,
         ),
-        dict(qu=low, qv=low, table=sds((SPAN, model), bf16)),
-        flops=2 * tokens * model * 2 * model,
-        moved=4 << 20,
+        dict(
+            qu=low, qv=low, table=sds((SPAN, model), bf16), slope=sds((tokens, hidden), bf16)
+        ),
+        flops=2 * tokens * model * (hidden + 2 * model),
+        moved=10 << 20,
     )
 
 
@@ -699,8 +719,8 @@
     w_in, w_out = feed_slabs(feed_in, feed_out, 1)
     ins = dict(
         gain=gain, shift=shift, depth=depth, bias=bias,
-        convolve_out=convolve_out, stream=stream, b_in=feed_in_bias, w_in=w_in, w_out=w_out,
-        cotangent=cotangent,
+        convolve_out=convolve_out, stream=stream, b_in=feed_in_bias, w_in=w_in,
+        cotangent=cotangent, w_out=w_out,
     )
     low = sds((tokens, model), bf16)
     wide = sds((tokens, model), f32)
@@ -889,13 +909,13 @@
                 turned[2] = dot(turn, k.qv[row][here]).astype(bf16)
                 blocks = [k.lo[row], k.hi[row]]
                 blocks = blocks + [k.next[row]] if block else [k.before[row]] + blocks
-                prob = k.prob[2 * row + block]
+                prob = k.prob[row]
                 for group in range(GROUPS):
                     cut = slice(WIDE * group, WIDE * (group + 1))
                     cut_v = slice(model + WIDE * group, model + WIDE * (group + 1))
                     keys = jnp.concatenate([b[:, cut] for b in blocks], axis=0)
                     values = jnp.concatenate([b[:, cut_v] for b in blocks], axis=0)
-                    weights = below(prob[group])
+                    weights = below(prob[block, group])
                     grad_mixed = heads_apart(turned[0, :, cut])
                     grad = dot_last(grad_mixed, values)
                     wide = weights.astype(f32)
@@ -930,14 +950,9 @@
             k.send(k.gq[row])
 
     ins = dict(
-        gm=by_row(gm, rows), qu=by_row(query.qu, rows), qv=by_row(query.qv, rows),
-        before=each_of(before), lo=each_of(start.lo), hi=each_of(start.hi),
-        prob=[
-            slab(prob, block, (0, GROUPS), (0, WIN), (0, MANY * SPAN))
-            for prob in probs
-            for block in range(2)
-        ],
-        table=query.table, next=each_of(after),
+        table=query.table, gm=by_row(gm, rows), qu=by_row(query.qu, rows),
+        qv=by_row(query.qv, rows), before=each_of(before), lo=each_of(start.lo),
+        hi=each_of(start.hi), prob=list(probs), next=each_of(after),
     )
     kv = (WIN, 2 * model)
     return staged(
@@ -1410,7 +1425,10 @@
         features, feed_in, feed_in_bias, feed_out, attend_in, norm_gain, norm_shift, biases
     )
     before, after = neighbours(start.hi, start.lo)
-    query = queries(start.na, attend_in, biases, sinusoid, position_proj)
+    query = queries(
+        start, feed_in, feed_in_bias, attend_in, biases, sinusoid, position_proj
+    )
+    start.slope = query.slope
     mix = attend(
         row_len, info, ends, start, query, before, after, attend_out, convolve_in, norm_gain,
         norm_shift, biases,

time: 262 us -> 260 us (level)
  starting transfers between devices: 69.6 us -> 65.9 us
    ppermute x4, starting transfers between devices: 19.9 us -> 16.9 us  [neighbours(): lax.ppermute(last_block, 'frames', up)]
  transfers between devices with their start and end apart: 32 -> 32, of which waited for: 11 -> 11; matrix products, arithmetic and copies ran while one was open for 1% -> 1% of each run, Pallas kernels for 21% -> 22%
where the time goes in v6:
time: 260 us; the launch traced here: 256 us
  Pallas kernels  112 us (43%)
  starting transfers between devices  65.9 us (25%)
  waiting for transfers between devices  55.2 us (21%)
  between operations  14.9 us (6%)
  local copies, waits for them, and re-layouts  7.65 us (3%)
    pallas_call x12, Pallas kernels, staged(): pl.pallas_call(run, in_specs=[pl.BlockSpec(memory_space=pltpu.SMEM)] * n_...  104 us
    ppermute x16, waiting for transfers between devices, swap(): return lax.ppermute(x, 'frames', [(i, i ^ k) for i in range(n)])  39.7 us
    ppermute x16, starting transfers between devices, swap(): return lax.ppermute(x, 'frames', [(i, i ^ k) for i in range(n)])  29.7 us
    ppermute x4, starting transfers between devices, neighbours(): lax.ppermute(last_block, 'frames', up)  16.9 us
    all_to_all x2, starting transfers between devices, gather(): return lax.all_to_all(copies, DEVICES, 0, 0, tiled=True)  8.72 us
    all_to_all x2, waiting for transfers between devices, gather(): return lax.all_to_all(copies, DEVICES, 0, 0, tiled=True)  7.78 us
    pallas_call x5, Pallas kernels, fold(): pl.pallas_call(body, in_specs=[pl.BlockSpec(memory_space=pltpu.SMEM)] + [...  5.99 us
    ppermute x4, starting transfers between devices, neighbours(): lax.ppermute(first_block, 'frames', down)  5.38 us
  transfers between devices with their start and end apart: 32, of which 11 were waited for; matrix products, arithmetic and copies ran while one was open for 1% of the time, Pallas kernels for 22%

profile of v6, /device:TPU:0, one launch (start us, length us, event | category | flops | bytes accessed | tf_op | source)
XLA Modules:
  0.0 256.2 jit_solution(15699161932429687)
XLA Ops:
  7.2 6.8 %front.1 = (f32[512,512]{1,0:T(8,128)}, bf16[512,512]{1,0:T(8,128)(2,1)}, bf16[512,512]{1,0:T(8,128)(2,1)}, bf16[2,128,1024]{2,1,0:T(8,128)(2,1)}, bf16[2,128,10...) custom-call(bf16[2,256,512]{2,1,0:T(8,128)(2,1)} %refs_1_.5, f32[6,512]{1,0:T(8,128)} %refs_0_.3, f32[6,512]{1,0:T(8,128)} %refs_4_.8, ...), custom_call_target="tpu_custom_call" | custom-call | flops 2684354560 | bytes 16777216 | tf_op jit(solution)/shard_map/front/pallas_call | solution.py:260
  14.0 1.3 collective-permute-start.1
  15.3 3.2 %collective-permute-start = (bf16[2,128,1024]{2,1,0:T(8,128)(2,1)}, bf16[2,128,1024]{2,1,0:T(8,128)(2,1)S(1)}, u32[]{:S(2)}, u32[]{:S(2)}) collective-permute-start(bf16[2,128,1024]{2,1,0:T(8,128)(2,1)} %get-tuple-element.126.refs_6_), channel_id=1, source_target_pairs={{0,1},{1,2},{2,3},{3,4},{4,5},{5,6},{6,7},{7,8},{8,9},{9,10},{10,1... | collective-permute-start | bytes 1572872 | tf_op jit(solution)/shard_map/ppermute | solution.py:1206
  20.3 6.0 %queries.1 = (bf16[512,512]{1,0:T(8,128)(2,1)}, bf16[512,512]{1,0:T(8,128)(2,1)}, bf16[384,512]{1,0:T(8,128)(2,1)}, bf16[512,2048]{1,0:T(8,128)(2,1)}) custom-call(bf16[512,512]{1,0:T(8,128)(2,1)} %get-tuple-element.120.refs_0_.refs_1_.refs_13_, bf16[512,1536]{1,0:T(8,128)(2,1)} %refs_10_.5, f32[10,512]{1,0:T(8,128)} %refs_6_.5, ...), custom_call_target="tpu_custom_call" | custom-call | flops 1610612736 | bytes 10485760 | tf_op jit(solution)/shard_map/queries/pallas_call | solution.py:260
  27.3 15.1 %attend.1 = (bf16[2,2,128,1536]{3,2,1,0:T(8,128)(2,1)}, bf16[2,2,128,1536]{3,2,1,0:T(8,128)(2,1)}, bf16[512,512]{1,0:T(8,128)(2,1)}, f32[512,512]{1,0:T(8,128)},...) custom-call(s32[9]{0:T(128)} %concatenate.6.refs_0_.info, ...), custom_call_target="tpu_custom_call" | custom-call | flops 1610612736 | bytes 16777216 | tf_op jit(solution)/shard_map/attend/pallas_call | solution.py:260
  42.4 7.4 %collective-permute-start.2 = (bf16[2,16,512]{2,1,0:T(8,128)(2,1)}, bf16[2,16,512]{2,1,0:T(8,128)(2,1)S(1)}, u32[]{:S(2)}, u32[]{:S(2)}) collective-permute-start(bf16[2,16,512]{2,1,0:T(8,128)(2,1)} %get-tuple-element.128), channel_id=1, source_target_pairs={{0,1},{1,2},{2,3},{3,4},{4,5},{5,6},{6,7},{7,8},{8,9},{9,10},{10,1... | collective-permute-start | bytes 98312 | tf_op jit(solution)/shard_map/ppermute | solution.py:1206
  49.8 1.3 collective-permute-start.3
  51.1 3.9 %collective-permute-done.3.refs_2_.refs_9_ = bf16[2,16,512]{2,1,0:T(8,128)(2,1)S(1)} collective-permute-done((bf16[2,16,512]{2,1,0:T(8,128)(2,1)}, bf16[2,16,512]{2,1,0:T(8,128)(2,1)S(1)}, u32[]{:S(2)}, u32[]{:S(2)}) %collective-permute-start.3) | collective-permute-done | bytes 32800 | tf_op jit(solution)/shard_map/ppermute | solution.py:1206
  55.6 6.0 %depth_conv.1 = (f32[512,512]{1,0:T(8,128)}, f32[32,8,128]{2,1,0:T(8,128)}) custom-call(s32[9]{0:T(128)} %concatenate.6.refs_0_.info, bf16[2,16,512]{2,1,0:T(8,128)(2,1)} %copy-done.16, bf16[2,16,512]{2,1,0:T(8,128)(2,1)} %copy-done.17, f32[8,128]{1,0:T(8,128)} %pad.4.refs_1_.refs_3_.refs_6_, f32[9,512]{1,0:T(8,128)} %refs_7_.8, ...), custom_call_target="tpu_custom_call" | custom-call | flops 7864320 | bytes 2097152 | tf_op jit(solution)/shard_map/depth_conv/pallas_call | solution.py:260
  61.6 6.1 %all-to-all-start = ((f32[32,8,128]{2,1,0:T(8,128)}), f32[32,8,128]{2,1,0:T(8,128)S(1)}, u32[]{:S(2)}, u32[]{:S(2)}) async-start(f32[32,8,128]{2,1,0:T(8,128)} %get-tuple-element.131), calls=%async_computation | async-start | bytes 262144 | tf_op jit(solution)/shard_map/all_to_all | solution.py:1210
  68.2 7.8 %all-to-all-done.refs_1_ = f32[32,8,128]{2,1,0:T(8,128)S(1)} async-done(((f32[32,8,128]{2,1,0:T(8,128)}), f32[32,8,128]{2,1,0:T(8,128)S(1)}, u32[]{:S(2)}, u32[]{:S(2)}) %all-to-all-start) | async-done | bytes 131104 | tf_op jit(solution)/shard_map/all_to_all | solution.py:1210
  76.6 12.6 %middle.1 = (bf16[512,512]{1,0:T(8,128)(2,1)}, bf16[512,2048]{1,0:T(8,128)(2,1)}, bf16[512,2048]{1,0:T(8,128)(2,1)}, bf16[512,512]{1,0:T(8,128)(2,1)}, bf16[512,...) custom-call(s32[9]{0:T(128)} %concatenate.6.refs_0_.info, ...), custom_call_target="tpu_custom_call" | custom-call | flops 4831838208 | bytes 25165824 | tf_op jit(solution)/shard_map/middle/pallas_call | solution.py:260
  89.2 2.6 %all-to-all-start.1 = ((f32[32,8,128]{2,1,0:T(8,128)}), f32[32,8,128]{2,1,0:T(8,128)S(1)}, u32[]{:S(2)}, u32[]{:S(2)}) async-start(f32[32,8,128]{2,1,0:T(8,128)} %get-tuple-element.135), calls=%async_computation.1 | async-start | bytes 262144 | tf_op jit(solution)/shard_map/all_to_all | solution.py:1210
  91.9 2.0 collective-permute-start.4
  93.9 1.3 collective-permute-start.5
  95.2 5.9 %feed_weights.1.refs_22_ = bf16[16,192,1024]{2,1,0:T(8,128)(2,1)} custom-call(bf16[512,512]{1,0:T(8,128)(2,1)} %get-tuple-element.136.refs_0_, bf16[512,2048]{1,0:T(8,128)(2,1)} %get-tuple-element.137.refs_1_, bf16[512,512]{1,0:T(8,128)(2,1)} %get-tuple-element.138.refs_2_, bf16[512,2048]{1,0:T(8,128)(2,1)} %get-tuple-element.139.refs_3_), custom_call_target="tpu_custom_call" | custom-call | flops 2147483648 | bytes 10485760 | tf_op jit(solution)/shard_map/feed_weights/pallas_call | solution.py:260
  101.9 13.8 %conv_back.1 = (bf16[16,192,1024]{2,1,0:T(8,128)(2,1)}, f32[512,512]{1,0:T(8,128)}, bf16[512,512]{1,0:T(8,128)(2,1)}, f32[16,512]{1,0:T(8,128)}) custom-call(s32[9]{0:T(128)} %concatenate.6.refs_0_.info, f32[32,8,128]{2,1,0:T(8,128)} %copy-done.11, f32[2,8,1024]{2,1,0:T(8,128)} %copy-done.20, ...), custom_call_target="tpu_custom_call", output_to_operand_aliasing={{0}: (22, {})} | custom-call | flops 1879048192 | bytes 16777216 | tf_op jit(solution)/shard_map/conv_back/pallas_call | solution.py:260
  115.7 13.2 %attend_back.1 = (bf16[256,512]{1,0:T(8,128)(2,1)}, bf16[256,512]{1,0:T(8,128)(2,1)}, bf16[2,128,1024]{2,1,0:T(8,128)(2,1)}, f32[128,1024]{1,0:T(8,128)}, f32[12...) custom-call(bf16[384,512]{1,0:T(8,128)(2,1)} %get-tuple-element.122., ...), custom_call_target="tpu_custom_call" | custom-call | flops 2818572288 | bytes 16777216 | tf_op jit(solution)/shard_map/attend_back/pallas_call | solution.py:260
  128.9 4.2 %collective-permute-start.6 = (bf16[2,128,1024]{2,1,0:T(8,128)(2,1)}, bf16[2,128,1024]{2,1,0:T(8,128)(2,1)S(1)}, u32[]{:S(2)}, u32[]{:S(2)}) collective-permute-start(bf16[2,128,1024]{2,1,0:T(8,128)(2,1)} %get-tuple-element.158), channel_id=1, source_target_pairs={{0,1},{1,2},{2,3},{3,4},{4,5},{5,6},{6,7},{7,8},{8,9},{9,10},{10,1... | collective-permute-start | bytes 1572872 | tf_op jit(solution)/shard_map/ppermute | solution.py:1206
  133.2 1.5 collective-permute-start.7
  134.7 4.3 %place_weights.1 = (bf16[8,64,512]{2,1,0:T(8,128)(2,1)}, bf16[8,64,512]{2,1,0:T(8,128)(2,1)}) custom-call(s32[9]{0:T(128)} %concatenate.6.refs_0_.info, bf16[512,512]{1,0:T(8,128)(2,1)} %get-tuple-element.120.refs_0_.refs_1_.refs_13_, bf16[256,512]{1,0:T(8,128)(2,1)} %get-tuple-element.160.refs_2_.refs_4_, ...), custom_call_target="tpu_custom_call" | custom-call | flops 536870912 | bytes 4194304 | tf_op jit(solution)/shard_map/place_weights/pallas_call | solution.py:260
  140.0 9.5 %back.1 = (bf16[8,224,512]{2,1,0:T(8,128)(2,1)}, bf16[8,224,512]{2,1,0:T(8,128)(2,1)}, bf16[512,512]{1,0:T(8,128)(2,1)}, bf16[512,512]{1,0:T(8,128)(2,1)}, f32[2...) custom-call(s32[9]{0:T(128)} %concatenate.6.refs_0_.info, bf16[2,128,1024]{2,1,0:T(8,128)(2,1)} %copy-done.12, ...), custom_call_target="tpu_custom_call" | custom-call | flops 2684354560 | bytes 18874368 | tf_op jit(solution)/shard_map/back/pallas_call | solution.py:260
  149.5 6.3 %collective-permute-start.9 = (bf16[8,224,512]{2,1,0:T(8,128)(2,1)}, bf16[8,224,512]{2,1,0:T(8,128)(2,1)S(1)}, u32[]{:S(2)}, u32[]{:S(2)}) collective-permute-start(bf16[8,224,512]{2,1,0:T(8,128)(2,1)} %get-tuple-element.184), channel_id=1, source_target_pairs={{0,1},{1,0},{2,3},{3,2},{4,5},{5,4},{6,7},{7,6},{8,9},{9,8},{10,11... | collective-permute-start | bytes 5505032 | tf_op jit(solution)/shard_map/ppermute | solution.py:1224
  155.8 8.6 %first_back.1 = (bf16[8,160,512]{2,1,0:T(8,128)(2,1)}, bf16[8,160,512]{2,1,0:T(8,128)(2,1)}, f32[4,512]{1,0:T(4,128)}, f32[512,512]{1,0:T(8,128)}) custom-call(s32[9]{0:T(128)} %concatenate.6.refs_0_.info, bf16[512,512]{1,0:T(8,128)(2,1)} %get-tuple-element.120.refs_0_.refs_1_.refs_13_, bf16[512,512]{1,0:T(8,128)(2,1)} %get-tuple-element.171.refs_2_, ...), custom_call_target="tpu_custom_call" | custom-call | flops 3221225472 | bytes 12582912 | tf_op jit(solution)/shard_map/first_back/pallas_call | solution.py:260
  165.3 2.0 fold_b.1
  167.3 1.5 collective-permute-start.11
  168.9 1.6 fold_a.1
  170.5 5.0 %collective-permute-start.10 = (bf16[4,160,512]{2,1,0:T(8,128)(2,1)}, bf16[4,160,512]{2,1,0:T(8,128)(2,1)S(1)}, u32[]{:S(2)}, u32[]{:S(2)}) collective-permute-start(bf16[4,160,512]{2,1,0:T(8,128)(2,1)} %bitcast.12), channel_id=1, source_target_pairs={{0,2},{1,3},{2,0},{3,1},{4,6},{5,7},{6,4},{7,5},{8,10},{9,11},{10,... | collective-permute-start | bytes 1966088 | tf_op jit(solution)/shard_map/ppermute | solution.py:1224
  175.7 2.4 last.1
  180.3 16.2 %collective-permute-done.14.refs_7_ = f32[37,512]{1,0:T(8,128)S(1)} collective-permute-done((f32[37,512]{1,0:T(8,128)S(1)}, f32[37,512]{1,0:T(8,128)S(1)}, u32[]{:S(2)}, u32[]{:S(2)}) %collective-permute-start.14) | collective-permute-done | bytes 75808 | tf_op jit(solution)/shard_map/ppermute | solution.py:1224
  196.5 1.6 collective-permute-done.13.refs_6_
  199.1 1.8 collective-permute-start.18
  200.9 1.5 collective-permute-start.15
  202.4 2.3 collective-permute-start.16
  205.9 3.8 %collective-permute-done.19.refs_7_ = f32[37,512]{1,0:T(8,128)S(1)} collective-permute-done((f32[37,512]{1,0:T(8,128)S(1)}, f32[37,512]{1,0:T(8,128)S(1)}, u32[]{:S(2)}, u32[]{:S(2)}) %collective-permute-start.19) | collective-permute-done | bytes 75808 | tf_op jit(solution)/shard_map/ppermute | solution.py:1494
  209.7 4.4 %collective-permute-done.15.refs_2_ = bf16[1,160,512]{2,1,0:T(8,128)(2,1)S(1)} collective-permute-done((bf16[1,160,512]{2,1,0:T(8,128)(2,1)S(1)}, bf16[1,160,512]{2,1,0:T(8,128)(2,1)S(1)}, u32[]{:S(2)}, u32[]{:S(2)}) %collective-permute-start.15) | collective-permute-done | bytes 163872 | tf_op jit(solution)/shard_map/ppermute | solution.py:1224
  214.1 5.2 %collective-permute-done.17.refs_4_ = bf16[1,160,512]{2,1,0:T(8,128)(2,1)S(1)} collective-permute-done((bf16[1,160,512]{2,1,0:T(8,128)(2,1)S(1)}, bf16[1,160,512]{2,1,0:T(8,128)(2,1)S(1)}, u32[]{:S(2)}, u32[]{:S(2)}) %collective-permute-start.17) | collective-permute-done | bytes 163872 | tf_op jit(solution)/shard_map/ppermute | solution.py:1224
  220.1 1.2 collective-permute-start.24
  222.2 3.3 %collective-permute-start.20 = (bf16[1,224,256]{2,1,0:T(8,128)(2,1)S(1)}, bf16[1,224,256]{2,1,0:T(8,128)(2,1)S(1)}, u32[]{:S(2)}, u32[]{:S(2)}) collective-permute-start(bf16[1,224,256]{2,1,0:T(8,128)(2,1)S(1)} %bitcast.51), channel_id=1, source_target_pairs={{0,4},{1,5},{2,6},{3,7},{4,0},{5,1},{6,2},{7,3},{8,12},{9,13},{10,... | collective-permute-start | bytes 344072 | tf_op jit(solution)/shard_map/ppermute | solution.py:1224
  225.5 2.4 collective-permute-start.22
  227.8 1.2 collective-permute-done.20.refs_3_
  229.1 6.8 %collective-permute-done.21.refs_4_ = bf16[1,224,256]{2,1,0:T(8,128)(2,1)S(1)} collective-permute-done((bf16[1,224,256]{2,1,0:T(8,128)(2,1)S(1)}, bf16[1,224,256]{2,1,0:T(8,128)(2,1)S(1)}, u32[]{:S(2)}, u32[]{:S(2)}) %collective-permute-start.21) | collective-permute-done | bytes 114720 | tf_op jit(solution)/shard_map/ppermute | solution.py:1224
  238.6 1.5 collective-permute-start.28
  240.0 1.8 collective-permute-start.27
  241.8 1.1 collective-permute-start.26
  243.0 2.0 collective-permute-done.28.refs_3_
  244.9 2.2 collective-permute-done.27.refs_2_
  247.2 1.9 finish.1
  (111 shorter events, 15.5 us)
Async XLA Ops:
  7.2 11.5 %copy-start.26 = (s32[4,17]{1,0:T(4,128)S(1)}, s32[4,17]{1,0:T(4,128)}, u32[]{:S(2)}) copy-start(s32[4,17]{1,0:T(4,128)} %param.18) | copy-start | bytes 820
  7.2 12.5 %copy-start.27 = (s32[2]{0:T(128)S(1)}, s32[2]{0:T(128)}, u32[]{:S(2)}) copy-start(s32[2]{0:T(128)} %param.19) | copy-start | bytes 28
  14.0 12.3 %collective-permute-start.1 = (bf16[2,128,1024]{2,1,0:T(8,128)(2,1)}, bf16[2,128,1024]{2,1,0:T(8,128)(2,1)S(1)}, u32[]{:S(2)}, u32[]{:S(2)}) collective-permute-start(bf16[2,128,1024]{2,1,0:T(8,128)(2,1)} %get-tuple-element.125.refs_5_), channel_id=1, source_target_pairs={{1,0},{2,1},{3,2},{4,3},{5,4},{6,5},{7,6},{8,7},{9,8},{10,9},{11,1... | collective-permute-start | bytes 1572872 | tf_op jit(solution)/shard_map/ppermute | solution.py:1206
  15.3 11.0 %collective-permute-start = (bf16[2,128,1024]{2,1,0:T(8,128)(2,1)}, bf16[2,128,1024]{2,1,0:T(8,128)(2,1)S(1)}, u32[]{:S(2)}, u32[]{:S(2)}) collective-permute-start(bf16[2,128,1024]{2,1,0:T(8,128)(2,1)} %get-tuple-element.126.refs_6_), channel_id=1, source_target_pairs={{0,1},{1,2},{2,3},{3,4},{4,5},{5,6},{6,7},{7,8},{8,9},{9,10},{10,1... | collective-permute-start | bytes 1572872 | tf_op jit(solution)/shard_map/ppermute | solution.py:1206
  42.4 8.7 %collective-permute-start.2 = (bf16[2,16,512]{2,1,0:T(8,128)(2,1)}, bf16[2,16,512]{2,1,0:T(8,128)(2,1)S(1)}, u32[]{:S(2)}, u32[]{:S(2)}) collective-permute-start(bf16[2,16,512]{2,1,0:T(8,128)(2,1)} %get-tuple-element.128), channel_id=1, source_target_pairs={{0,1},{1,2},{2,3},{3,4},{4,5},{5,6},{6,7},{7,8},{8,9},{9,10},{10,1... | collective-permute-start | bytes 98312 | tf_op jit(solution)/shard_map/ppermute | solution.py:1206
  49.8 5.2 %collective-permute-start.3 = (bf16[2,16,512]{2,1,0:T(8,128)(2,1)}, bf16[2,16,512]{2,1,0:T(8,128)(2,1)S(1)}, u32[]{:S(2)}, u32[]{:S(2)}) collective-permute-start(bf16[2,16,512]{2,1,0:T(8,128)(2,1)} %get-tuple-element.129), channel_id=1, source_target_pairs={{1,0},{2,1},{3,2},{4,3},{5,4},{6,5},{7,6},{8,7},{9,8},{10,9},{11,1... | collective-permute-start | bytes 98312 | tf_op jit(solution)/shard_map/ppermute | solution.py:1206
  51.1 3.9 %copy-start.16 = (bf16[2,16,512]{2,1,0:T(8,128)(2,1)}, bf16[2,16,512]{2,1,0:T(8,128)(2,1)S(1)}, u32[]{:S(2)}) copy-start(bf16[2,16,512]{2,1,0:T(8,128)(2,1)S(1)} %collective-permute-done.2.refs_1_.refs_8_) | copy-start | bytes 98308
  61.6 14.4 %all-to-all-start = ((f32[32,8,128]{2,1,0:T(8,128)}), f32[32,8,128]{2,1,0:T(8,128)S(1)}, u32[]{:S(2)}, u32[]{:S(2)}) async-start(f32[32,8,128]{2,1,0:T(8,128)} %get-tuple-element.131), calls=%async_computation | async-start | bytes 262144 | tf_op jit(solution)/shard_map/all_to_all | solution.py:1210
  89.2 11.9 %all-to-all-start.1 = ((f32[32,8,128]{2,1,0:T(8,128)}), f32[32,8,128]{2,1,0:T(8,128)S(1)}, u32[]{:S(2)}, u32[]{:S(2)}) async-start(f32[32,8,128]{2,1,0:T(8,128)} %get-tuple-element.135), calls=%async_computation.1 | async-start | bytes 262144 | tf_op jit(solution)/shard_map/all_to_all | solution.py:1210
  91.8 128.2 %reduce-scatter.2.cloned.1.call-start = ((), (), s32[]{:S(2)}) async-start(), calls=%async_computation.3 | async-start | bytes 6684672 | tf_op jit(solution)/shard_map/reduce_scatter | solution.py:1214
  91.9 9.3 %collective-permute-start.4 = (f32[2,8,1024]{2,1,0:T(8,128)}, f32[2,8,1024]{2,1,0:T(8,128)S(1)}, u32[]{:S(2)}, u32[]{:S(2)}) collective-permute-start(f32[2,8,1024]{2,1,0:T(8,128)} %get-tuple-element.141), channel_id=1, source_target_pairs={{0,1},{1,2},{2,3},{3,4},{4,5},{5,6},{6,7},{7,8},{8,9},{9,10},{10,1... | collective-permute-start | bytes 196616 | tf_op jit(solution)/shard_map/ppermute | solution.py:1206
  93.9 7.3 %collective-permute-start.5 = (f32[2,8,1024]{2,1,0:T(8,128)}, f32[2,8,1024]{2,1,0:T(8,128)S(1)}, u32[]{:S(2)}, u32[]{:S(2)}) collective-permute-start(f32[2,8,1024]{2,1,0:T(8,128)} %get-tuple-element.142), channel_id=1, source_target_pairs={{1,0},{2,1},{3,2},{4,3},{5,4},{6,5},{7,6},{8,7},{9,8},{10,9},{11,1... | collective-permute-start | bytes 196616 | tf_op jit(solution)/shard_map/ppermute | solution.py:1206
  128.9 10.0 %collective-permute-start.6 = (bf16[2,128,1024]{2,1,0:T(8,128)(2,1)}, bf16[2,128,1024]{2,1,0:T(8,128)(2,1)S(1)}, u32[]{:S(2)}, u32[]{:S(2)}) collective-permute-start(bf16[2,128,1024]{2,1,0:T(8,128)(2,1)} %get-tuple-element.158), channel_id=1, source_target_pairs={{0,1},{1,2},{2,3},{3,4},{4,5},{5,6},{6,7},{7,8},{8,9},{9,10},{10,1... | collective-permute-start | bytes 1572872 | tf_op jit(solution)/shard_map/ppermute | solution.py:1206
  133.2 5.8 %collective-permute-start.7 = (bf16[2,128,1024]{2,1,0:T(8,128)(2,1)}, bf16[2,128,1024]{2,1,0:T(8,128)(2,1)S(1)}, u32[]{:S(2)}, u32[]{:S(2)}) collective-permute-start(bf16[2,128,1024]{2,1,0:T(8,128)(2,1)} %get-tuple-element.159), channel_id=1, source_target_pairs={{1,0},{2,1},{3,2},{4,3},{5,4},{6,5},{7,6},{8,7},{9,8},{10,9},{11,1... | collective-permute-start | bytes 1572872 | tf_op jit(solution)/shard_map/ppermute | solution.py:1206
  149.5 15.8 %collective-permute-start.9 = (bf16[8,224,512]{2,1,0:T(8,128)(2,1)}, bf16[8,224,512]{2,1,0:T(8,128)(2,1)S(1)}, u32[]{:S(2)}, u32[]{:S(2)}) collective-permute-start(bf16[8,224,512]{2,1,0:T(8,128)(2,1)} %get-tuple-element.184), channel_id=1, source_target_pairs={{0,1},{1,0},{2,3},{3,2},{4,5},{5,4},{6,7},{7,6},{8,9},{9,8},{10,11... | collective-permute-start | bytes 5505032 | tf_op jit(solution)/shard_map/ppermute | solution.py:1224
  155.8 8.7 %copy-start.22 = (f32[8,512]{1,0:T(8,128)S(1)}, f32[8,512]{1,0:T(8,128)}, u32[]{:S(2)}) copy-start(f32[8,512]{1,0:T(8,128)} %get-tuple-element.191) | copy-start | bytes 49156
  155.8 9.4 %copy-start.1 = (bf16[8,224,512]{2,1,0:T(8,128)(2,1)S(1)}, bf16[8,224,512]{2,1,0:T(8,128)(2,1)}, u32[]{:S(2)}) copy-start(bf16[8,224,512]{2,1,0:T(8,128)(2,1)} %get-tuple-element.183.refs_0_) | copy-start | bytes 5505028
  155.8 9.4 %copy-start.10 = (s32[9]{0:T(128)S(1)}, s32[9]{0:T(128)}, u32[]{:S(2)}) copy-start(s32[9]{0:T(128)} %concatenate.6.refs_0_.info) | copy-start | bytes 112
  164.4 4.5 %collective-permute-start.8 = (bf16[8,160,512]{2,1,0:T(8,128)(2,1)}, bf16[8,160,512]{2,1,0:T(8,128)(2,1)S(1)}, u32[]{:S(2)}, u32[]{:S(2)}) collective-permute-start(bf16[8,160,512]{2,1,0:T(8,128)(2,1)} %get-tuple-element.176), channel_id=1, source_target_pairs={{0,1},{1,0},{2,3},{3,2},{4,5},{5,4},{6,7},{7,6},{8,9},{9,8},{10,11... | collective-permute-start | bytes 3932168 | tf_op jit(solution)/shard_map/ppermute | solution.py:1224
  165.3 3.6 %copy-start.2 = (bf16[8,160,512]{2,1,0:T(8,128)(2,1)S(1)}, bf16[8,160,512]{2,1,0:T(8,128)(2,1)}, u32[]{:S(2)}) copy-start(bf16[8,160,512]{2,1,0:T(8,128)(2,1)} %get-tuple-element.175) | copy-start | bytes 3932164
  167.3 8.3 %copy-start.25 = (f32[8,512]{1,0:T(8,128)S(1)}, f32[8,512]{1,0:T(8,128)}, u32[]{:S(2)}) copy-start(f32[8,512]{1,0:T(8,128)} %get-tuple-element.190) | copy-start | bytes 49156
  167.3 8.3 %copy-start = (bf16[2,256,512]{2,1,0:T(8,128)(2,1)S(1)}, bf16[2,256,512]{2,1,0:T(8,128)(2,1)}, u32[]{:S(2)}) copy-start(bf16[2,256,512]{2,1,0:T(8,128)(2,1)} %refs_1_.5) | copy-start | bytes 1572868
  167.3 8.4 %copy-start.3 = (f32[512,512]{1,0:T(8,128)S(1)}, f32[512,512]{1,0:T(8,128)}, u32[]{:S(2)}) copy-start(f32[512,512]{1,0:T(8,128)} %get-tuple-element.178.refs_2_) | copy-start | bytes 3145732
  167.3 8.4 %copy-start.6 = (f32[256,512]{1,0:T(8,128)S(1)}, f32[256,512]{1,0:T(8,128)}, u32[]{:S(2)}) copy-start(f32[256,512]{1,0:T(8,128)} %get-tuple-element.179.refs_3_) | copy-start | bytes 1572868
  167.3 8.4 %copy-start.7 = (f32[256,512]{1,0:T(8,128)S(1)}, f32[256,512]{1,0:T(8,128)}, u32[]{:S(2)}) copy-start(f32[256,512]{1,0:T(8,128)} %get-tuple-element.180.refs_4_) | copy-start | bytes 1572868
  167.3 8.4 %copy-start.8 = (f32[6,512]{1,0:T(8,128)S(1)}, f32[6,512]{1,0:T(8,128)}, u32[]{:S(2)}) copy-start(f32[6,512]{1,0:T(8,128)} %refs_0_.3) | copy-start | bytes 36868
  167.3 30.9 %collective-permute-start.11 = (bf16[8,224,256]{2,1,0:T(8,128)(2,1)}, bf16[8,224,256]{2,1,0:T(8,128)(2,1)S(1)}, u32[]{:S(2)}, u32[]{:S(2)}) collective-permute-start(bf16[8,224,256]{2,1,0:T(8,128)(2,1)} %get-tuple-element.187), channel_id=1, source_target_pairs={{0,16},{16,0},{1,17},{17,1},{2,18},{18,2},{3,19},{19,3},{4,20},{20... | collective-permute-start | bytes 2752520 | tf_op jit(solution)/shard_map/ppermute | solution.py:1461
  170.5 7.6 %copy-start.23 = (f32[4,512]{1,0:T(4,128)S(1)}, f32[4,512]{1,0:T(4,128)}, u32[]{:S(2)}) copy-start(f32[4,512]{1,0:T(4,128)} %get-tuple-element.194) | copy-start | bytes 24580
  170.5 7.6 %copy-start.24 = (f32[4,512]{1,0:T(4,128)S(1)}, f32[4,512]{1,0:T(4,128)}, u32[]{:S(2)}) copy-start(f32[4,512]{1,0:T(4,128)} %get-tuple-element.193) | copy-start | bytes 24580
  170.5 27.6 %copy-start.5 = (bf16[8,224,256]{2,1,0:T(8,128)(2,1)S(1)}, bf16[8,224,256]{2,1,0:T(8,128)(2,1)}, u32[]{:S(2)}) copy-start(bf16[8,224,256]{2,1,0:T(8,128)(2,1)} %copy-done.4) | copy-start | bytes 2752516
  170.5 27.6 %collective-permute-start.10 = (bf16[4,160,512]{2,1,0:T(8,128)(2,1)}, bf16[4,160,512]{2,1,0:T(8,128)(2,1)S(1)}, u32[]{:S(2)}, u32[]{:S(2)}) collective-permute-start(bf16[4,160,512]{2,1,0:T(8,128)(2,1)} %bitcast.12), channel_id=1, source_target_pairs={{0,2},{1,3},{2,0},{3,1},{4,6},{5,7},{6,4},{7,5},{8,10},{9,11},{10,... | collective-permute-start | bytes 1966088 | tf_op jit(solution)/shard_map/ppermute | solution.py:1224
  178.4 18.2 %collective-permute-start.14 = (f32[37,512]{1,0:T(8,128)S(1)}, f32[37,512]{1,0:T(8,128)S(1)}, u32[]{:S(2)}, u32[]{:S(2)}) collective-permute-start(f32[37,512]{1,0:T(8,128)S(1)} %concatenate.7.refs_4_), channel_id=1, source_target_pairs={{0,3},{1,2},{2,1},{3,0},{4,7},{5,6},{6,5},{7,4},{8,11},{9,10},{10,... | collective-permute-start | bytes 227336 | tf_op jit(solution)/shard_map/ppermute | solution.py:1224
  178.4 19.7 %collective-permute-start.13 = (f32[37,512]{1,0:T(8,128)S(1)}, f32[37,512]{1,0:T(8,128)S(1)}, u32[]{:S(2)}, u32[]{:S(2)}) collective-permute-start(f32[37,512]{1,0:T(8,128)S(1)} %concatenate.7.refs_4_), channel_id=1, source_target_pairs={{0,2},{1,3},{2,0},{3,1},{4,6},{5,7},{6,4},{7,5},{8,10},{9,11},{10,... | collective-permute-start | bytes 227336 | tf_op jit(solution)/shard_map/ppermute | solution.py:1224
  179.5 18.6 %collective-permute-start.12 = (f32[37,512]{1,0:T(8,128)S(1)}, f32[37,512]{1,0:T(8,128)S(1)}, u32[]{:S(2)}, u32[]{:S(2)}) collective-permute-start(f32[37,512]{1,0:T(8,128)S(1)} %concatenate.7.refs_4_), channel_id=1, source_target_pairs={{0,1},{1,0},{2,3},{3,2},{4,5},{5,4},{6,7},{7,6},{8,9},{9,8},{10,11... | collective-permute-start | bytes 227336 | tf_op jit(solution)/shard_map/ppermute | solution.py:1224
  199.1 20.2 %collective-permute-start.18 = (bf16[4,224,256]{2,1,0:T(8,128)(2,1)S(1)}, bf16[4,224,256]{2,1,0:T(8,128)(2,1)S(1)}, u32[]{:S(2)}, u32[]{:S(2)}) collective-permute-start(bf16[4,224,256]{2,1,0:T(8,128)(2,1)S(1)} %bitcast.45), channel_id=1, source_target_pairs={{0,2},{1,3},{2,0},{3,1},{4,6},{5,7},{6,4},{7,5},{8,10},{9,11},{10,... | collective-permute-start | bytes 1376264 | tf_op jit(solution)/shard_map/ppermute | solution.py:1224
  200.9 13.2 %collective-permute-start.15 = (bf16[1,160,512]{2,1,0:T(8,128)(2,1)S(1)}, bf16[1,160,512]{2,1,0:T(8,128)(2,1)S(1)}, u32[]{:S(2)}, u32[]{:S(2)}) collective-permute-start(bf16[1,160,512]{2,1,0:T(8,128)(2,1)S(1)} %bitcast.48), channel_id=1, source_target_pairs={{0,4},{1,5},{2,6},{3,7},{4,0},{5,1},{6,2},{7,3},{8,12},{9,13},{10,... | collective-permute-start | bytes 491528 | tf_op jit(solution)/shard_map/ppermute | solution.py:1224
  202.4 11.7 %collective-permute-start.16 = (bf16[1,160,512]{2,1,0:T(8,128)(2,1)S(1)}, bf16[1,160,512]{2,1,0:T(8,128)(2,1)S(1)}, u32[]{:S(2)}, u32[]{:S(2)}) collective-permute-start(bf16[1,160,512]{2,1,0:T(8,128)(2,1)S(1)} %bitcast.47), channel_id=1, source_target_pairs={{0,8},{1,9},{2,10},{3,11},{4,12},{5,13},{6,14},{7,15},{8,0},{9,1},... | collective-permute-start | bytes 491528 | tf_op jit(solution)/shard_map/ppermute | solution.py:1224
  204.7 14.6 %collective-permute-start.17 = (bf16[1,160,512]{2,1,0:T(8,128)(2,1)S(1)}, bf16[1,160,512]{2,1,0:T(8,128)(2,1)S(1)}, u32[]{:S(2)}, u32[]{:S(2)}) collective-permute-start(bf16[1,160,512]{2,1,0:T(8,128)(2,1)S(1)} %bitcast.46), channel_id=1, source_target_pairs={{0,12},{1,13},{2,14},{3,15},{4,8},{5,9},{6,10},{7,11},{8,4},{9,5},... | collective-permute-start | bytes 491528 | tf_op jit(solution)/shard_map/ppermute | solution.py:1224
  205.3 4.4 %collective-permute-start.19 = (f32[37,512]{1,0:T(8,128)S(1)}, f32[37,512]{1,0:T(8,128)S(1)}, u32[]{:S(2)}, u32[]{:S(2)}) collective-permute-start(f32[37,512]{1,0:T(8,128)S(1)} %get-tuple-element.201.refs_6_), channel_id=1, source_target_pairs={{0,16},{16,0},{1,17},{17,1},{2,18},{18,2},{3,19},{19,3},{4,20},{20... | collective-permute-start | bytes 227336 | tf_op jit(solution)/shard_map/ppermute | solution.py:1494
  220.1 15.9 %collective-permute-start.24 = (bf16[1,192,1024]{2,1,0:T(8,128)(2,1)}, bf16[1,192,1024]{2,1,0:T(8,128)(2,1)S(1)}, u32[]{:S(2)}, u32[]{:S(2)}) collective-permute-start(bf16[1,192,1024]{2,1,0:T(8,128)(2,1)} %reduce-scatter.2.cloned.1.call-done.refs_2_), channel_id=1, source_target_pairs={{0,16},{16,0},{1,17},{17,1},{2,18},{18,2},{3,19},{19,3},{4,20},{20... | collective-permute-start | bytes 1179656 | tf_op jit(solution)/shard_map/ppermute | solution.py:1491
  221.2 14.7 %collective-permute-start.23 = (bf16[1,160,512]{2,1,0:T(8,128)(2,1)S(1)}, bf16[1,160,512]{2,1,0:T(8,128)(2,1)S(1)}, u32[]{:S(2)}, u32[]{:S(2)}) collective-permute-start(bf16[1,160,512]{2,1,0:T(8,128)(2,1)S(1)} %get-tuple-element.205.refs_1_), channel_id=1, source_target_pairs={{0,16},{16,0},{1,17},{17,1},{2,18},{18,2},{3,19},{19,3},{4,20},{20... | collective-permute-start | bytes 491528 | tf_op jit(solution)/shard_map/ppermute | solution.py:1490
  222.2 6.9 %collective-permute-start.20 = (bf16[1,224,256]{2,1,0:T(8,128)(2,1)S(1)}, bf16[1,224,256]{2,1,0:T(8,128)(2,1)S(1)}, u32[]{:S(2)}, u32[]{:S(2)}) collective-permute-start(bf16[1,224,256]{2,1,0:T(8,128)(2,1)S(1)} %bitcast.51), channel_id=1, source_target_pairs={{0,4},{1,5},{2,6},{3,7},{4,0},{5,1},{6,2},{7,3},{8,12},{9,13},{10,... | collective-permute-start | bytes 344072 | tf_op jit(solution)/shard_map/ppermute | solution.py:1224
  225.5 10.4 %collective-permute-start.21 = (bf16[1,224,256]{2,1,0:T(8,128)(2,1)S(1)}, bf16[1,224,256]{2,1,0:T(8,128)(2,1)S(1)}, u32[]{:S(2)}, u32[]{:S(2)}) collective-permute-start(bf16[1,224,256]{2,1,0:T(8,128)(2,1)S(1)} %bitcast.50), channel_id=1, source_target_pairs={{0,8},{1,9},{2,10},{3,11},{4,12},{5,13},{6,14},{7,15},{8,0},{9,1},... | collective-permute-start | bytes 344072 | tf_op jit(solution)/shard_map/ppermute | solution.py:1224
  225.5 10.4 %collective-permute-start.22 = (bf16[1,224,256]{2,1,0:T(8,128)(2,1)S(1)}, bf16[1,224,256]{2,1,0:T(8,128)(2,1)S(1)}, u32[]{:S(2)}, u32[]{:S(2)}) collective-permute-start(bf16[1,224,256]{2,1,0:T(8,128)(2,1)S(1)} %bitcast.49), channel_id=1, source_target_pairs={{0,12},{1,13},{2,14},{3,15},{4,8},{5,9},{6,10},{7,11},{8,4},{9,5},... | collective-permute-start | bytes 344072 | tf_op jit(solution)/shard_map/ppermute | solution.py:1224
  237.7 9.5 %collective-permute-start.25 = (bf16[1,224,256]{2,1,0:T(8,128)(2,1)S(1)}, bf16[1,224,256]{2,1,0:T(8,128)(2,1)S(1)}, u32[]{:S(2)}, u32[]{:S(2)}) collective-permute-start(bf16[1,224,256]{2,1,0:T(8,128)(2,1)S(1)} %get-tuple-element.211), channel_id=1, source_target_pairs={{0,16},{16,0},{1,17},{17,1},{2,18},{18,2},{3,19},{19,3},{4,20},{20... | collective-permute-start | bytes 344072 | tf_op jit(solution)/shard_map/ppermute | solution.py:1499
  238.6 6.3 %collective-permute-start.28 = (f32[37,512]{1,0:T(8,128)S(1)}, f32[37,512]{1,0:T(8,128)S(1)}, u32[]{:S(2)}, u32[]{:S(2)}) collective-permute-start(f32[37,512]{1,0:T(8,128)S(1)} %get-tuple-element.213.refs_0_), channel_id=1, source_target_pairs={{0,12},{1,13},{2,14},{3,15},{4,8},{5,9},{6,10},{7,11},{8,4},{9,5},... | collective-permute-start | bytes 227336 | tf_op jit(solution)/shard_map/ppermute | solution.py:1224
  240.0 7.1 %collective-permute-start.27 = (f32[37,512]{1,0:T(8,128)S(1)}, f32[37,512]{1,0:T(8,128)S(1)}, u32[]{:S(2)}, u32[]{:S(2)}) collective-permute-start(f32[37,512]{1,0:T(8,128)S(1)} %get-tuple-element.213.refs_0_), channel_id=1, source_target_pairs={{0,8},{1,9},{2,10},{3,11},{4,12},{5,13},{6,14},{7,15},{8,0},{9,1},... | collective-permute-start | bytes 227336 | tf_op jit(solution)/shard_map/ppermute | solution.py:1224
  241.8 5.3 %collective-permute-start.26 = (f32[37,512]{1,0:T(8,128)S(1)}, f32[37,512]{1,0:T(8,128)S(1)}, u32[]{:S(2)}, u32[]{:S(2)}) collective-permute-start(f32[37,512]{1,0:T(8,128)S(1)} %get-tuple-element.213.refs_0_), channel_id=1, source_target_pairs={{0,4},{1,5},{2,6},{3,7},{4,0},{5,1},{6,2},{7,3},{8,12},{9,13},{10,... | collective-permute-start | bytes 227336 | tf_op jit(solution)/shard_map/ppermute | solution.py:1224
  (12 other events, 14.6 us)
Sparse Core Ops, SparseCore 0:
  115.8 97.5 reduce-scatter.1

commit v7 on v6

--- a/solution.py
+++ b/solution.py
@@ -442,7 +442,7 @@
                 allowed = ((key_at >= lower) & (key_at <= upper))[None]
                 here = slice(row * frames + WIN * block, row * frames + WIN * (block + 1))
                 some = [k.lo[row], k.hi[row]]
-                some = some + [k.next[row]] if block else [k.before[row]] + some
+                some = some + [k.next.at[row]] if block else [k.before.at[row]] + some
                 for group in range(GROUPS):
                     cut = slice(WIDE * group, WIDE * (group + 1))
                     cut_v = slice(model + WIDE * group, model + WIDE * (group + 1))
@@ -492,8 +492,7 @@
         body,
         dict(
             ends=ends, table=query.table, qv=query.qv, qu=query.qu, lo=each_of(start.lo),
-            hi=each_of(start.hi), before=each_of(before), next=each_of(after), after=start.after,
-            attend_out=attend_out, bias=bias, gain=gain, shift=shift, convolve_in=convolve_in,
+            hi=each_of(start.hi), after=start.after, attend_out=attend_out, bias=bias, gain=gain, shift=shift, convolve_in=convolve_in,
         ),
         dict(
             prob=[sds((2, GROUPS, WIN, MANY * SPAN), bf16)] * rows, mixed=low,
@@ -501,6 +500,7 @@
             gated=low, first=rim, last=rim,
         ),
         smem=[info],
+        kept=dict(before=before, next=after),
         flops=16 * 8 * 256 * 384 * 128,
         moved=16 << 20,
     )

time: 260 us -> 260 us (level)
  no operation moved by 1% of the time
where the time goes in v7:
time: 260 us; the launch traced here: 255 us
  Pallas kernels  112 us (43%)
  starting transfers between devices  65.1 us (25%)
  waiting for transfers between devices  55.2 us (21%)
  between operations  14.9 us (6%)
  local copies, waits for them, and re-layouts  7.63 us (3%)
    pallas_call x12, Pallas kernels, staged(): pl.pallas_call(run, in_specs=[pl.BlockSpec(memory_space=pltpu.SMEM)] * n_...  104 us
    ppermute x16, waiting for transfers between devices, swap(): return lax.ppermute(x, 'frames', [(i, i ^ k) for i in range(n)])  39.7 us
    ppermute x16, starting transfers between devices, swap(): return lax.ppermute(x, 'frames', [(i, i ^ k) for i in range(n)])  29.7 us
    ppermute x4, starting transfers between devices, neighbours(): lax.ppermute(last_block, 'frames', up)  16 us
    all_to_all x2, starting transfers between devices, gather(): return lax.all_to_all(copies, DEVICES, 0, 0, tiled=True)  8.72 us
    all_to_all x2, waiting for transfers between devices, gather(): return lax.all_to_all(copies, DEVICES, 0, 0, tiled=True)  7.78 us
    pallas_call x5, Pallas kernels, fold(): pl.pallas_call(body, in_specs=[pl.BlockSpec(memory_space=pltpu.SMEM)] + [...  5.99 us
    ppermute x4, starting transfers between devices, neighbours(): lax.ppermute(first_block, 'frames', down)  5.56 us
  transfers between devices with their start and end apart: 32, of which 11 were waited for; matrix products, arithmetic and copies ran while one was open for 1% of the time, Pallas kernels for 22%

profile of v7, /device:TPU:0, one launch (start us, length us, event | category | flops | bytes accessed | tf_op | source)
XLA Modules:
  0.0 255.5 jit_solution(2335707082190775052)
XLA Ops:
  7.2 6.8 %front.1 = (f32[512,512]{1,0:T(8,128)}, bf16[512,512]{1,0:T(8,128)(2,1)}, bf16[512,512]{1,0:T(8,128)(2,1)}, bf16[2,128,1024]{2,1,0:T(8,128)(2,1)}, bf16[2,128,10...) custom-call(bf16[2,256,512]{2,1,0:T(8,128)(2,1)} %refs_1_.5, f32[6,512]{1,0:T(8,128)} %refs_0_.3, f32[6,512]{1,0:T(8,128)} %refs_4_.8, ...), custom_call_target="tpu_custom_call" | custom-call | flops 2684354560 | bytes 16777216 | tf_op jit(solution)/shard_map/front/pallas_call | solution.py:260
  14.0 2.4 collective-permute-start
  16.4 1.5 collective-permute-start.1
  19.6 6.0 %queries.1 = (bf16[512,512]{1,0:T(8,128)(2,1)}, bf16[512,512]{1,0:T(8,128)(2,1)}, bf16[384,512]{1,0:T(8,128)(2,1)}, bf16[512,2048]{1,0:T(8,128)(2,1)}) custom-call(bf16[512,512]{1,0:T(8,128)(2,1)} %get-tuple-element.122.refs_0_.refs_1_.refs_13_, bf16[512,1536]{1,0:T(8,128)(2,1)} %refs_10_.5, f32[10,512]{1,0:T(8,128)} %refs_6_.5, ...), custom_call_target="tpu_custom_call" | custom-call | flops 1610612736 | bytes 10485760 | tf_op jit(solution)/shard_map/queries/pallas_call | solution.py:260
  26.6 15.1 %attend.1 = (bf16[2,2,128,1536]{3,2,1,0:T(8,128)(2,1)}, bf16[2,2,128,1536]{3,2,1,0:T(8,128)(2,1)}, bf16[512,512]{1,0:T(8,128)(2,1)}, f32[512,512]{1,0:T(8,128)},...) custom-call(s32[9]{0:T(128)} %concatenate.6.refs_0_.info, ...), custom_call_target="tpu_custom_call" | custom-call | flops 1610612736 | bytes 16777216 | tf_op jit(solution)/shard_map/attend/pallas_call | solution.py:260
  41.8 7.3 %collective-permute-start.2 = (bf16[2,16,512]{2,1,0:T(8,128)(2,1)}, bf16[2,16,512]{2,1,0:T(8,128)(2,1)S(1)}, u32[]{:S(2)}, u32[]{:S(2)}) collective-permute-start(bf16[2,16,512]{2,1,0:T(8,128)(2,1)} %get-tuple-element.128), channel_id=1, source_target_pairs={{0,1},{1,2},{2,3},{3,4},{4,5},{5,6},{6,7},{7,8},{8,9},{9,10},{10,1... | collective-permute-start | bytes 98312 | tf_op jit(solution)/shard_map/ppermute | solution.py:1206
  49.1 1.3 collective-permute-start.3
  50.4 3.9 %collective-permute-done.3.refs_2_.refs_9_ = bf16[2,16,512]{2,1,0:T(8,128)(2,1)S(1)} collective-permute-done((bf16[2,16,512]{2,1,0:T(8,128)(2,1)}, bf16[2,16,512]{2,1,0:T(8,128)(2,1)S(1)}, u32[]{:S(2)}, u32[]{:S(2)}) %collective-permute-start.3) | collective-permute-done | bytes 32800 | tf_op jit(solution)/shard_map/ppermute | solution.py:1206
  54.9 6.0 %depth_conv.1 = (f32[512,512]{1,0:T(8,128)}, f32[32,8,128]{2,1,0:T(8,128)}) custom-call(s32[9]{0:T(128)} %concatenate.6.refs_0_.info, bf16[2,16,512]{2,1,0:T(8,128)(2,1)} %copy-done.16, bf16[2,16,512]{2,1,0:T(8,128)(2,1)} %copy-done.17, f32[8,128]{1,0:T(8,128)} %pad.4.refs_3_.refs_6_, f32[9,512]{1,0:T(8,128)} %refs_7_.8, ...), custom_call_target="tpu_custom_call" | custom-call | flops 7864320 | bytes 2097152 | tf_op jit(solution)/shard_map/depth_conv/pallas_call | solution.py:260
  60.9 6.1 %all-to-all-start = ((f32[32,8,128]{2,1,0:T(8,128)}), f32[32,8,128]{2,1,0:T(8,128)S(1)}, u32[]{:S(2)}, u32[]{:S(2)}) async-start(f32[32,8,128]{2,1,0:T(8,128)} %get-tuple-element.131), calls=%async_computation | async-start | bytes 262144 | tf_op jit(solution)/shard_map/all_to_all | solution.py:1210
  67.4 7.8 %all-to-all-done.refs_1_ = f32[32,8,128]{2,1,0:T(8,128)S(1)} async-done(((f32[32,8,128]{2,1,0:T(8,128)}), f32[32,8,128]{2,1,0:T(8,128)S(1)}, u32[]{:S(2)}, u32[]{:S(2)}) %all-to-all-start) | async-done | bytes 131104 | tf_op jit(solution)/shard_map/all_to_all | solution.py:1210
  75.9 12.6 %middle.1 = (bf16[512,512]{1,0:T(8,128)(2,1)}, bf16[512,2048]{1,0:T(8,128)(2,1)}, bf16[512,2048]{1,0:T(8,128)(2,1)}, bf16[512,512]{1,0:T(8,128)(2,1)}, bf16[512,...) custom-call(s32[9]{0:T(128)} %concatenate.6.refs_0_.info, ...), custom_call_target="tpu_custom_call" | custom-call | flops 4831838208 | bytes 25165824 | tf_op jit(solution)/shard_map/middle/pallas_call | solution.py:260
  88.5 2.6 %all-to-all-start.1 = ((f32[32,8,128]{2,1,0:T(8,128)}), f32[32,8,128]{2,1,0:T(8,128)S(1)}, u32[]{:S(2)}, u32[]{:S(2)}) async-start(f32[32,8,128]{2,1,0:T(8,128)} %get-tuple-element.135), calls=%async_computation.1 | async-start | bytes 262144 | tf_op jit(solution)/shard_map/all_to_all | solution.py:1210
  91.2 2.0 collective-permute-start.4
  93.2 1.3 collective-permute-start.5
  94.5 5.9 %feed_weights.1.refs_22_ = bf16[16,192,1024]{2,1,0:T(8,128)(2,1)} custom-call(bf16[512,512]{1,0:T(8,128)(2,1)} %get-tuple-element.136.refs_0_, bf16[512,2048]{1,0:T(8,128)(2,1)} %get-tuple-element.137.refs_1_, bf16[512,512]{1,0:T(8,128)(2,1)} %get-tuple-element.138.refs_2_, bf16[512,2048]{1,0:T(8,128)(2,1)} %get-tuple-element.139.refs_3_), custom_call_target="tpu_custom_call" | custom-call | flops 2147483648 | bytes 10485760 | tf_op jit(solution)/shard_map/feed_weights/pallas_call | solution.py:260
  101.2 13.8 %conv_back.1 = (bf16[16,192,1024]{2,1,0:T(8,128)(2,1)}, f32[512,512]{1,0:T(8,128)}, bf16[512,512]{1,0:T(8,128)(2,1)}, f32[16,512]{1,0:T(8,128)}) custom-call(s32[9]{0:T(128)} %concatenate.6.refs_0_.info, f32[32,8,128]{2,1,0:T(8,128)} %copy-done.11, f32[2,8,1024]{2,1,0:T(8,128)} %copy-done.20, ...), custom_call_target="tpu_custom_call", output_to_operand_aliasing={{0}: (22, {})} | custom-call | flops 1879048192 | bytes 16777216 | tf_op jit(solution)/shard_map/conv_back/pallas_call | solution.py:260
  115.0 13.2 %attend_back.1 = (bf16[256,512]{1,0:T(8,128)(2,1)}, bf16[256,512]{1,0:T(8,128)(2,1)}, bf16[2,128,1024]{2,1,0:T(8,128)(2,1)}, f32[128,1024]{1,0:T(8,128)}, f32[12...) custom-call(bf16[384,512]{1,0:T(8,128)(2,1)} %get-tuple-element.124., ...), custom_call_target="tpu_custom_call" | custom-call | flops 2818572288 | bytes 16777216 | tf_op jit(solution)/shard_map/attend_back/pallas_call | solution.py:260
  128.2 4.2 %collective-permute-start.6 = (bf16[2,128,1024]{2,1,0:T(8,128)(2,1)}, bf16[2,128,1024]{2,1,0:T(8,128)(2,1)S(1)}, u32[]{:S(2)}, u32[]{:S(2)}) collective-permute-start(bf16[2,128,1024]{2,1,0:T(8,128)(2,1)} %get-tuple-element.158), channel_id=1, source_target_pairs={{0,1},{1,2},{2,3},{3,4},{4,5},{5,6},{6,7},{7,8},{8,9},{9,10},{10,1... | collective-permute-start | bytes 1572872 | tf_op jit(solution)/shard_map/ppermute | solution.py:1206
  132.5 1.5 collective-permute-start.7
  134.0 4.3 %place_weights.1 = (bf16[8,64,512]{2,1,0:T(8,128)(2,1)}, bf16[8,64,512]{2,1,0:T(8,128)(2,1)}) custom-call(s32[9]{0:T(128)} %concatenate.6.refs_0_.info, bf16[512,512]{1,0:T(8,128)(2,1)} %get-tuple-element.122.refs_0_.refs_1_.refs_13_, bf16[256,512]{1,0:T(8,128)(2,1)} %get-tuple-element.160.refs_2_.refs_4_, ...), custom_call_target="tpu_custom_call" | custom-call | flops 536870912 | bytes 4194304 | tf_op jit(solution)/shard_map/place_weights/pallas_call | solution.py:260
  139.3 9.5 %back.1 = (bf16[8,224,512]{2,1,0:T(8,128)(2,1)}, bf16[8,224,512]{2,1,0:T(8,128)(2,1)}, bf16[512,512]{1,0:T(8,128)(2,1)}, bf16[512,512]{1,0:T(8,128)(2,1)}, f32[2...) custom-call(s32[9]{0:T(128)} %concatenate.6.refs_0_.info, bf16[2,128,1024]{2,1,0:T(8,128)(2,1)} %copy-done.12, ...), custom_call_target="tpu_custom_call" | custom-call | flops 2684354560 | bytes 18874368 | tf_op jit(solution)/shard_map/back/pallas_call | solution.py:260
  148.8 6.3 %collective-permute-start.9 = (bf16[8,224,512]{2,1,0:T(8,128)(2,1)}, bf16[8,224,512]{2,1,0:T(8,128)(2,1)S(1)}, u32[]{:S(2)}, u32[]{:S(2)}) collective-permute-start(bf16[8,224,512]{2,1,0:T(8,128)(2,1)} %get-tuple-element.184), channel_id=1, source_target_pairs={{0,1},{1,0},{2,3},{3,2},{4,5},{5,4},{6,7},{7,6},{8,9},{9,8},{10,11... | collective-permute-start | bytes 5505032 | tf_op jit(solution)/shard_map/ppermute | solution.py:1224
  155.1 8.6 %first_back.1 = (bf16[8,160,512]{2,1,0:T(8,128)(2,1)}, bf16[8,160,512]{2,1,0:T(8,128)(2,1)}, f32[4,512]{1,0:T(4,128)}, f32[512,512]{1,0:T(8,128)}) custom-call(s32[9]{0:T(128)} %concatenate.6.refs_0_.info, bf16[512,512]{1,0:T(8,128)(2,1)} %get-tuple-element.122.refs_0_.refs_1_.refs_13_, bf16[512,512]{1,0:T(8,128)(2,1)} %get-tuple-element.171.refs_2_, ...), custom_call_target="tpu_custom_call" | custom-call | flops 3221225472 | bytes 12582912 | tf_op jit(solution)/shard_map/first_back/pallas_call | solution.py:260
  164.6 2.0 fold_b.1
  166.6 1.5 collective-permute-start.11
  168.2 1.6 fold_a.1
  169.8 5.0 %collective-permute-start.10 = (bf16[4,160,512]{2,1,0:T(8,128)(2,1)}, bf16[4,160,512]{2,1,0:T(8,128)(2,1)S(1)}, u32[]{:S(2)}, u32[]{:S(2)}) collective-permute-start(bf16[4,160,512]{2,1,0:T(8,128)(2,1)} %bitcast.12), channel_id=1, source_target_pairs={{0,2},{1,3},{2,0},{3,1},{4,6},{5,7},{6,4},{7,5},{8,10},{9,11},{10,... | collective-permute-start | bytes 1966088 | tf_op jit(solution)/shard_map/ppermute | solution.py:1224
  175.0 2.4 last.1
  179.6 16.2 %collective-permute-done.14.refs_7_ = f32[37,512]{1,0:T(8,128)S(1)} collective-permute-done((f32[37,512]{1,0:T(8,128)S(1)}, f32[37,512]{1,0:T(8,128)S(1)}, u32[]{:S(2)}, u32[]{:S(2)}) %collective-permute-start.14) | collective-permute-done | bytes 75808 | tf_op jit(solution)/shard_map/ppermute | solution.py:1224
  195.8 1.6 collective-permute-done.13.refs_6_
  198.4 1.8 collective-permute-start.18
  200.2 1.5 collective-permute-start.15
  201.7 2.3 collective-permute-start.16
  205.2 3.8 %collective-permute-done.19.refs_7_ = f32[37,512]{1,0:T(8,128)S(1)} collective-permute-done((f32[37,512]{1,0:T(8,128)S(1)}, f32[37,512]{1,0:T(8,128)S(1)}, u32[]{:S(2)}, u32[]{:S(2)}) %collective-permute-start.19) | collective-permute-done | bytes 75808 | tf_op jit(solution)/shard_map/ppermute | solution.py:1494
  209.0 4.4 %collective-permute-done.15.refs_2_ = bf16[1,160,512]{2,1,0:T(8,128)(2,1)S(1)} collective-permute-done((bf16[1,160,512]{2,1,0:T(8,128)(2,1)S(1)}, bf16[1,160,512]{2,1,0:T(8,128)(2,1)S(1)}, u32[]{:S(2)}, u32[]{:S(2)}) %collective-permute-start.15) | collective-permute-done | bytes 163872 | tf_op jit(solution)/shard_map/ppermute | solution.py:1224
  213.4 5.2 %collective-permute-done.17.refs_4_ = bf16[1,160,512]{2,1,0:T(8,128)(2,1)S(1)} collective-permute-done((bf16[1,160,512]{2,1,0:T(8,128)(2,1)S(1)}, bf16[1,160,512]{2,1,0:T(8,128)(2,1)S(1)}, u32[]{:S(2)}, u32[]{:S(2)}) %collective-permute-start.17) | collective-permute-done | bytes 163872 | tf_op jit(solution)/shard_map/ppermute | solution.py:1224
  219.4 1.2 collective-permute-start.24
  221.5 3.3 %collective-permute-start.20 = (bf16[1,224,256]{2,1,0:T(8,128)(2,1)S(1)}, bf16[1,224,256]{2,1,0:T(8,128)(2,1)S(1)}, u32[]{:S(2)}, u32[]{:S(2)}) collective-permute-start(bf16[1,224,256]{2,1,0:T(8,128)(2,1)S(1)} %bitcast.51), channel_id=1, source_target_pairs={{0,4},{1,5},{2,6},{3,7},{4,0},{5,1},{6,2},{7,3},{8,12},{9,13},{10,... | collective-permute-start | bytes 344072 | tf_op jit(solution)/shard_map/ppermute | solution.py:1224
  224.8 2.4 collective-permute-start.22
  227.1 1.2 collective-permute-done.20.refs_3_
  228.4 6.8 %collective-permute-done.21.refs_4_ = bf16[1,224,256]{2,1,0:T(8,128)(2,1)S(1)} collective-permute-done((bf16[1,224,256]{2,1,0:T(8,128)(2,1)S(1)}, bf16[1,224,256]{2,1,0:T(8,128)(2,1)S(1)}, u32[]{:S(2)}, u32[]{:S(2)}) %collective-permute-start.21) | collective-permute-done | bytes 114720 | tf_op jit(solution)/shard_map/ppermute | solution.py:1224
  237.9 1.5 collective-permute-start.28
  239.3 1.8 collective-permute-start.27
  241.1 1.1 collective-permute-start.26
  242.3 2.0 collective-permute-done.28.refs_3_
  244.2 2.2 collective-permute-done.27.refs_2_
  246.5 1.9 finish.1
  (111 shorter events, 15.5 us)
Async XLA Ops:
  7.2 10.8 %copy-start.26 = (s32[4,17]{1,0:T(4,128)S(1)}, s32[4,17]{1,0:T(4,128)}, u32[]{:S(2)}) copy-start(s32[4,17]{1,0:T(4,128)} %param.18) | copy-start | bytes 820
  7.2 11.8 %copy-start.27 = (s32[2]{0:T(128)S(1)}, s32[2]{0:T(128)}, u32[]{:S(2)}) copy-start(s32[2]{0:T(128)} %param.19) | copy-start | bytes 28
  14.0 11.6 %collective-permute-start = (bf16[2,128,1024]{2,1,0:T(8,128)(2,1)}, bf16[2,128,1024]{2,1,0:T(8,128)(2,1)S(1)}, u32[]{:S(2)}, u32[]{:S(2)}) collective-permute-start(bf16[2,128,1024]{2,1,0:T(8,128)(2,1)} %get-tuple-element.120.refs_8_.refs_6_), channel_id=1, source_target_pairs={{0,1},{1,2},{2,3},{3,4},{4,5},{5,6},{6,7},{7,8},{8,9},{9,10},{10,1... | collective-permute-start | bytes 1572872 | tf_op jit(solution)/shard_map/ppermute | solution.py:1206
  16.4 9.2 %collective-permute-start.1 = (bf16[2,128,1024]{2,1,0:T(8,128)(2,1)}, bf16[2,128,1024]{2,1,0:T(8,128)(2,1)S(1)}, u32[]{:S(2)}, u32[]{:S(2)}) collective-permute-start(bf16[2,128,1024]{2,1,0:T(8,128)(2,1)} %get-tuple-element.121.refs_7_.refs_5_), channel_id=1, source_target_pairs={{1,0},{2,1},{3,2},{4,3},{5,4},{6,5},{7,6},{8,7},{9,8},{10,9},{11,1... | collective-permute-start | bytes 1572872 | tf_op jit(solution)/shard_map/ppermute | solution.py:1206
  41.8 8.6 %collective-permute-start.2 = (bf16[2,16,512]{2,1,0:T(8,128)(2,1)}, bf16[2,16,512]{2,1,0:T(8,128)(2,1)S(1)}, u32[]{:S(2)}, u32[]{:S(2)}) collective-permute-start(bf16[2,16,512]{2,1,0:T(8,128)(2,1)} %get-tuple-element.128), channel_id=1, source_target_pairs={{0,1},{1,2},{2,3},{3,4},{4,5},{5,6},{6,7},{7,8},{8,9},{9,10},{10,1... | collective-permute-start | bytes 98312 | tf_op jit(solution)/shard_map/ppermute | solution.py:1206
  49.1 5.2 %collective-permute-start.3 = (bf16[2,16,512]{2,1,0:T(8,128)(2,1)}, bf16[2,16,512]{2,1,0:T(8,128)(2,1)S(1)}, u32[]{:S(2)}, u32[]{:S(2)}) collective-permute-start(bf16[2,16,512]{2,1,0:T(8,128)(2,1)} %get-tuple-element.129), channel_id=1, source_target_pairs={{1,0},{2,1},{3,2},{4,3},{5,4},{6,5},{7,6},{8,7},{9,8},{10,9},{11,1... | collective-permute-start | bytes 98312 | tf_op jit(solution)/shard_map/ppermute | solution.py:1206
  50.4 3.9 %copy-start.16 = (bf16[2,16,512]{2,1,0:T(8,128)(2,1)}, bf16[2,16,512]{2,1,0:T(8,128)(2,1)S(1)}, u32[]{:S(2)}) copy-start(bf16[2,16,512]{2,1,0:T(8,128)(2,1)S(1)} %collective-permute-done.2.refs_1_.refs_8_) | copy-start | bytes 98308
  60.9 14.4 %all-to-all-start = ((f32[32,8,128]{2,1,0:T(8,128)}), f32[32,8,128]{2,1,0:T(8,128)S(1)}, u32[]{:S(2)}, u32[]{:S(2)}) async-start(f32[32,8,128]{2,1,0:T(8,128)} %get-tuple-element.131), calls=%async_computation | async-start | bytes 262144 | tf_op jit(solution)/shard_map/all_to_all | solution.py:1210
  88.5 11.9 %all-to-all-start.1 = ((f32[32,8,128]{2,1,0:T(8,128)}), f32[32,8,128]{2,1,0:T(8,128)S(1)}, u32[]{:S(2)}, u32[]{:S(2)}) async-start(f32[32,8,128]{2,1,0:T(8,128)} %get-tuple-element.135), calls=%async_computation.1 | async-start | bytes 262144 | tf_op jit(solution)/shard_map/all_to_all | solution.py:1210
  91.2 128.2 %reduce-scatter.2.cloned.1.call-start = ((), (), s32[]{:S(2)}) async-start(), calls=%async_computation.3 | async-start | bytes 6684672 | tf_op jit(solution)/shard_map/reduce_scatter | solution.py:1214
  91.2 9.3 %collective-permute-start.4 = (f32[2,8,1024]{2,1,0:T(8,128)}, f32[2,8,1024]{2,1,0:T(8,128)S(1)}, u32[]{:S(2)}, u32[]{:S(2)}) collective-permute-start(f32[2,8,1024]{2,1,0:T(8,128)} %get-tuple-element.141), channel_id=1, source_target_pairs={{0,1},{1,2},{2,3},{3,4},{4,5},{5,6},{6,7},{7,8},{8,9},{9,10},{10,1... | collective-permute-start | bytes 196616 | tf_op jit(solution)/shard_map/ppermute | solution.py:1206
  93.2 7.3 %collective-permute-start.5 = (f32[2,8,1024]{2,1,0:T(8,128)}, f32[2,8,1024]{2,1,0:T(8,128)S(1)}, u32[]{:S(2)}, u32[]{:S(2)}) collective-permute-start(f32[2,8,1024]{2,1,0:T(8,128)} %get-tuple-element.142), channel_id=1, source_target_pairs={{1,0},{2,1},{3,2},{4,3},{5,4},{6,5},{7,6},{8,7},{9,8},{10,9},{11,1... | collective-permute-start | bytes 196616 | tf_op jit(solution)/shard_map/ppermute | solution.py:1206
  128.2 10.0 %collective-permute-start.6 = (bf16[2,128,1024]{2,1,0:T(8,128)(2,1)}, bf16[2,128,1024]{2,1,0:T(8,128)(2,1)S(1)}, u32[]{:S(2)}, u32[]{:S(2)}) collective-permute-start(bf16[2,128,1024]{2,1,0:T(8,128)(2,1)} %get-tuple-element.158), channel_id=1, source_target_pairs={{0,1},{1,2},{2,3},{3,4},{4,5},{5,6},{6,7},{7,8},{8,9},{9,10},{10,1... | collective-permute-start | bytes 1572872 | tf_op jit(solution)/shard_map/ppermute | solution.py:1206
  132.5 5.8 %collective-permute-start.7 = (bf16[2,128,1024]{2,1,0:T(8,128)(2,1)}, bf16[2,128,1024]{2,1,0:T(8,128)(2,1)S(1)}, u32[]{:S(2)}, u32[]{:S(2)}) collective-permute-start(bf16[2,128,1024]{2,1,0:T(8,128)(2,1)} %get-tuple-element.159), channel_id=1, source_target_pairs={{1,0},{2,1},{3,2},{4,3},{5,4},{6,5},{7,6},{8,7},{9,8},{10,9},{11,1... | collective-permute-start | bytes 1572872 | tf_op jit(solution)/shard_map/ppermute | solution.py:1206
  148.8 15.8 %collective-permute-start.9 = (bf16[8,224,512]{2,1,0:T(8,128)(2,1)}, bf16[8,224,512]{2,1,0:T(8,128)(2,1)S(1)}, u32[]{:S(2)}, u32[]{:S(2)}) collective-permute-start(bf16[8,224,512]{2,1,0:T(8,128)(2,1)} %get-tuple-element.184), channel_id=1, source_target_pairs={{0,1},{1,0},{2,3},{3,2},{4,5},{5,4},{6,7},{7,6},{8,9},{9,8},{10,11... | collective-permute-start | bytes 5505032 | tf_op jit(solution)/shard_map/ppermute | solution.py:1224
  155.1 8.7 %copy-start.22 = (f32[8,512]{1,0:T(8,128)S(1)}, f32[8,512]{1,0:T(8,128)}, u32[]{:S(2)}) copy-start(f32[8,512]{1,0:T(8,128)} %get-tuple-element.191) | copy-start | bytes 49156
  155.1 9.4 %copy-start.1 = (bf16[8,224,512]{2,1,0:T(8,128)(2,1)S(1)}, bf16[8,224,512]{2,1,0:T(8,128)(2,1)}, u32[]{:S(2)}) copy-start(bf16[8,224,512]{2,1,0:T(8,128)(2,1)} %get-tuple-element.183.refs_0_) | copy-start | bytes 5505028
  155.1 9.4 %copy-start.10 = (s32[9]{0:T(128)S(1)}, s32[9]{0:T(128)}, u32[]{:S(2)}) copy-start(s32[9]{0:T(128)} %concatenate.6.refs_0_.info) | copy-start | bytes 112
  163.7 4.5 %collective-permute-start.8 = (bf16[8,160,512]{2,1,0:T(8,128)(2,1)}, bf16[8,160,512]{2,1,0:T(8,128)(2,1)S(1)}, u32[]{:S(2)}, u32[]{:S(2)}) collective-permute-start(bf16[8,160,512]{2,1,0:T(8,128)(2,1)} %get-tuple-element.176), channel_id=1, source_target_pairs={{0,1},{1,0},{2,3},{3,2},{4,5},{5,4},{6,7},{7,6},{8,9},{9,8},{10,11... | collective-permute-start | bytes 3932168 | tf_op jit(solution)/shard_map/ppermute | solution.py:1224
  164.6 3.6 %copy-start.2 = (bf16[8,160,512]{2,1,0:T(8,128)(2,1)S(1)}, bf16[8,160,512]{2,1,0:T(8,128)(2,1)}, u32[]{:S(2)}) copy-start(bf16[8,160,512]{2,1,0:T(8,128)(2,1)} %get-tuple-element.175) | copy-start | bytes 3932164
  166.6 8.3 %copy-start.25 = (f32[8,512]{1,0:T(8,128)S(1)}, f32[8,512]{1,0:T(8,128)}, u32[]{:S(2)}) copy-start(f32[8,512]{1,0:T(8,128)} %get-tuple-element.190) | copy-start | bytes 49156
  166.6 8.3 %copy-start = (bf16[2,256,512]{2,1,0:T(8,128)(2,1)S(1)}, bf16[2,256,512]{2,1,0:T(8,128)(2,1)}, u32[]{:S(2)}) copy-start(bf16[2,256,512]{2,1,0:T(8,128)(2,1)} %refs_1_.5) | copy-start | bytes 1572868
  166.6 8.4 %copy-start.3 = (f32[512,512]{1,0:T(8,128)S(1)}, f32[512,512]{1,0:T(8,128)}, u32[]{:S(2)}) copy-start(f32[512,512]{1,0:T(8,128)} %get-tuple-element.178.refs_2_) | copy-start | bytes 3145732
  166.6 8.4 %copy-start.6 = (f32[256,512]{1,0:T(8,128)S(1)}, f32[256,512]{1,0:T(8,128)}, u32[]{:S(2)}) copy-start(f32[256,512]{1,0:T(8,128)} %get-tuple-element.179.refs_3_) | copy-start | bytes 1572868
  166.6 8.4 %copy-start.7 = (f32[256,512]{1,0:T(8,128)S(1)}, f32[256,512]{1,0:T(8,128)}, u32[]{:S(2)}) copy-start(f32[256,512]{1,0:T(8,128)} %get-tuple-element.180.refs_4_) | copy-start | bytes 1572868
  166.6 8.4 %copy-start.8 = (f32[6,512]{1,0:T(8,128)S(1)}, f32[6,512]{1,0:T(8,128)}, u32[]{:S(2)}) copy-start(f32[6,512]{1,0:T(8,128)} %refs_0_.3) | copy-start | bytes 36868
  166.6 30.9 %collective-permute-start.11 = (bf16[8,224,256]{2,1,0:T(8,128)(2,1)}, bf16[8,224,256]{2,1,0:T(8,128)(2,1)S(1)}, u32[]{:S(2)}, u32[]{:S(2)}) collective-permute-start(bf16[8,224,256]{2,1,0:T(8,128)(2,1)} %get-tuple-element.187), channel_id=1, source_target_pairs={{0,16},{16,0},{1,17},{17,1},{2,18},{18,2},{3,19},{19,3},{4,20},{20... | collective-permute-start | bytes 2752520 | tf_op jit(solution)/shard_map/ppermute | solution.py:1461
  169.8 7.6 %copy-start.23 = (f32[4,512]{1,0:T(4,128)S(1)}, f32[4,512]{1,0:T(4,128)}, u32[]{:S(2)}) copy-start(f32[4,512]{1,0:T(4,128)} %get-tuple-element.194) | copy-start | bytes 24580
  169.8 7.6 %copy-start.24 = (f32[4,512]{1,0:T(4,128)S(1)}, f32[4,512]{1,0:T(4,128)}, u32[]{:S(2)}) copy-start(f32[4,512]{1,0:T(4,128)} %get-tuple-element.193) | copy-start | bytes 24580
  169.8 27.6 %copy-start.5 = (bf16[8,224,256]{2,1,0:T(8,128)(2,1)S(1)}, bf16[8,224,256]{2,1,0:T(8,128)(2,1)}, u32[]{:S(2)}) copy-start(bf16[8,224,256]{2,1,0:T(8,128)(2,1)} %copy-done.4) | copy-start | bytes 2752516
  169.8 27.6 %collective-permute-start.10 = (bf16[4,160,512]{2,1,0:T(8,128)(2,1)}, bf16[4,160,512]{2,1,0:T(8,128)(2,1)S(1)}, u32[]{:S(2)}, u32[]{:S(2)}) collective-permute-start(bf16[4,160,512]{2,1,0:T(8,128)(2,1)} %bitcast.12), channel_id=1, source_target_pairs={{0,2},{1,3},{2,0},{3,1},{4,6},{5,7},{6,4},{7,5},{8,10},{9,11},{10,... | collective-permute-start | bytes 1966088 | tf_op jit(solution)/shard_map/ppermute | solution.py:1224
  177.7 18.2 %collective-permute-start.14 = (f32[37,512]{1,0:T(8,128)S(1)}, f32[37,512]{1,0:T(8,128)S(1)}, u32[]{:S(2)}, u32[]{:S(2)}) collective-permute-start(f32[37,512]{1,0:T(8,128)S(1)} %concatenate.7.refs_4_), channel_id=1, source_target_pairs={{0,3},{1,2},{2,1},{3,0},{4,7},{5,6},{6,5},{7,4},{8,11},{9,10},{10,... | collective-permute-start | bytes 227336 | tf_op jit(solution)/shard_map/ppermute | solution.py:1224
  177.7 19.7 %collective-permute-start.13 = (f32[37,512]{1,0:T(8,128)S(1)}, f32[37,512]{1,0:T(8,128)S(1)}, u32[]{:S(2)}, u32[]{:S(2)}) collective-permute-start(f32[37,512]{1,0:T(8,128)S(1)} %concatenate.7.refs_4_), channel_id=1, source_target_pairs={{0,2},{1,3},{2,0},{3,1},{4,6},{5,7},{6,4},{7,5},{8,10},{9,11},{10,... | collective-permute-start | bytes 227336 | tf_op jit(solution)/shard_map/ppermute | solution.py:1224
  178.8 18.6 %collective-permute-start.12 = (f32[37,512]{1,0:T(8,128)S(1)}, f32[37,512]{1,0:T(8,128)S(1)}, u32[]{:S(2)}, u32[]{:S(2)}) collective-permute-start(f32[37,512]{1,0:T(8,128)S(1)} %concatenate.7.refs_4_), channel_id=1, source_target_pairs={{0,1},{1,0},{2,3},{3,2},{4,5},{5,4},{6,7},{7,6},{8,9},{9,8},{10,11... | collective-permute-start | bytes 227336 | tf_op jit(solution)/shard_map/ppermute | solution.py:1224
  198.4 20.2 %collective-permute-start.18 = (bf16[4,224,256]{2,1,0:T(8,128)(2,1)S(1)}, bf16[4,224,256]{2,1,0:T(8,128)(2,1)S(1)}, u32[]{:S(2)}, u32[]{:S(2)}) collective-permute-start(bf16[4,224,256]{2,1,0:T(8,128)(2,1)S(1)} %bitcast.45), channel_id=1, source_target_pairs={{0,2},{1,3},{2,0},{3,1},{4,6},{5,7},{6,4},{7,5},{8,10},{9,11},{10,... | collective-permute-start | bytes 1376264 | tf_op jit(solution)/shard_map/ppermute | solution.py:1224
  200.2 13.2 %collective-permute-start.15 = (bf16[1,160,512]{2,1,0:T(8,128)(2,1)S(1)}, bf16[1,160,512]{2,1,0:T(8,128)(2,1)S(1)}, u32[]{:S(2)}, u32[]{:S(2)}) collective-permute-start(bf16[1,160,512]{2,1,0:T(8,128)(2,1)S(1)} %bitcast.48), channel_id=1, source_target_pairs={{0,4},{1,5},{2,6},{3,7},{4,0},{5,1},{6,2},{7,3},{8,12},{9,13},{10,... | collective-permute-start | bytes 491528 | tf_op jit(solution)/shard_map/ppermute | solution.py:1224
  201.7 11.7 %collective-permute-start.16 = (bf16[1,160,512]{2,1,0:T(8,128)(2,1)S(1)}, bf16[1,160,512]{2,1,0:T(8,128)(2,1)S(1)}, u32[]{:S(2)}, u32[]{:S(2)}) collective-permute-start(bf16[1,160,512]{2,1,0:T(8,128)(2,1)S(1)} %bitcast.47), channel_id=1, source_target_pairs={{0,8},{1,9},{2,10},{3,11},{4,12},{5,13},{6,14},{7,15},{8,0},{9,1},... | collective-permute-start | bytes 491528 | tf_op jit(solution)/shard_map/ppermute | solution.py:1224
  204.0 14.6 %collective-permute-start.17 = (bf16[1,160,512]{2,1,0:T(8,128)(2,1)S(1)}, bf16[1,160,512]{2,1,0:T(8,128)(2,1)S(1)}, u32[]{:S(2)}, u32[]{:S(2)}) collective-permute-start(bf16[1,160,512]{2,1,0:T(8,128)(2,1)S(1)} %bitcast.46), channel_id=1, source_target_pairs={{0,12},{1,13},{2,14},{3,15},{4,8},{5,9},{6,10},{7,11},{8,4},{9,5},... | collective-permute-start | bytes 491528 | tf_op jit(solution)/shard_map/ppermute | solution.py:1224
  204.6 4.4 %collective-permute-start.19 = (f32[37,512]{1,0:T(8,128)S(1)}, f32[37,512]{1,0:T(8,128)S(1)}, u32[]{:S(2)}, u32[]{:S(2)}) collective-permute-start(f32[37,512]{1,0:T(8,128)S(1)} %get-tuple-element.201.refs_6_), channel_id=1, source_target_pairs={{0,16},{16,0},{1,17},{17,1},{2,18},{18,2},{3,19},{19,3},{4,20},{20... | collective-permute-start | bytes 227336 | tf_op jit(solution)/shard_map/ppermute | solution.py:1494
  219.4 15.9 %collective-permute-start.24 = (bf16[1,192,1024]{2,1,0:T(8,128)(2,1)}, bf16[1,192,1024]{2,1,0:T(8,128)(2,1)S(1)}, u32[]{:S(2)}, u32[]{:S(2)}) collective-permute-start(bf16[1,192,1024]{2,1,0:T(8,128)(2,1)} %reduce-scatter.2.cloned.1.call-done.refs_2_), channel_id=1, source_target_pairs={{0,16},{16,0},{1,17},{17,1},{2,18},{18,2},{3,19},{19,3},{4,20},{20... | collective-permute-start | bytes 1179656 | tf_op jit(solution)/shard_map/ppermute | solution.py:1491
  220.5 14.7 %collective-permute-start.23 = (bf16[1,160,512]{2,1,0:T(8,128)(2,1)S(1)}, bf16[1,160,512]{2,1,0:T(8,128)(2,1)S(1)}, u32[]{:S(2)}, u32[]{:S(2)}) collective-permute-start(bf16[1,160,512]{2,1,0:T(8,128)(2,1)S(1)} %get-tuple-element.205.refs_1_), channel_id=1, source_target_pairs={{0,16},{16,0},{1,17},{17,1},{2,18},{18,2},{3,19},{19,3},{4,20},{20... | collective-permute-start | bytes 491528 | tf_op jit(solution)/shard_map/ppermute | solution.py:1490
  221.5 6.9 %collective-permute-start.20 = (bf16[1,224,256]{2,1,0:T(8,128)(2,1)S(1)}, bf16[1,224,256]{2,1,0:T(8,128)(2,1)S(1)}, u32[]{:S(2)}, u32[]{:S(2)}) collective-permute-start(bf16[1,224,256]{2,1,0:T(8,128)(2,1)S(1)} %bitcast.51), channel_id=1, source_target_pairs={{0,4},{1,5},{2,6},{3,7},{4,0},{5,1},{6,2},{7,3},{8,12},{9,13},{10,... | collective-permute-start | bytes 344072 | tf_op jit(solution)/shard_map/ppermute | solution.py:1224
  224.8 10.4 %collective-permute-start.21 = (bf16[1,224,256]{2,1,0:T(8,128)(2,1)S(1)}, bf16[1,224,256]{2,1,0:T(8,128)(2,1)S(1)}, u32[]{:S(2)}, u32[]{:S(2)}) collective-permute-start(bf16[1,224,256]{2,1,0:T(8,128)(2,1)S(1)} %bitcast.50), channel_id=1, source_target_pairs={{0,8},{1,9},{2,10},{3,11},{4,12},{5,13},{6,14},{7,15},{8,0},{9,1},... | collective-permute-start | bytes 344072 | tf_op jit(solution)/shard_map/ppermute | solution.py:1224
  224.8 10.4 %collective-permute-start.22 = (bf16[1,224,256]{2,1,0:T(8,128)(2,1)S(1)}, bf16[1,224,256]{2,1,0:T(8,128)(2,1)S(1)}, u32[]{:S(2)}, u32[]{:S(2)}) collective-permute-start(bf16[1,224,256]{2,1,0:T(8,128)(2,1)S(1)} %bitcast.49), channel_id=1, source_target_pairs={{0,12},{1,13},{2,14},{3,15},{4,8},{5,9},{6,10},{7,11},{8,4},{9,5},... | collective-permute-start | bytes 344072 | tf_op jit(solution)/shard_map/ppermute | solution.py:1224
  237.0 9.5 %collective-permute-start.25 = (bf16[1,224,256]{2,1,0:T(8,128)(2,1)S(1)}, bf16[1,224,256]{2,1,0:T(8,128)(2,1)S(1)}, u32[]{:S(2)}, u32[]{:S(2)}) collective-permute-start(bf16[1,224,256]{2,1,0:T(8,128)(2,1)S(1)} %get-tuple-element.211), channel_id=1, source_target_pairs={{0,16},{16,0},{1,17},{17,1},{2,18},{18,2},{3,19},{19,3},{4,20},{20... | collective-permute-start | bytes 344072 | tf_op jit(solution)/shard_map/ppermute | solution.py:1499
  237.9 6.3 %collective-permute-start.28 = (f32[37,512]{1,0:T(8,128)S(1)}, f32[37,512]{1,0:T(8,128)S(1)}, u32[]{:S(2)}, u32[]{:S(2)}) collective-permute-start(f32[37,512]{1,0:T(8,128)S(1)} %get-tuple-element.213.refs_0_), channel_id=1, source_target_pairs={{0,12},{1,13},{2,14},{3,15},{4,8},{5,9},{6,10},{7,11},{8,4},{9,5},... | collective-permute-start | bytes 227336 | tf_op jit(solution)/shard_map/ppermute | solution.py:1224
  239.3 7.1 %collective-permute-start.27 = (f32[37,512]{1,0:T(8,128)S(1)}, f32[37,512]{1,0:T(8,128)S(1)}, u32[]{:S(2)}, u32[]{:S(2)}) collective-permute-start(f32[37,512]{1,0:T(8,128)S(1)} %get-tuple-element.213.refs_0_), channel_id=1, source_target_pairs={{0,8},{1,9},{2,10},{3,11},{4,12},{5,13},{6,14},{7,15},{8,0},{9,1},... | collective-permute-start | bytes 227336 | tf_op jit(solution)/shard_map/ppermute | solution.py:1224
  241.1 5.3 %collective-permute-start.26 = (f32[37,512]{1,0:T(8,128)S(1)}, f32[37,512]{1,0:T(8,128)S(1)}, u32[]{:S(2)}, u32[]{:S(2)}) collective-permute-start(f32[37,512]{1,0:T(8,128)S(1)} %get-tuple-element.213.refs_0_), channel_id=1, source_target_pairs={{0,4},{1,5},{2,6},{3,7},{4,0},{5,1},{6,2},{7,3},{8,12},{9,13},{10,... | collective-permute-start | bytes 227336 | tf_op jit(solution)/shard_map/ppermute | solution.py:1224
  (12 other events, 14.6 us)
Sparse Core Ops, SparseCore 0:
  115.1 97.5 reduce-scatter.1
